TPU v7x, 32 devices: a whole 2x2x4 slice. The times are simulated.
32 devices in a mesh: wide: 16 (over z, y, core), narrow: 2 (over x).
Axes of the slice: x: 2, y: 2, z: 4, core: 2. Of those that a mesh axis runs over, the one named last changes fastest.
Arguments:
- state: float32 [2, 4194304], P(None, ('wide', 'narrow')), may hold values from -6 to 6
- gate_re: float32 [6, 128, 128], replicated, may hold values from -0.375 to 0.375
- gate_im: float32 [6, 128, 128], replicated, may hold values from -0.375 to 0.375
- bit_orders: int32 [6, 8], replicated, may hold values from 0 to 7, each once within a row
- phase_pairs: int32 [6, 16, 2], replicated, may hold values from 0 to 11
- phase_angles: float32 [6, 16], replicated, may hold values from -3.140625 to 3.140625
Outputs:
- final_state: float32 [2, 4194304], P(None, ('wide', 'narrow'))
Inputs may be any that keep to these rules, and one draw needn't show every extreme that they name: `bit_orders`: each row is a permutation of 0 to 7. `phase_pairs`: qubit positions among the lowest 12; the two of a pair may coincide.
All inputs are finite; a program needn't handle non-finite values.
Results may differ from a plain program's by a relative error of at most 0.00012.
Values sent between devices are 32-bit elements; how exact they have to be, the bound alone decides.
No kernel may reach another device: no remote copies, remote signals or barrier semaphores. Data moves between devices by JAX's collectives and lax.ppermute only.
A program may use at most 64 MiB of HBM per device.

v0:
```python
from functools import partial

import jax
import jax.numpy as jnp
from jax import lax
from jax.experimental import pallas as pl
from jax.experimental.pallas import tpu as pltpu
from jax.sharding import PartitionSpec as P

LAYERS = 6
GATE = 128
LOW = 256
LOW_BITS = 8
PHASES = 16
PHASE_BITS = 12
LANES = 128


def split(x):
    high = x.astype(jnp.bfloat16)
    low = (x - high.astype(jnp.float32)).astype(jnp.bfloat16)
    return high, low


def tables_kernel(spect, narrow, order_ref, pair_ref, angle_ref, place_ref, re_ref, im_ref, high_ref, low_ref, turn_ref):
    layer = pl.program_id(0)

    t = lax.broadcasted_iota(jnp.int32, (LOW, LOW), 1)
    source = jnp.zeros((LOW, LOW), jnp.int32)
    for bit in range(LOW_BITS):
        source = source + lax.shift_left((t >> bit) & 1, jnp.full((LOW, LOW), order_ref[layer, bit], jnp.int32))
    hot = jnp.where(lax.broadcasted_iota(jnp.int32, (LOW, LOW), 0) == source, 1.0, 0.0).astype(jnp.bfloat16)
    contract = (((1,), (1,)), ((), ()))
    for part, gate in enumerate((re_ref[0], im_ref[0])):
        for out_ref, piece in zip((high_ref, low_ref), split(gate)):
            for e in range(2):
                moved = lax.dot_general(
                    hot[:, e * GATE : (e + 1) * GATE], piece, contract, preferred_element_type=jnp.float32
                ).astype(jnp.bfloat16)
                lanes = slice(e * GATE, (e + 1) * GATE)
                shifted = slice(LOW + e * GATE, LOW + (e + 1) * GATE)
                if part == 0:
                    out_ref[0, :LOW, lanes] = moved
                    out_ref[0, LOW:, shifted] = moved
                else:
                    out_ref[0, :LOW, shifted] = moved
                    out_ref[0, LOW:, lanes] = -moved

    row = lax.broadcasted_iota(jnp.int32, (spect, LOW), 0)
    lane = lax.broadcasted_iota(jnp.int32, (spect, LOW), 1)
    r = place_ref[0] * (spect // narrow) + row // narrow
    b = jnp.where(layer % 2 == 0, jnp.full((spect, LOW), place_ref[1], jnp.int32), row % narrow)
    u = ((r * narrow + b) * LOW + lane) & (2**PHASE_BITS - 1)
    phase = jnp.zeros((spect, LOW), jnp.float32)
    for gate in range(PHASES):
        first = u >> jnp.full((spect, LOW), pair_ref[layer, 2 * gate], jnp.int32)
        second = u >> jnp.full((spect, LOW), pair_ref[layer, 2 * gate + 1], jnp.int32)
        phase = phase + jnp.where((first & second & 1) == 1, angle_ref[layer, gate], 0.0)
    turn_ref[0, 0] = jnp.cos(phase)
    turn_ref[0, 1] = jnp.sin(phase)


def exchange_modes(rows, span):
    rows = list(rows)
    lane = lax.broadcasted_iota(jnp.int32, rows[0].shape, 1)
    step = 1
    while step < len(rows):
        shift = step * span
        upper = (lane & shift) != 0
        for m in range(len(rows)):
            if m & step:
                continue
            x0, x1 = rows[m], rows[m + step]
            if 2 * shift == LANES:
                crossing = pltpu.roll(jnp.where(upper, x0, x1), shift, 1)
                rows[m] = jnp.where(upper, crossing, x0)
                rows[m + step] = jnp.where(upper, x1, crossing)
            else:
                rows[m] = jnp.where(upper, pltpu.roll(x1, shift, 1), x0)
                rows[m + step] = jnp.where(upper, x1, pltpu.roll(x0, LANES - shift, 1))
        step *= 2
    return rows


def layers_kernel(wide, spect, x_ref, high_ref, low_ref, turn_ref, out_ref, state, left_high, left_low):
    layer = pl.program_id(0)
    count = wide * spect
    span = LOW // wide
    half = wide // 2

    @pl.when(layer == 0)
    def _():
        for part in range(2):
            for lanes in range(2):
                state[part, :, lanes * LANES : (lanes + 1) * LANES] = x_ref[pl.ds(2 * lanes + part, count, stride=4), :]

    for part in range(2):
        for top in range(2):
            for lanes in range(2):
                first = top * half * spect
                block = state[part, first : first + half * spect, lanes * LANES : (lanes + 1) * LANES]
                rows = exchange_modes([block[m * spect : (m + 1) * spect] for m in range(half)], span)
                for g in range(half):
                    at = (lanes * half + g) * spect
                    column = part * LOW + top * LANES
                    high, low = split(rows[g])
                    left_high[at : at + spect, column : column + LANES] = high
                    left_low[at : at + spect, column : column + LANES] = low

    cosine = turn_ref[0, 0][None]
    sine = turn_ref[0, 1][None]
    for block in range(2):
        rows = slice(block * half * spect, (block + 1) * half * spect)
        dot = partial(jnp.dot, preferred_element_type=jnp.float32)
        gated = dot(left_high[rows], high_ref[0])
        gated = gated + dot(left_low[rows], high_ref[0])
        gated = gated + dot(left_high[rows], low_ref[0])
        real = gated[:, :LOW].reshape(half, spect, LOW)
        imag = gated[:, LOW:].reshape(half, spect, LOW)
        state[0, rows] = (real * cosine - imag * sine).reshape(half * spect, LOW)
        state[1, rows] = (real * sine + imag * cosine).reshape(half * spect, LOW)

    @pl.when(layer == LAYERS - 1)
    def _():
        for part in range(2):
            for lanes in range(2):
                out_ref[pl.ds(2 * lanes + part, count, stride=4), :] = state[part, :, lanes * LANES : (lanes + 1) * LANES]


def local(state, gate_re, gate_im, bit_orders, phase_pairs, phase_angles):
    wide = lax.axis_size("wide")
    narrow = lax.axis_size("narrow")
    amps = state.shape[1]
    spect = amps // (wide * LOW)
    count = wide * spect

    rows = state.reshape(2, amps // LANES, LANES).transpose(1, 0, 2).reshape(2 * amps // LANES, LANES)
    gathered = lax.all_to_all(rows, "wide", split_axis=0, concat_axis=0, tiled=True)

    place = jnp.stack([lax.axis_index("wide"), lax.axis_index("narrow")]).astype(jnp.int32)
    smem = pl.BlockSpec(memory_space=pltpu.SMEM)
    gate_spec = pl.BlockSpec((1, GATE, GATE), lambda l: (l, 0, 0))
    square_spec = pl.BlockSpec((1, 2 * LOW, 2 * LOW), lambda l: (l, 0, 0))
    turn_spec = pl.BlockSpec((1, 2, spect, LOW), lambda l: (l, 0, 0, 0))
    square = jax.ShapeDtypeStruct((LAYERS, 2 * LOW, 2 * LOW), jnp.bfloat16)
    high, low, turn = pl.pallas_call(
        partial(tables_kernel, spect, narrow),
        grid=(LAYERS,),
        in_specs=[smem, smem, smem, smem, gate_spec, gate_spec],
        out_specs=[square_spec, square_spec, turn_spec],
        out_shape=[square, square, jax.ShapeDtypeStruct((LAYERS, 2, spect, LOW), jnp.float32)],
        cost_estimate=pl.CostEstimate(flops=10**9, bytes_accessed=8 * 10**6, transcendentals=10**5),
        name="tables",
    )(bit_orders, phase_pairs.reshape(LAYERS, 2 * PHASES), phase_angles, place, gate_re, gate_im)

    whole = pl.BlockSpec((4 * count, LANES), lambda l: (0, 0))
    done = pl.pallas_call(
        partial(layers_kernel, wide, spect),
        grid=(LAYERS,),
        in_specs=[whole, square_spec, square_spec, turn_spec],
        out_specs=whole,
        out_shape=jax.ShapeDtypeStruct((4 * count, LANES), jnp.float32),
        scratch_shapes=[
            pltpu.VMEM((2, count, LOW), jnp.float32),
            pltpu.VMEM((count, 2 * LOW), jnp.bfloat16),
            pltpu.VMEM((count, 2 * LOW), jnp.bfloat16),
        ],
        compiler_params=pltpu.CompilerParams(vmem_limit_bytes=32 * 2**20),
        cost_estimate=pl.CostEstimate(flops=5 * 10**9, bytes_accessed=10**7, transcendentals=0),
        name="layers",
    )(gathered, high, low, turn)

    back = lax.all_to_all(done, "wide", split_axis=0, concat_axis=0, tiled=True)
    return back.reshape(amps // LANES, 2, LANES).transpose(1, 0, 2).reshape(2, amps)


def solution(mesh):
    return jax.shard_map(
        local,
        mesh=mesh,
        in_specs=(P(None, ("wide", "narrow")), P(), P(), P(), P(), P()),
        out_specs=P(None, ("wide", "narrow")),
        check_vma=False,
    )
```

profile of v0, /device:TPU:0, one launch (start us, length us, event | category | flops | bytes accessed | tf_op | source)
XLA Modules:
  0.0 80.0 jit_solution(17074424887903144258)
XLA Ops:
  0.0 0.0 copy-start.3
  0.0 1.3 %copy.20 = f32[1,2,1024,128]{3,2,1,0:T(8,128)S(1)} copy(f32[1,2,1024,128]{3,1,2,0:T(2,128)} %bitcast.26) | data formatting | bytes 2097152
  1.3 1.8 %copy.10 = f32[1024,2,128]{2,1,0:T(2,128)} copy(f32[1024,2,128]{2,0,1:T(8,128)S(1)} %bitcast.25) | data formatting | bytes 2097152 | tf_op jit(solution)/shard_map/transpose | solution.py:137
  3.1 7.4 %all-to-all-start = ((f32[16,128,128]{2,1,0:T(8,128)}), f32[16,128,128]{2,1,0:T(8,128)S(1)}, u32[]{:S(2)}, u32[]{:S(2)}) async-start(f32[16,128,128]{2,1,0:T(8,128)} %bitcast.1), calls=%async_computation | async-start | bytes 2097152 | tf_op jit(solution)/shard_map/all_to_all | solution.py:138
  10.5 0.0 copy-done.3
  10.5 0.1 copy.11
  10.6 0.7 copy.12.pair_ref
  11.3 0.7 pad_add_fusion.place_ref
  11.9 6.1 %tables.1 = (bf16[6,512,512]{2,1,0:T(8,128)(2,1)}, bf16[6,512,512]{2,1,0:T(8,128)(2,1)}, f32[6,2,32,256]{3,2,1,0:T(8,128)}) custom-call(s32[6,8]{1,0:T(8,128)} %order_ref.1, s32[6,32]{1,0:T(8,128)} %copy.12.pair_ref, f32[6,16]{1,0:T(8,128)} %angle_ref.1, s32[2]{0:T(128)} %pad_add_fusion.place_ref, f32[6,128,128]{2,1,0:T(8,128)} %re_ref.1, f32[6,128,128]{2,1,0:T(8,128)} %im_ref.1), custom_call_target="tpu_custom_call" | custom-call | flops 1000000000 | bytes 8000000 | tf_op jit(solution)/shard_map/tables/pallas_call | solution.py:146
  18.0 15.4 %all-to-all-done = f32[16,128,128]{2,1,0:T(8,128)S(1)} async-done(((f32[16,128,128]{2,1,0:T(8,128)}), f32[16,128,128]{2,1,0:T(8,128)S(1)}, u32[]{:S(2)}, u32[]{:S(2)}) %all-to-all-start) | async-done | bytes 1048608 | tf_op jit(solution)/shard_map/all_to_all | solution.py:138
  33.4 0.0 copy-start
  33.4 1.9 %copy-done = bf16[6,512,512]{2,1,0:T(8,128)(2,1)S(1)} copy-done((bf16[6,512,512]{2,1,0:T(8,128)(2,1)S(1)}, bf16[6,512,512]{2,1,0:T(8,128)(2,1)}, u32[]{:S(2)}) %copy-start) | copy-done | bytes 3145752
  35.3 0.0 copy-start.1
  35.3 1.9 %copy-done.1 = bf16[6,512,512]{2,1,0:T(8,128)(2,1)S(1)} copy-done((bf16[6,512,512]{2,1,0:T(8,128)(2,1)S(1)}, bf16[6,512,512]{2,1,0:T(8,128)(2,1)}, u32[]{:S(2)}) %copy-start.1) | copy-done | bytes 3145752
  37.2 0.0 copy-start.2
  37.2 1.0 %copy-done.2 = f32[6,2,32,256]{3,2,1,0:T(8,128)S(1)} copy-done((f32[6,2,32,256]{3,2,1,0:T(8,128)S(1)}, f32[6,2,32,256]{3,2,1,0:T(8,128)}, u32[]{:S(2)}) %copy-start.2) | copy-done | bytes 393240
  38.2 8.4 %layers.1 = f32[2048,128]{1,0:T(8,128)S(1)} custom-call(f32[2048,128]{1,0:T(8,128)S(1)} %bitcast.21, bf16[6,512,512]{2,1,0:T(8,128)(2,1)S(1)} %copy-done, bf16[6,512,512]{2,1,0:T(8,128)(2,1)S(1)} %copy-done.1, f32[6,2,32,256]{3,2,1,0:T(8,128)S(1)} %copy-done.2), custom_call_target="tpu_custom_call" | custom-call | flops 5000000000 | bytes 10000000 | tf_op jit(solution)/shard_map/layers/pallas_call | solution.py:157
  46.6 31.5 %all_to_all.20 = f32[16,128,128]{2,1,0:T(8,128)S(1)} all-to-all(f32[16,128,128]{2,1,0:T(8,128)S(1)} %bitcast.22), channel_id=1, replica_groups=mesh['wide'=16,'narrow'=2] {'wide'}, dimensions={0} | all-to-all | bytes 2097152 | tf_op jit(solution)/shard_map/all_to_all | solution.py:173
  78.1 0.1 copy.21
  78.2 1.8 %copy.19 = f32[1,2,1024,128]{3,1,2,0:T(2,128)} copy(f32[1,2,1024,128]{3,2,1,0:T(8,128)S(1)} %bitcast.24) | data formatting | bytes 2097152
Async XLA Ops:
  0.0 10.5 %copy-start.3 = (s32[6,16,2]{1,2,0:T(2,128)S(1)}, s32[6,16,2]{1,2,0:T(2,128)}, u32[]{:S(2)}) copy-start(s32[6,16,2]{1,2,0:T(2,128)} %param.10) | copy-start | bytes 2308
  3.1 30.3 %all-to-all-start = ((f32[16,128,128]{2,1,0:T(8,128)}), f32[16,128,128]{2,1,0:T(8,128)S(1)}, u32[]{:S(2)}, u32[]{:S(2)}) async-start(f32[16,128,128]{2,1,0:T(8,128)} %bitcast.1), calls=%async_computation | async-start | bytes 2097152 | tf_op jit(solution)/shard_map/all_to_all | solution.py:138
  33.4 1.9 %copy-start = (bf16[6,512,512]{2,1,0:T(8,128)(2,1)S(1)}, bf16[6,512,512]{2,1,0:T(8,128)(2,1)}, u32[]{:S(2)}) copy-start(bf16[6,512,512]{2,1,0:T(8,128)(2,1)} %get-tuple-element.8.high_ref) | copy-start | bytes 9437188
  35.3 1.9 %copy-start.1 = (bf16[6,512,512]{2,1,0:T(8,128)(2,1)S(1)}, bf16[6,512,512]{2,1,0:T(8,128)(2,1)}, u32[]{:S(2)}) copy-start(bf16[6,512,512]{2,1,0:T(8,128)(2,1)} %get-tuple-element.9.low_ref) | copy-start | bytes 9437188
  37.2 1.0 %copy-start.2 = (f32[6,2,32,256]{3,2,1,0:T(8,128)S(1)}, f32[6,2,32,256]{3,2,1,0:T(8,128)}, u32[]{:S(2)}) copy-start(f32[6,2,32,256]{3,2,1,0:T(8,128)} %get-tuple-element.10.turn_ref) | copy-start | bytes 1179652
where the time goes:
time: 81 us; the launch traced here: 80 us
  blocking collectives  31.5 us (39%)
  waiting for transfers between devices  15.4 us (19%)
  Pallas kernels  14.5 us (18%)
  local copies, waits for them, and re-layouts  10.5 us (13%)
  starting transfers between devices  7.39 us (9%)
    all_to_all x1, blocking collectives, local(): back = lax.all_to_all(done, 'wide', split_axis=0, concat_axis=0, tiled=True)  31.5 us
    all_to_all x1, waiting for transfers between devices, local(): lax.all_to_all(rows, 'wide', split_axis=0, concat_axis=0, tiled=True)  15.4 us
    pallas_call x1, Pallas kernels, local(): pl.pallas_call(partial(layers_kernel, wide, spect), grid=(LAYERS,), in_sp...  8.43 us
    unnamed x11, local copies, waits for them, and re-layouts  7.96 us
    all_to_all x1, starting transfers between devices, local(): lax.all_to_all(rows, 'wide', split_axis=0, concat_axis=0, tiled=True)  7.39 us
    pallas_call x1, Pallas kernels, local(): pl.pallas_call(partial(tables_kernel, spect, narrow), grid=(LAYERS,), in_...  6.08 us
    transpose x1, local copies, waits for them, and re-layouts, local(): state.reshape(2, amps // LANES, LANES).transpose(1, 0, 2)  1.78 us
  transfers between devices with their start and end apart: 1, of which 1 were waited for; matrix products, arithmetic and copies ran while one was open for 2% of the time, Pallas kernels for 8%

commit v1 on v0

--- a/solution.py
+++ b/solution.py
@@ -4,6 +4,7 @@
 import jax.numpy as jnp
 from jax import lax
 from jax.experimental import pallas as pl
+from jax.experimental.layout import Layout, with_layout_constraint
 from jax.experimental.pallas import tpu as pltpu
 from jax.sharding import PartitionSpec as P
 
@@ -14,6 +15,7 @@
 PHASES = 16
 PHASE_BITS = 12
 LANES = 128
+PAIRED = Layout(major_to_minor=(1, 0, 2))
 
 
 def split(x):
@@ -134,7 +136,8 @@
     spect = amps // (wide * LOW)
     count = wide * spect
 
-    rows = state.reshape(2, amps // LANES, LANES).transpose(1, 0, 2).reshape(2 * amps // LANES, LANES)
+    view = with_layout_constraint(state.reshape(2, amps // LANES, LANES), PAIRED)
+    rows = view.transpose(1, 0, 2).reshape(2 * amps // LANES, LANES)
     gathered = lax.all_to_all(rows, "wide", split_axis=0, concat_axis=0, tiled=True)
 
     place = jnp.stack([lax.axis_index("wide"), lax.axis_index("narrow")]).astype(jnp.int32)
@@ -149,6 +152,7 @@
         in_specs=[smem, smem, smem, smem, gate_spec, gate_spec],
         out_specs=[square_spec, square_spec, turn_spec],
         out_shape=[square, square, jax.ShapeDtypeStruct((LAYERS, 2, spect, LOW), jnp.float32)],
+        compiler_params=pltpu.CompilerParams(vmem_limit_bytes=16 * 2**20),
         cost_estimate=pl.CostEstimate(flops=10**9, bytes_accessed=8 * 10**6, transcendentals=10**5),
         name="tables",
     )(bit_orders, phase_pairs.reshape(LAYERS, 2 * PHASES), phase_angles, place, gate_re, gate_im)
@@ -171,7 +175,8 @@
     )(gathered, high, low, turn)
 
     back = lax.all_to_all(done, "wide", split_axis=0, concat_axis=0, tiled=True)
-    return back.reshape(amps // LANES, 2, LANES).transpose(1, 0, 2).reshape(2, amps)
+    view = with_layout_constraint(back.reshape(amps // LANES, 2, LANES).transpose(1, 0, 2), PAIRED)
+    return view.reshape(2, amps)
 
 
 def solution(mesh):

time: 81 us -> 75.8 us (0.936)
  waiting for transfers between devices: 15.4 us -> 11.3 us
  Pallas kernels: 14.5 us -> 12.4 us
  local copies, waits for them, and re-layouts: 10.5 us -> 12.3 us
    unnamed x11 -> x18, local copies, waits for them, and re-layouts: 7.96 us -> 12.2 us
    all_to_all x1, waiting for transfers between devices: 15.4 us -> 11.3 us  [local(): lax.all_to_all(rows, 'wide', split_axis=0, concat_axis=0, tiled=True)]
    pallas_call x1, Pallas kernels: 6.08 us -> 3.99 us  [local(): pl.pallas_call(partial(tables_kernel, spect, narrow), grid=(LAYERS,), in_...]
    transpose x1 -> x0, local copies, waits for them, and re-layouts: 1.78 us -> none  [local(): state.reshape(2, amps // LANES, LANES).transpose(1, 0, 2)]
  transfers between devices with their start and end apart: 1 -> 1, of which waited for: 1 -> 1; matrix products, arithmetic and copies ran while one was open for 2% -> 1% of each run, Pallas kernels for 8% -> 5%
where the time goes in v1:
time: 75.8 us; the launch traced here: 75 us
  blocking collectives  31.5 us (42%)
  Pallas kernels  12.4 us (16%)
  local copies, waits for them, and re-layouts  12.3 us (16%)
  waiting for transfers between devices  11.3 us (15%)
  starting transfers between devices  7.39 us (10%)
    all_to_all x1, blocking collectives, local(): back = lax.all_to_all(done, 'wide', split_axis=0, concat_axis=0, tiled=True)  31.5 us
    unnamed x18, local copies, waits for them, and re-layouts  12.2 us
    all_to_all x1, waiting for transfers between devices, local(): lax.all_to_all(rows, 'wide', split_axis=0, concat_axis=0, tiled=True)  11.3 us
    pallas_call x1, Pallas kernels, local(): pl.pallas_call(partial(layers_kernel, wide, spect), grid=(LAYERS,), in_sp...  8.4 us
    all_to_all x1, starting transfers between devices, local(): lax.all_to_all(rows, 'wide', split_axis=0, concat_axis=0, tiled=True)  7.39 us
    pallas_call x1, Pallas kernels, local(): pl.pallas_call(partial(tables_kernel, spect, narrow), grid=(LAYERS,), in_...  3.99 us
  transfers between devices with their start and end apart: 1, of which 1 were waited for; matrix products, arithmetic and copies ran while one was open for 1% of the time, Pallas kernels for 5%

profile of v1, /device:TPU:0, one launch (start us, length us, event | category | flops | bytes accessed | tf_op | source)
XLA Modules:
  0.0 75.0 jit_solution(6962471284943515563)
XLA Ops:
  0.0 7.4 %all-to-all-start = ((f32[16,128,128]{2,1,0:T(8,128)}), f32[16,128,128]{2,1,0:T(8,128)S(1)}, u32[]{:S(2)}, u32[]{:S(2)}) async-start(f32[16,128,128]{2,1,0:T(8,128)} %bitcast.18), calls=%async_computation | async-start | bytes 2097152 | tf_op jit(solution)/shard_map/all_to_all | solution.py:141
  7.4 0.8 %copy.8 = s32[6,16,2]{0,2,1:T(2,128)S(1)} copy(s32[6,16,2]{1,2,0:T(2,128)} %param.10) | data formatting | bytes 1536 | tf_op args[4]
  8.2 0.1 copy.9.pair_ref
  8.3 0.1 pad_add_fusion.place_ref
  8.3 0.0 copy-start
  8.3 1.0 %copy-done = f32[6,128,128]{2,1,0:T(8,128)S(1)} copy-done((f32[6,128,128]{2,1,0:T(8,128)S(1)}, f32[6,128,128]{2,1,0:T(8,128)}, u32[]{:S(2)}) %copy-start) | copy-done | bytes 393240
  9.3 0.0 copy-start.1
  9.3 1.0 %copy-done.1 = f32[6,128,128]{2,1,0:T(8,128)S(1)} copy-done((f32[6,128,128]{2,1,0:T(8,128)S(1)}, f32[6,128,128]{2,1,0:T(8,128)}, u32[]{:S(2)}) %copy-start.1) | copy-done | bytes 393240
  10.3 0.0 copy-start.2
  10.3 0.7 copy-done.2
  11.0 0.0 copy-start.3
  11.0 0.7 copy-done.3
  11.7 4.0 %tables.1 = (bf16[6,512,512]{2,1,0:T(8,128)(2,1)S(1)}, bf16[6,512,512]{2,1,0:T(8,128)(2,1)S(1)}, f32[6,2,32,256]{3,2,1,0:T(8,128)S(1)}) custom-call(s32[6,8]{1,0:T(8,128)S(1)} %copy-done.2, s32[6,32]{1,0:T(8,128)S(1)} %copy.9.pair_ref, f32[6,16]{1,0:T(8,128)S(1)} %copy-done.3, s32[2]{0:T(128)S(1)} %pad_add_fusion.place_ref, f32[6,128,128]{2,1,0:T(8,128)S(1)} %copy-done, ...), custom_call_target="tpu_custom_call" | custom-call | flops 1000000000 | bytes 8000000 | tf_op jit(solution)/shard_map/tables/pallas_call | solution.py:149
  15.7 0.0 copy-start.4
  15.7 1.6 %copy-done.4 = bf16[6,512,512]{2,1,0:T(8,128)(2,1)} copy-done((bf16[6,512,512]{2,1,0:T(8,128)(2,1)}, bf16[6,512,512]{2,1,0:T(8,128)(2,1)S(1)}, u32[]{:S(2)}) %copy-start.4) | copy-done | bytes 3145752
  17.3 0.0 copy-start.6
  17.3 1.7 %copy-done.6 = bf16[6,512,512]{2,1,0:T(8,128)(2,1)} copy-done((bf16[6,512,512]{2,1,0:T(8,128)(2,1)}, bf16[6,512,512]{2,1,0:T(8,128)(2,1)S(1)}, u32[]{:S(2)}) %copy-start.6) | copy-done | bytes 3145752
  19.0 11.3 %all-to-all-done = f32[16,128,128]{2,1,0:T(8,128)S(1)} async-done(((f32[16,128,128]{2,1,0:T(8,128)}), f32[16,128,128]{2,1,0:T(8,128)S(1)}, u32[]{:S(2)}, u32[]{:S(2)}) %all-to-all-start) | async-done | bytes 1048608 | tf_op jit(solution)/shard_map/all_to_all | solution.py:141
  30.3 0.0 copy-start.5
  30.3 1.9 %copy-done.5 = bf16[6,512,512]{2,1,0:T(8,128)(2,1)S(1)} copy-done((bf16[6,512,512]{2,1,0:T(8,128)(2,1)S(1)}, bf16[6,512,512]{2,1,0:T(8,128)(2,1)}, u32[]{:S(2)}) %copy-start.5) | copy-done | bytes 3145752
  32.2 0.0 copy-start.7
  32.2 1.9 %copy-done.7 = bf16[6,512,512]{2,1,0:T(8,128)(2,1)S(1)} copy-done((bf16[6,512,512]{2,1,0:T(8,128)(2,1)S(1)}, bf16[6,512,512]{2,1,0:T(8,128)(2,1)}, u32[]{:S(2)}) %copy-start.7) | copy-done | bytes 3145752
  34.1 8.4 %layers.1 = f32[2048,128]{1,0:T(8,128)S(1)} custom-call(f32[2048,128]{1,0:T(8,128)S(1)} %bitcast.15, bf16[6,512,512]{2,1,0:T(8,128)(2,1)S(1)} %copy-done.5, bf16[6,512,512]{2,1,0:T(8,128)(2,1)S(1)} %copy-done.7, f32[6,2,32,256]{3,2,1,0:T(8,128)S(1)} %get-tuple-element.10.turn_ref), custom_call_target="tpu_custom_call" | custom-call | flops 5000000000 | bytes 10000000 | tf_op jit(solution)/shard_map/layers/pallas_call | solution.py:161
  42.5 31.5 %all_to_all.20 = f32[16,128,128]{2,1,0:T(8,128)S(1)} all-to-all(f32[16,128,128]{2,1,0:T(8,128)S(1)} %bitcast.16), channel_id=1, replica_groups=mesh['wide'=16,'narrow'=2] {'wide'}, dimensions={0} | all-to-all | bytes 2097152 | tf_op jit(solution)/shard_map/all_to_all | solution.py:177
  74.1 1.0 %copy.11 = f32[2,131072]{1,0:T(2,128)} copy(f32[2,131072]{1,0:T(2,128)S(1)} %bitcast.17) | data formatting | bytes 2097152
Async XLA Ops:
  0.0 30.3 %all-to-all-start = ((f32[16,128,128]{2,1,0:T(8,128)}), f32[16,128,128]{2,1,0:T(8,128)S(1)}, u32[]{:S(2)}, u32[]{:S(2)}) async-start(f32[16,128,128]{2,1,0:T(8,128)} %bitcast.18), calls=%async_computation | async-start | bytes 2097152 | tf_op jit(solution)/shard_map/all_to_all | solution.py:141
  8.3 1.0 %copy-start = (f32[6,128,128]{2,1,0:T(8,128)S(1)}, f32[6,128,128]{2,1,0:T(8,128)}, u32[]{:S(2)}) copy-start(f32[6,128,128]{2,1,0:T(8,128)} %re_ref.1) | copy-start | bytes 1179652
  9.3 1.0 %copy-start.1 = (f32[6,128,128]{2,1,0:T(8,128)S(1)}, f32[6,128,128]{2,1,0:T(8,128)}, u32[]{:S(2)}) copy-start(f32[6,128,128]{2,1,0:T(8,128)} %im_ref.1) | copy-start | bytes 1179652
  10.3 0.7 copy-start.2
  11.0 0.7 copy-start.3
  15.7 1.6 %copy-start.4 = (bf16[6,512,512]{2,1,0:T(8,128)(2,1)}, bf16[6,512,512]{2,1,0:T(8,128)(2,1)S(1)}, u32[]{:S(2)}) copy-start(bf16[6,512,512]{2,1,0:T(8,128)(2,1)S(1)} %get-tuple-element.8.high_ref) | copy-start | bytes 9437188
  17.3 1.7 %copy-start.6 = (bf16[6,512,512]{2,1,0:T(8,128)(2,1)}, bf16[6,512,512]{2,1,0:T(8,128)(2,1)S(1)}, u32[]{:S(2)}) copy-start(bf16[6,512,512]{2,1,0:T(8,128)(2,1)S(1)} %get-tuple-element.9.low_ref) | copy-start | bytes 9437188
  30.3 1.9 %copy-start.5 = (bf16[6,512,512]{2,1,0:T(8,128)(2,1)S(1)}, bf16[6,512,512]{2,1,0:T(8,128)(2,1)}, u32[]{:S(2)}) copy-start(bf16[6,512,512]{2,1,0:T(8,128)(2,1)} %copy-done.4) | copy-start | bytes 9437188
  32.2 1.9 %copy-start.7 = (bf16[6,512,512]{2,1,0:T(8,128)(2,1)S(1)}, bf16[6,512,512]{2,1,0:T(8,128)(2,1)}, u32[]{:S(2)}) copy-start(bf16[6,512,512]{2,1,0:T(8,128)(2,1)} %copy-done.6) | copy-start | bytes 9437188

commit v2 on v1

--- a/solution.py
+++ b/solution.py
@@ -15,6 +15,8 @@
 PHASES = 16
 PHASE_BITS = 12
 LANES = 128
+PACKED = 16
+CHUNKS = 2
 PAIRED = Layout(major_to_minor=(1, 0, 2))
 
 
@@ -96,18 +98,19 @@
             for lanes in range(2):
                 state[part, :, lanes * LANES : (lanes + 1) * LANES] = x_ref[pl.ds(2 * lanes + part, count, stride=4), :]
 
+    joined = max(1, PACKED // spect)
     for part in range(2):
         for top in range(2):
             for lanes in range(2):
                 first = top * half * spect
                 block = state[part, first : first + half * spect, lanes * LANES : (lanes + 1) * LANES]
                 rows = exchange_modes([block[m * spect : (m + 1) * spect] for m in range(half)], span)
-                for g in range(half):
+                for g in range(0, half, joined):
                     at = (lanes * half + g) * spect
                     column = part * LOW + top * LANES
-                    high, low = split(rows[g])
-                    left_high[at : at + spect, column : column + LANES] = high
-                    left_low[at : at + spect, column : column + LANES] = low
+                    high, low = split(jnp.concatenate(rows[g : g + joined], axis=0))
+                    left_high[at : at + joined * spect, column : column + LANES] = high
+                    left_low[at : at + joined * spect, column : column + LANES] = low
 
     cosine = turn_ref[0, 0][None]
     sine = turn_ref[0, 1][None]
@@ -133,12 +136,14 @@
     wide = lax.axis_size("wide")
     narrow = lax.axis_size("narrow")
     amps = state.shape[1]
-    spect = amps // (wide * LOW)
+    spect = amps // (CHUNKS * wide * LOW)
     count = wide * spect
 
     view = with_layout_constraint(state.reshape(2, amps // LANES, LANES), PAIRED)
-    rows = view.transpose(1, 0, 2).reshape(2 * amps // LANES, LANES)
-    gathered = lax.all_to_all(rows, "wide", split_axis=0, concat_axis=0, tiled=True)
+    rows = view.transpose(1, 0, 2).reshape(CHUNKS, 4 * count, LANES)
+    gathered = [
+        lax.all_to_all(rows[chunk], "wide", split_axis=0, concat_axis=0, tiled=True) for chunk in range(CHUNKS)
+    ]
 
     place = jnp.stack([lax.axis_index("wide"), lax.axis_index("narrow")]).astype(jnp.int32)
     smem = pl.BlockSpec(memory_space=pltpu.SMEM)
@@ -152,13 +157,13 @@
         in_specs=[smem, smem, smem, smem, gate_spec, gate_spec],
         out_specs=[square_spec, square_spec, turn_spec],
         out_shape=[square, square, jax.ShapeDtypeStruct((LAYERS, 2, spect, LOW), jnp.float32)],
-        compiler_params=pltpu.CompilerParams(vmem_limit_bytes=16 * 2**20),
+        compiler_params=pltpu.CompilerParams(vmem_limit_bytes=60 * 2**20),
         cost_estimate=pl.CostEstimate(flops=10**9, bytes_accessed=8 * 10**6, transcendentals=10**5),
         name="tables",
     )(bit_orders, phase_pairs.reshape(LAYERS, 2 * PHASES), phase_angles, place, gate_re, gate_im)
 
     whole = pl.BlockSpec((4 * count, LANES), lambda l: (0, 0))
-    done = pl.pallas_call(
+    layers = pl.pallas_call(
         partial(layers_kernel, wide, spect),
         grid=(LAYERS,),
         in_specs=[whole, square_spec, square_spec, turn_spec],
@@ -169,14 +174,16 @@
             pltpu.VMEM((count, 2 * LOW), jnp.bfloat16),
             pltpu.VMEM((count, 2 * LOW), jnp.bfloat16),
         ],
-        compiler_params=pltpu.CompilerParams(vmem_limit_bytes=32 * 2**20),
+        compiler_params=pltpu.CompilerParams(vmem_limit_bytes=60 * 2**20),
         cost_estimate=pl.CostEstimate(flops=5 * 10**9, bytes_accessed=10**7, transcendentals=0),
         name="layers",
-    )(gathered, high, low, turn)
-
-    back = lax.all_to_all(done, "wide", split_axis=0, concat_axis=0, tiled=True)
-    view = with_layout_constraint(back.reshape(amps // LANES, 2, LANES).transpose(1, 0, 2), PAIRED)
-    return view.reshape(2, amps)
+    )
+    back = []
+    for chunk in range(CHUNKS):
+        done = layers(gathered[chunk], high, low, turn)
+        back.append(lax.all_to_all(done, "wide", split_axis=0, concat_axis=0, tiled=True))
+    view = jnp.concatenate(back).reshape(amps // LANES, 2, LANES).transpose(1, 0, 2)
+    return with_layout_constraint(view, PAIRED).reshape(2, amps)
 
 
 def solution(mesh):

time: 75.8 us -> 85.3 us (1.13)
  Pallas kernels: 12.4 us -> 23.7 us
  local copies, waits for them, and re-layouts: 12.3 us -> 2.84 us
  blocking collectives: 31.5 us -> 40.3 us
  waiting for transfers between devices: 11.3 us -> 5.56 us
  starting transfers between devices: 7.39 us -> 10.1 us
  other arithmetic: 0.07 us -> 1.65 us
    unnamed x18 -> x5, local copies, waits for them, and re-layouts: 12.2 us -> 0.1 us
    pallas_call x1 -> x2, Pallas kernels: 8.4 us -> 17.8 us  [local(): done = layers(gathered[chunk], high, low, turn)]
    all_to_all x1 -> x2, blocking collectives: 31.5 us -> 40.3 us  [the longest x1 21.7 us: local(): lax.all_to_all(rows[chunk], 'wide', split_axis=0, concat_axis=0, tiled=True)]
    all_to_all x1 -> x2, waiting for transfers between devices: 11.3 us -> 5.56 us  [the longest x1 5.56 us: local(): lax.all_to_all(done, 'wide', split_axis=0, concat_axis=0, tiled=True)]
    all_to_all x1 -> x2, starting transfers between devices: 7.39 us -> 10.1 us  [the longest x1 6.01 us: local(): lax.all_to_all(done, 'wide', split_axis=0, concat_axis=0, tiled=True)]
    slice x0 -> x1, local copies, waits for them, and re-layouts: none -> 2.07 us  [local(): rows[chunk]]
    pallas_call x1, Pallas kernels: 3.99 us -> 5.96 us  [local(): pl.pallas_call(partial(tables_kernel, spect, narrow), grid=(LAYERS,), in_...]
    concatenate x0 -> x1, other arithmetic: none -> 1.04 us  [local(): jnp.concatenate(back).reshape(amps // LANES, 2, LANES).transpose(1, 0, 2)]
  transfers between devices with their start and end apart: 1 -> 2, of which waited for: 1 -> 1; matrix products, arithmetic and copies ran while one was open for 1% -> 2% of each run, Pallas kernels for 5% -> 28%
where the time goes in v2:
time: 85.3 us; the launch traced here: 84.3 us
  blocking collectives  40.3 us (47%)
  Pallas kernels  23.7 us (28%)
  starting transfers between devices  10.1 us (12%)
  waiting for transfers between devices  5.56 us (7%)
  local copies, waits for them, and re-layouts  2.84 us (3%)
  other arithmetic  1.65 us (2%)
    all_to_all x1, blocking collectives, local(): lax.all_to_all(rows[chunk], 'wide', split_axis=0, concat_axis=0, tiled=True)  21.7 us
    all_to_all x1, blocking collectives, local(): lax.all_to_all(done, 'wide', split_axis=0, concat_axis=0, tiled=True)  18.6 us
    pallas_call x2, Pallas kernels, local(): done = layers(gathered[chunk], high, low, turn)  17.8 us
    all_to_all x1, starting transfers between devices, local(): lax.all_to_all(done, 'wide', split_axis=0, concat_axis=0, tiled=True)  6.01 us
    pallas_call x1, Pallas kernels, local(): pl.pallas_call(partial(tables_kernel, spect, narrow), grid=(LAYERS,), in_...  5.96 us
    all_to_all x1, waiting for transfers between devices, local(): lax.all_to_all(done, 'wide', split_axis=0, concat_axis=0, tiled=True)  5.56 us
    all_to_all x1, starting transfers between devices, local(): lax.all_to_all(rows[chunk], 'wide', split_axis=0, concat_axis=0, tiled=True)  4.1 us
    slice x1, local copies, waits for them, and re-layouts, local(): rows[chunk]  2.07 us
  transfers between devices with their start and end apart: 2, of which 1 were waited for; matrix products, arithmetic and copies ran while one was open for 2% of the time, Pallas kernels for 28%

profile of v2, /device:TPU:0, one launch (start us, length us, event | category | flops | bytes accessed | tf_op | source)
XLA Modules:
  0.0 84.3 jit_solution(554033348222700560)
XLA Ops:
  0.0 0.0 copy-start.1
  0.0 2.1 %fusion = (f32[512,2,128]{2,1,0:T(2,128)}, f32[512,2,128]{2,1,0:T(2,128)S(1)}) fusion(f32[1024,2,128]{2,1,0:T(2,128)} %bitcast.22), kind=kLoop, calls=%fused_computation.2 | loop fusion | bytes 2097152 | tf_op jit(solution)/shard_map/slice | solution.py:145
  2.1 21.7 %all_to_all.46 = f32[16,64,128]{2,1,0:T(8,128)} all-to-all(f32[16,64,128]{2,1,0:T(8,128)S(1)} %bitcast.20), channel_id=1, replica_groups=mesh['wide'=16,'narrow'=2] {'wide'}, dimensions={0} | all-to-all | bytes 1048576 | tf_op jit(solution)/shard_map/all_to_all | solution.py:145
  23.8 4.1 %all-to-all-start = ((f32[16,64,128]{2,1,0:T(8,128)}), f32[16,64,128]{2,1,0:T(8,128)S(1)}, u32[]{:S(2)}, u32[]{:S(2)}) async-start(f32[16,64,128]{2,1,0:T(8,128)} %bitcast.2), calls=%async_computation | async-start | bytes 1048576 | tf_op jit(solution)/shard_map/all_to_all | solution.py:145
  27.9 0.0 copy-done.1
  27.9 0.1 copy.8
  28.0 0.7 copy.9.pair_ref
  28.7 0.6 pad_add_fusion.place_ref
  29.3 6.0 %tables.1 = (bf16[6,512,512]{2,1,0:T(8,128)(2,1)}, bf16[6,512,512]{2,1,0:T(8,128)(2,1)}, f32[6,2,16,256]{3,2,1,0:T(8,128)}) custom-call(s32[6,8]{1,0:T(8,128)} %order_ref.1, s32[6,32]{1,0:T(8,128)} %copy.9.pair_ref, f32[6,16]{1,0:T(8,128)} %angle_ref.1, s32[2]{0:T(128)} %pad_add_fusion.place_ref, f32[6,128,128]{2,1,0:T(8,128)} %re_ref.1, f32[6,128,128]{2,1,0:T(8,128)} %im_ref.1), custom_call_target="tpu_custom_call" | custom-call | flops 1000000000 | bytes 8000000 | tf_op jit(solution)/shard_map/tables/pallas_call | solution.py:154
  35.3 8.9 %layers.3 = f32[1024,128]{1,0:T(8,128)} custom-call(f32[1024,128]{1,0:T(8,128)} %bitcast.24, bf16[6,512,512]{2,1,0:T(8,128)(2,1)} %get-tuple-element.8.high_ref, bf16[6,512,512]{2,1,0:T(8,128)(2,1)} %get-tuple-element.9.low_ref, f32[6,2,16,256]{3,2,1,0:T(8,128)} %get-tuple-element.10.turn_ref), custom_call_target="tpu_custom_call" | custom-call | flops 5000000000 | bytes 10000000 | tf_op jit(solution)/shard_map/layers/pallas_call | solution.py:183
  44.2 0.0 all-to-all-done
  44.2 0.0 copy-start
  44.2 6.0 %all-to-all-start.3 = ((f32[16,64,128]{2,1,0:T(8,128)}), f32[16,64,128]{2,1,0:T(8,128)S(1)}, u32[]{:S(2)}, u32[]{:S(2)}) async-start(f32[16,64,128]{2,1,0:T(8,128)} %bitcast.25), calls=%async_computation.3 | async-start | bytes 1048576 | tf_op jit(solution)/shard_map/all_to_all | solution.py:184
  50.2 0.0 copy-done
  50.2 8.9 %layers.2 = f32[1024,128]{1,0:T(8,128)} custom-call(f32[1024,128]{1,0:T(8,128)} %bitcast.23, bf16[6,512,512]{2,1,0:T(8,128)(2,1)} %get-tuple-element.8.high_ref, bf16[6,512,512]{2,1,0:T(8,128)(2,1)} %get-tuple-element.9.low_ref, f32[6,2,16,256]{3,2,1,0:T(8,128)} %get-tuple-element.10.turn_ref), custom_call_target="tpu_custom_call" | custom-call | flops 5000000000 | bytes 10000000 | tf_op jit(solution)/shard_map/layers/pallas_call | solution.py:183
  59.1 5.6 %all-to-all-done.3 = f32[16,64,128]{2,1,0:T(8,128)S(1)} async-done(((f32[16,64,128]{2,1,0:T(8,128)}), f32[16,64,128]{2,1,0:T(8,128)S(1)}, u32[]{:S(2)}, u32[]{:S(2)}) %all-to-all-start.3) | async-done | bytes 524320 | tf_op jit(solution)/shard_map/all_to_all | solution.py:184
  64.6 18.6 %all_to_all.47 = f32[16,64,128]{2,1,0:T(8,128)S(1)} all-to-all(f32[16,64,128]{2,1,0:T(8,128)} %bitcast.26), channel_id=1, replica_groups=mesh['wide'=16,'narrow'=2] {'wide'}, dimensions={0} | all-to-all | bytes 1048576 | tf_op jit(solution)/shard_map/all_to_all | solution.py:184
  83.2 1.0 %pad_maximum_fusion = f32[2048,128]{1,0:T(8,128)} fusion(f32[1024,128]{1,0:T(8,128)S(1)} %bitcast.19, f32[1024,128]{1,0:T(8,128)S(1)} %bitcast.21), kind=kLoop, calls=%fused_computation | loop fusion | flops 262144 | bytes 2097152 | tf_op jit(solution)/shard_map/concatenate | solution.py:185
Async XLA Ops:
  0.0 27.9 %copy-start.1 = (s32[6,16,2]{1,2,0:T(2,128)S(1)}, s32[6,16,2]{1,2,0:T(2,128)}, u32[]{:S(2)}) copy-start(s32[6,16,2]{1,2,0:T(2,128)} %param.10) | copy-start | bytes 2308
  23.8 20.3 %all-to-all-start = ((f32[16,64,128]{2,1,0:T(8,128)}), f32[16,64,128]{2,1,0:T(8,128)S(1)}, u32[]{:S(2)}, u32[]{:S(2)}) async-start(f32[16,64,128]{2,1,0:T(8,128)} %bitcast.2), calls=%async_computation | async-start | bytes 1048576 | tf_op jit(solution)/shard_map/all_to_all | solution.py:145
  44.2 6.0 %copy-start = (f32[16,64,128]{2,1,0:T(8,128)}, f32[16,64,128]{2,1,0:T(8,128)S(1)}, u32[]{:S(2)}) copy-start(f32[16,64,128]{2,1,0:T(8,128)S(1)} %all-to-all-done) | copy-start | bytes 1572868
  44.2 20.5 %all-to-all-start.3 = ((f32[16,64,128]{2,1,0:T(8,128)}), f32[16,64,128]{2,1,0:T(8,128)S(1)}, u32[]{:S(2)}, u32[]{:S(2)}) async-start(f32[16,64,128]{2,1,0:T(8,128)} %bitcast.25), calls=%async_computation.3 | async-start | bytes 1048576 | tf_op jit(solution)/shard_map/all_to_all | solution.py:184

commit v3 on v1

v3 whole, which is shorter than its diff:
```python
from functools import partial

import jax
import jax.numpy as jnp
from jax import lax
from jax.experimental import pallas as pl
from jax.experimental.layout import Layout, with_layout_constraint
from jax.experimental.pallas import tpu as pltpu
from jax.sharding import PartitionSpec as P

LAYERS = 6
GATE = 128
LOW = 256
LOW_BITS = 8
PHASES = 16
PHASE_BITS = 12
LANES = 128
PACKED = 16
PAIRED = Layout(major_to_minor=(1, 0, 2))


def split(x):
    high = x.astype(jnp.bfloat16)
    low = (x - high.astype(jnp.float32)).astype(jnp.bfloat16)
    return high, low


def tables_kernel(spect, narrow, order_ref, pair_ref, angle_ref, place_ref, re_ref, im_ref, gate_ref, turn_ref):
    layer = pl.program_id(0)

    t = lax.broadcasted_iota(jnp.int32, (LOW, LOW), 1)
    source = jnp.zeros((LOW, LOW), jnp.int32)
    for bit in range(LOW_BITS):
        source = source + lax.shift_left((t >> bit) & 1, jnp.full((LOW, LOW), order_ref[layer, bit], jnp.int32))
    hot = jnp.where(lax.broadcasted_iota(jnp.int32, (LOW, LOW), 0) == source, 1.0, 0.0).astype(jnp.bfloat16)
    contract = (((1,), (1,)), ((), ()))
    for part, gate in enumerate((re_ref[0], im_ref[0])):
        for which, piece in enumerate(split(gate)):
            for e in range(2):
                moved = lax.dot_general(
                    hot[:, e * GATE : (e + 1) * GATE], piece, contract, preferred_element_type=jnp.float32
                )
                start = part * LOW + e * GATE
                gate_ref[0, which, :, start : start + GATE] = moved.astype(jnp.bfloat16)

    row = lax.broadcasted_iota(jnp.int32, (spect, LOW), 0)
    lane = lax.broadcasted_iota(jnp.int32, (spect, LOW), 1)
    r = place_ref[0] * (spect // narrow) + row // narrow
    b = jnp.where(layer % 2 == 0, jnp.full((spect, LOW), place_ref[1], jnp.int32), row % narrow)
    u = ((r * narrow + b) * LOW + lane) & (2**PHASE_BITS - 1)
    phase = jnp.zeros((spect, LOW), jnp.float32)
    for gate in range(PHASES):
        first = u >> jnp.full((spect, LOW), pair_ref[layer, 2 * gate], jnp.int32)
        second = u >> jnp.full((spect, LOW), pair_ref[layer, 2 * gate + 1], jnp.int32)
        phase = phase + jnp.where((first & second & 1) == 1, angle_ref[layer, gate], 0.0)
    turn_ref[0, 0] = jnp.cos(phase)
    turn_ref[0, 1] = jnp.sin(phase)


def exchange_modes(rows, span):
    rows = list(rows)
    lane = lax.broadcasted_iota(jnp.int32, rows[0].shape, 1)
    step = 1
    while step < len(rows):
        shift = step * span
        upper = (lane & shift) != 0
        for m in range(len(rows)):
            if m & step:
                continue
            x0, x1 = rows[m], rows[m + step]
            if 2 * shift == LANES:
                crossing = pltpu.roll(jnp.where(upper, x0, x1), shift, 1)
                rows[m] = jnp.where(upper, crossing, x0)
                rows[m + step] = jnp.where(upper, x1, crossing)
            else:
                rows[m] = jnp.where(upper, pltpu.roll(x1, shift, 1), x0)
                rows[m + step] = jnp.where(upper, x1, pltpu.roll(x0, LANES - shift, 1))
        step *= 2
    return rows


def layers_kernel(
    wide, spect, x_hbm, gate_hbm, turn_hbm, out_hbm, x, gate, turn, state, left, x_sem, gate_sem, turn_sem, out_sem
):
    count = wide * spect
    span = LOW // wide
    half = wide // 2
    joined = max(1, PACKED // spect)
    block = 4 * spect

    x_copies = [
        pltpu.make_async_copy(x_hbm.at[pl.ds(m * block, block)], x.at[pl.ds(m * block, block)], x_sem.at[m])
        for m in range(wide)
    ]
    for copy in x_copies:
        copy.start()
    for layer in range(LAYERS):
        pltpu.make_async_copy(gate_hbm.at[layer], gate.at[layer], gate_sem.at[layer]).start()
        pltpu.make_async_copy(turn_hbm.at[layer], turn.at[layer], turn_sem.at[layer]).start()
    for copy in x_copies:
        copy.wait()

    for part in range(2):
        for lanes in range(2):
            state[part, :, lanes * LANES : (lanes + 1) * LANES] = x[pl.ds(2 * lanes + part, count, stride=4), :]

    def one_layer(layer, carry):
        for part in range(2):
            for top in range(2):
                for lanes in range(2):
                    first = top * half * spect
                    piece = state[part, first : first + half * spect, lanes * LANES : (lanes + 1) * LANES]
                    rows = exchange_modes([piece[m * spect : (m + 1) * spect] for m in range(half)], span)
                    for g in range(0, half, joined):
                        at = (lanes * half + g) * spect
                        high, low = split(jnp.concatenate(rows[g : g + joined], axis=0))
                        left[0, part, at : at + joined * spect, top * LANES : (top + 1) * LANES] = high
                        left[1, part, at : at + joined * spect, top * LANES : (top + 1) * LANES] = low

        pltpu.make_async_copy(gate_hbm.at[layer], gate.at[layer], gate_sem.at[layer]).wait()
        pltpu.make_async_copy(turn_hbm.at[layer], turn.at[layer], turn_sem.at[layer]).wait()
        cosine = turn[layer, 0][None]
        sine = turn[layer, 1][None]
        dot = partial(jnp.dot, preferred_element_type=jnp.float32)
        for part in range(2):
            rows = slice(part * half * spect, (part + 1) * half * spect)
            by_re, by_im = (
                dot(left[0, which, rows], gate[layer, 0])
                + dot(left[1, which, rows], gate[layer, 0])
                + dot(left[0, which, rows], gate[layer, 1])
                for which in range(2)
            )
            real = (by_re[:, :LOW] - by_im[:, LOW:]).reshape(half, spect, LOW)
            imag = (by_re[:, LOW:] + by_im[:, :LOW]).reshape(half, spect, LOW)
            state[0, rows] = (real * cosine - imag * sine).reshape(half * spect, LOW)
            state[1, rows] = (real * sine + imag * cosine).reshape(half * spect, LOW)
        return carry

    lax.fori_loop(0, LAYERS, one_layer, 0)

    for part in range(2):
        for lanes in range(2):
            x[pl.ds(2 * lanes + part, count, stride=4), :] = state[part, :, lanes * LANES : (lanes + 1) * LANES]
    out_copies = [
        pltpu.make_async_copy(x.at[pl.ds(m * block, block)], out_hbm.at[pl.ds(m * block, block)], out_sem.at[m])
        for m in range(wide)
    ]
    for copy in out_copies:
        copy.start()
    for copy in out_copies:
        copy.wait()


def local(state, gate_re, gate_im, bit_orders, phase_pairs, phase_angles):
    wide = lax.axis_size("wide")
    narrow = lax.axis_size("narrow")
    amps = state.shape[1]
    spect = amps // (wide * LOW)
    count = wide * spect

    view = with_layout_constraint(state.reshape(2, amps // LANES, LANES), PAIRED)
    rows = view.transpose(1, 0, 2).reshape(2 * amps // LANES, LANES)
    gathered = lax.all_to_all(rows, "wide", split_axis=0, concat_axis=0, tiled=True)

    place = jnp.stack([lax.axis_index("wide"), lax.axis_index("narrow")]).astype(jnp.int32)
    smem = pl.BlockSpec(memory_space=pltpu.SMEM)
    gate_spec = pl.BlockSpec((1, GATE, GATE), lambda l: (l, 0, 0))
    gates = (LAYERS, 2, LOW, 2 * LOW)
    turns = (LAYERS, 2, spect, LOW)
    gate, turn = pl.pallas_call(
        partial(tables_kernel, spect, narrow),
        grid=(LAYERS,),
        in_specs=[smem, smem, smem, smem, gate_spec, gate_spec],
        out_specs=[
            pl.BlockSpec((1,) + gates[1:], lambda l: (l, 0, 0, 0)),
            pl.BlockSpec((1,) + turns[1:], lambda l: (l, 0, 0, 0)),
        ],
        out_shape=[jax.ShapeDtypeStruct(gates, jnp.bfloat16), jax.ShapeDtypeStruct(turns, jnp.float32)],
        compiler_params=pltpu.CompilerParams(vmem_limit_bytes=60 * 2**20),
        cost_estimate=pl.CostEstimate(flops=10**9, bytes_accessed=8 * 10**6, transcendentals=10**5),
        name="tables",
    )(bit_orders, phase_pairs.reshape(LAYERS, 2 * PHASES), phase_angles, place, gate_re, gate_im)

    anywhere = pl.BlockSpec(memory_space=pl.ANY)
    done = pl.pallas_call(
        partial(layers_kernel, wide, spect),
        in_specs=[anywhere, anywhere, anywhere],
        out_specs=anywhere,
        out_shape=jax.ShapeDtypeStruct((4 * count, LANES), jnp.float32),
        scratch_shapes=[
            pltpu.VMEM((4 * count, LANES), jnp.float32),
            pltpu.VMEM(gates, jnp.bfloat16),
            pltpu.VMEM(turns, jnp.float32),
            pltpu.VMEM((2, count, LOW), jnp.float32),
            pltpu.VMEM((2, 2, count, LOW), jnp.bfloat16),
            pltpu.SemaphoreType.DMA((wide,)),
            pltpu.SemaphoreType.DMA((LAYERS,)),
            pltpu.SemaphoreType.DMA((LAYERS,)),
            pltpu.SemaphoreType.DMA((wide,)),
        ],
        compiler_params=pltpu.CompilerParams(vmem_limit_bytes=60 * 2**20),
        cost_estimate=pl.CostEstimate(flops=5 * 10**9, bytes_accessed=10**7, transcendentals=0),
        name="layers",
    )(gathered, gate, turn)

    back = lax.all_to_all(done, "wide", split_axis=0, concat_axis=0, tiled=True)
    view = with_layout_constraint(back.reshape(amps // LANES, 2, LANES).transpose(1, 0, 2), PAIRED)
    return view.reshape(2, amps)


def solution(mesh):
    return jax.shard_map(
        local,
        mesh=mesh,
        in_specs=(P(None, ("wide", "narrow")), P(), P(), P(), P(), P()),
        out_specs=P(None, ("wide", "narrow")),
        check_vma=False,
    )
```

time: 75.8 us -> 83 us (1.095)
  Pallas kernels: 12.4 us -> 23.7 us
  local copies, waits for them, and re-layouts: 12.3 us -> 3.39 us
  waiting for transfers between devices: 11.3 us -> 15.3 us
    pallas_call x1, Pallas kernels: 8.4 us -> 18.1 us  [local(): pl.pallas_call(partial(layers_kernel, wide, spect), in_specs=[anywhere, a...]
    unnamed x18 -> x4, local copies, waits for them, and re-layouts: 12.2 us -> 2.72 us
    all_to_all x1, waiting for transfers between devices: 11.3 us -> 15.3 us  [local(): lax.all_to_all(rows, 'wide', split_axis=0, concat_axis=0, tiled=True)]
    pallas_call x1, Pallas kernels: 3.99 us -> 5.6 us  [local(): pl.pallas_call(partial(tables_kernel, spect, narrow), grid=(LAYERS,), in_...]
  transfers between devices with their start and end apart: 1 -> 1, of which waited for: 1 -> 1; matrix products, arithmetic and copies ran while one was open for 1% -> 2% of each run, Pallas kernels for 5% -> 7%
where the time goes in v3:
time: 83 us; the launch traced here: 82.1 us
  blocking collectives  31.7 us (38%)
  Pallas kernels  23.7 us (29%)
  waiting for transfers between devices  15.3 us (18%)
  starting transfers between devices  7.39 us (9%)
  local copies, waits for them, and re-layouts  3.39 us (4%)
    all_to_all x1, blocking collectives, local(): back = lax.all_to_all(done, 'wide', split_axis=0, concat_axis=0, tiled=True)  31.7 us
    pallas_call x1, Pallas kernels, local(): pl.pallas_call(partial(layers_kernel, wide, spect), in_specs=[anywhere, a...  18.1 us
    all_to_all x1, waiting for transfers between devices, local(): lax.all_to_all(rows, 'wide', split_axis=0, concat_axis=0, tiled=True)  15.3 us
    all_to_all x1, starting transfers between devices, local(): lax.all_to_all(rows, 'wide', split_axis=0, concat_axis=0, tiled=True)  7.39 us
    pallas_call x1, Pallas kernels, local(): pl.pallas_call(partial(tables_kernel, spect, narrow), grid=(LAYERS,), in_...  5.6 us
    unnamed x4, local copies, waits for them, and re-layouts  2.72 us
  transfers between devices with their start and end apart: 1, of which 1 were waited for; matrix products, arithmetic and copies ran while one was open for 2% of the time, Pallas kernels for 7%

profile of v3, /device:TPU:0, one launch (start us, length us, event | category | flops | bytes accessed | tf_op | source)
XLA Modules:
  0.0 82.1 jit_solution(18146212481234239105)
XLA Ops:
  0.0 7.4 %all-to-all-start = ((f32[16,128,128]{2,1,0:T(8,128)}), f32[16,128,128]{2,1,0:T(8,128)S(1)}, u32[]{:S(2)}, u32[]{:S(2)}) async-start(f32[16,128,128]{2,1,0:T(8,128)} %bitcast.16), calls=%async_computation | async-start | bytes 2097152 | tf_op jit(solution)/shard_map/all_to_all | solution.py:163
  7.4 0.8 copy.8
  8.2 0.7 copy.9.pair_ref
  8.8 0.6 pad_add_fusion.place_ref
  9.4 5.6 %tables.1 = (bf16[6,2,256,512]{3,2,1,0:T(8,128)(2,1)}, f32[6,2,32,256]{3,2,1,0:T(8,128)}) custom-call(s32[6,8]{1,0:T(8,128)} %order_ref.1, s32[6,32]{1,0:T(8,128)} %copy.9.pair_ref, f32[6,16]{1,0:T(8,128)} %angle_ref.1, s32[2]{0:T(128)} %pad_add_fusion.place_ref, f32[6,128,128]{2,1,0:T(8,128)} %re_ref.1, f32[6,128,128]{2,1,0:T(8,128)} %im_ref.1), custom_call_target="tpu_custom_call" | custom-call | flops 1000000000 | bytes 8000000 | tf_op jit(solution)/shard_map/tables/pallas_call | solution.py:170
  15.0 15.3 %all-to-all-done = f32[16,128,128]{2,1,0:T(8,128)S(1)} async-done(((f32[16,128,128]{2,1,0:T(8,128)}), f32[16,128,128]{2,1,0:T(8,128)S(1)}, u32[]{:S(2)}, u32[]{:S(2)}) %all-to-all-start) | async-done | bytes 1048608 | tf_op jit(solution)/shard_map/all_to_all | solution.py:163
  30.3 0.0 copy-start
  30.3 1.0 %copy-done = f32[16,128,128]{2,1,0:T(8,128)} copy-done((f32[16,128,128]{2,1,0:T(8,128)}, f32[16,128,128]{2,1,0:T(8,128)S(1)}, u32[]{:S(2)}) %copy-start) | copy-done | bytes 1048600
  31.3 18.1 %layers.1 = f32[2048,128]{1,0:T(8,128)} custom-call(f32[2048,128]{1,0:T(8,128)} %bitcast.17, bf16[6,2,256,512]{3,2,1,0:T(8,128)(2,1)} %get-tuple-element.7.gate_hbm, f32[6,2,32,256]{3,2,1,0:T(8,128)} %get-tuple-element.8.turn_hbm), custom_call_target="tpu_custom_call" | custom-call | flops 5000000000 | bytes 10000000 | tf_op jit(solution)/shard_map/layers/pallas_call | solution.py:185
  49.4 31.7 %all_to_all.20 = f32[16,128,128]{2,1,0:T(8,128)S(1)} all-to-all(f32[16,128,128]{2,1,0:T(8,128)} %bitcast.18), channel_id=1, replica_groups=mesh['wide'=16,'narrow'=2] {'wide'}, dimensions={0} | all-to-all | bytes 2097152 | tf_op jit(solution)/shard_map/all_to_all | solution.py:206
  81.1 1.0 %copy.11 = f32[2,131072]{1,0:T(2,128)} copy(f32[2,131072]{1,0:T(2,128)S(1)} %bitcast.15) | data formatting | bytes 2097152
Async XLA Ops:
  0.0 30.3 %all-to-all-start = ((f32[16,128,128]{2,1,0:T(8,128)}), f32[16,128,128]{2,1,0:T(8,128)S(1)}, u32[]{:S(2)}, u32[]{:S(2)}) async-start(f32[16,128,128]{2,1,0:T(8,128)} %bitcast.16), calls=%async_computation | async-start | bytes 2097152 | tf_op jit(solution)/shard_map/all_to_all | solution.py:163
  30.3 1.0 %copy-start = (f32[16,128,128]{2,1,0:T(8,128)}, f32[16,128,128]{2,1,0:T(8,128)S(1)}, u32[]{:S(2)}) copy-start(f32[16,128,128]{2,1,0:T(8,128)S(1)} %all-to-all-done) | copy-start | bytes 3145732

commit v4 on v3

--- a/solution.py
+++ b/solution.py
@@ -79,18 +79,49 @@
     return rows
 
 
-def layers_kernel(
-    wide, spect, x_hbm, gate_hbm, turn_hbm, out_hbm, x, gate, turn, state, left, x_sem, gate_sem, turn_sem, out_sem
-):
+def pick_kernel(wide, x_hbm, *rest):
+    sends, sem = rest[:-1], rest[-1]
+    me = lax.axis_index("wide")
+    block = x_hbm.shape[0] // wide
+    copies = [
+        pltpu.make_async_copy(x_hbm.at[pl.ds((me ^ k) * block, block)], sends[k - 1], sem.at[k]) for k in range(1, wide)
+    ]
+    for copy in copies:
+        copy.start()
+    for copy in copies:
+        copy.wait()
+
+
+def place_kernel(wide, *rest):
+    blocks, out_hbm, sem = rest[:wide], rest[wide], rest[wide + 1]
+    me = lax.axis_index("wide")
+    block = blocks[0].shape[0]
+    copies = [
+        pltpu.make_async_copy(blocks[k], out_hbm.at[pl.ds((me ^ k) * block, block)], sem.at[k]) for k in range(wide)
+    ]
+    for copy in copies:
+        copy.start()
+    for copy in copies:
+        copy.wait()
+
+
+def layers_kernel(wide, spect, x_hbm, *rest):
+    received = rest[: wide - 1]
+    gate_hbm, turn_hbm = rest[wide - 1 : wide + 1]
+    outs = rest[wide + 1 : 2 * wide + 1]
+    x, gate, turn, state, left, x_sem, gate_sem, turn_sem, out_sem = rest[2 * wide + 1 :]
+    me = lax.axis_index("wide")
     count = wide * spect
     span = LOW // wide
     half = wide // 2
     joined = max(1, PACKED // spect)
     block = 4 * spect
 
+    def rows_of(ref, k):
+        return ref.at[pl.ds((me ^ k) * block, block)]
+
     x_copies = [
-        pltpu.make_async_copy(x_hbm.at[pl.ds(m * block, block)], x.at[pl.ds(m * block, block)], x_sem.at[m])
-        for m in range(wide)
+        pltpu.make_async_copy(received[k - 1] if k else rows_of(x_hbm, 0), rows_of(x, k), x_sem.at[k]) for k in range(wide)
     ]
     for copy in x_copies:
         copy.start()
@@ -121,19 +152,18 @@
         pltpu.make_async_copy(turn_hbm.at[layer], turn.at[layer], turn_sem.at[layer]).wait()
         cosine = turn[layer, 0][None]
         sine = turn[layer, 1][None]
-        dot = partial(jnp.dot, preferred_element_type=jnp.float32)
-        for part in range(2):
-            rows = slice(part * half * spect, (part + 1) * half * spect)
-            by_re, by_im = (
-                dot(left[0, which, rows], gate[layer, 0])
-                + dot(left[1, which, rows], gate[layer, 0])
-                + dot(left[0, which, rows], gate[layer, 1])
-                for which in range(2)
-            )
-            real = (by_re[:, :LOW] - by_im[:, LOW:]).reshape(half, spect, LOW)
-            imag = (by_re[:, LOW:] + by_im[:, :LOW]).reshape(half, spect, LOW)
-            state[0, rows] = (real * cosine - imag * sine).reshape(half * spect, LOW)
-            state[1, rows] = (real * sine + imag * cosine).reshape(half * spect, LOW)
+        both = []
+        for which in range(2):
+            real, imag = gate[layer, which, :, :LOW], gate[layer, which, :, LOW:]
+            both.append(jnp.concatenate([gate[layer, which], jnp.concatenate([-imag, real], axis=1)], axis=0))
+        factors = jnp.concatenate([left[0, 0], left[0, 1], left[1, 0], left[1, 1], left[0, 0], left[0, 1]], axis=1)
+        gated = jnp.dot(
+            factors, jnp.concatenate([both[0], both[0], both[1]], axis=0), preferred_element_type=jnp.float32
+        )
+        real = gated[:, :LOW].reshape(wide, spect, LOW)
+        imag = gated[:, LOW:].reshape(wide, spect, LOW)
+        state[0] = (real * cosine - imag * sine).reshape(count, LOW)
+        state[1] = (real * sine + imag * cosine).reshape(count, LOW)
         return carry
 
     lax.fori_loop(0, LAYERS, one_layer, 0)
@@ -141,10 +171,7 @@
     for part in range(2):
         for lanes in range(2):
             x[pl.ds(2 * lanes + part, count, stride=4), :] = state[part, :, lanes * LANES : (lanes + 1) * LANES]
-    out_copies = [
-        pltpu.make_async_copy(x.at[pl.ds(m * block, block)], out_hbm.at[pl.ds(m * block, block)], out_sem.at[m])
-        for m in range(wide)
-    ]
+    out_copies = [pltpu.make_async_copy(rows_of(x, k), outs[k], out_sem.at[k]) for k in range(wide)]
     for copy in out_copies:
         copy.start()
     for copy in out_copies:
@@ -160,7 +187,25 @@
 
     view = with_layout_constraint(state.reshape(2, amps // LANES, LANES), PAIRED)
     rows = view.transpose(1, 0, 2).reshape(2 * amps // LANES, LANES)
-    gathered = lax.all_to_all(rows, "wide", split_axis=0, concat_axis=0, tiled=True)
+    anywhere = pl.BlockSpec(memory_space=pl.ANY)
+    piece = jax.ShapeDtypeStruct((4 * spect, LANES), jnp.float32)
+    part_of_vmem = pltpu.CompilerParams(vmem_limit_bytes=24 * 2**20)
+
+    def swap(blocks):
+        return [
+            lax.ppermute(blocks[k - 1], "wide", [(i, i ^ k) for i in range(wide)]) for k in range(1, wide)
+        ]
+
+    sends = pl.pallas_call(
+        partial(pick_kernel, wide),
+        in_specs=[anywhere],
+        out_specs=[anywhere] * (wide - 1),
+        out_shape=[piece] * (wide - 1),
+        scratch_shapes=[pltpu.SemaphoreType.DMA((wide,))],
+        compiler_params=part_of_vmem,
+        name="pick",
+    )(rows)
+    received = swap(sends)
 
     place = jnp.stack([lax.axis_index("wide"), lax.axis_index("narrow")]).astype(jnp.int32)
     smem = pl.BlockSpec(memory_space=pltpu.SMEM)
@@ -176,17 +221,16 @@
             pl.BlockSpec((1,) + turns[1:], lambda l: (l, 0, 0, 0)),
         ],
         out_shape=[jax.ShapeDtypeStruct(gates, jnp.bfloat16), jax.ShapeDtypeStruct(turns, jnp.float32)],
-        compiler_params=pltpu.CompilerParams(vmem_limit_bytes=60 * 2**20),
+        compiler_params=part_of_vmem,
         cost_estimate=pl.CostEstimate(flops=10**9, bytes_accessed=8 * 10**6, transcendentals=10**5),
         name="tables",
     )(bit_orders, phase_pairs.reshape(LAYERS, 2 * PHASES), phase_angles, place, gate_re, gate_im)
 
-    anywhere = pl.BlockSpec(memory_space=pl.ANY)
     done = pl.pallas_call(
         partial(layers_kernel, wide, spect),
-        in_specs=[anywhere, anywhere, anywhere],
-        out_specs=anywhere,
-        out_shape=jax.ShapeDtypeStruct((4 * count, LANES), jnp.float32),
+        in_specs=[anywhere] * (wide + 2),
+        out_specs=[anywhere] * wide,
+        out_shape=[piece] * wide,
         scratch_shapes=[
             pltpu.VMEM((4 * count, LANES), jnp.float32),
             pltpu.VMEM(gates, jnp.bfloat16),
@@ -198,12 +242,20 @@
             pltpu.SemaphoreType.DMA((LAYERS,)),
             pltpu.SemaphoreType.DMA((wide,)),
         ],
-        compiler_params=pltpu.CompilerParams(vmem_limit_bytes=60 * 2**20),
+        compiler_params=part_of_vmem,
         cost_estimate=pl.CostEstimate(flops=5 * 10**9, bytes_accessed=10**7, transcendentals=0),
         name="layers",
-    )(gathered, gate, turn)
-
-    back = lax.all_to_all(done, "wide", split_axis=0, concat_axis=0, tiled=True)
+    )(rows, *received, gate, turn)
+
+    back = pl.pallas_call(
+        partial(place_kernel, wide),
+        in_specs=[anywhere] * wide,
+        out_specs=anywhere,
+        out_shape=jax.ShapeDtypeStruct(rows.shape, jnp.float32),
+        scratch_shapes=[pltpu.SemaphoreType.DMA((wide,))],
+        compiler_params=part_of_vmem,
+        name="place",
+    )(done[0], *swap(done[1:]))
     view = with_layout_constraint(back.reshape(amps // LANES, 2, LANES).transpose(1, 0, 2), PAIRED)
     return view.reshape(2, amps)
 

time: 83 us -> 90.5 us (1.090)
  starting transfers between devices: 7.39 us -> 50 us
  blocking collectives: 31.7 us -> 0 us
  waiting for transfers between devices: 15.3 us -> 8.22 us
  local copies, waits for them, and re-layouts: 3.39 us -> 5.45 us
  Pallas kernels: 23.7 us -> 25.6 us
    ppermute x0 -> x30, starting transfers between devices: none -> 50 us  [swap(): lax.ppermute(blocks[k - 1], 'wide', [(i, i ^ k) for i in range(wide)])]
    all_to_all x1 -> x0, blocking collectives: 31.7 us -> none  [local(): back = lax.all_to_all(done, 'wide', split_axis=0, concat_axis=0, tiled=True)]
    all_to_all x1 -> x0, waiting for transfers between devices: 15.3 us -> none  [local(): lax.all_to_all(rows, 'wide', split_axis=0, concat_axis=0, tiled=True)]
    ppermute x0 -> x30, waiting for transfers between devices: none -> 8.22 us  [swap(): lax.ppermute(blocks[k - 1], 'wide', [(i, i ^ k) for i in range(wide)])]
    all_to_all x1 -> x0, starting transfers between devices: 7.39 us -> none  [local(): lax.all_to_all(rows, 'wide', split_axis=0, concat_axis=0, tiled=True)]
    pallas_call x1 -> x3, Pallas kernels: 18.1 us -> 21.7 us  [the longest x1 19 us: local(): pl.pallas_call(partial(layers_kernel, wide, spect), in_specs=[anywhere] *...]
    unnamed x4 -> x13, local copies, waits for them, and re-layouts: 2.72 us -> 5.37 us
    pallas_call x1, Pallas kernels: 5.6 us -> 3.96 us  [local(): pl.pallas_call(partial(tables_kernel, spect, narrow), grid=(LAYERS,), in_...]
  transfers between devices with their start and end apart: 1 -> 30, of which waited for: 1 -> 6; matrix products, arithmetic and copies ran while one was open for 2% -> 1% of each run, Pallas kernels for 7% -> 4%
where the time goes in v4:
time: 90.5 us; the launch traced here: 89.5 us
  starting transfers between devices  50 us (55%)
  Pallas kernels  25.6 us (28%)
  waiting for transfers between devices  8.22 us (9%)
  local copies, waits for them, and re-layouts  5.45 us (6%)
    ppermute x30, starting transfers between devices, swap(): lax.ppermute(blocks[k - 1], 'wide', [(i, i ^ k) for i in range(wide)])  50 us
    pallas_call x1, Pallas kernels, local(): pl.pallas_call(partial(layers_kernel, wide, spect), in_specs=[anywhere] *...  19 us
    ppermute x30, waiting for transfers between devices, swap(): lax.ppermute(blocks[k - 1], 'wide', [(i, i ^ k) for i in range(wide)])  8.22 us
    unnamed x13, local copies, waits for them, and re-layouts  5.37 us
    pallas_call x1, Pallas kernels, local(): pl.pallas_call(partial(tables_kernel, spect, narrow), grid=(LAYERS,), in_...  3.96 us
  transfers between devices with their start and end apart: 30, of which 6 were waited for; matrix products, arithmetic and copies ran while one was open for 1% of the time, Pallas kernels for 4%

profile of v4, /device:TPU:0, one launch (start us, length us, event | category | flops | bytes accessed | tf_op | source)
XLA Modules:
  0.0 89.5 jit_solution(3709954717936339147)
XLA Ops:
  0.0 1.2 %copy-done = f32[2,131072]{1,0:T(2,128)S(1)} copy-done((f32[2,131072]{1,0:T(2,128)S(1)}, f32[2,131072]{1,0:T(2,128)}, u32[]{:S(2)}) %copy-start) | copy-done | bytes 1048600
  1.2 1.6 %pick.1 = (f32[128,128]{1,0:T(8,128)S(1)}, f32[128,128]{1,0:T(8,128)S(1)}, f32[128,128]{1,0:T(8,128)S(1)}, f32[128,128]{1,0:T(8,128)S(1)}, f32[128,128]{1,0:T(8,...) custom-call(f32[2048,128]{1,0:T(8,128)S(1)} %bitcast.13), custom_call_target="tpu_custom_call" | custom-call | tf_op jit(solution)/shard_map/pick/pallas_call | solution.py:199
  3.3 2.6 %collective-permute-start.1 = (f32[128,128]{1,0:T(8,128)S(1)}, f32[128,128]{1,0:T(8,128)S(1)}, u32[]{:S(2)}, u32[]{:S(2)}) collective-permute-start(f32[128,128]{1,0:T(8,128)S(1)} %get-tuple-element.39), channel_id=1, source_target_pairs={{0,4},{2,6},{4,0},{6,2},{8,12},{10,14},{12,8},{14,10},{16,20},{18,... | collective-permute-start | bytes 196616 | tf_op jit(solution)/shard_map/ppermute | solution.py:196
  6.0 1.8 %collective-permute-start.3 = (f32[128,128]{1,0:T(8,128)S(1)}, f32[128,128]{1,0:T(8,128)S(1)}, u32[]{:S(2)}, u32[]{:S(2)}) collective-permute-start(f32[128,128]{1,0:T(8,128)S(1)} %get-tuple-element.41), channel_id=1, source_target_pairs={{0,8},{2,10},{4,12},{6,14},{8,0},{10,2},{12,4},{14,6},{16,24},{18,... | collective-permute-start | bytes 196616 | tf_op jit(solution)/shard_map/ppermute | solution.py:196
  7.8 0.8 copy.8
  8.6 2.6 %collective-permute-start.5 = (f32[128,128]{1,0:T(8,128)S(1)}, f32[128,128]{1,0:T(8,128)S(1)}, u32[]{:S(2)}, u32[]{:S(2)}) collective-permute-start(f32[128,128]{1,0:T(8,128)S(1)} %get-tuple-element.43), channel_id=1, source_target_pairs={{0,12},{2,14},{4,8},{6,10},{8,4},{10,6},{12,0},{14,2},{16,28},{18,... | collective-permute-start | bytes 196616 | tf_op jit(solution)/shard_map/ppermute | solution.py:196
  11.4 2.6 %collective-permute-start.7 = (f32[128,128]{1,0:T(8,128)S(1)}, f32[128,128]{1,0:T(8,128)S(1)}, u32[]{:S(2)}, u32[]{:S(2)}) collective-permute-start(f32[128,128]{1,0:T(8,128)S(1)} %get-tuple-element.45), channel_id=1, source_target_pairs={{0,16},{2,18},{4,20},{6,22},{8,24},{10,26},{12,28},{14,30},{16,0},... | collective-permute-start | bytes 196616 | tf_op jit(solution)/shard_map/ppermute | solution.py:196
  14.2 3.4 %collective-permute-start.9 = (f32[128,128]{1,0:T(8,128)S(1)}, f32[128,128]{1,0:T(8,128)S(1)}, u32[]{:S(2)}, u32[]{:S(2)}) collective-permute-start(f32[128,128]{1,0:T(8,128)S(1)} %get-tuple-element.47), channel_id=1, source_target_pairs={{0,20},{2,22},{4,16},{6,18},{8,28},{10,30},{12,24},{14,26},{16,4},... | collective-permute-start | bytes 196616 | tf_op jit(solution)/shard_map/ppermute | solution.py:196
  17.7 3.6 %collective-permute-start.11 = (f32[128,128]{1,0:T(8,128)S(1)}, f32[128,128]{1,0:T(8,128)S(1)}, u32[]{:S(2)}, u32[]{:S(2)}) collective-permute-start(f32[128,128]{1,0:T(8,128)S(1)} %get-tuple-element.49), channel_id=1, source_target_pairs={{0,24},{2,26},{4,28},{6,30},{8,16},{10,18},{12,20},{14,22},{16,8},... | collective-permute-start | bytes 196616 | tf_op jit(solution)/shard_map/ppermute | solution.py:196
  21.3 4.2 %collective-permute-start.12 = (f32[128,128]{1,0:T(8,128)S(1)}, f32[128,128]{1,0:T(8,128)S(1)}, u32[]{:S(2)}, u32[]{:S(2)}) collective-permute-start(f32[128,128]{1,0:T(8,128)S(1)} %get-tuple-element.50), channel_id=1, source_target_pairs={{0,26},{2,24},{4,30},{6,28},{8,18},{10,16},{12,22},{14,20},{16,10}... | collective-permute-start | bytes 196616 | tf_op jit(solution)/shard_map/ppermute | solution.py:196
  25.9 3.6 %collective-permute-start.13 = (f32[128,128]{1,0:T(8,128)S(1)}, f32[128,128]{1,0:T(8,128)S(1)}, u32[]{:S(2)}, u32[]{:S(2)}) collective-permute-start(f32[128,128]{1,0:T(8,128)S(1)} %get-tuple-element.51), channel_id=1, source_target_pairs={{0,28},{2,30},{4,24},{6,26},{8,20},{10,22},{12,16},{14,18},{16,12}... | collective-permute-start | bytes 196616 | tf_op jit(solution)/shard_map/ppermute | solution.py:196
  30.6 1.0 %copy-done.2 = f32[6,128,128]{2,1,0:T(8,128)S(1)} copy-done((f32[6,128,128]{2,1,0:T(8,128)S(1)}, f32[6,128,128]{2,1,0:T(8,128)}, u32[]{:S(2)}) %copy-start.2) | copy-done | bytes 393240
  31.6 1.0 %copy-done.3 = f32[6,128,128]{2,1,0:T(8,128)S(1)} copy-done((f32[6,128,128]{2,1,0:T(8,128)S(1)}, f32[6,128,128]{2,1,0:T(8,128)}, u32[]{:S(2)}) %copy-start.3) | copy-done | bytes 393240
  32.6 0.7 copy-done.4
  34.0 4.0 %tables.1 = (bf16[6,2,256,512]{3,2,1,0:T(8,128)(2,1)S(1)}, f32[6,2,32,256]{3,2,1,0:T(8,128)S(1)}) custom-call(s32[6,8]{1,0:T(8,128)S(1)} %copy-done.4, s32[6,32]{1,0:T(8,128)S(1)} %copy.9.pair_ref, f32[6,16]{1,0:T(8,128)S(1)} %copy-done.5, s32[2]{0:T(128)S(1)} %pad_add_fusion.place_ref, f32[6,128,128]{2,1,0:T(8,128)S(1)} %copy-done.2, ...), custom_call_target="tpu_custom_call" | custom-call | flops 1000000000 | bytes 8000000 | tf_op jit(solution)/shard_map/tables/pallas_call | solution.py:215
  38.0 19.0 %layers.1 = (f32[128,128]{1,0:T(8,128)S(1)}, f32[128,128]{1,0:T(8,128)S(1)}, f32[128,128]{1,0:T(8,128)S(1)}, f32[128,128]{1,0:T(8,128)S(1)}, f32[128,128]{1,0:T(...) custom-call(f32[2048,128]{1,0:T(8,128)S(1)} %bitcast.14, ...), custom_call_target="tpu_custom_call" | custom-call | flops 5000000000 | bytes 10000000 | tf_op jit(solution)/shard_map/layers/pallas_call | solution.py:229
  57.1 0.7 collective-permute-start.15
  57.8 1.3 %collective-permute-start.16 = (f32[128,128]{1,0:T(8,128)S(1)}, f32[128,128]{1,0:T(8,128)S(1)}, u32[]{:S(2)}, u32[]{:S(2)}) collective-permute-start(f32[128,128]{1,0:T(8,128)S(1)} %get-tuple-element.57), channel_id=1, source_target_pairs={{0,4},{2,6},{4,0},{6,2},{8,12},{10,14},{12,8},{14,10},{16,20},{18,... | collective-permute-start | bytes 196616 | tf_op jit(solution)/shard_map/ppermute | solution.py:196
  59.2 1.7 %collective-permute-start.18 = (f32[128,128]{1,0:T(8,128)S(1)}, f32[128,128]{1,0:T(8,128)S(1)}, u32[]{:S(2)}, u32[]{:S(2)}) collective-permute-start(f32[128,128]{1,0:T(8,128)S(1)} %get-tuple-element.59), channel_id=1, source_target_pairs={{0,8},{2,10},{4,12},{6,14},{8,0},{10,2},{12,4},{14,6},{16,24},{18,... | collective-permute-start | bytes 196616 | tf_op jit(solution)/shard_map/ppermute | solution.py:196
  61.3 1.3 %collective-permute-start.20 = (f32[128,128]{1,0:T(8,128)S(1)}, f32[128,128]{1,0:T(8,128)S(1)}, u32[]{:S(2)}, u32[]{:S(2)}) collective-permute-start(f32[128,128]{1,0:T(8,128)S(1)} %get-tuple-element.61), channel_id=1, source_target_pairs={{0,12},{2,14},{4,8},{6,10},{8,4},{10,6},{12,0},{14,2},{16,28},{18,... | collective-permute-start | bytes 196616 | tf_op jit(solution)/shard_map/ppermute | solution.py:196
  62.7 1.0 %collective-permute-start.21 = (f32[128,128]{1,0:T(8,128)S(1)}, f32[128,128]{1,0:T(8,128)S(1)}, u32[]{:S(2)}, u32[]{:S(2)}) collective-permute-start(f32[128,128]{1,0:T(8,128)S(1)} %get-tuple-element.62), channel_id=1, source_target_pairs={{0,14},{2,12},{4,10},{6,8},{8,6},{10,4},{12,2},{14,0},{16,30},{18,... | collective-permute-start | bytes 196616 | tf_op jit(solution)/shard_map/ppermute | solution.py:196
  63.6 2.9 %collective-permute-start.22 = (f32[128,128]{1,0:T(8,128)S(1)}, f32[128,128]{1,0:T(8,128)S(1)}, u32[]{:S(2)}, u32[]{:S(2)}) collective-permute-start(f32[128,128]{1,0:T(8,128)S(1)} %get-tuple-element.63), channel_id=1, source_target_pairs={{0,16},{2,18},{4,20},{6,22},{8,24},{10,26},{12,28},{14,30},{16,0},... | collective-permute-start | bytes 196616 | tf_op jit(solution)/shard_map/ppermute | solution.py:196
  66.7 2.6 %collective-permute-start.24 = (f32[128,128]{1,0:T(8,128)S(1)}, f32[128,128]{1,0:T(8,128)S(1)}, u32[]{:S(2)}, u32[]{:S(2)}) collective-permute-start(f32[128,128]{1,0:T(8,128)S(1)} %get-tuple-element.65), channel_id=1, source_target_pairs={{0,20},{2,22},{4,16},{6,18},{8,28},{10,30},{12,24},{14,26},{16,4},... | collective-permute-start | bytes 196616 | tf_op jit(solution)/shard_map/ppermute | solution.py:196
  69.2 1.1 %collective-permute-start.25 = (f32[128,128]{1,0:T(8,128)S(1)}, f32[128,128]{1,0:T(8,128)S(1)}, u32[]{:S(2)}, u32[]{:S(2)}) collective-permute-start(f32[128,128]{1,0:T(8,128)S(1)} %get-tuple-element.66), channel_id=1, source_target_pairs={{0,22},{2,20},{4,18},{6,16},{8,30},{10,28},{12,26},{14,24},{16,6},... | collective-permute-start | bytes 196616 | tf_op jit(solution)/shard_map/ppermute | solution.py:196
  70.3 2.2 %collective-permute-start.26 = (f32[128,128]{1,0:T(8,128)S(1)}, f32[128,128]{1,0:T(8,128)S(1)}, u32[]{:S(2)}, u32[]{:S(2)}) collective-permute-start(f32[128,128]{1,0:T(8,128)S(1)} %get-tuple-element.67), channel_id=1, source_target_pairs={{0,24},{2,26},{4,28},{6,30},{8,16},{10,18},{12,20},{14,22},{16,8},... | collective-permute-start | bytes 196616 | tf_op jit(solution)/shard_map/ppermute | solution.py:196
  72.5 4.4 %collective-permute-start.27 = (f32[128,128]{1,0:T(8,128)S(1)}, f32[128,128]{1,0:T(8,128)S(1)}, u32[]{:S(2)}, u32[]{:S(2)}) collective-permute-start(f32[128,128]{1,0:T(8,128)S(1)} %get-tuple-element.68), channel_id=1, source_target_pairs={{0,26},{2,24},{4,30},{6,28},{8,18},{10,16},{12,22},{14,20},{16,10}... | collective-permute-start | bytes 196616 | tf_op jit(solution)/shard_map/ppermute | solution.py:196
  76.9 2.1 %collective-permute-done.23.rest_9_ = f32[128,128]{1,0:T(8,128)S(1)} collective-permute-done((f32[128,128]{1,0:T(8,128)S(1)}, f32[128,128]{1,0:T(8,128)S(1)}, u32[]{:S(2)}, u32[]{:S(2)}) %collective-permute-start.23) | collective-permute-done | bytes 65568 | tf_op jit(solution)/shard_map/ppermute | solution.py:196
  79.0 2.1 %collective-permute-start.28 = (f32[128,128]{1,0:T(8,128)S(1)}, f32[128,128]{1,0:T(8,128)S(1)}, u32[]{:S(2)}, u32[]{:S(2)}) collective-permute-start(f32[128,128]{1,0:T(8,128)S(1)} %get-tuple-element.69), channel_id=1, source_target_pairs={{0,28},{2,30},{4,24},{6,26},{8,20},{10,22},{12,16},{14,18},{16,12}... | collective-permute-start | bytes 196616 | tf_op jit(solution)/shard_map/ppermute | solution.py:196
  81.5 2.1 %collective-permute-start.29 = (f32[128,128]{1,0:T(8,128)S(1)}, f32[128,128]{1,0:T(8,128)S(1)}, u32[]{:S(2)}, u32[]{:S(2)}) collective-permute-start(f32[128,128]{1,0:T(8,128)S(1)} %get-tuple-element.70), channel_id=1, source_target_pairs={{0,30},{2,28},{4,26},{6,24},{8,22},{10,20},{12,18},{14,16},{16,14}... | collective-permute-start | bytes 196616 | tf_op jit(solution)/shard_map/ppermute | solution.py:196
  83.6 2.7 %collective-permute-done.28.rest_14_ = f32[128,128]{1,0:T(8,128)S(1)} collective-permute-done((f32[128,128]{1,0:T(8,128)S(1)}, f32[128,128]{1,0:T(8,128)S(1)}, u32[]{:S(2)}, u32[]{:S(2)}) %collective-permute-start.28) | collective-permute-done | bytes 65568 | tf_op jit(solution)/shard_map/ppermute | solution.py:196
  86.3 2.1 %collective-permute-done.29.rest_15_ = f32[128,128]{1,0:T(8,128)S(1)} collective-permute-done((f32[128,128]{1,0:T(8,128)S(1)}, f32[128,128]{1,0:T(8,128)S(1)}, u32[]{:S(2)}, u32[]{:S(2)}) %collective-permute-start.29) | collective-permute-done | bytes 65568 | tf_op jit(solution)/shard_map/ppermute | solution.py:196
  88.4 1.1 %place.1 = f32[2048,128]{1,0:T(8,128)} custom-call(f32[128,128]{1,0:T(8,128)S(1)} %get-tuple-element.55.rest_0_, f32[128,128]{1,0:T(8,128)S(1)} %collective-permute-done.15.rest_1_, f32[128,128]{1,0:T(8,128)S(1)} %collective-permute-done.16.rest_2_, f32[128,128]{1,0:T(8,128)S(1)} %collective-permute-done.17.rest_3_, ...), custom_call_target="tpu_custom_call" | custom-call | tf_op jit(solution)/shard_map/place/pallas_call | solution.py:250
  (47 shorter events, 4.3 us)
Async XLA Ops:
  0.0 1.2 %copy-start = (f32[2,131072]{1,0:T(2,128)S(1)}, f32[2,131072]{1,0:T(2,128)}, u32[]{:S(2)}) copy-start(f32[2,131072]{1,0:T(2,128)} %param.6) | copy-start | bytes 3145732
  1.2 36.8 %copy-start.1 = (f32[2,131072]{1,0:T(2,128)S(1)}, f32[2,131072]{1,0:T(2,128)}, u32[]{:S(2)}) copy-start(f32[2,131072]{1,0:T(2,128)} %param.6) | copy-start | bytes 3145732
  2.8 5.8 %collective-permute-start = (f32[128,128]{1,0:T(8,128)S(1)}, f32[128,128]{1,0:T(8,128)S(1)}, u32[]{:S(2)}, u32[]{:S(2)}) collective-permute-start(f32[128,128]{1,0:T(8,128)S(1)} %get-tuple-element.38), channel_id=1, source_target_pairs={{0,2},{2,0},{4,6},{6,4},{8,10},{10,8},{12,14},{14,12},{16,18},{18,... | collective-permute-start | bytes 196616 | tf_op jit(solution)/shard_map/ppermute | solution.py:196
  3.3 8.0 %collective-permute-start.1 = (f32[128,128]{1,0:T(8,128)S(1)}, f32[128,128]{1,0:T(8,128)S(1)}, u32[]{:S(2)}, u32[]{:S(2)}) collective-permute-start(f32[128,128]{1,0:T(8,128)S(1)} %get-tuple-element.39), channel_id=1, source_target_pairs={{0,4},{2,6},{4,0},{6,2},{8,12},{10,14},{12,8},{14,10},{16,20},{18,... | collective-permute-start | bytes 196616 | tf_op jit(solution)/shard_map/ppermute | solution.py:196
  5.9 5.5 %collective-permute-start.2 = (f32[128,128]{1,0:T(8,128)S(1)}, f32[128,128]{1,0:T(8,128)S(1)}, u32[]{:S(2)}, u32[]{:S(2)}) collective-permute-start(f32[128,128]{1,0:T(8,128)S(1)} %get-tuple-element.40), channel_id=1, source_target_pairs={{0,6},{2,4},{4,2},{6,0},{8,14},{10,12},{12,10},{14,8},{16,22},{18,... | collective-permute-start | bytes 196616 | tf_op jit(solution)/shard_map/ppermute | solution.py:196
  6.0 8.1 %collective-permute-start.3 = (f32[128,128]{1,0:T(8,128)S(1)}, f32[128,128]{1,0:T(8,128)S(1)}, u32[]{:S(2)}, u32[]{:S(2)}) collective-permute-start(f32[128,128]{1,0:T(8,128)S(1)} %get-tuple-element.41), channel_id=1, source_target_pairs={{0,8},{2,10},{4,12},{6,14},{8,0},{10,2},{12,4},{14,6},{16,24},{18,... | collective-permute-start | bytes 196616 | tf_op jit(solution)/shard_map/ppermute | solution.py:196
  7.8 6.4 %collective-permute-start.4 = (f32[128,128]{1,0:T(8,128)S(1)}, f32[128,128]{1,0:T(8,128)S(1)}, u32[]{:S(2)}, u32[]{:S(2)}) collective-permute-start(f32[128,128]{1,0:T(8,128)S(1)} %get-tuple-element.42), channel_id=1, source_target_pairs={{0,10},{2,8},{4,14},{6,12},{8,2},{10,0},{12,6},{14,4},{16,26},{18,... | collective-permute-start | bytes 196616 | tf_op jit(solution)/shard_map/ppermute | solution.py:196
  8.6 9.0 %collective-permute-start.5 = (f32[128,128]{1,0:T(8,128)S(1)}, f32[128,128]{1,0:T(8,128)S(1)}, u32[]{:S(2)}, u32[]{:S(2)}) collective-permute-start(f32[128,128]{1,0:T(8,128)S(1)} %get-tuple-element.43), channel_id=1, source_target_pairs={{0,12},{2,14},{4,8},{6,10},{8,4},{10,6},{12,0},{14,2},{16,28},{18,... | collective-permute-start | bytes 196616 | tf_op jit(solution)/shard_map/ppermute | solution.py:196
  11.3 6.5 %collective-permute-start.6 = (f32[128,128]{1,0:T(8,128)S(1)}, f32[128,128]{1,0:T(8,128)S(1)}, u32[]{:S(2)}, u32[]{:S(2)}) collective-permute-start(f32[128,128]{1,0:T(8,128)S(1)} %get-tuple-element.44), channel_id=1, source_target_pairs={{0,14},{2,12},{4,10},{6,8},{8,6},{10,4},{12,2},{14,0},{16,30},{18,... | collective-permute-start | bytes 196616 | tf_op jit(solution)/shard_map/ppermute | solution.py:196
  11.4 9.9 %collective-permute-start.7 = (f32[128,128]{1,0:T(8,128)S(1)}, f32[128,128]{1,0:T(8,128)S(1)}, u32[]{:S(2)}, u32[]{:S(2)}) collective-permute-start(f32[128,128]{1,0:T(8,128)S(1)} %get-tuple-element.45), channel_id=1, source_target_pairs={{0,16},{2,18},{4,20},{6,22},{8,24},{10,26},{12,28},{14,30},{16,0},... | collective-permute-start | bytes 196616 | tf_op jit(solution)/shard_map/ppermute | solution.py:196
  14.0 11.9 %collective-permute-start.8 = (f32[128,128]{1,0:T(8,128)S(1)}, f32[128,128]{1,0:T(8,128)S(1)}, u32[]{:S(2)}, u32[]{:S(2)}) collective-permute-start(f32[128,128]{1,0:T(8,128)S(1)} %get-tuple-element.46), channel_id=1, source_target_pairs={{0,18},{2,16},{4,22},{6,20},{8,26},{10,24},{12,30},{14,28},{16,2},... | collective-permute-start | bytes 196616 | tf_op jit(solution)/shard_map/ppermute | solution.py:196
  14.2 15.7 %collective-permute-start.9 = (f32[128,128]{1,0:T(8,128)S(1)}, f32[128,128]{1,0:T(8,128)S(1)}, u32[]{:S(2)}, u32[]{:S(2)}) collective-permute-start(f32[128,128]{1,0:T(8,128)S(1)} %get-tuple-element.47), channel_id=1, source_target_pairs={{0,20},{2,22},{4,16},{6,18},{8,28},{10,30},{12,24},{14,26},{16,4},... | collective-permute-start | bytes 196616 | tf_op jit(solution)/shard_map/ppermute | solution.py:196
  17.7 20.3 %collective-permute-start.10 = (f32[128,128]{1,0:T(8,128)S(1)}, f32[128,128]{1,0:T(8,128)S(1)}, u32[]{:S(2)}, u32[]{:S(2)}) collective-permute-start(f32[128,128]{1,0:T(8,128)S(1)} %get-tuple-element.48), channel_id=1, source_target_pairs={{0,22},{2,20},{4,18},{6,16},{8,30},{10,28},{12,26},{14,24},{16,6},... | collective-permute-start | bytes 196616 | tf_op jit(solution)/shard_map/ppermute | solution.py:196
  17.7 20.2 %collective-permute-start.11 = (f32[128,128]{1,0:T(8,128)S(1)}, f32[128,128]{1,0:T(8,128)S(1)}, u32[]{:S(2)}, u32[]{:S(2)}) collective-permute-start(f32[128,128]{1,0:T(8,128)S(1)} %get-tuple-element.49), channel_id=1, source_target_pairs={{0,24},{2,26},{4,28},{6,30},{8,16},{10,18},{12,20},{14,22},{16,8},... | collective-permute-start | bytes 196616 | tf_op jit(solution)/shard_map/ppermute | solution.py:196
  21.3 16.6 %collective-permute-start.12 = (f32[128,128]{1,0:T(8,128)S(1)}, f32[128,128]{1,0:T(8,128)S(1)}, u32[]{:S(2)}, u32[]{:S(2)}) collective-permute-start(f32[128,128]{1,0:T(8,128)S(1)} %get-tuple-element.50), channel_id=1, source_target_pairs={{0,26},{2,24},{4,30},{6,28},{8,18},{10,16},{12,22},{14,20},{16,10}... | collective-permute-start | bytes 196616 | tf_op jit(solution)/shard_map/ppermute | solution.py:196
  25.9 12.1 %collective-permute-start.13 = (f32[128,128]{1,0:T(8,128)S(1)}, f32[128,128]{1,0:T(8,128)S(1)}, u32[]{:S(2)}, u32[]{:S(2)}) collective-permute-start(f32[128,128]{1,0:T(8,128)S(1)} %get-tuple-element.51), channel_id=1, source_target_pairs={{0,28},{2,30},{4,24},{6,26},{8,20},{10,22},{12,16},{14,18},{16,12}... | collective-permute-start | bytes 196616 | tf_op jit(solution)/shard_map/ppermute | solution.py:196
  29.9 8.1 %collective-permute-start.14 = (f32[128,128]{1,0:T(8,128)S(1)}, f32[128,128]{1,0:T(8,128)S(1)}, u32[]{:S(2)}, u32[]{:S(2)}) collective-permute-start(f32[128,128]{1,0:T(8,128)S(1)} %get-tuple-element.52), channel_id=1, source_target_pairs={{0,30},{2,28},{4,26},{6,24},{8,22},{10,20},{12,18},{14,16},{16,14}... | collective-permute-start | bytes 196616 | tf_op jit(solution)/shard_map/ppermute | solution.py:196
  57.1 4.2 %collective-permute-start.15 = (f32[128,128]{1,0:T(8,128)S(1)}, f32[128,128]{1,0:T(8,128)S(1)}, u32[]{:S(2)}, u32[]{:S(2)}) collective-permute-start(f32[128,128]{1,0:T(8,128)S(1)} %get-tuple-element.56), channel_id=1, source_target_pairs={{0,2},{2,0},{4,6},{6,4},{8,10},{10,8},{12,14},{14,12},{16,18},{18,... | collective-permute-start | bytes 196616 | tf_op jit(solution)/shard_map/ppermute | solution.py:196
  57.8 4.9 %collective-permute-start.16 = (f32[128,128]{1,0:T(8,128)S(1)}, f32[128,128]{1,0:T(8,128)S(1)}, u32[]{:S(2)}, u32[]{:S(2)}) collective-permute-start(f32[128,128]{1,0:T(8,128)S(1)} %get-tuple-element.57), channel_id=1, source_target_pairs={{0,4},{2,6},{4,0},{6,2},{8,12},{10,14},{12,8},{14,10},{16,20},{18,... | collective-permute-start | bytes 196616 | tf_op jit(solution)/shard_map/ppermute | solution.py:196
  59.1 4.5 %collective-permute-start.17 = (f32[128,128]{1,0:T(8,128)S(1)}, f32[128,128]{1,0:T(8,128)S(1)}, u32[]{:S(2)}, u32[]{:S(2)}) collective-permute-start(f32[128,128]{1,0:T(8,128)S(1)} %get-tuple-element.58), channel_id=1, source_target_pairs={{0,6},{2,4},{4,2},{6,0},{8,14},{10,12},{12,10},{14,8},{16,22},{18,... | collective-permute-start | bytes 196616 | tf_op jit(solution)/shard_map/ppermute | solution.py:196
  59.2 7.3 %collective-permute-start.18 = (f32[128,128]{1,0:T(8,128)S(1)}, f32[128,128]{1,0:T(8,128)S(1)}, u32[]{:S(2)}, u32[]{:S(2)}) collective-permute-start(f32[128,128]{1,0:T(8,128)S(1)} %get-tuple-element.59), channel_id=1, source_target_pairs={{0,8},{2,10},{4,12},{6,14},{8,0},{10,2},{12,4},{14,6},{16,24},{18,... | collective-permute-start | bytes 196616 | tf_op jit(solution)/shard_map/ppermute | solution.py:196
  61.0 5.7 %collective-permute-start.19 = (f32[128,128]{1,0:T(8,128)S(1)}, f32[128,128]{1,0:T(8,128)S(1)}, u32[]{:S(2)}, u32[]{:S(2)}) collective-permute-start(f32[128,128]{1,0:T(8,128)S(1)} %get-tuple-element.60), channel_id=1, source_target_pairs={{0,10},{2,8},{4,14},{6,12},{8,2},{10,0},{12,6},{14,4},{16,26},{18,... | collective-permute-start | bytes 196616 | tf_op jit(solution)/shard_map/ppermute | solution.py:196
  61.3 7.9 %collective-permute-start.20 = (f32[128,128]{1,0:T(8,128)S(1)}, f32[128,128]{1,0:T(8,128)S(1)}, u32[]{:S(2)}, u32[]{:S(2)}) collective-permute-start(f32[128,128]{1,0:T(8,128)S(1)} %get-tuple-element.61), channel_id=1, source_target_pairs={{0,12},{2,14},{4,8},{6,10},{8,4},{10,6},{12,0},{14,2},{16,28},{18,... | collective-permute-start | bytes 196616 | tf_op jit(solution)/shard_map/ppermute | solution.py:196
  62.7 7.6 %collective-permute-start.21 = (f32[128,128]{1,0:T(8,128)S(1)}, f32[128,128]{1,0:T(8,128)S(1)}, u32[]{:S(2)}, u32[]{:S(2)}) collective-permute-start(f32[128,128]{1,0:T(8,128)S(1)} %get-tuple-element.62), channel_id=1, source_target_pairs={{0,14},{2,12},{4,10},{6,8},{8,6},{10,4},{12,2},{14,0},{16,30},{18,... | collective-permute-start | bytes 196616 | tf_op jit(solution)/shard_map/ppermute | solution.py:196
  63.6 8.8 %collective-permute-start.22 = (f32[128,128]{1,0:T(8,128)S(1)}, f32[128,128]{1,0:T(8,128)S(1)}, u32[]{:S(2)}, u32[]{:S(2)}) collective-permute-start(f32[128,128]{1,0:T(8,128)S(1)} %get-tuple-element.63), channel_id=1, source_target_pairs={{0,16},{2,18},{4,20},{6,22},{8,24},{10,26},{12,28},{14,30},{16,0},... | collective-permute-start | bytes 196616 | tf_op jit(solution)/shard_map/ppermute | solution.py:196
  66.5 12.5 %collective-permute-start.23 = (f32[128,128]{1,0:T(8,128)S(1)}, f32[128,128]{1,0:T(8,128)S(1)}, u32[]{:S(2)}, u32[]{:S(2)}) collective-permute-start(f32[128,128]{1,0:T(8,128)S(1)} %get-tuple-element.64), channel_id=1, source_target_pairs={{0,18},{2,16},{4,22},{6,20},{8,26},{10,24},{12,30},{14,28},{16,2},... | collective-permute-start | bytes 196616 | tf_op jit(solution)/shard_map/ppermute | solution.py:196
  66.7 14.8 %collective-permute-start.24 = (f32[128,128]{1,0:T(8,128)S(1)}, f32[128,128]{1,0:T(8,128)S(1)}, u32[]{:S(2)}, u32[]{:S(2)}) collective-permute-start(f32[128,128]{1,0:T(8,128)S(1)} %get-tuple-element.65), channel_id=1, source_target_pairs={{0,20},{2,22},{4,16},{6,18},{8,28},{10,30},{12,24},{14,26},{16,4},... | collective-permute-start | bytes 196616 | tf_op jit(solution)/shard_map/ppermute | solution.py:196
  69.2 14.4 %collective-permute-start.25 = (f32[128,128]{1,0:T(8,128)S(1)}, f32[128,128]{1,0:T(8,128)S(1)}, u32[]{:S(2)}, u32[]{:S(2)}) collective-permute-start(f32[128,128]{1,0:T(8,128)S(1)} %get-tuple-element.66), channel_id=1, source_target_pairs={{0,22},{2,20},{4,18},{6,16},{8,30},{10,28},{12,26},{14,24},{16,6},... | collective-permute-start | bytes 196616 | tf_op jit(solution)/shard_map/ppermute | solution.py:196
  70.3 13.3 %collective-permute-start.26 = (f32[128,128]{1,0:T(8,128)S(1)}, f32[128,128]{1,0:T(8,128)S(1)}, u32[]{:S(2)}, u32[]{:S(2)}) collective-permute-start(f32[128,128]{1,0:T(8,128)S(1)} %get-tuple-element.67), channel_id=1, source_target_pairs={{0,24},{2,26},{4,28},{6,30},{8,16},{10,18},{12,20},{14,22},{16,8},... | collective-permute-start | bytes 196616 | tf_op jit(solution)/shard_map/ppermute | solution.py:196
  72.5 11.1 %collective-permute-start.27 = (f32[128,128]{1,0:T(8,128)S(1)}, f32[128,128]{1,0:T(8,128)S(1)}, u32[]{:S(2)}, u32[]{:S(2)}) collective-permute-start(f32[128,128]{1,0:T(8,128)S(1)} %get-tuple-element.68), channel_id=1, source_target_pairs={{0,26},{2,24},{4,30},{6,28},{8,18},{10,16},{12,22},{14,20},{16,10}... | collective-permute-start | bytes 196616 | tf_op jit(solution)/shard_map/ppermute | solution.py:196
  79.0 7.3 %collective-permute-start.28 = (f32[128,128]{1,0:T(8,128)S(1)}, f32[128,128]{1,0:T(8,128)S(1)}, u32[]{:S(2)}, u32[]{:S(2)}) collective-permute-start(f32[128,128]{1,0:T(8,128)S(1)} %get-tuple-element.69), channel_id=1, source_target_pairs={{0,28},{2,30},{4,24},{6,26},{8,20},{10,22},{12,16},{14,18},{16,12}... | collective-permute-start | bytes 196616 | tf_op jit(solution)/shard_map/ppermute | solution.py:196
  81.5 7.0 %collective-permute-start.29 = (f32[128,128]{1,0:T(8,128)S(1)}, f32[128,128]{1,0:T(8,128)S(1)}, u32[]{:S(2)}, u32[]{:S(2)}) collective-permute-start(f32[128,128]{1,0:T(8,128)S(1)} %get-tuple-element.70), channel_id=1, source_target_pairs={{0,30},{2,28},{4,26},{6,24},{8,22},{10,20},{12,18},{14,16},{16,14}... | collective-permute-start | bytes 196616 | tf_op jit(solution)/shard_map/ppermute | solution.py:196
  (4 other events, 3.4 us)

commit v5 on v1

--- a/solution.py
+++ b/solution.py
@@ -15,6 +15,7 @@
 PHASES = 16
 PHASE_BITS = 12
 LANES = 128
+PACKED = 16
 PAIRED = Layout(major_to_minor=(1, 0, 2))
 
 
@@ -84,49 +85,96 @@
     return rows
 
 
-def layers_kernel(wide, spect, x_ref, high_ref, low_ref, turn_ref, out_ref, state, left_high, left_low):
-    layer = pl.program_id(0)
-    count = wide * spect
+def exchange_order(wide):
+    order = [0]
+    for far, near in zip(range(wide // 2, wide), list(range(wide // 2 - 1, 0, -1)) + [None]):
+        order += [far] if near is None else [far, near]
+    return order
+
+
+def pick_kernel(wide, x_hbm, *rest):
+    sends, sem = rest[:-1], rest[-1]
+    me = lax.axis_index("wide")
+    block = x_hbm.shape[0] // wide
+    copies = [
+        pltpu.make_async_copy(x_hbm.at[pl.ds((me ^ k) * block, block)], sends[i], sem.at[i])
+        for i, k in enumerate(exchange_order(wide))
+    ]
+    for copy in copies:
+        copy.start()
+    for copy in copies:
+        copy.wait()
+
+
+def place_kernel(wide, *rest):
+    blocks, out_hbm, sem = rest[:wide], rest[wide], rest[wide + 1]
+    me = lax.axis_index("wide")
+    block = blocks[0].shape[0]
+    copies = [
+        pltpu.make_async_copy(blocks[i], out_hbm.at[pl.ds((me ^ k) * block, block)], sem.at[i])
+        for i, k in enumerate(exchange_order(wide))
+    ]
+    for copy in copies:
+        copy.start()
+    for copy in copies:
+        copy.wait()
+
+
+def layers_kernel(wide, spect, *rest):
+    received = rest[:wide]
+    high_ref, low_ref, turn_ref = rest[wide : wide + 3]
+    outs = rest[wide + 3 : 2 * wide + 3]
+    state, left_high, left_low = rest[2 * wide + 3 :]
+    me = lax.axis_index("wide")
     span = LOW // wide
     half = wide // 2
-
-    @pl.when(layer == 0)
-    def _():
+    joined = max(1, PACKED // spect)
+
+    for i, k in enumerate(exchange_order(wide)):
+        rows = pl.ds(pl.multiple_of((me ^ k) * spect, spect), spect)
         for part in range(2):
             for lanes in range(2):
-                state[part, :, lanes * LANES : (lanes + 1) * LANES] = x_ref[pl.ds(2 * lanes + part, count, stride=4), :]
-
-    for part in range(2):
-        for top in range(2):
-            for lanes in range(2):
-                first = top * half * spect
-                block = state[part, first : first + half * spect, lanes * LANES : (lanes + 1) * LANES]
-                rows = exchange_modes([block[m * spect : (m + 1) * spect] for m in range(half)], span)
-                for g in range(half):
-                    at = (lanes * half + g) * spect
-                    column = part * LOW + top * LANES
-                    high, low = split(rows[g])
-                    left_high[at : at + spect, column : column + LANES] = high
-                    left_low[at : at + spect, column : column + LANES] = low
-
-    cosine = turn_ref[0, 0][None]
-    sine = turn_ref[0, 1][None]
-    for block in range(2):
-        rows = slice(block * half * spect, (block + 1) * half * spect)
-        dot = partial(jnp.dot, preferred_element_type=jnp.float32)
-        gated = dot(left_high[rows], high_ref[0])
-        gated = gated + dot(left_low[rows], high_ref[0])
-        gated = gated + dot(left_high[rows], low_ref[0])
-        real = gated[:, :LOW].reshape(half, spect, LOW)
-        imag = gated[:, LOW:].reshape(half, spect, LOW)
-        state[0, rows] = (real * cosine - imag * sine).reshape(half * spect, LOW)
-        state[1, rows] = (real * sine + imag * cosine).reshape(half * spect, LOW)
-
-    @pl.when(layer == LAYERS - 1)
-    def _():
+                state[part, rows, lanes * LANES : (lanes + 1) * LANES] = received[i][
+                    pl.ds(2 * lanes + part, spect, stride=4), :
+                ]
+
+    def one_layer(layer, carry):
+        for part in range(2):
+            for top in range(2):
+                for lanes in range(2):
+                    first = top * half * spect
+                    piece = state[part, first : first + half * spect, lanes * LANES : (lanes + 1) * LANES]
+                    rows = exchange_modes([piece[m * spect : (m + 1) * spect] for m in range(half)], span)
+                    for g in range(0, half, joined):
+                        at = (lanes * half + g) * spect
+                        column = part * LOW + top * LANES
+                        high, low = split(jnp.concatenate(rows[g : g + joined], axis=0))
+                        left_high[at : at + joined * spect, column : column + LANES] = high
+                        left_low[at : at + joined * spect, column : column + LANES] = low
+
+        cosine = turn_ref[layer, 0][None]
+        sine = turn_ref[layer, 1][None]
+        for block in range(2):
+            rows = slice(block * half * spect, (block + 1) * half * spect)
+            dot = partial(jnp.dot, preferred_element_type=jnp.float32)
+            gated = dot(left_high[rows], high_ref[layer])
+            gated = gated + dot(left_low[rows], high_ref[layer])
+            gated = gated + dot(left_high[rows], low_ref[layer])
+            real = gated[:, :LOW].reshape(half, spect, LOW)
+            imag = gated[:, LOW:].reshape(half, spect, LOW)
+            state[0, rows] = (real * cosine - imag * sine).reshape(half * spect, LOW)
+            state[1, rows] = (real * sine + imag * cosine).reshape(half * spect, LOW)
+        return carry
+
+    lax.fori_loop(0, LAYERS, one_layer, 0)
+
+    for i, k in enumerate(exchange_order(wide)):
+        rows = pl.ds(pl.multiple_of((me ^ k) * spect, spect), spect)
         for part in range(2):
             for lanes in range(2):
-                out_ref[pl.ds(2 * lanes + part, count, stride=4), :] = state[part, :, lanes * LANES : (lanes + 1) * LANES]
+                outs[i][pl.ds(2 * lanes + part, spect, stride=4), :] = state[
+                    part, rows, lanes * LANES : (lanes + 1) * LANES
+                ]
 
 
 def local(state, gate_re, gate_im, bit_orders, phase_pairs, phase_angles):
@@ -138,7 +186,27 @@
 
     view = with_layout_constraint(state.reshape(2, amps // LANES, LANES), PAIRED)
     rows = view.transpose(1, 0, 2).reshape(2 * amps // LANES, LANES)
-    gathered = lax.all_to_all(rows, "wide", split_axis=0, concat_axis=0, tiled=True)
+    anywhere = pl.BlockSpec(memory_space=pl.ANY)
+    piece = jax.ShapeDtypeStruct((4 * spect, LANES), jnp.float32)
+    part_of_vmem = pltpu.CompilerParams(vmem_limit_bytes=24 * 2**20)
+
+    def swap(blocks):
+        arrived = [
+            lax.ppermute(block, "wide", [(i, i ^ k) for i in range(wide)])
+            for block, k in zip(blocks[1:], exchange_order(wide)[1:])
+        ]
+        return [blocks[0]] + arrived
+
+    sends = pl.pallas_call(
+        partial(pick_kernel, wide),
+        in_specs=[anywhere],
+        out_specs=[anywhere] * wide,
+        out_shape=[piece] * wide,
+        scratch_shapes=[pltpu.SemaphoreType.DMA((wide,))],
+        compiler_params=pltpu.CompilerParams(vmem_limit_bytes=60 * 2**20),
+        name="pick",
+    )(rows)
+    received = swap(sends)
 
     place = jnp.stack([lax.axis_index("wide"), lax.axis_index("narrow")]).astype(jnp.int32)
     smem = pl.BlockSpec(memory_space=pltpu.SMEM)
@@ -152,29 +220,36 @@
         in_specs=[smem, smem, smem, smem, gate_spec, gate_spec],
         out_specs=[square_spec, square_spec, turn_spec],
         out_shape=[square, square, jax.ShapeDtypeStruct((LAYERS, 2, spect, LOW), jnp.float32)],
-        compiler_params=pltpu.CompilerParams(vmem_limit_bytes=16 * 2**20),
+        compiler_params=part_of_vmem,
         cost_estimate=pl.CostEstimate(flops=10**9, bytes_accessed=8 * 10**6, transcendentals=10**5),
         name="tables",
     )(bit_orders, phase_pairs.reshape(LAYERS, 2 * PHASES), phase_angles, place, gate_re, gate_im)
 
-    whole = pl.BlockSpec((4 * count, LANES), lambda l: (0, 0))
+    in_vmem = pl.BlockSpec(memory_space=pltpu.VMEM)
     done = pl.pallas_call(
         partial(layers_kernel, wide, spect),
-        grid=(LAYERS,),
-        in_specs=[whole, square_spec, square_spec, turn_spec],
-        out_specs=whole,
-        out_shape=jax.ShapeDtypeStruct((4 * count, LANES), jnp.float32),
+        in_specs=[in_vmem] * (wide + 3),
+        out_specs=[in_vmem] * wide,
+        out_shape=[piece] * wide,
         scratch_shapes=[
             pltpu.VMEM((2, count, LOW), jnp.float32),
             pltpu.VMEM((count, 2 * LOW), jnp.bfloat16),
             pltpu.VMEM((count, 2 * LOW), jnp.bfloat16),
         ],
-        compiler_params=pltpu.CompilerParams(vmem_limit_bytes=32 * 2**20),
+        compiler_params=part_of_vmem,
         cost_estimate=pl.CostEstimate(flops=5 * 10**9, bytes_accessed=10**7, transcendentals=0),
         name="layers",
-    )(gathered, high, low, turn)
-
-    back = lax.all_to_all(done, "wide", split_axis=0, concat_axis=0, tiled=True)
+    )(*received, high, low, turn)
+
+    back = pl.pallas_call(
+        partial(place_kernel, wide),
+        in_specs=[anywhere] * wide,
+        out_specs=anywhere,
+        out_shape=jax.ShapeDtypeStruct(rows.shape, jnp.float32),
+        scratch_shapes=[pltpu.SemaphoreType.DMA((wide,))],
+        compiler_params=part_of_vmem,
+        name="place",
+    )(*swap(done))
     view = with_layout_constraint(back.reshape(amps // LANES, 2, LANES).transpose(1, 0, 2), PAIRED)
     return view.reshape(2, amps)
 

time: 75.8 us -> 103 us (1.36)
  starting transfers between devices: 7.39 us -> 47.4 us
  Pallas kernels: 12.4 us -> 46.5 us
  blocking collectives: 31.5 us -> 0 us
  local copies, waits for them, and re-layouts: 12.3 us -> 4.23 us
  waiting for transfers between devices: 11.3 us -> 4.37 us
    ppermute x0 -> x30, starting transfers between devices: none -> 47.4 us  [swap(): lax.ppermute(block, 'wide', [(i, i ^ k) for i in range(wide)])]
    pallas_call x1 -> x3, Pallas kernels: 8.4 us -> 42.5 us  [the longest x1 33 us: local(): pl.pallas_call(partial(pick_kernel, wide), in_specs=[anywhere], out_specs...]
    all_to_all x1 -> x0, blocking collectives: 31.5 us -> none  [local(): back = lax.all_to_all(done, 'wide', split_axis=0, concat_axis=0, tiled=True)]
    all_to_all x1 -> x0, waiting for transfers between devices: 11.3 us -> none  [local(): lax.all_to_all(rows, 'wide', split_axis=0, concat_axis=0, tiled=True)]
    unnamed x18 -> x11, local copies, waits for them, and re-layouts: 12.2 us -> 4.15 us
    all_to_all x1 -> x0, starting transfers between devices: 7.39 us -> none  [local(): lax.all_to_all(rows, 'wide', split_axis=0, concat_axis=0, tiled=True)]
    ppermute x0 -> x30, waiting for transfers between devices: none -> 4.37 us  [swap(): lax.ppermute(block, 'wide', [(i, i ^ k) for i in range(wide)])]
  transfers between devices with their start and end apart: 1 -> 30, of which waited for: 1 -> 3; matrix products, arithmetic and copies ran while one was open for 1% -> 1% of each run, Pallas kernels for 5% -> 4%
where the time goes in v5:
time: 103 us
  starting transfers between devices  47.4 us (46%)
  Pallas kernels  46.5 us (45%)
  waiting for transfers between devices  4.37 us (4%)
  local copies, waits for them, and re-layouts  4.23 us (4%)
    ppermute x30, starting transfers between devices, swap(): lax.ppermute(block, 'wide', [(i, i ^ k) for i in range(wide)])  47.4 us
    pallas_call x1, Pallas kernels, local(): pl.pallas_call(partial(pick_kernel, wide), in_specs=[anywhere], out_specs...  33 us
    pallas_call x1, Pallas kernels, local(): pl.pallas_call(partial(layers_kernel, wide, spect), in_specs=[in_vmem] *...  8.37 us
    ppermute x30, waiting for transfers between devices, swap(): lax.ppermute(block, 'wide', [(i, i ^ k) for i in range(wide)])  4.37 us
    unnamed x11, local copies, waits for them, and re-layouts  4.15 us
    pallas_call x1, Pallas kernels, local(): pl.pallas_call(partial(tables_kernel, spect, narrow), grid=(LAYERS,), in_...  3.99 us
  transfers between devices with their start and end apart: 30, of which 3 were waited for; matrix products, arithmetic and copies ran while one was open for 1% of the time, Pallas kernels for 4%

profile of v5, /device:TPU:0, one launch (start us, length us, event | category | flops | bytes accessed | tf_op | source)
XLA Modules:
  0.0 102.6 jit_solution(7339077265860704985)
XLA Ops:
  0.0 33.0 %pick.1 = (f32[128,128]{1,0:T(8,128)}, f32[128,128]{1,0:T(8,128)}, f32[128,128]{1,0:T(8,128)}, f32[128,128]{1,0:T(8,128)}, f32[128,128]{1,0:T(8,128)}, /*index=5...) custom-call(f32[2048,128]{1,0:T(8,128)} %bitcast.13), custom_call_target="tpu_custom_call" | custom-call | tf_op jit(solution)/shard_map/pick/pallas_call | solution.py:200
  33.0 4.1 %collective-permute-start = (f32[128,128]{1,0:T(8,128)}, f32[128,128]{1,0:T(8,128)S(1)}, u32[]{:S(2)}, u32[]{:S(2)}) collective-permute-start(f32[128,128]{1,0:T(8,128)} %get-tuple-element.41), channel_id=1, source_target_pairs={{0,16},{2,18},{4,20},{6,22},{8,24},{10,26},{12,28},{14,30},{16,0},... | collective-permute-start | bytes 196616 | tf_op jit(solution)/shard_map/ppermute | solution.py:195
  37.1 1.7 %collective-permute-start.1 = (f32[128,128]{1,0:T(8,128)}, f32[128,128]{1,0:T(8,128)S(1)}, u32[]{:S(2)}, u32[]{:S(2)}) collective-permute-start(f32[128,128]{1,0:T(8,128)} %get-tuple-element.42), channel_id=1, source_target_pairs={{0,14},{2,12},{4,10},{6,8},{8,6},{10,4},{12,2},{14,0},{16,30},{18,... | collective-permute-start | bytes 196616 | tf_op jit(solution)/shard_map/ppermute | solution.py:195
  38.8 0.9 collective-permute-start.2
  39.9 3.8 %collective-permute-start.4 = (f32[128,128]{1,0:T(8,128)}, f32[128,128]{1,0:T(8,128)S(1)}, u32[]{:S(2)}, u32[]{:S(2)}) collective-permute-start(f32[128,128]{1,0:T(8,128)} %get-tuple-element.45), channel_id=1, source_target_pairs={{0,20},{2,22},{4,16},{6,18},{8,28},{10,30},{12,24},{14,26},{16,4},... | collective-permute-start | bytes 196616 | tf_op jit(solution)/shard_map/ppermute | solution.py:195
  43.7 0.8 copy.8
  44.7 1.6 %collective-permute-start.6 = (f32[128,128]{1,0:T(8,128)}, f32[128,128]{1,0:T(8,128)S(1)}, u32[]{:S(2)}, u32[]{:S(2)}) collective-permute-start(f32[128,128]{1,0:T(8,128)} %get-tuple-element.47), channel_id=1, source_target_pairs={{0,22},{2,20},{4,18},{6,16},{8,30},{10,28},{12,26},{14,24},{16,6},... | collective-permute-start | bytes 196616 | tf_op jit(solution)/shard_map/ppermute | solution.py:195
  46.3 1.3 %collective-permute-start.7 = (f32[128,128]{1,0:T(8,128)}, f32[128,128]{1,0:T(8,128)S(1)}, u32[]{:S(2)}, u32[]{:S(2)}) collective-permute-start(f32[128,128]{1,0:T(8,128)} %get-tuple-element.48), channel_id=1, source_target_pairs={{0,8},{2,10},{4,12},{6,14},{8,0},{10,2},{12,4},{14,6},{16,24},{18,... | collective-permute-start | bytes 196616 | tf_op jit(solution)/shard_map/ppermute | solution.py:195
  47.6 2.5 %collective-permute-start.8 = (f32[128,128]{1,0:T(8,128)}, f32[128,128]{1,0:T(8,128)S(1)}, u32[]{:S(2)}, u32[]{:S(2)}) collective-permute-start(f32[128,128]{1,0:T(8,128)} %get-tuple-element.49), channel_id=1, source_target_pairs={{0,24},{2,26},{4,28},{6,30},{8,16},{10,18},{12,20},{14,22},{16,8},... | collective-permute-start | bytes 196616 | tf_op jit(solution)/shard_map/ppermute | solution.py:195
  50.5 1.5 %collective-permute-start.10 = (f32[128,128]{1,0:T(8,128)}, f32[128,128]{1,0:T(8,128)S(1)}, u32[]{:S(2)}, u32[]{:S(2)}) collective-permute-start(f32[128,128]{1,0:T(8,128)} %get-tuple-element.51), channel_id=1, source_target_pairs={{0,26},{2,24},{4,30},{6,28},{8,18},{10,16},{12,22},{14,20},{16,10}... | collective-permute-start | bytes 196616 | tf_op jit(solution)/shard_map/ppermute | solution.py:195
  52.1 1.2 %collective-permute-start.11 = (f32[128,128]{1,0:T(8,128)}, f32[128,128]{1,0:T(8,128)S(1)}, u32[]{:S(2)}, u32[]{:S(2)}) collective-permute-start(f32[128,128]{1,0:T(8,128)} %get-tuple-element.52), channel_id=1, source_target_pairs={{0,4},{2,6},{4,0},{6,2},{8,12},{10,14},{12,8},{14,10},{16,20},{18,... | collective-permute-start | bytes 196616 | tf_op jit(solution)/shard_map/ppermute | solution.py:195
  53.3 3.5 %collective-permute-start.12 = (f32[128,128]{1,0:T(8,128)}, f32[128,128]{1,0:T(8,128)S(1)}, u32[]{:S(2)}, u32[]{:S(2)}) collective-permute-start(f32[128,128]{1,0:T(8,128)} %get-tuple-element.53), channel_id=1, source_target_pairs={{0,28},{2,30},{4,24},{6,26},{8,20},{10,22},{12,16},{14,18},{16,12}... | collective-permute-start | bytes 196616 | tf_op jit(solution)/shard_map/ppermute | solution.py:195
  56.8 2.0 %collective-permute-start.14 = (f32[128,128]{1,0:T(8,128)}, f32[128,128]{1,0:T(8,128)S(1)}, u32[]{:S(2)}, u32[]{:S(2)}) collective-permute-start(f32[128,128]{1,0:T(8,128)} %get-tuple-element.55), channel_id=1, source_target_pairs={{0,30},{2,28},{4,26},{6,24},{8,22},{10,20},{12,18},{14,16},{16,14}... | collective-permute-start | bytes 196616 | tf_op jit(solution)/shard_map/ppermute | solution.py:195
  58.8 1.0 copy-done
  59.8 1.0 copy-done.1
  60.8 0.7 copy-done.3
  61.5 0.7 copy-done.4
  62.2 4.0 %tables.1 = (bf16[6,512,512]{2,1,0:T(8,128)(2,1)S(1)}, bf16[6,512,512]{2,1,0:T(8,128)(2,1)S(1)}, f32[6,2,32,256]{3,2,1,0:T(8,128)S(1)}) custom-call(s32[6,8]{1,0:T(8,128)S(1)} %copy-done.3, s32[6,32]{1,0:T(8,128)S(1)} %copy.9.pair_ref, f32[6,16]{1,0:T(8,128)S(1)} %copy-done.4, s32[2]{0:T(128)S(1)} %pad_add_fusion.place_ref, f32[6,128,128]{2,1,0:T(8,128)S(1)} %copy-done, ...), custom_call_target="tpu_custom_call" | custom-call | flops 1000000000 | bytes 8000000 | tf_op jit(solution)/shard_map/tables/pallas_call | solution.py:217
  66.3 8.4 %layers.1 = (f32[128,128]{1,0:T(8,128)S(1)}, f32[128,128]{1,0:T(8,128)S(1)}, f32[128,128]{1,0:T(8,128)S(1)}, f32[128,128]{1,0:T(8,128)S(1)}, f32[128,128]{1,0:T(...) custom-call(f32[128,128]{1,0:T(8,128)S(1)} %copy-done.2, ...), custom_call_target="tpu_custom_call" | custom-call | flops 5000000000 | bytes 10000000 | tf_op jit(solution)/shard_map/layers/pallas_call | solution.py:229
  74.7 2.7 %collective-permute-start.16 = (f32[128,128]{1,0:T(8,128)S(1)}, f32[128,128]{1,0:T(8,128)S(1)}, u32[]{:S(2)}, u32[]{:S(2)}) collective-permute-start(f32[128,128]{1,0:T(8,128)S(1)} %get-tuple-element.61), channel_id=1, source_target_pairs={{0,14},{2,12},{4,10},{6,8},{8,6},{10,4},{12,2},{14,0},{16,30},{18,... | collective-permute-start | bytes 196616 | tf_op jit(solution)/shard_map/ppermute | solution.py:195
  78.0 2.3 %collective-permute-start.18 = (f32[128,128]{1,0:T(8,128)S(1)}, f32[128,128]{1,0:T(8,128)S(1)}, u32[]{:S(2)}, u32[]{:S(2)}) collective-permute-start(f32[128,128]{1,0:T(8,128)S(1)} %get-tuple-element.63), channel_id=1, source_target_pairs={{0,12},{2,14},{4,8},{6,10},{8,4},{10,6},{12,0},{14,2},{16,28},{18,... | collective-permute-start | bytes 196616 | tf_op jit(solution)/shard_map/ppermute | solution.py:195
  80.3 1.3 %collective-permute-start.19 = (f32[128,128]{1,0:T(8,128)S(1)}, f32[128,128]{1,0:T(8,128)S(1)}, u32[]{:S(2)}, u32[]{:S(2)}) collective-permute-start(f32[128,128]{1,0:T(8,128)S(1)} %get-tuple-element.64), channel_id=1, source_target_pairs={{0,20},{2,22},{4,16},{6,18},{8,28},{10,30},{12,24},{14,26},{16,4},... | collective-permute-start | bytes 196616 | tf_op jit(solution)/shard_map/ppermute | solution.py:195
  81.5 0.9 collective-permute-start.20
  82.5 1.8 %collective-permute-start.21 = (f32[128,128]{1,0:T(8,128)S(1)}, f32[128,128]{1,0:T(8,128)S(1)}, u32[]{:S(2)}, u32[]{:S(2)}) collective-permute-start(f32[128,128]{1,0:T(8,128)S(1)} %get-tuple-element.66), channel_id=1, source_target_pairs={{0,22},{2,20},{4,18},{6,16},{8,30},{10,28},{12,26},{14,24},{16,6},... | collective-permute-start | bytes 196616 | tf_op jit(solution)/shard_map/ppermute | solution.py:195
  84.3 1.6 %collective-permute-start.22 = (f32[128,128]{1,0:T(8,128)S(1)}, f32[128,128]{1,0:T(8,128)S(1)}, u32[]{:S(2)}, u32[]{:S(2)}) collective-permute-start(f32[128,128]{1,0:T(8,128)S(1)} %get-tuple-element.67), channel_id=1, source_target_pairs={{0,8},{2,10},{4,12},{6,14},{8,0},{10,2},{12,4},{14,6},{16,24},{18,... | collective-permute-start | bytes 196616 | tf_op jit(solution)/shard_map/ppermute | solution.py:195
  85.9 1.8 %collective-permute-start.23 = (f32[128,128]{1,0:T(8,128)S(1)}, f32[128,128]{1,0:T(8,128)S(1)}, u32[]{:S(2)}, u32[]{:S(2)}) collective-permute-start(f32[128,128]{1,0:T(8,128)S(1)} %get-tuple-element.68), channel_id=1, source_target_pairs={{0,24},{2,26},{4,28},{6,30},{8,16},{10,18},{12,20},{14,22},{16,8},... | collective-permute-start | bytes 196616 | tf_op jit(solution)/shard_map/ppermute | solution.py:195
  87.7 4.9 %collective-permute-start.25 = (f32[128,128]{1,0:T(8,128)S(1)}, f32[128,128]{1,0:T(8,128)S(1)}, u32[]{:S(2)}, u32[]{:S(2)}) collective-permute-start(f32[128,128]{1,0:T(8,128)S(1)} %get-tuple-element.70), channel_id=1, source_target_pairs={{0,26},{2,24},{4,30},{6,28},{8,18},{10,16},{12,22},{14,20},{16,10}... | collective-permute-start | bytes 196616 | tf_op jit(solution)/shard_map/ppermute | solution.py:195
  92.6 2.0 %collective-permute-start.27 = (f32[128,128]{1,0:T(8,128)S(1)}, f32[128,128]{1,0:T(8,128)S(1)}, u32[]{:S(2)}, u32[]{:S(2)}) collective-permute-start(f32[128,128]{1,0:T(8,128)S(1)} %get-tuple-element.72), channel_id=1, source_target_pairs={{0,28},{2,30},{4,24},{6,26},{8,20},{10,22},{12,16},{14,18},{16,12}... | collective-permute-start | bytes 196616 | tf_op jit(solution)/shard_map/ppermute | solution.py:195
  94.9 2.7 %collective-permute-start.29 = (f32[128,128]{1,0:T(8,128)S(1)}, f32[128,128]{1,0:T(8,128)S(1)}, u32[]{:S(2)}, u32[]{:S(2)}) collective-permute-start(f32[128,128]{1,0:T(8,128)S(1)} %get-tuple-element.74), channel_id=1, source_target_pairs={{0,30},{2,28},{4,26},{6,24},{8,22},{10,20},{12,18},{14,16},{16,14}... | collective-permute-start | bytes 196616 | tf_op jit(solution)/shard_map/ppermute | solution.py:195
  97.5 2.1 %collective-permute-done.27.rest_13_ = f32[128,128]{1,0:T(8,128)S(1)} collective-permute-done((f32[128,128]{1,0:T(8,128)S(1)}, f32[128,128]{1,0:T(8,128)S(1)}, u32[]{:S(2)}, u32[]{:S(2)}) %collective-permute-start.27) | collective-permute-done | bytes 65568 | tf_op jit(solution)/shard_map/ppermute | solution.py:195
  99.7 1.9 %collective-permute-done.29.rest_15_ = f32[128,128]{1,0:T(8,128)S(1)} collective-permute-done((f32[128,128]{1,0:T(8,128)S(1)}, f32[128,128]{1,0:T(8,128)S(1)}, u32[]{:S(2)}, u32[]{:S(2)}) %collective-permute-start.29) | collective-permute-done | bytes 65568 | tf_op jit(solution)/shard_map/ppermute | solution.py:195
  101.6 1.1 %place.1 = f32[2048,128]{1,0:T(8,128)} custom-call(f32[128,128]{1,0:T(8,128)S(1)} %get-tuple-element.59.rest_0_, f32[128,128]{1,0:T(8,128)S(1)} %collective-permute-done.15.rest_1_, f32[128,128]{1,0:T(8,128)S(1)} %collective-permute-done.16.rest_2_, f32[128,128]{1,0:T(8,128)S(1)} %collective-permute-done.17.rest_3_, ...), custom_call_target="tpu_custom_call" | custom-call | tf_op jit(solution)/shard_map/place/pallas_call | solution.py:244
  (45 shorter events, 1.7 us)
Async XLA Ops:
  33.0 33.2 %copy-start.2 = (f32[128,128]{1,0:T(8,128)S(1)}, f32[128,128]{1,0:T(8,128)}, u32[]{:S(2)}) copy-start(f32[128,128]{1,0:T(8,128)} %get-tuple-element.40.rest_0_) | copy-start | bytes 196612
  33.0 11.5 %collective-permute-start = (f32[128,128]{1,0:T(8,128)}, f32[128,128]{1,0:T(8,128)S(1)}, u32[]{:S(2)}, u32[]{:S(2)}) collective-permute-start(f32[128,128]{1,0:T(8,128)} %get-tuple-element.41), channel_id=1, source_target_pairs={{0,16},{2,18},{4,20},{6,22},{8,24},{10,26},{12,28},{14,30},{16,0},... | collective-permute-start | bytes 196616 | tf_op jit(solution)/shard_map/ppermute | solution.py:195
  37.1 7.6 %collective-permute-start.1 = (f32[128,128]{1,0:T(8,128)}, f32[128,128]{1,0:T(8,128)S(1)}, u32[]{:S(2)}, u32[]{:S(2)}) collective-permute-start(f32[128,128]{1,0:T(8,128)} %get-tuple-element.42), channel_id=1, source_target_pairs={{0,14},{2,12},{4,10},{6,8},{8,6},{10,4},{12,2},{14,0},{16,30},{18,... | collective-permute-start | bytes 196616 | tf_op jit(solution)/shard_map/ppermute | solution.py:195
  38.8 7.5 %collective-permute-start.2 = (f32[128,128]{1,0:T(8,128)}, f32[128,128]{1,0:T(8,128)S(1)}, u32[]{:S(2)}, u32[]{:S(2)}) collective-permute-start(f32[128,128]{1,0:T(8,128)} %get-tuple-element.43), channel_id=1, source_target_pairs={{0,18},{2,16},{4,22},{6,20},{8,26},{10,24},{12,30},{14,28},{16,2},... | collective-permute-start | bytes 196616 | tf_op jit(solution)/shard_map/ppermute | solution.py:195
  39.7 7.9 %collective-permute-start.3 = (f32[128,128]{1,0:T(8,128)}, f32[128,128]{1,0:T(8,128)S(1)}, u32[]{:S(2)}, u32[]{:S(2)}) collective-permute-start(f32[128,128]{1,0:T(8,128)} %get-tuple-element.44), channel_id=1, source_target_pairs={{0,12},{2,14},{4,8},{6,10},{8,4},{10,6},{12,0},{14,2},{16,28},{18,... | collective-permute-start | bytes 196616 | tf_op jit(solution)/shard_map/ppermute | solution.py:195
  39.9 10.3 %collective-permute-start.4 = (f32[128,128]{1,0:T(8,128)}, f32[128,128]{1,0:T(8,128)S(1)}, u32[]{:S(2)}, u32[]{:S(2)}) collective-permute-start(f32[128,128]{1,0:T(8,128)} %get-tuple-element.45), channel_id=1, source_target_pairs={{0,20},{2,22},{4,16},{6,18},{8,28},{10,30},{12,24},{14,26},{16,4},... | collective-permute-start | bytes 196616 | tf_op jit(solution)/shard_map/ppermute | solution.py:195
  44.5 6.0 %collective-permute-start.5 = (f32[128,128]{1,0:T(8,128)}, f32[128,128]{1,0:T(8,128)S(1)}, u32[]{:S(2)}, u32[]{:S(2)}) collective-permute-start(f32[128,128]{1,0:T(8,128)} %get-tuple-element.46), channel_id=1, source_target_pairs={{0,10},{2,8},{4,14},{6,12},{8,2},{10,0},{12,6},{14,4},{16,26},{18,... | collective-permute-start | bytes 196616 | tf_op jit(solution)/shard_map/ppermute | solution.py:195
  44.7 7.4 %collective-permute-start.6 = (f32[128,128]{1,0:T(8,128)}, f32[128,128]{1,0:T(8,128)S(1)}, u32[]{:S(2)}, u32[]{:S(2)}) collective-permute-start(f32[128,128]{1,0:T(8,128)} %get-tuple-element.47), channel_id=1, source_target_pairs={{0,22},{2,20},{4,18},{6,16},{8,30},{10,28},{12,26},{14,24},{16,6},... | collective-permute-start | bytes 196616 | tf_op jit(solution)/shard_map/ppermute | solution.py:195
  46.3 7.0 %collective-permute-start.7 = (f32[128,128]{1,0:T(8,128)}, f32[128,128]{1,0:T(8,128)S(1)}, u32[]{:S(2)}, u32[]{:S(2)}) collective-permute-start(f32[128,128]{1,0:T(8,128)} %get-tuple-element.48), channel_id=1, source_target_pairs={{0,8},{2,10},{4,12},{6,14},{8,0},{10,2},{12,4},{14,6},{16,24},{18,... | collective-permute-start | bytes 196616 | tf_op jit(solution)/shard_map/ppermute | solution.py:195
  47.6 9.1 %collective-permute-start.8 = (f32[128,128]{1,0:T(8,128)}, f32[128,128]{1,0:T(8,128)S(1)}, u32[]{:S(2)}, u32[]{:S(2)}) collective-permute-start(f32[128,128]{1,0:T(8,128)} %get-tuple-element.49), channel_id=1, source_target_pairs={{0,24},{2,26},{4,28},{6,30},{8,16},{10,18},{12,20},{14,22},{16,8},... | collective-permute-start | bytes 196616 | tf_op jit(solution)/shard_map/ppermute | solution.py:195
  50.2 6.6 %collective-permute-start.9 = (f32[128,128]{1,0:T(8,128)}, f32[128,128]{1,0:T(8,128)S(1)}, u32[]{:S(2)}, u32[]{:S(2)}) collective-permute-start(f32[128,128]{1,0:T(8,128)} %get-tuple-element.50), channel_id=1, source_target_pairs={{0,6},{2,4},{4,2},{6,0},{8,14},{10,12},{12,10},{14,8},{16,22},{18,... | collective-permute-start | bytes 196616 | tf_op jit(solution)/shard_map/ppermute | solution.py:195
  50.5 15.7 %collective-permute-start.10 = (f32[128,128]{1,0:T(8,128)}, f32[128,128]{1,0:T(8,128)S(1)}, u32[]{:S(2)}, u32[]{:S(2)}) collective-permute-start(f32[128,128]{1,0:T(8,128)} %get-tuple-element.51), channel_id=1, source_target_pairs={{0,26},{2,24},{4,30},{6,28},{8,18},{10,16},{12,22},{14,20},{16,10}... | collective-permute-start | bytes 196616 | tf_op jit(solution)/shard_map/ppermute | solution.py:195
  52.1 14.1 %collective-permute-start.11 = (f32[128,128]{1,0:T(8,128)}, f32[128,128]{1,0:T(8,128)S(1)}, u32[]{:S(2)}, u32[]{:S(2)}) collective-permute-start(f32[128,128]{1,0:T(8,128)} %get-tuple-element.52), channel_id=1, source_target_pairs={{0,4},{2,6},{4,0},{6,2},{8,12},{10,14},{12,8},{14,10},{16,20},{18,... | collective-permute-start | bytes 196616 | tf_op jit(solution)/shard_map/ppermute | solution.py:195
  53.3 12.9 %collective-permute-start.12 = (f32[128,128]{1,0:T(8,128)}, f32[128,128]{1,0:T(8,128)S(1)}, u32[]{:S(2)}, u32[]{:S(2)}) collective-permute-start(f32[128,128]{1,0:T(8,128)} %get-tuple-element.53), channel_id=1, source_target_pairs={{0,28},{2,30},{4,24},{6,26},{8,20},{10,22},{12,16},{14,18},{16,12}... | collective-permute-start | bytes 196616 | tf_op jit(solution)/shard_map/ppermute | solution.py:195
  56.8 9.4 %collective-permute-start.13 = (f32[128,128]{1,0:T(8,128)}, f32[128,128]{1,0:T(8,128)S(1)}, u32[]{:S(2)}, u32[]{:S(2)}) collective-permute-start(f32[128,128]{1,0:T(8,128)} %get-tuple-element.54), channel_id=1, source_target_pairs={{0,2},{2,0},{4,6},{6,4},{8,10},{10,8},{12,14},{14,12},{16,18},{18,... | collective-permute-start | bytes 196616 | tf_op jit(solution)/shard_map/ppermute | solution.py:195
  56.8 9.4 %collective-permute-start.14 = (f32[128,128]{1,0:T(8,128)}, f32[128,128]{1,0:T(8,128)S(1)}, u32[]{:S(2)}, u32[]{:S(2)}) collective-permute-start(f32[128,128]{1,0:T(8,128)} %get-tuple-element.55), channel_id=1, source_target_pairs={{0,30},{2,28},{4,26},{6,24},{8,22},{10,20},{12,18},{14,16},{16,14}... | collective-permute-start | bytes 196616 | tf_op jit(solution)/shard_map/ppermute | solution.py:195
  58.8 1.0 copy-start
  74.6 6.9 %collective-permute-start.15 = (f32[128,128]{1,0:T(8,128)S(1)}, f32[128,128]{1,0:T(8,128)S(1)}, u32[]{:S(2)}, u32[]{:S(2)}) collective-permute-start(f32[128,128]{1,0:T(8,128)S(1)} %get-tuple-element.60), channel_id=1, source_target_pairs={{0,16},{2,18},{4,20},{6,22},{8,24},{10,26},{12,28},{14,30},{16,0},... | collective-permute-start | bytes 196616 | tf_op jit(solution)/shard_map/ppermute | solution.py:195
  74.7 7.7 %collective-permute-start.16 = (f32[128,128]{1,0:T(8,128)S(1)}, f32[128,128]{1,0:T(8,128)S(1)}, u32[]{:S(2)}, u32[]{:S(2)}) collective-permute-start(f32[128,128]{1,0:T(8,128)S(1)} %get-tuple-element.61), channel_id=1, source_target_pairs={{0,14},{2,12},{4,10},{6,8},{8,6},{10,4},{12,2},{14,0},{16,30},{18,... | collective-permute-start | bytes 196616 | tf_op jit(solution)/shard_map/ppermute | solution.py:195
  77.4 6.8 %collective-permute-start.17 = (f32[128,128]{1,0:T(8,128)S(1)}, f32[128,128]{1,0:T(8,128)S(1)}, u32[]{:S(2)}, u32[]{:S(2)}) collective-permute-start(f32[128,128]{1,0:T(8,128)S(1)} %get-tuple-element.62), channel_id=1, source_target_pairs={{0,18},{2,16},{4,22},{6,20},{8,26},{10,24},{12,30},{14,28},{16,2},... | collective-permute-start | bytes 196616 | tf_op jit(solution)/shard_map/ppermute | solution.py:195
  78.0 7.9 %collective-permute-start.18 = (f32[128,128]{1,0:T(8,128)S(1)}, f32[128,128]{1,0:T(8,128)S(1)}, u32[]{:S(2)}, u32[]{:S(2)}) collective-permute-start(f32[128,128]{1,0:T(8,128)S(1)} %get-tuple-element.63), channel_id=1, source_target_pairs={{0,12},{2,14},{4,8},{6,10},{8,4},{10,6},{12,0},{14,2},{16,28},{18,... | collective-permute-start | bytes 196616 | tf_op jit(solution)/shard_map/ppermute | solution.py:195
  80.3 7.4 %collective-permute-start.19 = (f32[128,128]{1,0:T(8,128)S(1)}, f32[128,128]{1,0:T(8,128)S(1)}, u32[]{:S(2)}, u32[]{:S(2)}) collective-permute-start(f32[128,128]{1,0:T(8,128)S(1)} %get-tuple-element.64), channel_id=1, source_target_pairs={{0,20},{2,22},{4,16},{6,18},{8,28},{10,30},{12,24},{14,26},{16,4},... | collective-permute-start | bytes 196616 | tf_op jit(solution)/shard_map/ppermute | solution.py:195
  81.5 6.2 %collective-permute-start.20 = (f32[128,128]{1,0:T(8,128)S(1)}, f32[128,128]{1,0:T(8,128)S(1)}, u32[]{:S(2)}, u32[]{:S(2)}) collective-permute-start(f32[128,128]{1,0:T(8,128)S(1)} %get-tuple-element.65), channel_id=1, source_target_pairs={{0,10},{2,8},{4,14},{6,12},{8,2},{10,0},{12,6},{14,4},{16,26},{18,... | collective-permute-start | bytes 196616 | tf_op jit(solution)/shard_map/ppermute | solution.py:195
  82.5 10.2 %collective-permute-start.21 = (f32[128,128]{1,0:T(8,128)S(1)}, f32[128,128]{1,0:T(8,128)S(1)}, u32[]{:S(2)}, u32[]{:S(2)}) collective-permute-start(f32[128,128]{1,0:T(8,128)S(1)} %get-tuple-element.66), channel_id=1, source_target_pairs={{0,22},{2,20},{4,18},{6,16},{8,30},{10,28},{12,26},{14,24},{16,6},... | collective-permute-start | bytes 196616 | tf_op jit(solution)/shard_map/ppermute | solution.py:195
  84.3 8.4 %collective-permute-start.22 = (f32[128,128]{1,0:T(8,128)S(1)}, f32[128,128]{1,0:T(8,128)S(1)}, u32[]{:S(2)}, u32[]{:S(2)}) collective-permute-start(f32[128,128]{1,0:T(8,128)S(1)} %get-tuple-element.67), channel_id=1, source_target_pairs={{0,8},{2,10},{4,12},{6,14},{8,0},{10,2},{12,4},{14,6},{16,24},{18,... | collective-permute-start | bytes 196616 | tf_op jit(solution)/shard_map/ppermute | solution.py:195
  85.9 8.8 %collective-permute-start.23 = (f32[128,128]{1,0:T(8,128)S(1)}, f32[128,128]{1,0:T(8,128)S(1)}, u32[]{:S(2)}, u32[]{:S(2)}) collective-permute-start(f32[128,128]{1,0:T(8,128)S(1)} %get-tuple-element.68), channel_id=1, source_target_pairs={{0,24},{2,26},{4,28},{6,30},{8,16},{10,18},{12,20},{14,22},{16,8},... | collective-permute-start | bytes 196616 | tf_op jit(solution)/shard_map/ppermute | solution.py:195
  87.7 7.2 %collective-permute-start.24 = (f32[128,128]{1,0:T(8,128)S(1)}, f32[128,128]{1,0:T(8,128)S(1)}, u32[]{:S(2)}, u32[]{:S(2)}) collective-permute-start(f32[128,128]{1,0:T(8,128)S(1)} %get-tuple-element.69), channel_id=1, source_target_pairs={{0,6},{2,4},{4,2},{6,0},{8,14},{10,12},{12,10},{14,8},{16,22},{18,... | collective-permute-start | bytes 196616 | tf_op jit(solution)/shard_map/ppermute | solution.py:195
  87.7 9.9 %collective-permute-start.25 = (f32[128,128]{1,0:T(8,128)S(1)}, f32[128,128]{1,0:T(8,128)S(1)}, u32[]{:S(2)}, u32[]{:S(2)}) collective-permute-start(f32[128,128]{1,0:T(8,128)S(1)} %get-tuple-element.70), channel_id=1, source_target_pairs={{0,26},{2,24},{4,30},{6,28},{8,18},{10,16},{12,22},{14,20},{16,10}... | collective-permute-start | bytes 196616 | tf_op jit(solution)/shard_map/ppermute | solution.py:195
  92.6 4.9 %collective-permute-start.26 = (f32[128,128]{1,0:T(8,128)S(1)}, f32[128,128]{1,0:T(8,128)S(1)}, u32[]{:S(2)}, u32[]{:S(2)}) collective-permute-start(f32[128,128]{1,0:T(8,128)S(1)} %get-tuple-element.71), channel_id=1, source_target_pairs={{0,4},{2,6},{4,0},{6,2},{8,12},{10,14},{12,8},{14,10},{16,20},{18,... | collective-permute-start | bytes 196616 | tf_op jit(solution)/shard_map/ppermute | solution.py:195
  92.6 7.0 %collective-permute-start.27 = (f32[128,128]{1,0:T(8,128)S(1)}, f32[128,128]{1,0:T(8,128)S(1)}, u32[]{:S(2)}, u32[]{:S(2)}) collective-permute-start(f32[128,128]{1,0:T(8,128)S(1)} %get-tuple-element.72), channel_id=1, source_target_pairs={{0,28},{2,30},{4,24},{6,26},{8,20},{10,22},{12,16},{14,18},{16,12}... | collective-permute-start | bytes 196616 | tf_op jit(solution)/shard_map/ppermute | solution.py:195
  94.6 5.0 %collective-permute-start.28 = (f32[128,128]{1,0:T(8,128)S(1)}, f32[128,128]{1,0:T(8,128)S(1)}, u32[]{:S(2)}, u32[]{:S(2)}) collective-permute-start(f32[128,128]{1,0:T(8,128)S(1)} %get-tuple-element.73), channel_id=1, source_target_pairs={{0,2},{2,0},{4,6},{6,4},{8,10},{10,8},{12,14},{14,12},{16,18},{18,... | collective-permute-start | bytes 196616 | tf_op jit(solution)/shard_map/ppermute | solution.py:195
  94.9 6.7 %collective-permute-start.29 = (f32[128,128]{1,0:T(8,128)S(1)}, f32[128,128]{1,0:T(8,128)S(1)}, u32[]{:S(2)}, u32[]{:S(2)}) collective-permute-start(f32[128,128]{1,0:T(8,128)S(1)} %get-tuple-element.74), channel_id=1, source_target_pairs={{0,30},{2,28},{4,26},{6,24},{8,22},{10,20},{12,18},{14,16},{16,14}... | collective-permute-start | bytes 196616 | tf_op jit(solution)/shard_map/ppermute | solution.py:195
  (3 other events, 2.4 us)

commit v6 on v5

--- a/solution.py
+++ b/solution.py
@@ -16,6 +16,7 @@
 PHASE_BITS = 12
 LANES = 128
 PACKED = 16
+EARLY = 5
 PAIRED = Layout(major_to_minor=(1, 0, 2))
 
 
@@ -25,42 +26,83 @@
     return high, low
 
 
-def tables_kernel(spect, narrow, order_ref, pair_ref, angle_ref, place_ref, re_ref, im_ref, high_ref, low_ref, turn_ref):
-    layer = pl.program_id(0)
-
-    t = lax.broadcasted_iota(jnp.int32, (LOW, LOW), 1)
-    source = jnp.zeros((LOW, LOW), jnp.int32)
-    for bit in range(LOW_BITS):
-        source = source + lax.shift_left((t >> bit) & 1, jnp.full((LOW, LOW), order_ref[layer, bit], jnp.int32))
-    hot = jnp.where(lax.broadcasted_iota(jnp.int32, (LOW, LOW), 0) == source, 1.0, 0.0).astype(jnp.bfloat16)
-    contract = (((1,), (1,)), ((), ()))
-    for part, gate in enumerate((re_ref[0], im_ref[0])):
-        for out_ref, piece in zip((high_ref, low_ref), split(gate)):
-            for e in range(2):
-                moved = lax.dot_general(
-                    hot[:, e * GATE : (e + 1) * GATE], piece, contract, preferred_element_type=jnp.float32
-                ).astype(jnp.bfloat16)
-                lanes = slice(e * GATE, (e + 1) * GATE)
-                shifted = slice(LOW + e * GATE, LOW + (e + 1) * GATE)
-                if part == 0:
-                    out_ref[0, :LOW, lanes] = moved
-                    out_ref[0, LOW:, shifted] = moved
-                else:
-                    out_ref[0, :LOW, shifted] = moved
-                    out_ref[0, LOW:, lanes] = -moved
+def exchange_order(wide):
+    far = list(range(wide // 2, wide, 2))
+    near = [k for top in (wide // 4, wide // 8) for k in range(top, 2 * top, 2) if top > 1]
+    near += [k for k in range(wide // 2 - 2, 0, -2) if k not in near]
+    pairs = []
+    for i, k in enumerate(far):
+        pairs += [k] + near[i : i + 1] * (i < len(near) - 1)
+    pairs += near[-1:]
+    return [0] + [k + j for k in pairs for j in range(2)] + [1]
+
+
+def block_of(ref, k, wide):
+    rows = ref.shape[0] // wide
+    start = (lax.axis_index("wide") ^ k) * rows
+    return ref.at[pl.ds(pl.multiple_of(start, rows), rows)]
+
+
+def pick_kernel(wide, ks, x_hbm, *rest):
+    sends, sem = rest[:-1], rest[-1]
+    copies = [pltpu.make_async_copy(block_of(x_hbm, k, wide), sends[i], sem.at[i]) for i, k in enumerate(ks)]
+    for copy in copies:
+        copy.start()
+    for copy in copies:
+        copy.wait()
+
+
+def tables_kernel(wide, ks, spect, narrow, x_hbm, re_hbm, im_hbm, order_ref, pair_ref, angle_ref, *rest):
+    sends = rest[: len(ks)]
+    high_ref, low_ref, turn_ref, gates, block_sem, gate_sem = rest[len(ks) :]
+    copies = [pltpu.make_async_copy(block_of(x_hbm, k, wide), sends[i], block_sem.at[i]) for i, k in enumerate(ks)]
+    gate_copies = [
+        pltpu.make_async_copy(hbm, gates.at[part], gate_sem.at[part]) for part, hbm in enumerate((re_hbm, im_hbm))
+    ]
+    for copy in gate_copies + copies:
+        copy.start()
 
     row = lax.broadcasted_iota(jnp.int32, (spect, LOW), 0)
     lane = lax.broadcasted_iota(jnp.int32, (spect, LOW), 1)
-    r = place_ref[0] * (spect // narrow) + row // narrow
-    b = jnp.where(layer % 2 == 0, jnp.full((spect, LOW), place_ref[1], jnp.int32), row % narrow)
-    u = ((r * narrow + b) * LOW + lane) & (2**PHASE_BITS - 1)
-    phase = jnp.zeros((spect, LOW), jnp.float32)
-    for gate in range(PHASES):
-        first = u >> jnp.full((spect, LOW), pair_ref[layer, 2 * gate], jnp.int32)
-        second = u >> jnp.full((spect, LOW), pair_ref[layer, 2 * gate + 1], jnp.int32)
-        phase = phase + jnp.where((first & second & 1) == 1, angle_ref[layer, gate], 0.0)
-    turn_ref[0, 0] = jnp.cos(phase)
-    turn_ref[0, 1] = jnp.sin(phase)
+    r = lax.axis_index("wide") * (spect // narrow) + row // narrow
+    for layer in range(LAYERS):
+        b = lax.axis_index("narrow") if layer % 2 == 0 else row % narrow
+        u = ((r * narrow + b) * LOW + lane) & (2**PHASE_BITS - 1)
+        phase = jnp.zeros((spect, LOW), jnp.float32)
+        for gate in range(PHASES):
+            first = u >> jnp.full((spect, LOW), pair_ref[layer, 0, gate], jnp.int32)
+            second = u >> jnp.full((spect, LOW), pair_ref[layer, 1, gate], jnp.int32)
+            phase = phase + jnp.where((first & second & 1) == 1, angle_ref[layer, gate], 0.0)
+        turn_ref[layer, 0] = jnp.cos(phase)
+        turn_ref[layer, 1] = jnp.sin(phase)
+
+    for copy in gate_copies:
+        copy.wait()
+    t = lax.broadcasted_iota(jnp.int32, (8, LOW), 1)
+    position = lax.broadcasted_iota(jnp.int32, (LOW // 8, 8, LOW), 0) * 8
+    position = position + lax.broadcasted_iota(jnp.int32, (LOW // 8, 8, LOW), 1)
+    contract = (((1,), (1,)), ((), ()))
+    for layer in range(LAYERS):
+        source = jnp.zeros((8, LOW), jnp.int32)
+        for bit in range(LOW_BITS):
+            source = source + (((t >> bit) & 1) << jnp.full((8, LOW), order_ref[layer, bit], jnp.int32))
+        hot = jnp.where(position == source[None], 1.0, 0.0).reshape(LOW, LOW).astype(jnp.bfloat16)
+        for part in range(2):
+            for out_ref, piece in zip((high_ref, low_ref), split(gates[part, layer])):
+                for e in range(2):
+                    moved = lax.dot_general(
+                        hot[:, e * GATE : (e + 1) * GATE], piece, contract, preferred_element_type=jnp.float32
+                    ).astype(jnp.bfloat16)
+                    lanes = slice(e * GATE, (e + 1) * GATE)
+                    shifted = slice(LOW + e * GATE, LOW + (e + 1) * GATE)
+                    if part == 0:
+                        out_ref[layer, :LOW, lanes] = moved
+                        out_ref[layer, LOW:, shifted] = moved
+                    else:
+                        out_ref[layer, :LOW, shifted] = moved
+                        out_ref[layer, LOW:, lanes] = -moved
+    for copy in copies:
+        copy.wait()
 
 
 def exchange_modes(rows, span):
@@ -85,33 +127,10 @@
     return rows
 
 
-def exchange_order(wide):
-    order = [0]
-    for far, near in zip(range(wide // 2, wide), list(range(wide // 2 - 1, 0, -1)) + [None]):
-        order += [far] if near is None else [far, near]
-    return order
-
-
-def pick_kernel(wide, x_hbm, *rest):
-    sends, sem = rest[:-1], rest[-1]
-    me = lax.axis_index("wide")
-    block = x_hbm.shape[0] // wide
-    copies = [
-        pltpu.make_async_copy(x_hbm.at[pl.ds((me ^ k) * block, block)], sends[i], sem.at[i])
-        for i, k in enumerate(exchange_order(wide))
-    ]
-    for copy in copies:
-        copy.start()
-    for copy in copies:
-        copy.wait()
-
-
 def place_kernel(wide, *rest):
     blocks, out_hbm, sem = rest[:wide], rest[wide], rest[wide + 1]
-    me = lax.axis_index("wide")
-    block = blocks[0].shape[0]
     copies = [
-        pltpu.make_async_copy(blocks[i], out_hbm.at[pl.ds((me ^ k) * block, block)], sem.at[i])
+        pltpu.make_async_copy(blocks[i], block_of(out_hbm, k, wide), sem.at[i])
         for i, k in enumerate(exchange_order(wide))
     ]
     for copy in copies:
@@ -186,46 +205,50 @@
 
     view = with_layout_constraint(state.reshape(2, amps // LANES, LANES), PAIRED)
     rows = view.transpose(1, 0, 2).reshape(2 * amps // LANES, LANES)
-    anywhere = pl.BlockSpec(memory_space=pl.ANY)
+    in_hbm = pl.BlockSpec(memory_space=pltpu.HBM)
+    in_vmem = pl.BlockSpec(memory_space=pltpu.VMEM)
+    in_smem = pl.BlockSpec(memory_space=pltpu.SMEM)
     piece = jax.ShapeDtypeStruct((4 * spect, LANES), jnp.float32)
     part_of_vmem = pltpu.CompilerParams(vmem_limit_bytes=24 * 2**20)
-
-    def swap(blocks):
-        arrived = [
-            lax.ppermute(block, "wide", [(i, i ^ k) for i in range(wide)])
-            for block, k in zip(blocks[1:], exchange_order(wide)[1:])
+    order = exchange_order(wide)
+    early, late = order[1 : 1 + EARLY], order[1 + EARLY :] + order[:1]
+
+    def swap(blocks, ks):
+        return [
+            lax.ppermute(block, "wide", [(i, i ^ k) for i in range(wide)]) if k else block
+            for block, k in zip(blocks, ks)
         ]
-        return [blocks[0]] + arrived
 
     sends = pl.pallas_call(
-        partial(pick_kernel, wide),
-        in_specs=[anywhere],
-        out_specs=[anywhere] * wide,
-        out_shape=[piece] * wide,
-        scratch_shapes=[pltpu.SemaphoreType.DMA((wide,))],
-        compiler_params=pltpu.CompilerParams(vmem_limit_bytes=60 * 2**20),
+        partial(pick_kernel, wide, early),
+        in_specs=[in_hbm],
+        out_specs=[in_vmem] * len(early),
+        out_shape=[piece] * len(early),
+        scratch_shapes=[pltpu.SemaphoreType.DMA((len(early),))],
+        compiler_params=part_of_vmem,
         name="pick",
     )(rows)
-    received = swap(sends)
-
-    place = jnp.stack([lax.axis_index("wide"), lax.axis_index("narrow")]).astype(jnp.int32)
-    smem = pl.BlockSpec(memory_space=pltpu.SMEM)
-    gate_spec = pl.BlockSpec((1, GATE, GATE), lambda l: (l, 0, 0))
-    square_spec = pl.BlockSpec((1, 2 * LOW, 2 * LOW), lambda l: (l, 0, 0))
-    turn_spec = pl.BlockSpec((1, 2, spect, LOW), lambda l: (l, 0, 0, 0))
+    received = swap(sends, early)
+
     square = jax.ShapeDtypeStruct((LAYERS, 2 * LOW, 2 * LOW), jnp.bfloat16)
-    high, low, turn = pl.pallas_call(
-        partial(tables_kernel, spect, narrow),
-        grid=(LAYERS,),
-        in_specs=[smem, smem, smem, smem, gate_spec, gate_spec],
-        out_specs=[square_spec, square_spec, turn_spec],
-        out_shape=[square, square, jax.ShapeDtypeStruct((LAYERS, 2, spect, LOW), jnp.float32)],
+    *sends, high, low, turn = pl.pallas_call(
+        partial(tables_kernel, wide, late, spect, narrow),
+        in_specs=[in_hbm, in_hbm, in_hbm, in_smem, in_smem, in_smem],
+        out_specs=[in_vmem] * (len(late) + 3),
+        out_shape=[piece] * len(late)
+        + [square, square, jax.ShapeDtypeStruct((LAYERS, 2, spect, LOW), jnp.float32)],
+        scratch_shapes=[
+            pltpu.VMEM((2,) + gate_re.shape, jnp.float32),
+            pltpu.SemaphoreType.DMA((len(late),)),
+            pltpu.SemaphoreType.DMA((2,)),
+        ],
         compiler_params=part_of_vmem,
         cost_estimate=pl.CostEstimate(flops=10**9, bytes_accessed=8 * 10**6, transcendentals=10**5),
         name="tables",
-    )(bit_orders, phase_pairs.reshape(LAYERS, 2 * PHASES), phase_angles, place, gate_re, gate_im)
-
-    in_vmem = pl.BlockSpec(memory_space=pltpu.VMEM)
+    )(rows, gate_re, gate_im, bit_orders, phase_pairs.transpose(0, 2, 1), phase_angles)
+    received = received + swap(sends, late)
+    received = received[-1:] + received[:-1]
+
     done = pl.pallas_call(
         partial(layers_kernel, wide, spect),
         in_specs=[in_vmem] * (wide + 3),
@@ -243,13 +266,13 @@
 
     back = pl.pallas_call(
         partial(place_kernel, wide),
-        in_specs=[anywhere] * wide,
-        out_specs=anywhere,
+        in_specs=[in_vmem] * wide,
+        out_specs=in_hbm,
         out_shape=jax.ShapeDtypeStruct(rows.shape, jnp.float32),
         scratch_shapes=[pltpu.SemaphoreType.DMA((wide,))],
         compiler_params=part_of_vmem,
         name="place",
-    )(*swap(done))
+    )(*swap(done, order))
     view = with_layout_constraint(back.reshape(amps // LANES, 2, LANES).transpose(1, 0, 2), PAIRED)
     return view.reshape(2, amps)
 

time: 103 us -> 75.8 us (0.74)
  Pallas kernels: 46.5 us -> 14.8 us
  waiting for transfers between devices: 4.37 us -> 14.1 us
  starting transfers between devices: 47.4 us -> 41.2 us
  local copies, waits for them, and re-layouts: 4.23 us -> 5.28 us
    pallas_call x3, Pallas kernels: 38.1 us -> 6.47 us  [the longest x1 4.94 us: local(): pl.pallas_call(partial(tables_kernel, wide, late, spect, narrow), in_spec...]
    ppermute x30, waiting for transfers between devices: 4.37 us -> 14.1 us  [swap(): lax.ppermute(block, 'wide', [(i, i ^ k) for i in range(wide)])]
    ppermute x30, starting transfers between devices: 47.4 us -> 41.2 us  [swap(): lax.ppermute(block, 'wide', [(i, i ^ k) for i in range(wide)])]
    unnamed x11 -> x12, local copies, waits for them, and re-layouts: 4.15 us -> 5.28 us
  transfers between devices with their start and end apart: 30 -> 30, of which waited for: 3 -> 13; matrix products, arithmetic and copies ran while one was open for 1% -> 0% of each run, Pallas kernels for 4% -> 7%
where the time goes in v6:
time: 75.8 us; the launch traced here: 75.5 us
  starting transfers between devices  41.2 us (54%)
  Pallas kernels  14.8 us (20%)
  waiting for transfers between devices  14.1 us (19%)
  local copies, waits for them, and re-layouts  5.28 us (7%)
    ppermute x30, starting transfers between devices, swap(): lax.ppermute(block, 'wide', [(i, i ^ k) for i in range(wide)])  41.2 us
    ppermute x30, waiting for transfers between devices, swap(): lax.ppermute(block, 'wide', [(i, i ^ k) for i in range(wide)])  14.1 us
    pallas_call x1, Pallas kernels, local(): pl.pallas_call(partial(layers_kernel, wide, spect), in_specs=[in_vmem] *...  8.31 us
    unnamed x12, local copies, waits for them, and re-layouts  5.28 us
    pallas_call x1, Pallas kernels, local(): pl.pallas_call(partial(tables_kernel, wide, late, spect, narrow), in_spec...  4.94 us
  transfers between devices with their start and end apart: 30, of which 13 were waited for; matrix products, arithmetic and copies ran while one was open for 0% of the time, Pallas kernels for 7%

profile of v6, /device:TPU:0, one launch (start us, length us, event | category | flops | bytes accessed | tf_op | source)
XLA Modules:
  0.0 75.5 jit_solution(17616595157205490417)
XLA Ops:
  0.0 1.2 %copy-done = f32[2,131072]{1,0:T(2,128)S(1)} copy-done((f32[2,131072]{1,0:T(2,128)S(1)}, f32[2,131072]{1,0:T(2,128)}, u32[]{:S(2)}) %copy-start) | copy-done | bytes 1048600
  1.7 4.1 %collective-permute-start = (f32[128,128]{1,0:T(8,128)S(1)}, f32[128,128]{1,0:T(8,128)S(1)}, u32[]{:S(2)}, u32[]{:S(2)}) collective-permute-start(f32[128,128]{1,0:T(8,128)S(1)} %get-tuple-element.41), channel_id=1, source_target_pairs={{0,16},{2,18},{4,20},{6,22},{8,24},{10,26},{12,28},{14,30},{16,0},... | collective-permute-start | bytes 196616 | tf_op jit(solution)/shard_map/ppermute | solution.py:218
  5.8 1.6 %collective-permute-start.2 = (f32[128,128]{1,0:T(8,128)S(1)}, f32[128,128]{1,0:T(8,128)S(1)}, u32[]{:S(2)}, u32[]{:S(2)}) collective-permute-start(f32[128,128]{1,0:T(8,128)S(1)} %get-tuple-element.43), channel_id=1, source_target_pairs={{0,8},{2,10},{4,12},{6,14},{8,0},{10,2},{12,4},{14,6},{16,24},{18,... | collective-permute-start | bytes 196616 | tf_op jit(solution)/shard_map/ppermute | solution.py:218
  7.4 3.7 %collective-permute-start.4 = (f32[128,128]{1,0:T(8,128)S(1)}, f32[128,128]{1,0:T(8,128)S(1)}, u32[]{:S(2)}, u32[]{:S(2)}) collective-permute-start(f32[128,128]{1,0:T(8,128)S(1)} %get-tuple-element.45), channel_id=1, source_target_pairs={{0,20},{2,22},{4,16},{6,18},{8,28},{10,30},{12,24},{14,26},{16,4},... | collective-permute-start | bytes 196616 | tf_op jit(solution)/shard_map/ppermute | solution.py:218
  11.1 1.0 %copy-done.1 = f32[6,128,128]{2,1,0:T(8,128)S(1)} copy-done((f32[6,128,128]{2,1,0:T(8,128)S(1)}, f32[6,128,128]{2,1,0:T(8,128)}, u32[]{:S(2)}) %copy-start.1) | copy-done | bytes 393240
  12.1 1.0 %copy-done.2 = f32[6,128,128]{2,1,0:T(8,128)S(1)} copy-done((f32[6,128,128]{2,1,0:T(8,128)S(1)}, f32[6,128,128]{2,1,0:T(8,128)}, u32[]{:S(2)}) %copy-start.2) | copy-done | bytes 393240
  15.2 4.9 %tables.1 = (f32[128,128]{1,0:T(8,128)S(1)}, f32[128,128]{1,0:T(8,128)S(1)}, f32[128,128]{1,0:T(8,128)S(1)}, f32[128,128]{1,0:T(8,128)S(1)}, f32[128,128]{1,0:T(...) custom-call(f32[2048,128]{1,0:T(8,128)S(1)} %bitcast.12, ...), custom_call_target="tpu_custom_call" | custom-call | flops 1000000000 | bytes 8000000 | tf_op jit(solution)/shard_map/tables/pallas_call | solution.py:234
  20.2 2.5 %collective-permute-start.6 = (f32[128,128]{1,0:T(8,128)S(1)}, f32[128,128]{1,0:T(8,128)S(1)}, u32[]{:S(2)}, u32[]{:S(2)}) collective-permute-start(f32[128,128]{1,0:T(8,128)S(1)} %get-tuple-element.47), channel_id=1, source_target_pairs={{0,12},{2,14},{4,8},{6,10},{8,4},{10,6},{12,0},{14,2},{16,28},{18,... | collective-permute-start | bytes 196616 | tf_op jit(solution)/shard_map/ppermute | solution.py:218
  22.8 3.6 %collective-permute-start.8 = (f32[128,128]{1,0:T(8,128)S(1)}, f32[128,128]{1,0:T(8,128)S(1)}, u32[]{:S(2)}, u32[]{:S(2)}) collective-permute-start(f32[128,128]{1,0:T(8,128)S(1)} %get-tuple-element.49), channel_id=1, source_target_pairs={{0,24},{2,26},{4,28},{6,30},{8,16},{10,18},{12,20},{14,22},{16,8},... | collective-permute-start | bytes 196616 | tf_op jit(solution)/shard_map/ppermute | solution.py:218
  26.5 1.2 %collective-permute-done.5.rest_6_ = f32[128,128]{1,0:T(8,128)S(1)} collective-permute-done((f32[128,128]{1,0:T(8,128)S(1)}, f32[128,128]{1,0:T(8,128)S(1)}, u32[]{:S(2)}, u32[]{:S(2)}) %collective-permute-start.5) | collective-permute-done | bytes 65568 | tf_op jit(solution)/shard_map/ppermute | solution.py:218
  27.8 2.7 %collective-permute-start.10 = (f32[128,128]{1,0:T(8,128)S(1)}, f32[128,128]{1,0:T(8,128)S(1)}, u32[]{:S(2)}, u32[]{:S(2)}) collective-permute-start(f32[128,128]{1,0:T(8,128)S(1)} %get-tuple-element.51), channel_id=1, source_target_pairs={{0,28},{2,30},{4,24},{6,26},{8,20},{10,22},{12,16},{14,18},{16,12}... | collective-permute-start | bytes 196616 | tf_op jit(solution)/shard_map/ppermute | solution.py:218
  30.4 1.2 %collective-permute-start.11 = (f32[128,128]{1,0:T(8,128)S(1)}, f32[128,128]{1,0:T(8,128)S(1)}, u32[]{:S(2)}, u32[]{:S(2)}) collective-permute-start(f32[128,128]{1,0:T(8,128)S(1)} %get-tuple-element.52), channel_id=1, source_target_pairs={{0,30},{2,28},{4,26},{6,24},{8,22},{10,20},{12,18},{14,16},{16,14}... | collective-permute-start | bytes 196616 | tf_op jit(solution)/shard_map/ppermute | solution.py:218
  32.4 1.6 %collective-permute-start.13 = (f32[128,128]{1,0:T(8,128)S(1)}, f32[128,128]{1,0:T(8,128)S(1)}, u32[]{:S(2)}, u32[]{:S(2)}) collective-permute-start(f32[128,128]{1,0:T(8,128)S(1)} %get-tuple-element.54), channel_id=1, source_target_pairs={{0,6},{2,4},{4,2},{6,0},{8,14},{10,12},{12,10},{14,8},{16,22},{18,... | collective-permute-start | bytes 196616 | tf_op jit(solution)/shard_map/ppermute | solution.py:218
  34.8 2.2 %collective-permute-done.11.rest_12_ = f32[128,128]{1,0:T(8,128)S(1)} collective-permute-done((f32[128,128]{1,0:T(8,128)S(1)}, f32[128,128]{1,0:T(8,128)S(1)}, u32[]{:S(2)}, u32[]{:S(2)}) %collective-permute-start.11) | collective-permute-done | bytes 65568 | tf_op jit(solution)/shard_map/ppermute | solution.py:218
  37.0 0.9 %collective-permute-done.12.rest_13_ = f32[128,128]{1,0:T(8,128)S(1)} collective-permute-done((f32[128,128]{1,0:T(8,128)S(1)}, f32[128,128]{1,0:T(8,128)S(1)}, u32[]{:S(2)}, u32[]{:S(2)}) %collective-permute-start.12) | collective-permute-done | bytes 65568 | tf_op jit(solution)/shard_map/ppermute | solution.py:218
  37.9 1.5 %collective-permute-done.13.rest_14_ = f32[128,128]{1,0:T(8,128)S(1)} collective-permute-done((f32[128,128]{1,0:T(8,128)S(1)}, f32[128,128]{1,0:T(8,128)S(1)}, u32[]{:S(2)}, u32[]{:S(2)}) %collective-permute-start.13) | collective-permute-done | bytes 65568 | tf_op jit(solution)/shard_map/ppermute | solution.py:218
  39.4 8.3 %layers.1 = (f32[128,128]{1,0:T(8,128)S(1)}, f32[128,128]{1,0:T(8,128)S(1)}, f32[128,128]{1,0:T(8,128)S(1)}, f32[128,128]{1,0:T(8,128)S(1)}, f32[128,128]{1,0:T(...) custom-call(f32[128,128]{1,0:T(8,128)S(1)} %get-tuple-element.40.res, ...), custom_call_target="tpu_custom_call" | custom-call | flops 5000000000 | bytes 10000000 | tf_op jit(solution)/shard_map/layers/pallas_call | solution.py:252
  48.2 1.9 %collective-permute-start.16 = (f32[128,128]{1,0:T(8,128)S(1)}, f32[128,128]{1,0:T(8,128)S(1)}, u32[]{:S(2)}, u32[]{:S(2)}) collective-permute-start(f32[128,128]{1,0:T(8,128)S(1)} %get-tuple-element.61), channel_id=1, source_target_pairs={{0,18},{2,16},{4,22},{6,20},{8,26},{10,24},{12,30},{14,28},{16,2},... | collective-permute-start | bytes 196616 | tf_op jit(solution)/shard_map/ppermute | solution.py:218
  50.5 1.6 %collective-permute-start.18 = (f32[128,128]{1,0:T(8,128)S(1)}, f32[128,128]{1,0:T(8,128)S(1)}, u32[]{:S(2)}, u32[]{:S(2)}) collective-permute-start(f32[128,128]{1,0:T(8,128)S(1)} %get-tuple-element.63), channel_id=1, source_target_pairs={{0,10},{2,8},{4,14},{6,12},{8,2},{10,0},{12,6},{14,4},{16,26},{18,... | collective-permute-start | bytes 196616 | tf_op jit(solution)/shard_map/ppermute | solution.py:218
  52.1 1.8 %collective-permute-start.19 = (f32[128,128]{1,0:T(8,128)S(1)}, f32[128,128]{1,0:T(8,128)S(1)}, u32[]{:S(2)}, u32[]{:S(2)}) collective-permute-start(f32[128,128]{1,0:T(8,128)S(1)} %get-tuple-element.64), channel_id=1, source_target_pairs={{0,20},{2,22},{4,16},{6,18},{8,28},{10,30},{12,24},{14,26},{16,4},... | collective-permute-start | bytes 196616 | tf_op jit(solution)/shard_map/ppermute | solution.py:218
  53.9 1.8 %collective-permute-done.15.rest_1_ = f32[128,128]{1,0:T(8,128)S(1)} collective-permute-done((f32[128,128]{1,0:T(8,128)S(1)}, f32[128,128]{1,0:T(8,128)S(1)}, u32[]{:S(2)}, u32[]{:S(2)}) %collective-permute-start.15) | collective-permute-done | bytes 65568 | tf_op jit(solution)/shard_map/ppermute | solution.py:218
  55.7 1.0 %collective-permute-done.16.rest_2_ = f32[128,128]{1,0:T(8,128)S(1)} collective-permute-done((f32[128,128]{1,0:T(8,128)S(1)}, f32[128,128]{1,0:T(8,128)S(1)}, u32[]{:S(2)}, u32[]{:S(2)}) %collective-permute-start.16) | collective-permute-done | bytes 65568 | tf_op jit(solution)/shard_map/ppermute | solution.py:218
  56.7 1.6 %collective-permute-start.21 = (f32[128,128]{1,0:T(8,128)S(1)}, f32[128,128]{1,0:T(8,128)S(1)}, u32[]{:S(2)}, u32[]{:S(2)}) collective-permute-start(f32[128,128]{1,0:T(8,128)S(1)} %get-tuple-element.66), channel_id=1, source_target_pairs={{0,12},{2,14},{4,8},{6,10},{8,4},{10,6},{12,0},{14,2},{16,28},{18,... | collective-permute-start | bytes 196616 | tf_op jit(solution)/shard_map/ppermute | solution.py:218
  58.4 0.8 %collective-permute-start.22 = (f32[128,128]{1,0:T(8,128)S(1)}, f32[128,128]{1,0:T(8,128)S(1)}, u32[]{:S(2)}, u32[]{:S(2)}) collective-permute-start(f32[128,128]{1,0:T(8,128)S(1)} %get-tuple-element.67), channel_id=1, source_target_pairs={{0,14},{2,12},{4,10},{6,8},{8,6},{10,4},{12,2},{14,0},{16,30},{18,... | collective-permute-start | bytes 196616 | tf_op jit(solution)/shard_map/ppermute | solution.py:218
  59.3 1.7 %collective-permute-start.23 = (f32[128,128]{1,0:T(8,128)S(1)}, f32[128,128]{1,0:T(8,128)S(1)}, u32[]{:S(2)}, u32[]{:S(2)}) collective-permute-start(f32[128,128]{1,0:T(8,128)S(1)} %get-tuple-element.68), channel_id=1, source_target_pairs={{0,24},{2,26},{4,28},{6,30},{8,16},{10,18},{12,20},{14,22},{16,8},... | collective-permute-start | bytes 196616 | tf_op jit(solution)/shard_map/ppermute | solution.py:218
  61.0 1.9 %collective-permute-start.24 = (f32[128,128]{1,0:T(8,128)S(1)}, f32[128,128]{1,0:T(8,128)S(1)}, u32[]{:S(2)}, u32[]{:S(2)}) collective-permute-start(f32[128,128]{1,0:T(8,128)S(1)} %get-tuple-element.69), channel_id=1, source_target_pairs={{0,26},{2,24},{4,30},{6,28},{8,18},{10,16},{12,22},{14,20},{16,10}... | collective-permute-start | bytes 196616 | tf_op jit(solution)/shard_map/ppermute | solution.py:218
  63.1 2.2 %collective-permute-start.25 = (f32[128,128]{1,0:T(8,128)S(1)}, f32[128,128]{1,0:T(8,128)S(1)}, u32[]{:S(2)}, u32[]{:S(2)}) collective-permute-start(f32[128,128]{1,0:T(8,128)S(1)} %get-tuple-element.70), channel_id=1, source_target_pairs={{0,28},{2,30},{4,24},{6,26},{8,20},{10,22},{12,16},{14,18},{16,12}... | collective-permute-start | bytes 196616 | tf_op jit(solution)/shard_map/ppermute | solution.py:218
  65.3 2.6 %collective-permute-start.26 = (f32[128,128]{1,0:T(8,128)S(1)}, f32[128,128]{1,0:T(8,128)S(1)}, u32[]{:S(2)}, u32[]{:S(2)}) collective-permute-start(f32[128,128]{1,0:T(8,128)S(1)} %get-tuple-element.71), channel_id=1, source_target_pairs={{0,30},{2,28},{4,26},{6,24},{8,22},{10,20},{12,18},{14,16},{16,14}... | collective-permute-start | bytes 196616 | tf_op jit(solution)/shard_map/ppermute | solution.py:218
  67.9 1.4 %collective-permute-start.27 = (f32[128,128]{1,0:T(8,128)S(1)}, f32[128,128]{1,0:T(8,128)S(1)}, u32[]{:S(2)}, u32[]{:S(2)}) collective-permute-start(f32[128,128]{1,0:T(8,128)S(1)} %get-tuple-element.72), channel_id=1, source_target_pairs={{0,4},{2,6},{4,0},{6,2},{8,12},{10,14},{12,8},{14,10},{16,20},{18,... | collective-permute-start | bytes 196616 | tf_op jit(solution)/shard_map/ppermute | solution.py:218
  70.6 1.2 %collective-permute-done.26.rest_12_ = f32[128,128]{1,0:T(8,128)S(1)} collective-permute-done((f32[128,128]{1,0:T(8,128)S(1)}, f32[128,128]{1,0:T(8,128)S(1)}, u32[]{:S(2)}, u32[]{:S(2)}) %collective-permute-start.26) | collective-permute-done | bytes 65568 | tf_op jit(solution)/shard_map/ppermute | solution.py:218
  71.8 2.1 %collective-permute-done.27.rest_13_ = f32[128,128]{1,0:T(8,128)S(1)} collective-permute-done((f32[128,128]{1,0:T(8,128)S(1)}, f32[128,128]{1,0:T(8,128)S(1)}, u32[]{:S(2)}, u32[]{:S(2)}) %collective-permute-start.27) | collective-permute-done | bytes 65568 | tf_op jit(solution)/shard_map/ppermute | solution.py:218
  74.4 1.1 %place.1 = f32[2048,128]{1,0:T(8,128)} custom-call(f32[128,128]{1,0:T(8,128)S(1)} %get-tuple-element.59.rest_0_, f32[128,128]{1,0:T(8,128)S(1)} %collective-permute-done.15.rest_1_, f32[128,128]{1,0:T(8,128)S(1)} %collective-permute-done.16.rest_2_, f32[128,128]{1,0:T(8,128)S(1)} %collective-permute-done.17.rest_3_, ...), custom_call_target="tpu_custom_call" | custom-call | tf_op jit(solution)/shard_map/place/pallas_call | solution.py:267
  (44 shorter events, 7.7 us)
Async XLA Ops:
  0.0 1.2 %copy-start = (f32[2,131072]{1,0:T(2,128)S(1)}, f32[2,131072]{1,0:T(2,128)}, u32[]{:S(2)}) copy-start(f32[2,131072]{1,0:T(2,128)} %param.6) | copy-start | bytes 3145732
  1.7 18.5 %collective-permute-start = (f32[128,128]{1,0:T(8,128)S(1)}, f32[128,128]{1,0:T(8,128)S(1)}, u32[]{:S(2)}, u32[]{:S(2)}) collective-permute-start(f32[128,128]{1,0:T(8,128)S(1)} %get-tuple-element.41), channel_id=1, source_target_pairs={{0,16},{2,18},{4,20},{6,22},{8,24},{10,26},{12,28},{14,30},{16,0},... | collective-permute-start | bytes 196616 | tf_op jit(solution)/shard_map/ppermute | solution.py:218
  5.8 14.4 %collective-permute-start.1 = (f32[128,128]{1,0:T(8,128)S(1)}, f32[128,128]{1,0:T(8,128)S(1)}, u32[]{:S(2)}, u32[]{:S(2)}) collective-permute-start(f32[128,128]{1,0:T(8,128)S(1)} %get-tuple-element.42), channel_id=1, source_target_pairs={{0,18},{2,16},{4,22},{6,20},{8,26},{10,24},{12,30},{14,28},{16,2},... | collective-permute-start | bytes 196616 | tf_op jit(solution)/shard_map/ppermute | solution.py:218
  5.8 16.9 %collective-permute-start.2 = (f32[128,128]{1,0:T(8,128)S(1)}, f32[128,128]{1,0:T(8,128)S(1)}, u32[]{:S(2)}, u32[]{:S(2)}) collective-permute-start(f32[128,128]{1,0:T(8,128)S(1)} %get-tuple-element.43), channel_id=1, source_target_pairs={{0,8},{2,10},{4,12},{6,14},{8,0},{10,2},{12,4},{14,6},{16,24},{18,... | collective-permute-start | bytes 196616 | tf_op jit(solution)/shard_map/ppermute | solution.py:218
  7.4 15.5 %collective-permute-start.3 = (f32[128,128]{1,0:T(8,128)S(1)}, f32[128,128]{1,0:T(8,128)S(1)}, u32[]{:S(2)}, u32[]{:S(2)}) collective-permute-start(f32[128,128]{1,0:T(8,128)S(1)} %get-tuple-element.44), channel_id=1, source_target_pairs={{0,10},{2,8},{4,14},{6,12},{8,2},{10,0},{12,6},{14,4},{16,26},{18,... | collective-permute-start | bytes 196616 | tf_op jit(solution)/shard_map/ppermute | solution.py:218
  7.4 19.0 %collective-permute-start.4 = (f32[128,128]{1,0:T(8,128)S(1)}, f32[128,128]{1,0:T(8,128)S(1)}, u32[]{:S(2)}, u32[]{:S(2)}) collective-permute-start(f32[128,128]{1,0:T(8,128)S(1)} %get-tuple-element.45), channel_id=1, source_target_pairs={{0,20},{2,22},{4,16},{6,18},{8,28},{10,30},{12,24},{14,26},{16,4},... | collective-permute-start | bytes 196616 | tf_op jit(solution)/shard_map/ppermute | solution.py:218
  11.1 1.0 %copy-start.1 = (f32[6,128,128]{2,1,0:T(8,128)S(1)}, f32[6,128,128]{2,1,0:T(8,128)}, u32[]{:S(2)}) copy-start(f32[6,128,128]{2,1,0:T(8,128)} %re_hbm.1) | copy-start | bytes 1179652
  20.1 7.6 %collective-permute-start.5 = (f32[128,128]{1,0:T(8,128)S(1)}, f32[128,128]{1,0:T(8,128)S(1)}, u32[]{:S(2)}, u32[]{:S(2)}) collective-permute-start(f32[128,128]{1,0:T(8,128)S(1)} %get-tuple-element.46), channel_id=1, source_target_pairs={{0,22},{2,20},{4,18},{6,16},{8,30},{10,28},{12,26},{14,24},{16,6},... | collective-permute-start | bytes 196616 | tf_op jit(solution)/shard_map/ppermute | solution.py:218
  20.2 10.2 %collective-permute-start.6 = (f32[128,128]{1,0:T(8,128)S(1)}, f32[128,128]{1,0:T(8,128)S(1)}, u32[]{:S(2)}, u32[]{:S(2)}) collective-permute-start(f32[128,128]{1,0:T(8,128)S(1)} %get-tuple-element.47), channel_id=1, source_target_pairs={{0,12},{2,14},{4,8},{6,10},{8,4},{10,6},{12,0},{14,2},{16,28},{18,... | collective-permute-start | bytes 196616 | tf_op jit(solution)/shard_map/ppermute | solution.py:218
  22.7 8.9 %collective-permute-start.7 = (f32[128,128]{1,0:T(8,128)S(1)}, f32[128,128]{1,0:T(8,128)S(1)}, u32[]{:S(2)}, u32[]{:S(2)}) collective-permute-start(f32[128,128]{1,0:T(8,128)S(1)} %get-tuple-element.48), channel_id=1, source_target_pairs={{0,14},{2,12},{4,10},{6,8},{8,6},{10,4},{12,2},{14,0},{16,30},{18,... | collective-permute-start | bytes 196616 | tf_op jit(solution)/shard_map/ppermute | solution.py:218
  22.8 9.6 %collective-permute-start.8 = (f32[128,128]{1,0:T(8,128)S(1)}, f32[128,128]{1,0:T(8,128)S(1)}, u32[]{:S(2)}, u32[]{:S(2)}) collective-permute-start(f32[128,128]{1,0:T(8,128)S(1)} %get-tuple-element.49), channel_id=1, source_target_pairs={{0,24},{2,26},{4,28},{6,30},{8,16},{10,18},{12,20},{14,22},{16,8},... | collective-permute-start | bytes 196616 | tf_op jit(solution)/shard_map/ppermute | solution.py:218
  26.5 7.5 %collective-permute-start.9 = (f32[128,128]{1,0:T(8,128)S(1)}, f32[128,128]{1,0:T(8,128)S(1)}, u32[]{:S(2)}, u32[]{:S(2)}) collective-permute-start(f32[128,128]{1,0:T(8,128)S(1)} %get-tuple-element.50), channel_id=1, source_target_pairs={{0,26},{2,24},{4,30},{6,28},{8,18},{10,16},{12,22},{14,20},{16,10}... | collective-permute-start | bytes 196616 | tf_op jit(solution)/shard_map/ppermute | solution.py:218
  27.8 7.1 %collective-permute-start.10 = (f32[128,128]{1,0:T(8,128)S(1)}, f32[128,128]{1,0:T(8,128)S(1)}, u32[]{:S(2)}, u32[]{:S(2)}) collective-permute-start(f32[128,128]{1,0:T(8,128)S(1)} %get-tuple-element.51), channel_id=1, source_target_pairs={{0,28},{2,30},{4,24},{6,26},{8,20},{10,22},{12,16},{14,18},{16,12}... | collective-permute-start | bytes 196616 | tf_op jit(solution)/shard_map/ppermute | solution.py:218
  30.4 6.5 %collective-permute-start.11 = (f32[128,128]{1,0:T(8,128)S(1)}, f32[128,128]{1,0:T(8,128)S(1)}, u32[]{:S(2)}, u32[]{:S(2)}) collective-permute-start(f32[128,128]{1,0:T(8,128)S(1)} %get-tuple-element.52), channel_id=1, source_target_pairs={{0,30},{2,28},{4,26},{6,24},{8,22},{10,20},{12,18},{14,16},{16,14}... | collective-permute-start | bytes 196616 | tf_op jit(solution)/shard_map/ppermute | solution.py:218
  31.6 6.3 %collective-permute-start.12 = (f32[128,128]{1,0:T(8,128)S(1)}, f32[128,128]{1,0:T(8,128)S(1)}, u32[]{:S(2)}, u32[]{:S(2)}) collective-permute-start(f32[128,128]{1,0:T(8,128)S(1)} %get-tuple-element.53), channel_id=1, source_target_pairs={{0,4},{2,6},{4,0},{6,2},{8,12},{10,14},{12,8},{14,10},{16,20},{18,... | collective-permute-start | bytes 196616 | tf_op jit(solution)/shard_map/ppermute | solution.py:218
  32.4 7.0 %collective-permute-start.13 = (f32[128,128]{1,0:T(8,128)S(1)}, f32[128,128]{1,0:T(8,128)S(1)}, u32[]{:S(2)}, u32[]{:S(2)}) collective-permute-start(f32[128,128]{1,0:T(8,128)S(1)} %get-tuple-element.54), channel_id=1, source_target_pairs={{0,6},{2,4},{4,2},{6,0},{8,14},{10,12},{12,10},{14,8},{16,22},{18,... | collective-permute-start | bytes 196616 | tf_op jit(solution)/shard_map/ppermute | solution.py:218
  34.0 5.4 %collective-permute-start.14 = (f32[128,128]{1,0:T(8,128)S(1)}, f32[128,128]{1,0:T(8,128)S(1)}, u32[]{:S(2)}, u32[]{:S(2)}) collective-permute-start(f32[128,128]{1,0:T(8,128)S(1)} %get-tuple-element.55), channel_id=1, source_target_pairs={{0,2},{2,0},{4,6},{6,4},{8,10},{10,8},{12,14},{14,12},{16,18},{18,... | collective-permute-start | bytes 196616 | tf_op jit(solution)/shard_map/ppermute | solution.py:218
  47.7 8.1 %collective-permute-start.15 = (f32[128,128]{1,0:T(8,128)S(1)}, f32[128,128]{1,0:T(8,128)S(1)}, u32[]{:S(2)}, u32[]{:S(2)}) collective-permute-start(f32[128,128]{1,0:T(8,128)S(1)} %get-tuple-element.60), channel_id=1, source_target_pairs={{0,16},{2,18},{4,20},{6,22},{8,24},{10,26},{12,28},{14,30},{16,0},... | collective-permute-start | bytes 196616 | tf_op jit(solution)/shard_map/ppermute | solution.py:218
  48.2 8.6 %collective-permute-start.16 = (f32[128,128]{1,0:T(8,128)S(1)}, f32[128,128]{1,0:T(8,128)S(1)}, u32[]{:S(2)}, u32[]{:S(2)}) collective-permute-start(f32[128,128]{1,0:T(8,128)S(1)} %get-tuple-element.61), channel_id=1, source_target_pairs={{0,18},{2,16},{4,22},{6,20},{8,26},{10,24},{12,30},{14,28},{16,2},... | collective-permute-start | bytes 196616 | tf_op jit(solution)/shard_map/ppermute | solution.py:218
  50.0 8.3 %collective-permute-start.17 = (f32[128,128]{1,0:T(8,128)S(1)}, f32[128,128]{1,0:T(8,128)S(1)}, u32[]{:S(2)}, u32[]{:S(2)}) collective-permute-start(f32[128,128]{1,0:T(8,128)S(1)} %get-tuple-element.62), channel_id=1, source_target_pairs={{0,8},{2,10},{4,12},{6,14},{8,0},{10,2},{12,4},{14,6},{16,24},{18,... | collective-permute-start | bytes 196616 | tf_op jit(solution)/shard_map/ppermute | solution.py:218
  50.5 8.8 %collective-permute-start.18 = (f32[128,128]{1,0:T(8,128)S(1)}, f32[128,128]{1,0:T(8,128)S(1)}, u32[]{:S(2)}, u32[]{:S(2)}) collective-permute-start(f32[128,128]{1,0:T(8,128)S(1)} %get-tuple-element.63), channel_id=1, source_target_pairs={{0,10},{2,8},{4,14},{6,12},{8,2},{10,0},{12,6},{14,4},{16,26},{18,... | collective-permute-start | bytes 196616 | tf_op jit(solution)/shard_map/ppermute | solution.py:218
  52.1 8.9 %collective-permute-start.19 = (f32[128,128]{1,0:T(8,128)S(1)}, f32[128,128]{1,0:T(8,128)S(1)}, u32[]{:S(2)}, u32[]{:S(2)}) collective-permute-start(f32[128,128]{1,0:T(8,128)S(1)} %get-tuple-element.64), channel_id=1, source_target_pairs={{0,20},{2,22},{4,16},{6,18},{8,28},{10,30},{12,24},{14,26},{16,4},... | collective-permute-start | bytes 196616 | tf_op jit(solution)/shard_map/ppermute | solution.py:218
  55.7 7.4 %collective-permute-start.20 = (f32[128,128]{1,0:T(8,128)S(1)}, f32[128,128]{1,0:T(8,128)S(1)}, u32[]{:S(2)}, u32[]{:S(2)}) collective-permute-start(f32[128,128]{1,0:T(8,128)S(1)} %get-tuple-element.65), channel_id=1, source_target_pairs={{0,22},{2,20},{4,18},{6,16},{8,30},{10,28},{12,26},{14,24},{16,6},... | collective-permute-start | bytes 196616 | tf_op jit(solution)/shard_map/ppermute | solution.py:218
  56.7 8.6 %collective-permute-start.21 = (f32[128,128]{1,0:T(8,128)S(1)}, f32[128,128]{1,0:T(8,128)S(1)}, u32[]{:S(2)}, u32[]{:S(2)}) collective-permute-start(f32[128,128]{1,0:T(8,128)S(1)} %get-tuple-element.66), channel_id=1, source_target_pairs={{0,12},{2,14},{4,8},{6,10},{8,4},{10,6},{12,0},{14,2},{16,28},{18,... | collective-permute-start | bytes 196616 | tf_op jit(solution)/shard_map/ppermute | solution.py:218
  58.4 9.5 %collective-permute-start.22 = (f32[128,128]{1,0:T(8,128)S(1)}, f32[128,128]{1,0:T(8,128)S(1)}, u32[]{:S(2)}, u32[]{:S(2)}) collective-permute-start(f32[128,128]{1,0:T(8,128)S(1)} %get-tuple-element.67), channel_id=1, source_target_pairs={{0,14},{2,12},{4,10},{6,8},{8,6},{10,4},{12,2},{14,0},{16,30},{18,... | collective-permute-start | bytes 196616 | tf_op jit(solution)/shard_map/ppermute | solution.py:218
  59.3 10.0 %collective-permute-start.23 = (f32[128,128]{1,0:T(8,128)S(1)}, f32[128,128]{1,0:T(8,128)S(1)}, u32[]{:S(2)}, u32[]{:S(2)}) collective-permute-start(f32[128,128]{1,0:T(8,128)S(1)} %get-tuple-element.68), channel_id=1, source_target_pairs={{0,24},{2,26},{4,28},{6,30},{8,16},{10,18},{12,20},{14,22},{16,8},... | collective-permute-start | bytes 196616 | tf_op jit(solution)/shard_map/ppermute | solution.py:218
  61.0 8.3 %collective-permute-start.24 = (f32[128,128]{1,0:T(8,128)S(1)}, f32[128,128]{1,0:T(8,128)S(1)}, u32[]{:S(2)}, u32[]{:S(2)}) collective-permute-start(f32[128,128]{1,0:T(8,128)S(1)} %get-tuple-element.69), channel_id=1, source_target_pairs={{0,26},{2,24},{4,30},{6,28},{8,18},{10,16},{12,22},{14,20},{16,10}... | collective-permute-start | bytes 196616 | tf_op jit(solution)/shard_map/ppermute | solution.py:218
  63.1 7.5 %collective-permute-start.25 = (f32[128,128]{1,0:T(8,128)S(1)}, f32[128,128]{1,0:T(8,128)S(1)}, u32[]{:S(2)}, u32[]{:S(2)}) collective-permute-start(f32[128,128]{1,0:T(8,128)S(1)} %get-tuple-element.70), channel_id=1, source_target_pairs={{0,28},{2,30},{4,24},{6,26},{8,20},{10,22},{12,16},{14,18},{16,12}... | collective-permute-start | bytes 196616 | tf_op jit(solution)/shard_map/ppermute | solution.py:218
  65.3 6.5 %collective-permute-start.26 = (f32[128,128]{1,0:T(8,128)S(1)}, f32[128,128]{1,0:T(8,128)S(1)}, u32[]{:S(2)}, u32[]{:S(2)}) collective-permute-start(f32[128,128]{1,0:T(8,128)S(1)} %get-tuple-element.71), channel_id=1, source_target_pairs={{0,30},{2,28},{4,26},{6,24},{8,22},{10,20},{12,18},{14,16},{16,14}... | collective-permute-start | bytes 196616 | tf_op jit(solution)/shard_map/ppermute | solution.py:218
  67.9 6.0 %collective-permute-start.27 = (f32[128,128]{1,0:T(8,128)S(1)}, f32[128,128]{1,0:T(8,128)S(1)}, u32[]{:S(2)}, u32[]{:S(2)}) collective-permute-start(f32[128,128]{1,0:T(8,128)S(1)} %get-tuple-element.72), channel_id=1, source_target_pairs={{0,4},{2,6},{4,0},{6,2},{8,12},{10,14},{12,8},{14,10},{16,20},{18,... | collective-permute-start | bytes 196616 | tf_op jit(solution)/shard_map/ppermute | solution.py:218
  69.3 5.1 %collective-permute-start.28 = (f32[128,128]{1,0:T(8,128)S(1)}, f32[128,128]{1,0:T(8,128)S(1)}, u32[]{:S(2)}, u32[]{:S(2)}) collective-permute-start(f32[128,128]{1,0:T(8,128)S(1)} %get-tuple-element.73), channel_id=1, source_target_pairs={{0,6},{2,4},{4,2},{6,0},{8,14},{10,12},{12,10},{14,8},{16,22},{18,... | collective-permute-start | bytes 196616 | tf_op jit(solution)/shard_map/ppermute | solution.py:218
  69.3 5.0 %collective-permute-start.29 = (f32[128,128]{1,0:T(8,128)S(1)}, f32[128,128]{1,0:T(8,128)S(1)}, u32[]{:S(2)}, u32[]{:S(2)}) collective-permute-start(f32[128,128]{1,0:T(8,128)S(1)} %get-tuple-element.74), channel_id=1, source_target_pairs={{0,2},{2,0},{4,6},{6,4},{8,10},{10,8},{12,14},{14,12},{16,18},{18,... | collective-permute-start | bytes 196616 | tf_op jit(solution)/shard_map/ppermute | solution.py:218
  (4 other events, 3.1 us)

commit v7 on v6

v7 whole, which is shorter than its diff:
```python
from functools import partial

import jax
import jax.numpy as jnp
from jax import lax
from jax.experimental import pallas as pl
from jax.experimental.layout import Layout, with_layout_constraint
from jax.experimental.pallas import tpu as pltpu
from jax.sharding import PartitionSpec as P

LAYERS = 6
GATE = 128
LOW = 256
LOW_BITS = 8
PHASES = 16
PHASE_BITS = 12
LANES = 128
PACKED = 16
TILE = 128
PAIRED = Layout(major_to_minor=(1, 0, 2))


def split(x):
    high = x.astype(jnp.bfloat16)
    low = (x - high.astype(jnp.float32)).astype(jnp.bfloat16)
    return high, low


def exchange_order(wide):
    far = list(range(wide // 2, wide, 2))
    near = [k for top in (wide // 4, wide // 8) for k in range(top, 2 * top, 2) if top > 1]
    near += [k for k in range(wide // 2 - 2, 0, -2) if k not in near]
    pairs = []
    for i, k in enumerate(far):
        pairs += [k] + near[i : i + 1] * (i < len(near) - 1)
    pairs += near[-1:]
    return [0] + [k + j for k in pairs for j in range(2)] + [1]


def block_of(ref, k, wide):
    rows = ref.shape[0] // wide
    start = (lax.axis_index("wide") ^ k) * rows
    return ref.at[pl.ds(pl.multiple_of(start, rows), rows)]


def tables_kernel(spect, narrow, re_ref, im_ref, order_ref, pair_ref, angle_ref, gate_ref, turn_ref):
    row = lax.broadcasted_iota(jnp.int32, (spect, LOW), 0)
    lane = lax.broadcasted_iota(jnp.int32, (spect, LOW), 1)
    r = lax.axis_index("wide") * (spect // narrow) + row // narrow
    turn_ref[0, 0] = jnp.ones((spect, LOW), jnp.float32)
    turn_ref[0, 1] = jnp.zeros((spect, LOW), jnp.float32)
    for layer in range(LAYERS):
        b = lax.axis_index("narrow") if layer % 2 == 0 else row % narrow
        u = ((r * narrow + b) * LOW + lane) & (2**PHASE_BITS - 1)
        phase = jnp.zeros((spect, LOW), jnp.float32)
        for gate in range(PHASES):
            first = u >> jnp.full((spect, LOW), pair_ref[layer, 0, gate], jnp.int32)
            second = u >> jnp.full((spect, LOW), pair_ref[layer, 1, gate], jnp.int32)
            phase = phase + jnp.where((first & second & 1) == 1, angle_ref[layer, gate], 0.0)
        turn_ref[layer + 1, 0] = jnp.cos(phase)
        turn_ref[layer + 1, 1] = jnp.sin(phase)

    t = lax.broadcasted_iota(jnp.int32, (8, LOW), 1)
    position = lax.broadcasted_iota(jnp.int32, (LOW // 8, 8, LOW), 0) * 8
    position = position + lax.broadcasted_iota(jnp.int32, (LOW // 8, 8, LOW), 1)
    contract = (((1,), (1,)), ((), ()))
    for layer in range(LAYERS):
        source = jnp.zeros((8, LOW), jnp.int32)
        for bit in range(LOW_BITS):
            source = source + (((t >> bit) & 1) << jnp.full((8, LOW), order_ref[layer, bit], jnp.int32))
        hot = jnp.where(position == source[None], 1.0, 0.0).reshape(LOW, LOW).astype(jnp.bfloat16)
        for part, ref in enumerate((re_ref, im_ref)):
            for which, piece in enumerate(split(ref[layer])):
                for e in range(2):
                    moved = lax.dot_general(
                        hot[:, e * GATE : (e + 1) * GATE], piece, contract, preferred_element_type=jnp.float32
                    )
                    start = part * LOW + e * GATE
                    gate_ref[layer, which, :, start : start + GATE] = moved.astype(jnp.bfloat16)


def exchange_modes(rows, span):
    rows = list(rows)
    lane = lax.broadcasted_iota(jnp.int32, rows[0].shape, 1)
    step = 1
    while step < len(rows):
        shift = step * span
        upper = (lane & shift) != 0
        for m in range(len(rows)):
            if m & step:
                continue
            x0, x1 = rows[m], rows[m + step]
            if 2 * shift == LANES:
                crossing = pltpu.roll(jnp.where(upper, x0, x1), shift, 1)
                rows[m] = jnp.where(upper, crossing, x0)
                rows[m + step] = jnp.where(upper, x1, crossing)
            else:
                rows[m] = jnp.where(upper, pltpu.roll(x1, shift, 1), x0)
                rows[m + step] = jnp.where(upper, x1, pltpu.roll(x0, LANES - shift, 1))
        step *= 2
    return rows


def place_kernel(wide, *rest):
    blocks, out_hbm, sem = rest[:wide], rest[wide], rest[wide + 1]
    copies = [
        pltpu.make_async_copy(blocks[i], block_of(out_hbm, k, wide), sem.at[i])
        for i, k in enumerate(exchange_order(wide))
    ]
    for copy in copies:
        copy.start()
    for copy in copies:
        copy.wait()


def layers_kernel(wide, spect, x_hbm, gate_hbm, turn_hbm, *rest):
    outs = rest[:wide]
    x, gate, turn, state, left_high, left_low, minus_imag, x_sem, gate_sem, turn_sem, out_sem = rest[wide:]
    me = lax.axis_index("wide")
    count = wide * spect
    span = LOW // wide
    half = wide // 2
    rows_at_once = min(spect, PACKED)
    joined = PACKED // rows_at_once
    block = 4 * spect

    def gate_copy(layer):
        return pltpu.make_async_copy(gate_hbm.at[layer], gate.at[layer], gate_sem.at[layer])

    x_copies = [
        pltpu.make_async_copy(x_hbm.at[pl.ds(m * block, block)], x.at[pl.ds(m * block, block)], x_sem.at[m])
        for m in range(wide)
    ]
    turn_copy = pltpu.make_async_copy(turn_hbm, turn, turn_sem.at[0])
    for copy in x_copies:
        copy.start()
    turn_copy.start()
    for layer in range(LAYERS):
        gate_copy(layer).start()
    for m in range(wide):
        x_copies[m].wait()
        for part in range(2):
            for lanes in range(2):
                state[0, part, m * spect : (m + 1) * spect, lanes * LANES : (lanes + 1) * LANES] = x[
                    pl.ds(m * block + 2 * lanes + part, spect, stride=4), :
                ]
    turn_copy.wait()

    def turned(slot, entry, first, size, offset, lanes):
        rows, lanes = pl.ds(first + offset, size), slice(lanes * LANES, (lanes + 1) * LANES)
        real, imag = state[slot, 0, rows, lanes], state[slot, 1, rows, lanes]
        cosine, sine = turn[entry, 0, offset : offset + size, lanes], turn[entry, 1, offset : offset + size, lanes]
        return real * cosine - imag * sine, real * sine + imag * cosine

    def one_layer(layer, slot):
        gate_copy(layer).wait()
        for which in range(2):
            minus_imag[which] = -gate[layer, which, :, LOW:]

        for lanes in range(2):
            for top in range(2):
                for offset in range(0, spect, rows_at_once):
                    pieces = [
                        turned(slot, layer, (top * half + m) * spect, rows_at_once, offset, lanes) for m in range(half)
                    ]
                    for part in range(2):
                        rows = exchange_modes([piece[part] for piece in pieces], span)
                        column = part * LOW + top * LANES
                        for g in range(0, half, joined):
                            at = (lanes * half + g) * spect + offset
                            high, low = split(jnp.concatenate(rows[g : g + joined], axis=0))
                            left_high[at : at + PACKED, column : column + LANES] = high
                            left_low[at : at + PACKED, column : column + LANES] = low

        dot = partial(jnp.dot, preferred_element_type=jnp.float32)
        factors = []
        for which in range(2):
            real, imag = gate[layer, which, :, :LOW], gate[layer, which, :, LOW:]
            factors.append([[real, minus_imag[which]], [imag, real]])
        for first in range(0, count, TILE):
            rows = slice(first, first + TILE)
            for part in range(2):
                high = jnp.concatenate(factors[0][part], axis=0)
                low = jnp.concatenate(factors[1][part], axis=0)
                gated = dot(left_high[rows], high) + dot(left_low[rows], high) + dot(left_high[rows], low)
                state[1 - slot, part, rows] = gated

    def two_layers(step, carry):
        one_layer(2 * step, 0)
        one_layer(2 * step + 1, 1)
        return carry

    lax.fori_loop(0, LAYERS // 2, two_layers, 0)

    out_copies = []
    for i, k in enumerate(exchange_order(wide)):
        first = pl.multiple_of((me ^ k) * spect, spect)
        for lanes in range(2):
            for part, piece in enumerate(turned(0, LAYERS, first, spect, 0, lanes)):
                x[pl.ds(i * block + 2 * lanes + part, spect, stride=4), :] = piece
        out_copies.append(pltpu.make_async_copy(x.at[pl.ds(i * block, block)], outs[i], out_sem.at[i]))
        out_copies[-1].start()
    for copy in out_copies:
        copy.wait()


def local(state, gate_re, gate_im, bit_orders, phase_pairs, phase_angles):
    wide = lax.axis_size("wide")
    narrow = lax.axis_size("narrow")
    amps = state.shape[1]
    spect = amps // (wide * LOW)
    count = wide * spect

    view = with_layout_constraint(state.reshape(2, amps // LANES, LANES), PAIRED)
    rows = view.transpose(1, 0, 2).reshape(2 * amps // LANES, LANES)
    gathered = lax.all_to_all(rows, "wide", split_axis=0, concat_axis=0, tiled=True)

    in_hbm = pl.BlockSpec(memory_space=pltpu.HBM)
    in_vmem = pl.BlockSpec(memory_space=pltpu.VMEM)
    in_smem = pl.BlockSpec(memory_space=pltpu.SMEM)
    piece = jax.ShapeDtypeStruct((4 * spect, LANES), jnp.float32)
    all_of_vmem = pltpu.CompilerParams(vmem_limit_bytes=60 * 2**20)
    order = exchange_order(wide)

    gates = (LAYERS, 2, LOW, 2 * LOW)
    turns = (LAYERS + 1, 2, spect, LOW)
    gate, turn = pl.pallas_call(
        partial(tables_kernel, spect, narrow),
        in_specs=[in_vmem, in_vmem, in_smem, in_smem, in_smem],
        out_specs=[in_vmem, in_vmem],
        out_shape=[jax.ShapeDtypeStruct(gates, jnp.bfloat16), jax.ShapeDtypeStruct(turns, jnp.float32)],
        compiler_params=all_of_vmem,
        cost_estimate=pl.CostEstimate(flops=10**9, bytes_accessed=8 * 10**6, transcendentals=10**5),
        name="tables",
    )(gate_re, gate_im, bit_orders, phase_pairs.transpose(0, 2, 1), phase_angles)

    done = pl.pallas_call(
        partial(layers_kernel, wide, spect),
        in_specs=[in_hbm] * 3,
        out_specs=[in_hbm] * wide,
        out_shape=[piece] * wide,
        scratch_shapes=[
            pltpu.VMEM((4 * count, LANES), jnp.float32),
            pltpu.VMEM(gates, jnp.bfloat16),
            pltpu.VMEM(turns, jnp.float32),
            pltpu.VMEM((2, 2, count, LOW), jnp.float32),
            pltpu.VMEM((count, 2 * LOW), jnp.bfloat16),
            pltpu.VMEM((count, 2 * LOW), jnp.bfloat16),
            pltpu.VMEM((2, LOW, LOW), jnp.bfloat16),
            pltpu.SemaphoreType.DMA((wide,)),
            pltpu.SemaphoreType.DMA((LAYERS,)),
            pltpu.SemaphoreType.DMA((1,)),
            pltpu.SemaphoreType.DMA((wide,)),
        ],
        compiler_params=all_of_vmem,
        cost_estimate=pl.CostEstimate(flops=5 * 10**9, bytes_accessed=10**7, transcendentals=0),
        name="layers",
    )(gathered, gate, turn)

    def swap(blocks, ks):
        return [
            lax.ppermute(block, "wide", [(i, i ^ k) for i in range(wide)]) if k else block
            for block, k in zip(blocks, ks)
        ]

    back = pl.pallas_call(
        partial(place_kernel, wide),
        in_specs=[in_vmem] * wide,
        out_specs=in_hbm,
        out_shape=jax.ShapeDtypeStruct(rows.shape, jnp.float32),
        scratch_shapes=[pltpu.SemaphoreType.DMA((wide,))],
        compiler_params=pltpu.CompilerParams(vmem_limit_bytes=24 * 2**20),
        name="place",
    )(*swap(done, order))
    view = with_layout_constraint(back.reshape(amps // LANES, 2, LANES).transpose(1, 0, 2), PAIRED)
    return view.reshape(2, amps)


def solution(mesh):
    return jax.shard_map(
        local,
        mesh=mesh,
        in_specs=(P(None, ("wide", "narrow")), P(), P(), P(), P(), P()),
        out_specs=P(None, ("wide", "narrow")),
        check_vma=False,
    )
```

time: 75.8 us -> 75.3 us (level)
  waiting for transfers between devices: 14.1 us -> 26.3 us
  starting transfers between devices: 41.2 us -> 29.6 us
  local copies, waits for them, and re-layouts: 5.28 us -> 1.81 us
  Pallas kernels: 14.8 us -> 17.3 us
    ppermute x30 -> x15, starting transfers between devices: 41.2 us -> 22.2 us  [swap(): lax.ppermute(block, 'wide', [(i, i ^ k) for i in range(wide)])]
    all_to_all x0 -> x1, waiting for transfers between devices: none -> 18.7 us  [local(): lax.all_to_all(rows, 'wide', split_axis=0, concat_axis=0, tiled=True)]
    all_to_all x0 -> x1, starting transfers between devices: none -> 7.38 us  [local(): lax.all_to_all(rows, 'wide', split_axis=0, concat_axis=0, tiled=True)]
    ppermute x30 -> x15, waiting for transfers between devices: 14.1 us -> 7.58 us  [swap(): lax.ppermute(block, 'wide', [(i, i ^ k) for i in range(wide)])]
    unnamed x12 -> x4, local copies, waits for them, and re-layouts: 5.28 us -> 1.81 us
    pallas_call x3 -> x2, Pallas kernels: 13.7 us -> 16.2 us  [the longest x1 12 us: local(): pl.pallas_call(partial(layers_kernel, wide, spect), in_specs=[in_hbm] * 3...]
  transfers between devices with their start and end apart: 30 -> 16, of which waited for: 13 -> 8; matrix products, arithmetic and copies ran while one was open for 0% -> 0% of each run, Pallas kernels for 7% -> 6%
where the time goes in v7:
time: 75.3 us; the launch traced here: 75.1 us
  starting transfers between devices  29.6 us (39%)
  waiting for transfers between devices  26.3 us (35%)
  Pallas kernels  17.3 us (23%)
  local copies, waits for them, and re-layouts  1.81 us (2%)
    ppermute x15, starting transfers between devices, swap(): lax.ppermute(block, 'wide', [(i, i ^ k) for i in range(wide)])  22.2 us
    all_to_all x1, waiting for transfers between devices, local(): lax.all_to_all(rows, 'wide', split_axis=0, concat_axis=0, tiled=True)  18.7 us
    pallas_call x1, Pallas kernels, local(): pl.pallas_call(partial(layers_kernel, wide, spect), in_specs=[in_hbm] * 3...  12 us
    ppermute x15, waiting for transfers between devices, swap(): lax.ppermute(block, 'wide', [(i, i ^ k) for i in range(wide)])  7.58 us
    all_to_all x1, starting transfers between devices, local(): lax.all_to_all(rows, 'wide', split_axis=0, concat_axis=0, tiled=True)  7.38 us
    pallas_call x1, Pallas kernels, local(): pl.pallas_call(partial(tables_kernel, spect, narrow), in_specs=[in_vmem,...  4.25 us
    unnamed x4, local copies, waits for them, and re-layouts  1.81 us
  transfers between devices with their start and end apart: 16, of which 8 were waited for; matrix products, arithmetic and copies ran while one was open for 0% of the time, Pallas kernels for 6%

profile of v7, /device:TPU:0, one launch (start us, length us, event | category | flops | bytes accessed | tf_op | source)
XLA Modules:
  0.0 75.1 jit_solution(15689404620509842144)
XLA Ops:
  0.0 7.4 %all-to-all-start = ((f32[16,128,128]{2,1,0:T(8,128)}), f32[16,128,128]{2,1,0:T(8,128)S(1)}, u32[]{:S(2)}, u32[]{:S(2)}) async-start(f32[16,128,128]{2,1,0:T(8,128)} %bitcast.12), calls=%async_computation | async-start | bytes 2097152 | tf_op jit(solution)/shard_map/all_to_all | solution.py:216
  7.4 4.2 %tables.1 = (bf16[6,2,256,512]{3,2,1,0:T(8,128)(2,1)}, f32[7,2,32,256]{3,2,1,0:T(8,128)}) custom-call(f32[6,128,128]{2,1,0:T(8,128)} %re_ref.1, f32[6,128,128]{2,1,0:T(8,128)} %im_ref.1, s32[6,8]{1,0:T(8,128)} %order_ref.1, s32[6,2,16]{2,1,0:T(2,128)} %bitcast.14, f32[6,16]{1,0:T(8,128)} %angle_ref.1), custom_call_target="tpu_custom_call" | custom-call | flops 1000000000 | bytes 8000000 | tf_op jit(solution)/shard_map/tables/pallas_call | solution.py:227
  11.6 18.7 %all-to-all-done = f32[16,128,128]{2,1,0:T(8,128)S(1)} async-done(((f32[16,128,128]{2,1,0:T(8,128)}), f32[16,128,128]{2,1,0:T(8,128)S(1)}, u32[]{:S(2)}, u32[]{:S(2)}) %all-to-all-start) | async-done | bytes 1048608 | tf_op jit(solution)/shard_map/all_to_all | solution.py:216
  30.3 1.0 %copy-done.1 = f32[16,128,128]{2,1,0:T(8,128)} copy-done((f32[16,128,128]{2,1,0:T(8,128)}, f32[16,128,128]{2,1,0:T(8,128)S(1)}, u32[]{:S(2)}) %copy-start.1) | copy-done | bytes 1048600
  31.3 12.0 %layers.1 = (f32[128,128]{1,0:T(8,128)}, f32[128,128]{1,0:T(8,128)}, f32[128,128]{1,0:T(8,128)}, f32[128,128]{1,0:T(8,128)}, f32[128,128]{1,0:T(8,128)}, /*index...) custom-call(f32[2048,128]{1,0:T(8,128)} %bitcast.13, ...), custom_call_target="tpu_custom_call" | custom-call | flops 5000000000 | bytes 10000000 | tf_op jit(solution)/shard_map/layers/pallas_call | solution.py:237
  43.3 5.1 %collective-permute-start = (f32[128,128]{1,0:T(8,128)}, f32[128,128]{1,0:T(8,128)S(1)}, u32[]{:S(2)}, u32[]{:S(2)}) collective-permute-start(f32[128,128]{1,0:T(8,128)} %get-tuple-element.26), channel_id=1, source_target_pairs={{0,16},{2,18},{4,20},{6,22},{8,24},{10,26},{12,28},{14,30},{16,0},... | collective-permute-start | bytes 196616 | tf_op jit(solution)/shard_map/ppermute | solution.py:262
  48.4 0.0 collective-permute-start.1
  48.4 1.2 %collective-permute-start.2 = (f32[128,128]{1,0:T(8,128)}, f32[128,128]{1,0:T(8,128)S(1)}, u32[]{:S(2)}, u32[]{:S(2)}) collective-permute-start(f32[128,128]{1,0:T(8,128)} %get-tuple-element.28), channel_id=1, source_target_pairs={{0,8},{2,10},{4,12},{6,14},{8,0},{10,2},{12,4},{14,6},{16,24},{18,... | collective-permute-start | bytes 196616 | tf_op jit(solution)/shard_map/ppermute | solution.py:262
  49.6 0.4 collective-permute-start.3
  50.0 2.1 %collective-permute-start.4 = (f32[128,128]{1,0:T(8,128)}, f32[128,128]{1,0:T(8,128)S(1)}, u32[]{:S(2)}, u32[]{:S(2)}) collective-permute-start(f32[128,128]{1,0:T(8,128)} %get-tuple-element.30), channel_id=1, source_target_pairs={{0,20},{2,22},{4,16},{6,18},{8,28},{10,30},{12,24},{14,26},{16,4},... | collective-permute-start | bytes 196616 | tf_op jit(solution)/shard_map/ppermute | solution.py:262
  52.1 1.9 %collective-permute-done.rest_1_ = f32[128,128]{1,0:T(8,128)S(1)} collective-permute-done((f32[128,128]{1,0:T(8,128)}, f32[128,128]{1,0:T(8,128)S(1)}, u32[]{:S(2)}, u32[]{:S(2)}) %collective-permute-start) | collective-permute-done | bytes 65568 | tf_op jit(solution)/shard_map/ppermute | solution.py:262
  54.0 0.0 collective-permute-start.5
  54.0 0.9 %collective-permute-done.1.rest_2_ = f32[128,128]{1,0:T(8,128)S(1)} collective-permute-done((f32[128,128]{1,0:T(8,128)}, f32[128,128]{1,0:T(8,128)S(1)}, u32[]{:S(2)}, u32[]{:S(2)}) %collective-permute-start.1) | collective-permute-done | bytes 65568 | tf_op jit(solution)/shard_map/ppermute | solution.py:262
  55.0 0.9 %collective-permute-start.6 = (f32[128,128]{1,0:T(8,128)}, f32[128,128]{1,0:T(8,128)S(1)}, u32[]{:S(2)}, u32[]{:S(2)}) collective-permute-start(f32[128,128]{1,0:T(8,128)} %get-tuple-element.32), channel_id=1, source_target_pairs={{0,12},{2,14},{4,8},{6,10},{8,4},{10,6},{12,0},{14,2},{16,28},{18,... | collective-permute-start | bytes 196616 | tf_op jit(solution)/shard_map/ppermute | solution.py:262
  55.8 1.7 %collective-permute-start.7 = (f32[128,128]{1,0:T(8,128)}, f32[128,128]{1,0:T(8,128)S(1)}, u32[]{:S(2)}, u32[]{:S(2)}) collective-permute-start(f32[128,128]{1,0:T(8,128)} %get-tuple-element.33), channel_id=1, source_target_pairs={{0,14},{2,12},{4,10},{6,8},{8,6},{10,4},{12,2},{14,0},{16,30},{18,... | collective-permute-start | bytes 196616 | tf_op jit(solution)/shard_map/ppermute | solution.py:262
  57.5 1.6 %collective-permute-start.8 = (f32[128,128]{1,0:T(8,128)}, f32[128,128]{1,0:T(8,128)S(1)}, u32[]{:S(2)}, u32[]{:S(2)}) collective-permute-start(f32[128,128]{1,0:T(8,128)} %get-tuple-element.34), channel_id=1, source_target_pairs={{0,24},{2,26},{4,28},{6,30},{8,16},{10,18},{12,20},{14,22},{16,8},... | collective-permute-start | bytes 196616 | tf_op jit(solution)/shard_map/ppermute | solution.py:262
  59.1 0.0 collective-permute-done.4.rest_5_
  59.1 2.0 %collective-permute-start.9 = (f32[128,128]{1,0:T(8,128)}, f32[128,128]{1,0:T(8,128)S(1)}, u32[]{:S(2)}, u32[]{:S(2)}) collective-permute-start(f32[128,128]{1,0:T(8,128)} %get-tuple-element.35), channel_id=1, source_target_pairs={{0,26},{2,24},{4,30},{6,28},{8,18},{10,16},{12,22},{14,20},{16,10}... | collective-permute-start | bytes 196616 | tf_op jit(solution)/shard_map/ppermute | solution.py:262
  61.2 0.2 collective-permute-done.5.rest_6_
  61.3 3.4 %collective-permute-start.10 = (f32[128,128]{1,0:T(8,128)}, f32[128,128]{1,0:T(8,128)S(1)}, u32[]{:S(2)}, u32[]{:S(2)}) collective-permute-start(f32[128,128]{1,0:T(8,128)} %get-tuple-element.36), channel_id=1, source_target_pairs={{0,28},{2,30},{4,24},{6,26},{8,20},{10,22},{12,16},{14,18},{16,12}... | collective-permute-start | bytes 196616 | tf_op jit(solution)/shard_map/ppermute | solution.py:262
  64.7 0.0 collective-permute-done.6.rest_7_
  64.7 1.7 %collective-permute-start.11 = (f32[128,128]{1,0:T(8,128)}, f32[128,128]{1,0:T(8,128)S(1)}, u32[]{:S(2)}, u32[]{:S(2)}) collective-permute-start(f32[128,128]{1,0:T(8,128)} %get-tuple-element.37), channel_id=1, source_target_pairs={{0,30},{2,28},{4,26},{6,24},{8,22},{10,20},{12,18},{14,16},{16,14}... | collective-permute-start | bytes 196616 | tf_op jit(solution)/shard_map/ppermute | solution.py:262
  66.5 0.7 collective-permute-start.12
  67.1 0.0 collective-permute-done.8.rest_9_
  67.1 0.4 collective-permute-start.13
  67.5 1.1 %collective-permute-start.14 = (f32[128,128]{1,0:T(8,128)}, f32[128,128]{1,0:T(8,128)S(1)}, u32[]{:S(2)}, u32[]{:S(2)}) collective-permute-start(f32[128,128]{1,0:T(8,128)} %get-tuple-element.40), channel_id=1, source_target_pairs={{0,2},{2,0},{4,6},{6,4},{8,10},{10,8},{12,14},{14,12},{16,18},{18,... | collective-permute-start | bytes 196616 | tf_op jit(solution)/shard_map/ppermute | solution.py:262
  68.6 0.5 collective-permute-done.10.rest_11_
  69.1 3.0 %collective-permute-done.11.rest_12_ = f32[128,128]{1,0:T(8,128)S(1)} collective-permute-done((f32[128,128]{1,0:T(8,128)}, f32[128,128]{1,0:T(8,128)S(1)}, u32[]{:S(2)}, u32[]{:S(2)}) %collective-permute-start.11) | collective-permute-done | bytes 65568 | tf_op jit(solution)/shard_map/ppermute | solution.py:262
  72.1 0.8 %collective-permute-done.12.rest_13_ = f32[128,128]{1,0:T(8,128)S(1)} collective-permute-done((f32[128,128]{1,0:T(8,128)}, f32[128,128]{1,0:T(8,128)S(1)}, u32[]{:S(2)}, u32[]{:S(2)}) %collective-permute-start.12) | collective-permute-done | bytes 65568 | tf_op jit(solution)/shard_map/ppermute | solution.py:262
  72.9 0.2 collective-permute-done.13.rest_14_
  73.1 0.8 %copy-done = f32[128,128]{1,0:T(8,128)S(1)} copy-done((f32[128,128]{1,0:T(8,128)S(1)}, f32[128,128]{1,0:T(8,128)}, u32[]{:S(2)}) %copy-start) | copy-done | bytes 65560
  74.0 1.1 %place.1 = f32[2048,128]{1,0:T(8,128)} custom-call(f32[128,128]{1,0:T(8,128)S(1)} %copy-done, f32[128,128]{1,0:T(8,128)S(1)} %collective-permute-done.rest_1_, f32[128,128]{1,0:T(8,128)S(1)} %collective-permute-done.1.rest_2_, f32[128,128]{1,0:T(8,128)S(1)} %collective-permute-done.2.rest_3_, f32[128,128]{1,0:T(8,128)S(1)} %collective-permute-done.3.rest_4_, ...), custom_call_target="tpu_custom_call" | custom-call | tf_op jit(solution)/shard_map/place/pallas_call | solution.py:266
  (7 shorter events, 0.0 us)
Async XLA Ops:
  0.0 30.3 %all-to-all-start = ((f32[16,128,128]{2,1,0:T(8,128)}), f32[16,128,128]{2,1,0:T(8,128)S(1)}, u32[]{:S(2)}, u32[]{:S(2)}) async-start(f32[16,128,128]{2,1,0:T(8,128)} %bitcast.12), calls=%async_computation | async-start | bytes 2097152 | tf_op jit(solution)/shard_map/all_to_all | solution.py:216
  30.3 1.0 %copy-start.1 = (f32[16,128,128]{2,1,0:T(8,128)}, f32[16,128,128]{2,1,0:T(8,128)S(1)}, u32[]{:S(2)}) copy-start(f32[16,128,128]{2,1,0:T(8,128)S(1)} %all-to-all-done) | copy-start | bytes 3145732
  43.3 10.7 %collective-permute-start = (f32[128,128]{1,0:T(8,128)}, f32[128,128]{1,0:T(8,128)S(1)}, u32[]{:S(2)}, u32[]{:S(2)}) collective-permute-start(f32[128,128]{1,0:T(8,128)} %get-tuple-element.26), channel_id=1, source_target_pairs={{0,16},{2,18},{4,20},{6,22},{8,24},{10,26},{12,28},{14,30},{16,0},... | collective-permute-start | bytes 196616 | tf_op jit(solution)/shard_map/ppermute | solution.py:262
  48.4 6.5 %collective-permute-start.1 = (f32[128,128]{1,0:T(8,128)}, f32[128,128]{1,0:T(8,128)S(1)}, u32[]{:S(2)}, u32[]{:S(2)}) collective-permute-start(f32[128,128]{1,0:T(8,128)} %get-tuple-element.27), channel_id=1, source_target_pairs={{0,18},{2,16},{4,22},{6,20},{8,26},{10,24},{12,30},{14,28},{16,2},... | collective-permute-start | bytes 196616 | tf_op jit(solution)/shard_map/ppermute | solution.py:262
  48.4 7.4 %collective-permute-start.2 = (f32[128,128]{1,0:T(8,128)}, f32[128,128]{1,0:T(8,128)S(1)}, u32[]{:S(2)}, u32[]{:S(2)}) collective-permute-start(f32[128,128]{1,0:T(8,128)} %get-tuple-element.28), channel_id=1, source_target_pairs={{0,8},{2,10},{4,12},{6,14},{8,0},{10,2},{12,4},{14,6},{16,24},{18,... | collective-permute-start | bytes 196616 | tf_op jit(solution)/shard_map/ppermute | solution.py:262
  49.6 7.9 %collective-permute-start.3 = (f32[128,128]{1,0:T(8,128)}, f32[128,128]{1,0:T(8,128)S(1)}, u32[]{:S(2)}, u32[]{:S(2)}) collective-permute-start(f32[128,128]{1,0:T(8,128)} %get-tuple-element.29), channel_id=1, source_target_pairs={{0,10},{2,8},{4,14},{6,12},{8,2},{10,0},{12,6},{14,4},{16,26},{18,... | collective-permute-start | bytes 196616 | tf_op jit(solution)/shard_map/ppermute | solution.py:262
  50.0 9.2 %collective-permute-start.4 = (f32[128,128]{1,0:T(8,128)}, f32[128,128]{1,0:T(8,128)S(1)}, u32[]{:S(2)}, u32[]{:S(2)}) collective-permute-start(f32[128,128]{1,0:T(8,128)} %get-tuple-element.30), channel_id=1, source_target_pairs={{0,20},{2,22},{4,16},{6,18},{8,28},{10,30},{12,24},{14,26},{16,4},... | collective-permute-start | bytes 196616 | tf_op jit(solution)/shard_map/ppermute | solution.py:262
  54.0 7.3 %collective-permute-start.5 = (f32[128,128]{1,0:T(8,128)}, f32[128,128]{1,0:T(8,128)S(1)}, u32[]{:S(2)}, u32[]{:S(2)}) collective-permute-start(f32[128,128]{1,0:T(8,128)} %get-tuple-element.31), channel_id=1, source_target_pairs={{0,22},{2,20},{4,18},{6,16},{8,30},{10,28},{12,26},{14,24},{16,6},... | collective-permute-start | bytes 196616 | tf_op jit(solution)/shard_map/ppermute | solution.py:262
  55.0 9.8 %collective-permute-start.6 = (f32[128,128]{1,0:T(8,128)}, f32[128,128]{1,0:T(8,128)S(1)}, u32[]{:S(2)}, u32[]{:S(2)}) collective-permute-start(f32[128,128]{1,0:T(8,128)} %get-tuple-element.32), channel_id=1, source_target_pairs={{0,12},{2,14},{4,8},{6,10},{8,4},{10,6},{12,0},{14,2},{16,28},{18,... | collective-permute-start | bytes 196616 | tf_op jit(solution)/shard_map/ppermute | solution.py:262
  55.8 10.6 %collective-permute-start.7 = (f32[128,128]{1,0:T(8,128)}, f32[128,128]{1,0:T(8,128)S(1)}, u32[]{:S(2)}, u32[]{:S(2)}) collective-permute-start(f32[128,128]{1,0:T(8,128)} %get-tuple-element.33), channel_id=1, source_target_pairs={{0,14},{2,12},{4,10},{6,8},{8,6},{10,4},{12,2},{14,0},{16,30},{18,... | collective-permute-start | bytes 196616 | tf_op jit(solution)/shard_map/ppermute | solution.py:262
  57.5 9.6 %collective-permute-start.8 = (f32[128,128]{1,0:T(8,128)}, f32[128,128]{1,0:T(8,128)S(1)}, u32[]{:S(2)}, u32[]{:S(2)}) collective-permute-start(f32[128,128]{1,0:T(8,128)} %get-tuple-element.34), channel_id=1, source_target_pairs={{0,24},{2,26},{4,28},{6,30},{8,16},{10,18},{12,20},{14,22},{16,8},... | collective-permute-start | bytes 196616 | tf_op jit(solution)/shard_map/ppermute | solution.py:262
  59.1 8.4 %collective-permute-start.9 = (f32[128,128]{1,0:T(8,128)}, f32[128,128]{1,0:T(8,128)S(1)}, u32[]{:S(2)}, u32[]{:S(2)}) collective-permute-start(f32[128,128]{1,0:T(8,128)} %get-tuple-element.35), channel_id=1, source_target_pairs={{0,26},{2,24},{4,30},{6,28},{8,18},{10,16},{12,22},{14,20},{16,10}... | collective-permute-start | bytes 196616 | tf_op jit(solution)/shard_map/ppermute | solution.py:262
  61.3 7.8 %collective-permute-start.10 = (f32[128,128]{1,0:T(8,128)}, f32[128,128]{1,0:T(8,128)S(1)}, u32[]{:S(2)}, u32[]{:S(2)}) collective-permute-start(f32[128,128]{1,0:T(8,128)} %get-tuple-element.36), channel_id=1, source_target_pairs={{0,28},{2,30},{4,24},{6,26},{8,20},{10,22},{12,16},{14,18},{16,12}... | collective-permute-start | bytes 196616 | tf_op jit(solution)/shard_map/ppermute | solution.py:262
  64.7 7.3 %collective-permute-start.11 = (f32[128,128]{1,0:T(8,128)}, f32[128,128]{1,0:T(8,128)S(1)}, u32[]{:S(2)}, u32[]{:S(2)}) collective-permute-start(f32[128,128]{1,0:T(8,128)} %get-tuple-element.37), channel_id=1, source_target_pairs={{0,30},{2,28},{4,26},{6,24},{8,22},{10,20},{12,18},{14,16},{16,14}... | collective-permute-start | bytes 196616 | tf_op jit(solution)/shard_map/ppermute | solution.py:262
  66.5 6.5 %collective-permute-start.12 = (f32[128,128]{1,0:T(8,128)}, f32[128,128]{1,0:T(8,128)S(1)}, u32[]{:S(2)}, u32[]{:S(2)}) collective-permute-start(f32[128,128]{1,0:T(8,128)} %get-tuple-element.38), channel_id=1, source_target_pairs={{0,4},{2,6},{4,0},{6,2},{8,12},{10,14},{12,8},{14,10},{16,20},{18,... | collective-permute-start | bytes 196616 | tf_op jit(solution)/shard_map/ppermute | solution.py:262
  67.1 6.0 %collective-permute-start.13 = (f32[128,128]{1,0:T(8,128)}, f32[128,128]{1,0:T(8,128)S(1)}, u32[]{:S(2)}, u32[]{:S(2)}) collective-permute-start(f32[128,128]{1,0:T(8,128)} %get-tuple-element.39), channel_id=1, source_target_pairs={{0,6},{2,4},{4,2},{6,0},{8,14},{10,12},{12,10},{14,8},{16,22},{18,... | collective-permute-start | bytes 196616 | tf_op jit(solution)/shard_map/ppermute | solution.py:262
  67.5 5.6 %collective-permute-start.14 = (f32[128,128]{1,0:T(8,128)}, f32[128,128]{1,0:T(8,128)S(1)}, u32[]{:S(2)}, u32[]{:S(2)}) collective-permute-start(f32[128,128]{1,0:T(8,128)} %get-tuple-element.40), channel_id=1, source_target_pairs={{0,2},{2,0},{4,6},{6,4},{8,10},{10,8},{12,14},{14,12},{16,18},{18,... | collective-permute-start | bytes 196616 | tf_op jit(solution)/shard_map/ppermute | solution.py:262
  73.1 0.8 %copy-start = (f32[128,128]{1,0:T(8,128)S(1)}, f32[128,128]{1,0:T(8,128)}, u32[]{:S(2)}) copy-start(f32[128,128]{1,0:T(8,128)} %get-tuple-element.25.rest_0_) | copy-start | bytes 196612

commit v8 on v7

v8 whole, which is shorter than its diff:
```python
from functools import partial

import jax
import jax.numpy as jnp
from jax import lax
from jax.experimental import pallas as pl
from jax.experimental.layout import Layout, with_layout_constraint
from jax.experimental.pallas import tpu as pltpu
from jax.sharding import PartitionSpec as P

LAYERS = 6
GATE = 128
LOW = 256
LOW_BITS = 8
PHASES = 16
PHASE_BITS = 12
LANES = 128
PACKED = 16
TILE = 128
PAIRED = Layout(major_to_minor=(1, 0, 2))


def split(x):
    high = x.astype(jnp.bfloat16)
    low = (x - high.astype(jnp.float32)).astype(jnp.bfloat16)
    return high, low


def exchange_order(wide):
    far = range(wide // 2, wide, 2)
    near = list(range(wide // 4, wide // 2, 2))
    near = [k for pair in zip(near, list(range(2, wide // 4, 2)) + [None]) for k in pair if k]
    pairs = [k for pair in zip(far, near) for k in pair]
    return [0] + [k + j for k in pairs for j in range(2)] + [1, wide - 2, wide - 1]


def block_of(ref, k, wide):
    rows = ref.shape[0] // wide
    start = (lax.axis_index("wide") ^ k) * rows
    return ref.at[pl.ds(pl.multiple_of(start, rows), rows)]


def tables_kernel(spect, narrow, re_ref, im_ref, order_ref, pair_ref, angle_ref, gate_ref, turn_ref):
    row = lax.broadcasted_iota(jnp.int32, (spect, LOW), 0)
    lane = lax.broadcasted_iota(jnp.int32, (spect, LOW), 1)
    r = lax.axis_index("wide") * (spect // narrow) + row // narrow
    for layer in range(LAYERS):
        b = lax.axis_index("narrow") if layer % 2 == 0 else row % narrow
        u = ((r * narrow + b) * LOW + lane) & (2**PHASE_BITS - 1)
        phase = jnp.zeros((spect, LOW), jnp.float32)
        for gate in range(PHASES):
            first = u >> jnp.full((spect, LOW), pair_ref[layer, 0, gate], jnp.int32)
            second = u >> jnp.full((spect, LOW), pair_ref[layer, 1, gate], jnp.int32)
            phase = phase + jnp.where((first & second & 1) == 1, angle_ref[layer, gate], 0.0)
        turn_ref[layer, 0] = jnp.cos(phase)
        turn_ref[layer, 1] = jnp.sin(phase)

    j = lax.broadcasted_iota(jnp.int32, (8, GATE), 1)
    position = lax.broadcasted_iota(jnp.int32, (GATE // 8, 8, GATE), 0) * 8
    position = position + lax.broadcasted_iota(jnp.int32, (GATE // 8, 8, GATE), 1)
    contract = (((1,), (1,)), ((), ()))
    top = LOW_BITS - 1
    for layer in range(LAYERS):
        source = jnp.zeros((8, GATE), jnp.int32)
        for bit in range(top):
            place = order_ref[layer, bit]
            place = jnp.where(place == top, order_ref[layer, top], place)
            source = source + (((j >> bit) & 1) << jnp.full((8, GATE), place, jnp.int32))
        hot = jnp.where(position == source[None], 1.0, 0.0).reshape(GATE, GATE).astype(jnp.bfloat16)
        for part, ref in enumerate((re_ref, im_ref)):
            for which, piece in enumerate(split(ref[layer])):
                moved = lax.dot_general(hot, piece, contract, preferred_element_type=jnp.float32)
                gate_ref[layer, which, :, part * GATE : (part + 1) * GATE] = moved.astype(jnp.bfloat16)


def exchange_modes(rows, span):
    rows = list(rows)
    lane = lax.broadcasted_iota(jnp.int32, rows[0].shape, 1)
    step = 1
    while step < len(rows):
        shift = step * span
        upper = (lane & shift) != 0
        for m in range(len(rows)):
            if m & step:
                continue
            x0, x1 = rows[m], rows[m + step]
            if 2 * shift == LANES:
                crossing = pltpu.roll(jnp.where(upper, x0, x1), shift, 1)
                rows[m] = jnp.where(upper, crossing, x0)
                rows[m + step] = jnp.where(upper, x1, crossing)
            else:
                rows[m] = jnp.where(upper, pltpu.roll(x1, shift, 1), x0)
                rows[m + step] = jnp.where(upper, x1, pltpu.roll(x0, LANES - shift, 1))
        step *= 2
    return rows


def place_kernel(wide, *rest):
    blocks, out_hbm, sem = rest[:wide], rest[wide], rest[wide + 1]
    copies = [
        pltpu.make_async_copy(blocks[i], block_of(out_hbm, k, wide), sem.at[i])
        for i, k in enumerate(exchange_order(wide))
    ]
    for copy in copies:
        copy.start()
    for copy in copies:
        copy.wait()


def exchange_top(x0, x1, shift):
    at = lax.broadcasted_iota(jnp.int32, x0.shape, 1) & shift
    back = (LANES - shift) & (LANES - 1)
    forth = shift & (LANES - 1)
    return jnp.where(at != 0, pltpu.roll(x1, forth, 1), x0), jnp.where(at == forth, x1, pltpu.roll(x0, back, 1))


def layers_kernel(wide, spect, order_ref, x, gate, turn, *rest):
    outs = rest[:wide]
    state, left_high, left_low, factor = rest[wide:]
    me = lax.axis_index("wide")
    count = wide * spect
    span = LOW // wide
    half = wide // 2
    rows_at_once = min(spect, PACKED)
    joined = PACKED // rows_at_once
    tile = min(TILE, count)

    for part in range(2):
        for lanes in range(2):
            state[0, part, :, lanes * LANES : (lanes + 1) * LANES] = x[pl.ds(2 * lanes + part, count, stride=4), :]

    def one_layer(layer, slot):
        for which in range(2):
            factor[which, :GATE] = gate[layer, which]
            factor[which, GATE:, :GATE] = -gate[layer, which, :, GATE:]
            factor[which, GATE:, GATE:] = gate[layer, which, :, :GATE]

        shift = jnp.int32(1) << order_ref[layer, LOW_BITS - 1]
        for lanes in range(2):
            for part in range(2):
                for offset in range(0, spect, rows_at_once):
                    tops = []
                    for top in range(2):
                        first = top * half * spect + offset
                        pieces = [
                            state[
                                slot,
                                part,
                                first + m * spect : first + m * spect + rows_at_once,
                                lanes * LANES : (lanes + 1) * LANES,
                            ]
                            for m in range(half)
                        ]
                        tops.append(exchange_modes(pieces, span))
                    for g in range(0, half, joined):
                        at = (lanes * half + g) * spect + offset
                        ends = [jnp.concatenate(rows[g : g + joined], axis=0) for rows in tops]
                        for e, piece in enumerate(exchange_top(*ends, shift)):
                            high, low = split(piece)
                            left_high[e, at : at + PACKED, part * LANES : (part + 1) * LANES] = high
                            left_low[e, at : at + PACKED, part * LANES : (part + 1) * LANES] = low

        dot = partial(jnp.dot, preferred_element_type=jnp.float32)
        for first in range(0, count, tile):
            rows = slice(first, first + tile)
            for e in range(2):
                gated = dot(left_high[e, rows], factor[0])
                gated = gated + dot(left_low[e, rows], factor[0])
                gated = gated + dot(left_high[e, rows], factor[1])
                real = gated[:, :LANES].reshape(tile // spect, spect, LANES)
                imag = gated[:, LANES:].reshape(tile // spect, spect, LANES)
                lanes = slice(e * LANES, (e + 1) * LANES)
                cosine, sine = turn[layer, 0, :, lanes][None], turn[layer, 1, :, lanes][None]
                state[1 - slot, 0, rows, lanes] = (real * cosine - imag * sine).reshape(tile, LANES)
                state[1 - slot, 1, rows, lanes] = (real * sine + imag * cosine).reshape(tile, LANES)

    def two_layers(step, carry):
        one_layer(2 * step, 0)
        one_layer(2 * step + 1, 1)
        return carry

    lax.fori_loop(0, LAYERS // 2, two_layers, 0)

    for i, k in enumerate(exchange_order(wide)):
        rows = pl.ds(pl.multiple_of((me ^ k) * spect, spect), spect)
        for part in range(2):
            for lanes in range(2):
                outs[i][pl.ds(2 * lanes + part, spect, stride=4), :] = state[
                    0, part, rows, lanes * LANES : (lanes + 1) * LANES
                ]


def local(state, gate_re, gate_im, bit_orders, phase_pairs, phase_angles):
    wide = lax.axis_size("wide")
    narrow = lax.axis_size("narrow")
    amps = state.shape[1]
    spect = amps // (wide * LOW)
    count = wide * spect

    view = with_layout_constraint(state.reshape(2, amps // LANES, LANES), PAIRED)
    rows = view.transpose(1, 0, 2).reshape(2 * amps // LANES, LANES)
    gathered = lax.all_to_all(rows, "wide", split_axis=0, concat_axis=0, tiled=True)

    in_hbm = pl.BlockSpec(memory_space=pltpu.HBM)
    in_vmem = pl.BlockSpec(memory_space=pltpu.VMEM)
    in_smem = pl.BlockSpec(memory_space=pltpu.SMEM)
    piece = jax.ShapeDtypeStruct((4 * spect, LANES), jnp.float32)
    part_of_vmem = pltpu.CompilerParams(vmem_limit_bytes=24 * 2**20)
    order = exchange_order(wide)

    gates = (LAYERS, 2, GATE, 2 * GATE)
    turns = (LAYERS, 2, spect, LOW)
    gate, turn = pl.pallas_call(
        partial(tables_kernel, spect, narrow),
        in_specs=[in_vmem, in_vmem, in_smem, in_smem, in_smem],
        out_specs=[in_vmem, in_vmem],
        out_shape=[jax.ShapeDtypeStruct(gates, jnp.bfloat16), jax.ShapeDtypeStruct(turns, jnp.float32)],
        compiler_params=part_of_vmem,
        cost_estimate=pl.CostEstimate(flops=10**9, bytes_accessed=8 * 10**6, transcendentals=10**5),
        name="tables",
    )(gate_re, gate_im, bit_orders, phase_pairs.transpose(0, 2, 1), phase_angles)

    done = pl.pallas_call(
        partial(layers_kernel, wide, spect),
        in_specs=[in_smem] + [in_vmem] * 3,
        out_specs=[in_vmem] * wide,
        out_shape=[piece] * wide,
        scratch_shapes=[
            pltpu.VMEM((2, 2, count, LOW), jnp.float32),
            pltpu.VMEM((2, count, 2 * LANES), jnp.bfloat16),
            pltpu.VMEM((2, count, 2 * LANES), jnp.bfloat16),
            pltpu.VMEM((2, 2 * GATE, 2 * GATE), jnp.bfloat16),
        ],
        compiler_params=part_of_vmem,
        cost_estimate=pl.CostEstimate(flops=5 * 10**9, bytes_accessed=10**7, transcendentals=0),
        name="layers",
    )(bit_orders, gathered, gate, turn)

    def swap(blocks, ks):
        return [
            lax.ppermute(block, "wide", [(i, i ^ k) for i in range(wide)]) if k else block
            for block, k in zip(blocks, ks)
        ]

    back = pl.pallas_call(
        partial(place_kernel, wide),
        in_specs=[in_vmem] * wide,
        out_specs=in_hbm,
        out_shape=jax.ShapeDtypeStruct(rows.shape, jnp.float32),
        scratch_shapes=[pltpu.SemaphoreType.DMA((wide,))],
        compiler_params=part_of_vmem,
        name="place",
    )(*swap(done, order))
    view = with_layout_constraint(back.reshape(amps // LANES, 2, LANES).transpose(1, 0, 2), PAIRED)
    return view.reshape(2, amps)


def solution(mesh):
    return jax.shard_map(
        local,
        mesh=mesh,
        in_specs=(P(None, ("wide", "narrow")), P(), P(), P(), P(), P()),
        out_specs=P(None, ("wide", "narrow")),
        check_vma=False,
    )
```

time: 75.3 us -> 78.5 us (1.042)
  waiting for transfers between devices: 26.3 us -> 29.5 us
  Pallas kernels: 17.3 us -> 19.6 us
  local copies, waits for them, and re-layouts: 1.81 us -> 0.02 us
    pallas_call x1, Pallas kernels: 12 us -> 15.6 us  [local(): pl.pallas_call(partial(layers_kernel, wide, spect), in_specs=[in_smem] +...]
    ppermute x15, waiting for transfers between devices: 7.58 us -> 9.47 us  [swap(): lax.ppermute(block, 'wide', [(i, i ^ k) for i in range(wide)])]
    unnamed x4 -> x10, local copies, waits for them, and re-layouts: 1.81 us -> 0.02 us
    pallas_call x1, Pallas kernels: 4.25 us -> 2.82 us  [local(): pl.pallas_call(partial(tables_kernel, spect, narrow), in_specs=[in_vmem,...]
    all_to_all x1, waiting for transfers between devices: 18.7 us -> 20.1 us  [local(): lax.all_to_all(rows, 'wide', split_axis=0, concat_axis=0, tiled=True)]
  transfers between devices with their start and end apart: 16 -> 16, of which waited for: 8 -> 8; matrix products, arithmetic and copies ran while one was open for 0% -> 0% of each run, Pallas kernels for 6% -> 4%
where the time goes in v8:
time: 78.5 us; the launch traced here: 78.3 us
  waiting for transfers between devices  29.5 us (38%)
  starting transfers between devices  29.1 us (37%)
  Pallas kernels  19.6 us (25%)
    ppermute x15, starting transfers between devices, swap(): lax.ppermute(block, 'wide', [(i, i ^ k) for i in range(wide)])  21.6 us
    all_to_all x1, waiting for transfers between devices, local(): lax.all_to_all(rows, 'wide', split_axis=0, concat_axis=0, tiled=True)  20.1 us
    pallas_call x1, Pallas kernels, local(): pl.pallas_call(partial(layers_kernel, wide, spect), in_specs=[in_smem] +...  15.6 us
    ppermute x15, waiting for transfers between devices, swap(): lax.ppermute(block, 'wide', [(i, i ^ k) for i in range(wide)])  9.47 us
    all_to_all x1, starting transfers between devices, local(): lax.all_to_all(rows, 'wide', split_axis=0, concat_axis=0, tiled=True)  7.54 us
    pallas_call x1, Pallas kernels, local(): pl.pallas_call(partial(tables_kernel, spect, narrow), in_specs=[in_vmem,...  2.82 us
  transfers between devices with their start and end apart: 16, of which 8 were waited for; matrix products, arithmetic and copies ran while one was open for 0% of the time, Pallas kernels for 4%

profile of v8, /device:TPU:0, one launch (start us, length us, event | category | flops | bytes accessed | tf_op | source)
XLA Modules:
  0.0 78.3 jit_solution(2627452058805215610)
XLA Ops:
  0.0 7.5 %all-to-all-start = ((f32[16,128,128]{2,1,0:T(8,128)}), f32[16,128,128]{2,1,0:T(8,128)S(1)}, u32[]{:S(2)}, u32[]{:S(2)}) async-start(f32[16,128,128]{2,1,0:T(8,128)} %bitcast.14), calls=%async_computation | async-start | bytes 2097152 | tf_op jit(solution)/shard_map/all_to_all | solution.py:202
  7.6 2.8 %tables.1 = (bf16[6,2,128,256]{3,2,1,0:T(8,128)(2,1)S(1)}, f32[6,2,32,256]{3,2,1,0:T(8,128)S(1)}) custom-call(f32[6,128,128]{2,1,0:T(8,128)S(1)} %copy-done, f32[6,128,128]{2,1,0:T(8,128)S(1)} %copy-done.1, s32[6,8]{1,0:T(8,128)S(1)} %copy-done.4, s32[6,2,16]{2,1,0:T(2,128)S(1)} %bitcast.13, f32[6,16]{1,0:T(8,128)S(1)} %copy-done.3), custom_call_target="tpu_custom_call" | custom-call | flops 1000000000 | bytes 8000000 | tf_op jit(solution)/shard_map/tables/pallas_call | solution.py:213
  10.4 20.1 %all-to-all-done = f32[16,128,128]{2,1,0:T(8,128)S(1)} async-done(((f32[16,128,128]{2,1,0:T(8,128)}), f32[16,128,128]{2,1,0:T(8,128)S(1)}, u32[]{:S(2)}, u32[]{:S(2)}) %all-to-all-start) | async-done | bytes 1048608 | tf_op jit(solution)/shard_map/all_to_all | solution.py:202
  30.5 15.6 %layers.1 = (f32[128,128]{1,0:T(8,128)S(1)}, f32[128,128]{1,0:T(8,128)S(1)}, f32[128,128]{1,0:T(8,128)S(1)}, f32[128,128]{1,0:T(8,128)S(1)}, f32[128,128]{1,0:T(...) custom-call(s32[6,8]{1,0:T(8,128)S(1)} %copy-done.4, ...), custom_call_target="tpu_custom_call" | custom-call | flops 5000000000 | bytes 10000000 | tf_op jit(solution)/shard_map/layers/pallas_call | solution.py:223
  46.2 5.1 %collective-permute-start = (f32[128,128]{1,0:T(8,128)S(1)}, f32[128,128]{1,0:T(8,128)S(1)}, u32[]{:S(2)}, u32[]{:S(2)}) collective-permute-start(f32[128,128]{1,0:T(8,128)S(1)} %get-tuple-element.26), channel_id=1, source_target_pairs={{0,16},{2,18},{4,20},{6,22},{8,24},{10,26},{12,28},{14,30},{16,0},... | collective-permute-start | bytes 196616 | tf_op jit(solution)/shard_map/ppermute | solution.py:241
  51.3 0.0 collective-permute-start.1
  51.3 1.2 %collective-permute-start.2 = (f32[128,128]{1,0:T(8,128)S(1)}, f32[128,128]{1,0:T(8,128)S(1)}, u32[]{:S(2)}, u32[]{:S(2)}) collective-permute-start(f32[128,128]{1,0:T(8,128)S(1)} %get-tuple-element.28), channel_id=1, source_target_pairs={{0,8},{2,10},{4,12},{6,14},{8,0},{10,2},{12,4},{14,6},{16,24},{18,... | collective-permute-start | bytes 196616 | tf_op jit(solution)/shard_map/ppermute | solution.py:241
  52.5 0.4 collective-permute-start.3
  52.8 2.1 %collective-permute-start.4 = (f32[128,128]{1,0:T(8,128)S(1)}, f32[128,128]{1,0:T(8,128)S(1)}, u32[]{:S(2)}, u32[]{:S(2)}) collective-permute-start(f32[128,128]{1,0:T(8,128)S(1)} %get-tuple-element.30), channel_id=1, source_target_pairs={{0,20},{2,22},{4,16},{6,18},{8,28},{10,30},{12,24},{14,26},{16,4},... | collective-permute-start | bytes 196616 | tf_op jit(solution)/shard_map/ppermute | solution.py:241
  55.0 1.7 %collective-permute-done.rest_1_ = f32[128,128]{1,0:T(8,128)S(1)} collective-permute-done((f32[128,128]{1,0:T(8,128)S(1)}, f32[128,128]{1,0:T(8,128)S(1)}, u32[]{:S(2)}, u32[]{:S(2)}) %collective-permute-start) | collective-permute-done | bytes 65568 | tf_op jit(solution)/shard_map/ppermute | solution.py:241
  56.7 0.0 collective-permute-start.5
  56.7 0.9 %collective-permute-done.1.rest_2_ = f32[128,128]{1,0:T(8,128)S(1)} collective-permute-done((f32[128,128]{1,0:T(8,128)S(1)}, f32[128,128]{1,0:T(8,128)S(1)}, u32[]{:S(2)}, u32[]{:S(2)}) %collective-permute-start.1) | collective-permute-done | bytes 65568 | tf_op jit(solution)/shard_map/ppermute | solution.py:241
  57.6 1.1 %collective-permute-start.6 = (f32[128,128]{1,0:T(8,128)S(1)}, f32[128,128]{1,0:T(8,128)S(1)}, u32[]{:S(2)}, u32[]{:S(2)}) collective-permute-start(f32[128,128]{1,0:T(8,128)S(1)} %get-tuple-element.32), channel_id=1, source_target_pairs={{0,4},{2,6},{4,0},{6,2},{8,12},{10,14},{12,8},{14,10},{16,20},{18,... | collective-permute-start | bytes 196616 | tf_op jit(solution)/shard_map/ppermute | solution.py:241
  58.7 0.0 collective-permute-done.2.rest_3_
  58.7 0.6 collective-permute-start.7
  59.3 0.5 collective-permute-done.3.rest_4_
  59.8 2.7 %collective-permute-start.8 = (f32[128,128]{1,0:T(8,128)S(1)}, f32[128,128]{1,0:T(8,128)S(1)}, u32[]{:S(2)}, u32[]{:S(2)}) collective-permute-start(f32[128,128]{1,0:T(8,128)S(1)} %get-tuple-element.34), channel_id=1, source_target_pairs={{0,24},{2,26},{4,28},{6,30},{8,16},{10,18},{12,20},{14,22},{16,8},... | collective-permute-start | bytes 196616 | tf_op jit(solution)/shard_map/ppermute | solution.py:241
  62.5 0.0 collective-permute-done.4.rest_5_
  62.5 0.5 collective-permute-start.9
  63.1 0.9 %collective-permute-done.5.rest_6_ = f32[128,128]{1,0:T(8,128)S(1)} collective-permute-done((f32[128,128]{1,0:T(8,128)S(1)}, f32[128,128]{1,0:T(8,128)S(1)}, u32[]{:S(2)}, u32[]{:S(2)}) %collective-permute-start.5) | collective-permute-done | bytes 65568 | tf_op jit(solution)/shard_map/ppermute | solution.py:241
  64.0 0.0 collective-permute-start.10
  64.0 3.3 %collective-permute-start.11 = (f32[128,128]{1,0:T(8,128)S(1)}, f32[128,128]{1,0:T(8,128)S(1)}, u32[]{:S(2)}, u32[]{:S(2)}) collective-permute-start(f32[128,128]{1,0:T(8,128)S(1)} %get-tuple-element.37), channel_id=1, source_target_pairs={{0,14},{2,12},{4,10},{6,8},{8,6},{10,4},{12,2},{14,0},{16,30},{18,... | collective-permute-start | bytes 196616 | tf_op jit(solution)/shard_map/ppermute | solution.py:241
  67.3 0.0 collective-permute-done.7.rest_8_
  67.3 0.0 collective-permute-start.12
  67.3 0.0 collective-permute-done.8.rest_9_
  67.3 2.9 %collective-permute-start.13 = (f32[128,128]{1,0:T(8,128)S(1)}, f32[128,128]{1,0:T(8,128)S(1)}, u32[]{:S(2)}, u32[]{:S(2)}) collective-permute-start(f32[128,128]{1,0:T(8,128)S(1)} %get-tuple-element.39), channel_id=1, source_target_pairs={{0,28},{2,30},{4,24},{6,26},{8,20},{10,22},{12,16},{14,18},{16,12}... | collective-permute-start | bytes 196616 | tf_op jit(solution)/shard_map/ppermute | solution.py:241
  70.2 1.7 %collective-permute-start.14 = (f32[128,128]{1,0:T(8,128)S(1)}, f32[128,128]{1,0:T(8,128)S(1)}, u32[]{:S(2)}, u32[]{:S(2)}) collective-permute-start(f32[128,128]{1,0:T(8,128)S(1)} %get-tuple-element.40), channel_id=1, source_target_pairs={{0,30},{2,28},{4,26},{6,24},{8,22},{10,20},{12,18},{14,16},{16,14}... | collective-permute-start | bytes 196616 | tf_op jit(solution)/shard_map/ppermute | solution.py:241
  71.9 0.0 collective-permute-done.10.rest_11_
  71.9 0.8 collective-permute-done.11.rest_12_
  72.7 2.0 %collective-permute-done.13.rest_14_ = f32[128,128]{1,0:T(8,128)S(1)} collective-permute-done((f32[128,128]{1,0:T(8,128)S(1)}, f32[128,128]{1,0:T(8,128)S(1)}, u32[]{:S(2)}, u32[]{:S(2)}) %collective-permute-start.13) | collective-permute-done | bytes 65568 | tf_op jit(solution)/shard_map/ppermute | solution.py:241
  74.6 2.6 %collective-permute-done.14.rest_15_ = f32[128,128]{1,0:T(8,128)S(1)} collective-permute-done((f32[128,128]{1,0:T(8,128)S(1)}, f32[128,128]{1,0:T(8,128)S(1)}, u32[]{:S(2)}, u32[]{:S(2)}) %collective-permute-start.14) | collective-permute-done | bytes 65568 | tf_op jit(solution)/shard_map/ppermute | solution.py:241
  77.2 1.1 %place.1 = f32[2048,128]{1,0:T(8,128)} custom-call(f32[128,128]{1,0:T(8,128)S(1)} %get-tuple-element.25.rest_0_, f32[128,128]{1,0:T(8,128)S(1)} %collective-permute-done.rest_1_, f32[128,128]{1,0:T(8,128)S(1)} %collective-permute-done.1.rest_2_, f32[128,128]{1,0:T(8,128)S(1)} %collective-permute-done.2.rest_3_, ...), custom_call_target="tpu_custom_call" | custom-call | tf_op jit(solution)/shard_map/place/pallas_call | solution.py:245
  (13 shorter events, 0.0 us)
Async XLA Ops:
  0.0 7.6 %copy-start = (f32[6,128,128]{2,1,0:T(8,128)S(1)}, f32[6,128,128]{2,1,0:T(8,128)}, u32[]{:S(2)}) copy-start(f32[6,128,128]{2,1,0:T(8,128)} %re_ref.1) | copy-start | bytes 1179652
  0.0 7.6 %copy-start.1 = (f32[6,128,128]{2,1,0:T(8,128)S(1)}, f32[6,128,128]{2,1,0:T(8,128)}, u32[]{:S(2)}) copy-start(f32[6,128,128]{2,1,0:T(8,128)} %im_ref.1) | copy-start | bytes 1179652
  0.0 7.6 %copy-start.2 = (s32[6,16,2]{1,2,0:T(2,128)S(1)}, s32[6,16,2]{1,2,0:T(2,128)}, u32[]{:S(2)}) copy-start(s32[6,16,2]{1,2,0:T(2,128)} %param.10) | copy-start | bytes 2308
  0.0 7.6 %copy-start.3 = (f32[6,16]{1,0:T(8,128)S(1)}, f32[6,16]{1,0:T(8,128)}, u32[]{:S(2)}) copy-start(f32[6,16]{1,0:T(8,128)} %angle_ref.1) | copy-start | bytes 1156
  0.0 7.6 %copy-start.4 = (s32[6,8]{1,0:T(8,128)S(1)}, s32[6,8]{1,0:T(8,128)}, u32[]{:S(2)}) copy-start(s32[6,8]{1,0:T(8,128)} %order_ref.3) | copy-start | bytes 580
  0.0 30.5 %all-to-all-start = ((f32[16,128,128]{2,1,0:T(8,128)}), f32[16,128,128]{2,1,0:T(8,128)S(1)}, u32[]{:S(2)}, u32[]{:S(2)}) async-start(f32[16,128,128]{2,1,0:T(8,128)} %bitcast.14), calls=%async_computation | async-start | bytes 2097152 | tf_op jit(solution)/shard_map/all_to_all | solution.py:202
  46.2 10.5 %collective-permute-start = (f32[128,128]{1,0:T(8,128)S(1)}, f32[128,128]{1,0:T(8,128)S(1)}, u32[]{:S(2)}, u32[]{:S(2)}) collective-permute-start(f32[128,128]{1,0:T(8,128)S(1)} %get-tuple-element.26), channel_id=1, source_target_pairs={{0,16},{2,18},{4,20},{6,22},{8,24},{10,26},{12,28},{14,30},{16,0},... | collective-permute-start | bytes 196616 | tf_op jit(solution)/shard_map/ppermute | solution.py:241
  51.3 6.3 %collective-permute-start.1 = (f32[128,128]{1,0:T(8,128)S(1)}, f32[128,128]{1,0:T(8,128)S(1)}, u32[]{:S(2)}, u32[]{:S(2)}) collective-permute-start(f32[128,128]{1,0:T(8,128)S(1)} %get-tuple-element.27), channel_id=1, source_target_pairs={{0,18},{2,16},{4,22},{6,20},{8,26},{10,24},{12,30},{14,28},{16,2},... | collective-permute-start | bytes 196616 | tf_op jit(solution)/shard_map/ppermute | solution.py:241
  51.3 7.4 %collective-permute-start.2 = (f32[128,128]{1,0:T(8,128)S(1)}, f32[128,128]{1,0:T(8,128)S(1)}, u32[]{:S(2)}, u32[]{:S(2)}) collective-permute-start(f32[128,128]{1,0:T(8,128)S(1)} %get-tuple-element.28), channel_id=1, source_target_pairs={{0,8},{2,10},{4,12},{6,14},{8,0},{10,2},{12,4},{14,6},{16,24},{18,... | collective-permute-start | bytes 196616 | tf_op jit(solution)/shard_map/ppermute | solution.py:241
  52.5 7.3 %collective-permute-start.3 = (f32[128,128]{1,0:T(8,128)S(1)}, f32[128,128]{1,0:T(8,128)S(1)}, u32[]{:S(2)}, u32[]{:S(2)}) collective-permute-start(f32[128,128]{1,0:T(8,128)S(1)} %get-tuple-element.29), channel_id=1, source_target_pairs={{0,10},{2,8},{4,14},{6,12},{8,2},{10,0},{12,6},{14,4},{16,26},{18,... | collective-permute-start | bytes 196616 | tf_op jit(solution)/shard_map/ppermute | solution.py:241
  52.8 9.7 %collective-permute-start.4 = (f32[128,128]{1,0:T(8,128)S(1)}, f32[128,128]{1,0:T(8,128)S(1)}, u32[]{:S(2)}, u32[]{:S(2)}) collective-permute-start(f32[128,128]{1,0:T(8,128)S(1)} %get-tuple-element.30), channel_id=1, source_target_pairs={{0,20},{2,22},{4,16},{6,18},{8,28},{10,30},{12,24},{14,26},{16,4},... | collective-permute-start | bytes 196616 | tf_op jit(solution)/shard_map/ppermute | solution.py:241
  56.7 7.3 %collective-permute-start.5 = (f32[128,128]{1,0:T(8,128)S(1)}, f32[128,128]{1,0:T(8,128)S(1)}, u32[]{:S(2)}, u32[]{:S(2)}) collective-permute-start(f32[128,128]{1,0:T(8,128)S(1)} %get-tuple-element.31), channel_id=1, source_target_pairs={{0,22},{2,20},{4,18},{6,16},{8,30},{10,28},{12,26},{14,24},{16,6},... | collective-permute-start | bytes 196616 | tf_op jit(solution)/shard_map/ppermute | solution.py:241
  57.6 6.4 %collective-permute-start.6 = (f32[128,128]{1,0:T(8,128)S(1)}, f32[128,128]{1,0:T(8,128)S(1)}, u32[]{:S(2)}, u32[]{:S(2)}) collective-permute-start(f32[128,128]{1,0:T(8,128)S(1)} %get-tuple-element.32), channel_id=1, source_target_pairs={{0,4},{2,6},{4,0},{6,2},{8,12},{10,14},{12,8},{14,10},{16,20},{18,... | collective-permute-start | bytes 196616 | tf_op jit(solution)/shard_map/ppermute | solution.py:241
  58.7 8.6 %collective-permute-start.7 = (f32[128,128]{1,0:T(8,128)S(1)}, f32[128,128]{1,0:T(8,128)S(1)}, u32[]{:S(2)}, u32[]{:S(2)}) collective-permute-start(f32[128,128]{1,0:T(8,128)S(1)} %get-tuple-element.33), channel_id=1, source_target_pairs={{0,6},{2,4},{4,2},{6,0},{8,14},{10,12},{12,10},{14,8},{16,22},{18,... | collective-permute-start | bytes 196616 | tf_op jit(solution)/shard_map/ppermute | solution.py:241
  59.8 7.5 %collective-permute-start.8 = (f32[128,128]{1,0:T(8,128)S(1)}, f32[128,128]{1,0:T(8,128)S(1)}, u32[]{:S(2)}, u32[]{:S(2)}) collective-permute-start(f32[128,128]{1,0:T(8,128)S(1)} %get-tuple-element.34), channel_id=1, source_target_pairs={{0,24},{2,26},{4,28},{6,30},{8,16},{10,18},{12,20},{14,22},{16,8},... | collective-permute-start | bytes 196616 | tf_op jit(solution)/shard_map/ppermute | solution.py:241
  62.5 7.7 %collective-permute-start.9 = (f32[128,128]{1,0:T(8,128)S(1)}, f32[128,128]{1,0:T(8,128)S(1)}, u32[]{:S(2)}, u32[]{:S(2)}) collective-permute-start(f32[128,128]{1,0:T(8,128)S(1)} %get-tuple-element.35), channel_id=1, source_target_pairs={{0,26},{2,24},{4,30},{6,28},{8,18},{10,16},{12,22},{14,20},{16,10}... | collective-permute-start | bytes 196616 | tf_op jit(solution)/shard_map/ppermute | solution.py:241
  64.0 7.9 %collective-permute-start.10 = (f32[128,128]{1,0:T(8,128)S(1)}, f32[128,128]{1,0:T(8,128)S(1)}, u32[]{:S(2)}, u32[]{:S(2)}) collective-permute-start(f32[128,128]{1,0:T(8,128)S(1)} %get-tuple-element.36), channel_id=1, source_target_pairs={{0,12},{2,14},{4,8},{6,10},{8,4},{10,6},{12,0},{14,2},{16,28},{18,... | collective-permute-start | bytes 196616 | tf_op jit(solution)/shard_map/ppermute | solution.py:241
  64.0 8.7 %collective-permute-start.11 = (f32[128,128]{1,0:T(8,128)S(1)}, f32[128,128]{1,0:T(8,128)S(1)}, u32[]{:S(2)}, u32[]{:S(2)}) collective-permute-start(f32[128,128]{1,0:T(8,128)S(1)} %get-tuple-element.37), channel_id=1, source_target_pairs={{0,14},{2,12},{4,10},{6,8},{8,6},{10,4},{12,2},{14,0},{16,30},{18,... | collective-permute-start | bytes 196616 | tf_op jit(solution)/shard_map/ppermute | solution.py:241
  67.3 5.3 %collective-permute-start.12 = (f32[128,128]{1,0:T(8,128)S(1)}, f32[128,128]{1,0:T(8,128)S(1)}, u32[]{:S(2)}, u32[]{:S(2)}) collective-permute-start(f32[128,128]{1,0:T(8,128)S(1)} %get-tuple-element.38), channel_id=1, source_target_pairs={{0,2},{2,0},{4,6},{6,4},{8,10},{10,8},{12,14},{14,12},{16,18},{18,... | collective-permute-start | bytes 196616 | tf_op jit(solution)/shard_map/ppermute | solution.py:241
  67.3 7.3 %collective-permute-start.13 = (f32[128,128]{1,0:T(8,128)S(1)}, f32[128,128]{1,0:T(8,128)S(1)}, u32[]{:S(2)}, u32[]{:S(2)}) collective-permute-start(f32[128,128]{1,0:T(8,128)S(1)} %get-tuple-element.39), channel_id=1, source_target_pairs={{0,28},{2,30},{4,24},{6,26},{8,20},{10,22},{12,16},{14,18},{16,12}... | collective-permute-start | bytes 196616 | tf_op jit(solution)/shard_map/ppermute | solution.py:241
  70.2 7.0 %collective-permute-start.14 = (f32[128,128]{1,0:T(8,128)S(1)}, f32[128,128]{1,0:T(8,128)S(1)}, u32[]{:S(2)}, u32[]{:S(2)}) collective-permute-start(f32[128,128]{1,0:T(8,128)S(1)} %get-tuple-element.40), channel_id=1, source_target_pairs={{0,30},{2,28},{4,26},{6,24},{8,22},{10,20},{12,18},{14,16},{16,14}... | collective-permute-start | bytes 196616 | tf_op jit(solution)/shard_map/ppermute | solution.py:241

commit v9 on v6

--- a/solution.py
+++ b/solution.py
@@ -27,14 +27,13 @@
 
 
 def exchange_order(wide):
-    far = list(range(wide // 2, wide, 2))
-    near = [k for top in (wide // 4, wide // 8) for k in range(top, 2 * top, 2) if top > 1]
-    near += [k for k in range(wide // 2 - 2, 0, -2) if k not in near]
-    pairs = []
-    for i, k in enumerate(far):
-        pairs += [k] + near[i : i + 1] * (i < len(near) - 1)
-    pairs += near[-1:]
-    return [0] + [k + j for k in pairs for j in range(2)] + [1]
+    far = list(range(wide // 2, wide))
+    near = [k for low in (wide // 4, wide // 8, wide // 16) for k in range(low, 2 * low) if k]
+    near += [k for k in range(wide // 2 - 1, 0, -1) if k not in near]
+    order = [0] + far[:4]
+    for i, k in enumerate(near):
+        order += [k] + far[4 + i : 5 + i]
+    return order + far[4 + len(near) :]
 
 
 def block_of(ref, k, wide):

time: 75.8 us -> 76.9 us (1.015)
  waiting for transfers between devices: 14.1 us -> 20.3 us
  starting transfers between devices: 41.2 us -> 36.2 us
    ppermute x30, waiting for transfers between devices: 14.1 us -> 20.3 us  [swap(): lax.ppermute(block, 'wide', [(i, i ^ k) for i in range(wide)])]
    ppermute x30, starting transfers between devices: 41.2 us -> 36.2 us  [swap(): lax.ppermute(block, 'wide', [(i, i ^ k) for i in range(wide)])]
  transfers between devices with their start and end apart: 30 -> 30, of which waited for: 13 -> 15; matrix products, arithmetic and copies ran while one was open for 0% -> 0% of each run, Pallas kernels for 7% -> 6%
where the time goes in v9:
time: 76.9 us; the launch traced here: 76.6 us
  starting transfers between devices  36.2 us (47%)
  waiting for transfers between devices  20.3 us (26%)
  Pallas kernels  14.8 us (19%)
  local copies, waits for them, and re-layouts  5.28 us (7%)
    ppermute x30, starting transfers between devices, swap(): lax.ppermute(block, 'wide', [(i, i ^ k) for i in range(wide)])  36.2 us
    ppermute x30, waiting for transfers between devices, swap(): lax.ppermute(block, 'wide', [(i, i ^ k) for i in range(wide)])  20.3 us
    pallas_call x1, Pallas kernels, local(): pl.pallas_call(partial(layers_kernel, wide, spect), in_specs=[in_vmem] *...  8.33 us
    unnamed x12, local copies, waits for them, and re-layouts  5.28 us
    pallas_call x1, Pallas kernels, local(): pl.pallas_call(partial(tables_kernel, wide, late, spect, narrow), in_spec...  4.94 us
  transfers between devices with their start and end apart: 30, of which 15 were waited for; matrix products, arithmetic and copies ran while one was open for 0% of the time, Pallas kernels for 6%

profile of v9, /device:TPU:0, one launch (start us, length us, event | category | flops | bytes accessed | tf_op | source)
XLA Modules:
  0.0 76.6 jit_solution(3238781432674093810)
XLA Ops:
  0.0 1.2 %copy-done = f32[2,131072]{1,0:T(2,128)S(1)} copy-done((f32[2,131072]{1,0:T(2,128)S(1)}, f32[2,131072]{1,0:T(2,128)}, u32[]{:S(2)}) %copy-start) | copy-done | bytes 1048600
  1.7 4.1 %collective-permute-start = (f32[128,128]{1,0:T(8,128)S(1)}, f32[128,128]{1,0:T(8,128)S(1)}, u32[]{:S(2)}, u32[]{:S(2)}) collective-permute-start(f32[128,128]{1,0:T(8,128)S(1)} %get-tuple-element.41), channel_id=1, source_target_pairs={{0,16},{2,18},{4,20},{6,22},{8,24},{10,26},{12,28},{14,30},{16,0},... | collective-permute-start | bytes 196616 | tf_op jit(solution)/shard_map/ppermute | solution.py:217
  5.8 3.0 %collective-permute-start.2 = (f32[128,128]{1,0:T(8,128)S(1)}, f32[128,128]{1,0:T(8,128)S(1)}, u32[]{:S(2)}, u32[]{:S(2)}) collective-permute-start(f32[128,128]{1,0:T(8,128)S(1)} %get-tuple-element.43), channel_id=1, source_target_pairs={{0,20},{2,22},{4,16},{6,18},{8,28},{10,30},{12,24},{14,26},{16,4},... | collective-permute-start | bytes 196616 | tf_op jit(solution)/shard_map/ppermute | solution.py:217
  9.4 1.6 %collective-permute-start.4 = (f32[128,128]{1,0:T(8,128)S(1)}, f32[128,128]{1,0:T(8,128)S(1)}, u32[]{:S(2)}, u32[]{:S(2)}) collective-permute-start(f32[128,128]{1,0:T(8,128)S(1)} %get-tuple-element.45), channel_id=1, source_target_pairs={{0,8},{2,10},{4,12},{6,14},{8,0},{10,2},{12,4},{14,6},{16,24},{18,... | collective-permute-start | bytes 196616 | tf_op jit(solution)/shard_map/ppermute | solution.py:217
  11.0 1.0 %copy-done.1 = f32[6,128,128]{2,1,0:T(8,128)S(1)} copy-done((f32[6,128,128]{2,1,0:T(8,128)S(1)}, f32[6,128,128]{2,1,0:T(8,128)}, u32[]{:S(2)}) %copy-start.1) | copy-done | bytes 393240
  12.0 1.0 %copy-done.2 = f32[6,128,128]{2,1,0:T(8,128)S(1)} copy-done((f32[6,128,128]{2,1,0:T(8,128)S(1)}, f32[6,128,128]{2,1,0:T(8,128)}, u32[]{:S(2)}) %copy-start.2) | copy-done | bytes 393240
  15.0 4.9 %tables.1 = (f32[128,128]{1,0:T(8,128)S(1)}, f32[128,128]{1,0:T(8,128)S(1)}, f32[128,128]{1,0:T(8,128)S(1)}, f32[128,128]{1,0:T(8,128)S(1)}, f32[128,128]{1,0:T(...) custom-call(f32[2048,128]{1,0:T(8,128)S(1)} %bitcast.12, ...), custom_call_target="tpu_custom_call" | custom-call | flops 1000000000 | bytes 8000000 | tf_op jit(solution)/shard_map/tables/pallas_call | solution.py:233
  20.0 2.5 %collective-permute-start.5 = (f32[128,128]{1,0:T(8,128)S(1)}, f32[128,128]{1,0:T(8,128)S(1)}, u32[]{:S(2)}, u32[]{:S(2)}) collective-permute-start(f32[128,128]{1,0:T(8,128)S(1)} %get-tuple-element.46), channel_id=1, source_target_pairs={{0,24},{2,26},{4,28},{6,30},{8,16},{10,18},{12,20},{14,22},{16,8},... | collective-permute-start | bytes 196616 | tf_op jit(solution)/shard_map/ppermute | solution.py:217
  22.5 1.4 %collective-permute-start.7 = (f32[128,128]{1,0:T(8,128)S(1)}, f32[128,128]{1,0:T(8,128)S(1)}, u32[]{:S(2)}, u32[]{:S(2)}) collective-permute-start(f32[128,128]{1,0:T(8,128)S(1)} %get-tuple-element.48), channel_id=1, source_target_pairs={{0,26},{2,24},{4,30},{6,28},{8,18},{10,16},{12,22},{14,20},{16,10}... | collective-permute-start | bytes 196616 | tf_op jit(solution)/shard_map/ppermute | solution.py:217
  23.9 1.8 %collective-permute-start.8 = (f32[128,128]{1,0:T(8,128)S(1)}, f32[128,128]{1,0:T(8,128)S(1)}, u32[]{:S(2)}, u32[]{:S(2)}) collective-permute-start(f32[128,128]{1,0:T(8,128)S(1)} %get-tuple-element.49), channel_id=1, source_target_pairs={{0,12},{2,14},{4,8},{6,10},{8,4},{10,6},{12,0},{14,2},{16,28},{18,... | collective-permute-start | bytes 196616 | tf_op jit(solution)/shard_map/ppermute | solution.py:217
  25.7 2.4 %collective-permute-start.9 = (f32[128,128]{1,0:T(8,128)S(1)}, f32[128,128]{1,0:T(8,128)S(1)}, u32[]{:S(2)}, u32[]{:S(2)}) collective-permute-start(f32[128,128]{1,0:T(8,128)S(1)} %get-tuple-element.50), channel_id=1, source_target_pairs={{0,28},{2,30},{4,24},{6,26},{8,20},{10,22},{12,16},{14,18},{16,12}... | collective-permute-start | bytes 196616 | tf_op jit(solution)/shard_map/ppermute | solution.py:217
  28.6 1.9 %collective-permute-start.11 = (f32[128,128]{1,0:T(8,128)S(1)}, f32[128,128]{1,0:T(8,128)S(1)}, u32[]{:S(2)}, u32[]{:S(2)}) collective-permute-start(f32[128,128]{1,0:T(8,128)S(1)} %get-tuple-element.52), channel_id=1, source_target_pairs={{0,30},{2,28},{4,26},{6,24},{8,22},{10,20},{12,18},{14,16},{16,14}... | collective-permute-start | bytes 196616 | tf_op jit(solution)/shard_map/ppermute | solution.py:217
  30.4 1.5 %collective-permute-start.12 = (f32[128,128]{1,0:T(8,128)S(1)}, f32[128,128]{1,0:T(8,128)S(1)}, u32[]{:S(2)}, u32[]{:S(2)}) collective-permute-start(f32[128,128]{1,0:T(8,128)S(1)} %get-tuple-element.53), channel_id=1, source_target_pairs={{0,4},{2,6},{4,0},{6,2},{8,12},{10,14},{12,8},{14,10},{16,20},{18,... | collective-permute-start | bytes 196616 | tf_op jit(solution)/shard_map/ppermute | solution.py:217
  32.0 1.3 %collective-permute-done.9.rest_10_ = f32[128,128]{1,0:T(8,128)S(1)} collective-permute-done((f32[128,128]{1,0:T(8,128)S(1)}, f32[128,128]{1,0:T(8,128)S(1)}, u32[]{:S(2)}, u32[]{:S(2)}) %collective-permute-start.9) | collective-permute-done | bytes 65568 | tf_op jit(solution)/shard_map/ppermute | solution.py:217
  34.1 1.0 %collective-permute-done.11.rest_12_ = f32[128,128]{1,0:T(8,128)S(1)} collective-permute-done((f32[128,128]{1,0:T(8,128)S(1)}, f32[128,128]{1,0:T(8,128)S(1)}, u32[]{:S(2)}, u32[]{:S(2)}) %collective-permute-start.11) | collective-permute-done | bytes 65568 | tf_op jit(solution)/shard_map/ppermute | solution.py:217
  35.0 1.8 %collective-permute-done.12.rest_13_ = f32[128,128]{1,0:T(8,128)S(1)} collective-permute-done((f32[128,128]{1,0:T(8,128)S(1)}, f32[128,128]{1,0:T(8,128)S(1)}, u32[]{:S(2)}, u32[]{:S(2)}) %collective-permute-start.12) | collective-permute-done | bytes 65568 | tf_op jit(solution)/shard_map/ppermute | solution.py:217
  36.9 1.3 %collective-permute-done.13.rest_14_ = f32[128,128]{1,0:T(8,128)S(1)} collective-permute-done((f32[128,128]{1,0:T(8,128)S(1)}, f32[128,128]{1,0:T(8,128)S(1)}, u32[]{:S(2)}, u32[]{:S(2)}) %collective-permute-start.13) | collective-permute-done | bytes 65568 | tf_op jit(solution)/shard_map/ppermute | solution.py:217
  38.1 8.3 %layers.1 = (f32[128,128]{1,0:T(8,128)S(1)}, f32[128,128]{1,0:T(8,128)S(1)}, f32[128,128]{1,0:T(8,128)S(1)}, f32[128,128]{1,0:T(8,128)S(1)}, f32[128,128]{1,0:T(...) custom-call(f32[128,128]{1,0:T(8,128)S(1)} %get-tuple-element.40.res, ...), custom_call_target="tpu_custom_call" | custom-call | flops 5000000000 | bytes 10000000 | tf_op jit(solution)/shard_map/layers/pallas_call | solution.py:251
  47.1 1.8 %collective-permute-start.16 = (f32[128,128]{1,0:T(8,128)S(1)}, f32[128,128]{1,0:T(8,128)S(1)}, u32[]{:S(2)}, u32[]{:S(2)}) collective-permute-start(f32[128,128]{1,0:T(8,128)S(1)} %get-tuple-element.61), channel_id=1, source_target_pairs={{0,18},{2,16},{4,22},{6,20},{8,26},{10,24},{12,30},{14,28},{16,2},... | collective-permute-start | bytes 196616 | tf_op jit(solution)/shard_map/ppermute | solution.py:217
  49.7 3.0 %collective-permute-start.18 = (f32[128,128]{1,0:T(8,128)S(1)}, f32[128,128]{1,0:T(8,128)S(1)}, u32[]{:S(2)}, u32[]{:S(2)}) collective-permute-start(f32[128,128]{1,0:T(8,128)S(1)} %get-tuple-element.63), channel_id=1, source_target_pairs={{0,22},{2,20},{4,18},{6,16},{8,30},{10,28},{12,26},{14,24},{16,6},... | collective-permute-start | bytes 196616 | tf_op jit(solution)/shard_map/ppermute | solution.py:217
  53.3 4.1 %collective-permute-done.15.rest_1_ = f32[128,128]{1,0:T(8,128)S(1)} collective-permute-done((f32[128,128]{1,0:T(8,128)S(1)}, f32[128,128]{1,0:T(8,128)S(1)}, u32[]{:S(2)}, u32[]{:S(2)}) %collective-permute-start.15) | collective-permute-done | bytes 65568 | tf_op jit(solution)/shard_map/ppermute | solution.py:217
  57.4 1.1 %collective-permute-done.16.rest_2_ = f32[128,128]{1,0:T(8,128)S(1)} collective-permute-done((f32[128,128]{1,0:T(8,128)S(1)}, f32[128,128]{1,0:T(8,128)S(1)}, u32[]{:S(2)}, u32[]{:S(2)}) %collective-permute-start.16) | collective-permute-done | bytes 65568 | tf_op jit(solution)/shard_map/ppermute | solution.py:217
  58.5 2.5 %collective-permute-done.17.rest_3_ = f32[128,128]{1,0:T(8,128)S(1)} collective-permute-done((f32[128,128]{1,0:T(8,128)S(1)}, f32[128,128]{1,0:T(8,128)S(1)}, u32[]{:S(2)}, u32[]{:S(2)}) %collective-permute-start.17) | collective-permute-done | bytes 65568 | tf_op jit(solution)/shard_map/ppermute | solution.py:217
  62.4 2.6 %collective-permute-start.24 = (f32[128,128]{1,0:T(8,128)S(1)}, f32[128,128]{1,0:T(8,128)S(1)}, u32[]{:S(2)}, u32[]{:S(2)}) collective-permute-start(f32[128,128]{1,0:T(8,128)S(1)} %get-tuple-element.69), channel_id=1, source_target_pairs={{0,28},{2,30},{4,24},{6,26},{8,20},{10,22},{12,16},{14,18},{16,12}... | collective-permute-start | bytes 196616 | tf_op jit(solution)/shard_map/ppermute | solution.py:217
  65.1 1.2 %collective-permute-start.25 = (f32[128,128]{1,0:T(8,128)S(1)}, f32[128,128]{1,0:T(8,128)S(1)}, u32[]{:S(2)}, u32[]{:S(2)}) collective-permute-start(f32[128,128]{1,0:T(8,128)S(1)} %get-tuple-element.70), channel_id=1, source_target_pairs={{0,14},{2,12},{4,10},{6,8},{8,6},{10,4},{12,2},{14,0},{16,30},{18,... | collective-permute-start | bytes 196616 | tf_op jit(solution)/shard_map/ppermute | solution.py:217
  66.2 2.0 %collective-permute-start.26 = (f32[128,128]{1,0:T(8,128)S(1)}, f32[128,128]{1,0:T(8,128)S(1)}, u32[]{:S(2)}, u32[]{:S(2)}) collective-permute-start(f32[128,128]{1,0:T(8,128)S(1)} %get-tuple-element.71), channel_id=1, source_target_pairs={{0,30},{2,28},{4,26},{6,24},{8,22},{10,20},{12,18},{14,16},{16,14}... | collective-permute-start | bytes 196616 | tf_op jit(solution)/shard_map/ppermute | solution.py:217
  68.2 1.0 %collective-permute-start.27 = (f32[128,128]{1,0:T(8,128)S(1)}, f32[128,128]{1,0:T(8,128)S(1)}, u32[]{:S(2)}, u32[]{:S(2)}) collective-permute-start(f32[128,128]{1,0:T(8,128)S(1)} %get-tuple-element.72), channel_id=1, source_target_pairs={{0,4},{2,6},{4,0},{6,2},{8,12},{10,14},{12,8},{14,10},{16,20},{18,... | collective-permute-start | bytes 196616 | tf_op jit(solution)/shard_map/ppermute | solution.py:217
  70.4 1.2 %collective-permute-done.25.rest_11_ = f32[128,128]{1,0:T(8,128)S(1)} collective-permute-done((f32[128,128]{1,0:T(8,128)S(1)}, f32[128,128]{1,0:T(8,128)S(1)}, u32[]{:S(2)}, u32[]{:S(2)}) %collective-permute-start.25) | collective-permute-done | bytes 65568 | tf_op jit(solution)/shard_map/ppermute | solution.py:217
  71.6 1.1 %collective-permute-done.26.rest_12_ = f32[128,128]{1,0:T(8,128)S(1)} collective-permute-done((f32[128,128]{1,0:T(8,128)S(1)}, f32[128,128]{1,0:T(8,128)S(1)}, u32[]{:S(2)}, u32[]{:S(2)}) %collective-permute-start.26) | collective-permute-done | bytes 65568 | tf_op jit(solution)/shard_map/ppermute | solution.py:217
  72.8 1.8 %collective-permute-done.27.rest_13_ = f32[128,128]{1,0:T(8,128)S(1)} collective-permute-done((f32[128,128]{1,0:T(8,128)S(1)}, f32[128,128]{1,0:T(8,128)S(1)}, u32[]{:S(2)}, u32[]{:S(2)}) %collective-permute-start.27) | collective-permute-done | bytes 65568 | tf_op jit(solution)/shard_map/ppermute | solution.py:217
  74.6 0.9 %collective-permute-done.28.rest_14_ = f32[128,128]{1,0:T(8,128)S(1)} collective-permute-done((f32[128,128]{1,0:T(8,128)S(1)}, f32[128,128]{1,0:T(8,128)S(1)}, u32[]{:S(2)}, u32[]{:S(2)}) %collective-permute-start.28) | collective-permute-done | bytes 65568 | tf_op jit(solution)/shard_map/ppermute | solution.py:217
  75.5 1.1 %place.1 = f32[2048,128]{1,0:T(8,128)} custom-call(f32[128,128]{1,0:T(8,128)S(1)} %get-tuple-element.59.rest_0_, f32[128,128]{1,0:T(8,128)S(1)} %collective-permute-done.15.rest_1_, f32[128,128]{1,0:T(8,128)S(1)} %collective-permute-done.16.rest_2_, f32[128,128]{1,0:T(8,128)S(1)} %collective-permute-done.17.rest_3_, ...), custom_call_target="tpu_custom_call" | custom-call | tf_op jit(solution)/shard_map/place/pallas_call | solution.py:266
  (44 shorter events, 9.1 us)
Async XLA Ops:
  0.0 1.2 %copy-start = (f32[2,131072]{1,0:T(2,128)S(1)}, f32[2,131072]{1,0:T(2,128)}, u32[]{:S(2)}) copy-start(f32[2,131072]{1,0:T(2,128)} %param.6) | copy-start | bytes 3145732
  1.7 18.3 %collective-permute-start = (f32[128,128]{1,0:T(8,128)S(1)}, f32[128,128]{1,0:T(8,128)S(1)}, u32[]{:S(2)}, u32[]{:S(2)}) collective-permute-start(f32[128,128]{1,0:T(8,128)S(1)} %get-tuple-element.41), channel_id=1, source_target_pairs={{0,16},{2,18},{4,20},{6,22},{8,24},{10,26},{12,28},{14,30},{16,0},... | collective-permute-start | bytes 196616 | tf_op jit(solution)/shard_map/ppermute | solution.py:217
  5.8 16.7 %collective-permute-start.1 = (f32[128,128]{1,0:T(8,128)S(1)}, f32[128,128]{1,0:T(8,128)S(1)}, u32[]{:S(2)}, u32[]{:S(2)}) collective-permute-start(f32[128,128]{1,0:T(8,128)S(1)} %get-tuple-element.42), channel_id=1, source_target_pairs={{0,18},{2,16},{4,22},{6,20},{8,26},{10,24},{12,30},{14,28},{16,2},... | collective-permute-start | bytes 196616 | tf_op jit(solution)/shard_map/ppermute | solution.py:217
  5.8 16.7 %collective-permute-start.2 = (f32[128,128]{1,0:T(8,128)S(1)}, f32[128,128]{1,0:T(8,128)S(1)}, u32[]{:S(2)}, u32[]{:S(2)}) collective-permute-start(f32[128,128]{1,0:T(8,128)S(1)} %get-tuple-element.43), channel_id=1, source_target_pairs={{0,20},{2,22},{4,16},{6,18},{8,28},{10,30},{12,24},{14,26},{16,4},... | collective-permute-start | bytes 196616 | tf_op jit(solution)/shard_map/ppermute | solution.py:217
  8.8 15.1 %collective-permute-start.3 = (f32[128,128]{1,0:T(8,128)S(1)}, f32[128,128]{1,0:T(8,128)S(1)}, u32[]{:S(2)}, u32[]{:S(2)}) collective-permute-start(f32[128,128]{1,0:T(8,128)S(1)} %get-tuple-element.44), channel_id=1, source_target_pairs={{0,22},{2,20},{4,18},{6,16},{8,30},{10,28},{12,26},{14,24},{16,6},... | collective-permute-start | bytes 196616 | tf_op jit(solution)/shard_map/ppermute | solution.py:217
  9.4 16.3 %collective-permute-start.4 = (f32[128,128]{1,0:T(8,128)S(1)}, f32[128,128]{1,0:T(8,128)S(1)}, u32[]{:S(2)}, u32[]{:S(2)}) collective-permute-start(f32[128,128]{1,0:T(8,128)S(1)} %get-tuple-element.45), channel_id=1, source_target_pairs={{0,8},{2,10},{4,12},{6,14},{8,0},{10,2},{12,4},{14,6},{16,24},{18,... | collective-permute-start | bytes 196616 | tf_op jit(solution)/shard_map/ppermute | solution.py:217
  11.0 1.0 %copy-start.1 = (f32[6,128,128]{2,1,0:T(8,128)S(1)}, f32[6,128,128]{2,1,0:T(8,128)}, u32[]{:S(2)}) copy-start(f32[6,128,128]{2,1,0:T(8,128)} %re_hbm.1) | copy-start | bytes 1179652
  20.0 8.1 %collective-permute-start.5 = (f32[128,128]{1,0:T(8,128)S(1)}, f32[128,128]{1,0:T(8,128)S(1)}, u32[]{:S(2)}, u32[]{:S(2)}) collective-permute-start(f32[128,128]{1,0:T(8,128)S(1)} %get-tuple-element.46), channel_id=1, source_target_pairs={{0,24},{2,26},{4,28},{6,30},{8,16},{10,18},{12,20},{14,22},{16,8},... | collective-permute-start | bytes 196616 | tf_op jit(solution)/shard_map/ppermute | solution.py:217
  22.5 6.1 %collective-permute-start.6 = (f32[128,128]{1,0:T(8,128)S(1)}, f32[128,128]{1,0:T(8,128)S(1)}, u32[]{:S(2)}, u32[]{:S(2)}) collective-permute-start(f32[128,128]{1,0:T(8,128)S(1)} %get-tuple-element.47), channel_id=1, source_target_pairs={{0,10},{2,8},{4,14},{6,12},{8,2},{10,0},{12,6},{14,4},{16,26},{18,... | collective-permute-start | bytes 196616 | tf_op jit(solution)/shard_map/ppermute | solution.py:217
  22.5 7.9 %collective-permute-start.7 = (f32[128,128]{1,0:T(8,128)S(1)}, f32[128,128]{1,0:T(8,128)S(1)}, u32[]{:S(2)}, u32[]{:S(2)}) collective-permute-start(f32[128,128]{1,0:T(8,128)S(1)} %get-tuple-element.48), channel_id=1, source_target_pairs={{0,26},{2,24},{4,30},{6,28},{8,18},{10,16},{12,22},{14,20},{16,10}... | collective-permute-start | bytes 196616 | tf_op jit(solution)/shard_map/ppermute | solution.py:217
  23.9 8.0 %collective-permute-start.8 = (f32[128,128]{1,0:T(8,128)S(1)}, f32[128,128]{1,0:T(8,128)S(1)}, u32[]{:S(2)}, u32[]{:S(2)}) collective-permute-start(f32[128,128]{1,0:T(8,128)S(1)} %get-tuple-element.49), channel_id=1, source_target_pairs={{0,12},{2,14},{4,8},{6,10},{8,4},{10,6},{12,0},{14,2},{16,28},{18,... | collective-permute-start | bytes 196616 | tf_op jit(solution)/shard_map/ppermute | solution.py:217
  25.7 7.6 %collective-permute-start.9 = (f32[128,128]{1,0:T(8,128)S(1)}, f32[128,128]{1,0:T(8,128)S(1)}, u32[]{:S(2)}, u32[]{:S(2)}) collective-permute-start(f32[128,128]{1,0:T(8,128)S(1)} %get-tuple-element.50), channel_id=1, source_target_pairs={{0,28},{2,30},{4,24},{6,26},{8,20},{10,22},{12,16},{14,18},{16,12}... | collective-permute-start | bytes 196616 | tf_op jit(solution)/shard_map/ppermute | solution.py:217
  28.1 6.0 %collective-permute-start.10 = (f32[128,128]{1,0:T(8,128)S(1)}, f32[128,128]{1,0:T(8,128)S(1)}, u32[]{:S(2)}, u32[]{:S(2)}) collective-permute-start(f32[128,128]{1,0:T(8,128)S(1)} %get-tuple-element.51), channel_id=1, source_target_pairs={{0,14},{2,12},{4,10},{6,8},{8,6},{10,4},{12,2},{14,0},{16,30},{18,... | collective-permute-start | bytes 196616 | tf_op jit(solution)/shard_map/ppermute | solution.py:217
  28.6 6.5 %collective-permute-start.11 = (f32[128,128]{1,0:T(8,128)S(1)}, f32[128,128]{1,0:T(8,128)S(1)}, u32[]{:S(2)}, u32[]{:S(2)}) collective-permute-start(f32[128,128]{1,0:T(8,128)S(1)} %get-tuple-element.52), channel_id=1, source_target_pairs={{0,30},{2,28},{4,26},{6,24},{8,22},{10,20},{12,18},{14,16},{16,14}... | collective-permute-start | bytes 196616 | tf_op jit(solution)/shard_map/ppermute | solution.py:217
  30.4 6.4 %collective-permute-start.12 = (f32[128,128]{1,0:T(8,128)S(1)}, f32[128,128]{1,0:T(8,128)S(1)}, u32[]{:S(2)}, u32[]{:S(2)}) collective-permute-start(f32[128,128]{1,0:T(8,128)S(1)} %get-tuple-element.53), channel_id=1, source_target_pairs={{0,4},{2,6},{4,0},{6,2},{8,12},{10,14},{12,8},{14,10},{16,20},{18,... | collective-permute-start | bytes 196616 | tf_op jit(solution)/shard_map/ppermute | solution.py:217
  31.9 6.2 %collective-permute-start.13 = (f32[128,128]{1,0:T(8,128)S(1)}, f32[128,128]{1,0:T(8,128)S(1)}, u32[]{:S(2)}, u32[]{:S(2)}) collective-permute-start(f32[128,128]{1,0:T(8,128)S(1)} %get-tuple-element.54), channel_id=1, source_target_pairs={{0,6},{2,4},{4,2},{6,0},{8,14},{10,12},{12,10},{14,8},{16,22},{18,... | collective-permute-start | bytes 196616 | tf_op jit(solution)/shard_map/ppermute | solution.py:217
  33.3 4.9 %collective-permute-start.14 = (f32[128,128]{1,0:T(8,128)S(1)}, f32[128,128]{1,0:T(8,128)S(1)}, u32[]{:S(2)}, u32[]{:S(2)}) collective-permute-start(f32[128,128]{1,0:T(8,128)S(1)} %get-tuple-element.55), channel_id=1, source_target_pairs={{0,2},{2,0},{4,6},{6,4},{8,10},{10,8},{12,14},{14,12},{16,18},{18,... | collective-permute-start | bytes 196616 | tf_op jit(solution)/shard_map/ppermute | solution.py:217
  46.4 10.9 %collective-permute-start.15 = (f32[128,128]{1,0:T(8,128)S(1)}, f32[128,128]{1,0:T(8,128)S(1)}, u32[]{:S(2)}, u32[]{:S(2)}) collective-permute-start(f32[128,128]{1,0:T(8,128)S(1)} %get-tuple-element.60), channel_id=1, source_target_pairs={{0,16},{2,18},{4,20},{6,22},{8,24},{10,26},{12,28},{14,30},{16,0},... | collective-permute-start | bytes 196616 | tf_op jit(solution)/shard_map/ppermute | solution.py:217
  47.1 11.4 %collective-permute-start.16 = (f32[128,128]{1,0:T(8,128)S(1)}, f32[128,128]{1,0:T(8,128)S(1)}, u32[]{:S(2)}, u32[]{:S(2)}) collective-permute-start(f32[128,128]{1,0:T(8,128)S(1)} %get-tuple-element.61), channel_id=1, source_target_pairs={{0,18},{2,16},{4,22},{6,20},{8,26},{10,24},{12,30},{14,28},{16,2},... | collective-permute-start | bytes 196616 | tf_op jit(solution)/shard_map/ppermute | solution.py:217
  48.9 12.1 %collective-permute-start.17 = (f32[128,128]{1,0:T(8,128)S(1)}, f32[128,128]{1,0:T(8,128)S(1)}, u32[]{:S(2)}, u32[]{:S(2)}) collective-permute-start(f32[128,128]{1,0:T(8,128)S(1)} %get-tuple-element.62), channel_id=1, source_target_pairs={{0,20},{2,22},{4,16},{6,18},{8,28},{10,30},{12,24},{14,26},{16,4},... | collective-permute-start | bytes 196616 | tf_op jit(solution)/shard_map/ppermute | solution.py:217
  49.7 12.0 %collective-permute-start.18 = (f32[128,128]{1,0:T(8,128)S(1)}, f32[128,128]{1,0:T(8,128)S(1)}, u32[]{:S(2)}, u32[]{:S(2)}) collective-permute-start(f32[128,128]{1,0:T(8,128)S(1)} %get-tuple-element.63), channel_id=1, source_target_pairs={{0,22},{2,20},{4,18},{6,16},{8,30},{10,28},{12,26},{14,24},{16,6},... | collective-permute-start | bytes 196616 | tf_op jit(solution)/shard_map/ppermute | solution.py:217
  52.7 9.7 %collective-permute-start.19 = (f32[128,128]{1,0:T(8,128)S(1)}, f32[128,128]{1,0:T(8,128)S(1)}, u32[]{:S(2)}, u32[]{:S(2)}) collective-permute-start(f32[128,128]{1,0:T(8,128)S(1)} %get-tuple-element.64), channel_id=1, source_target_pairs={{0,8},{2,10},{4,12},{6,14},{8,0},{10,2},{12,4},{14,6},{16,24},{18,... | collective-permute-start | bytes 196616 | tf_op jit(solution)/shard_map/ppermute | solution.py:217
  57.4 7.7 %collective-permute-start.20 = (f32[128,128]{1,0:T(8,128)S(1)}, f32[128,128]{1,0:T(8,128)S(1)}, u32[]{:S(2)}, u32[]{:S(2)}) collective-permute-start(f32[128,128]{1,0:T(8,128)S(1)} %get-tuple-element.65), channel_id=1, source_target_pairs={{0,24},{2,26},{4,28},{6,30},{8,16},{10,18},{12,20},{14,22},{16,8},... | collective-permute-start | bytes 196616 | tf_op jit(solution)/shard_map/ppermute | solution.py:217
  58.5 7.7 %collective-permute-start.21 = (f32[128,128]{1,0:T(8,128)S(1)}, f32[128,128]{1,0:T(8,128)S(1)}, u32[]{:S(2)}, u32[]{:S(2)}) collective-permute-start(f32[128,128]{1,0:T(8,128)S(1)} %get-tuple-element.66), channel_id=1, source_target_pairs={{0,10},{2,8},{4,14},{6,12},{8,2},{10,0},{12,6},{14,4},{16,26},{18,... | collective-permute-start | bytes 196616 | tf_op jit(solution)/shard_map/ppermute | solution.py:217
  61.0 7.2 %collective-permute-start.22 = (f32[128,128]{1,0:T(8,128)S(1)}, f32[128,128]{1,0:T(8,128)S(1)}, u32[]{:S(2)}, u32[]{:S(2)}) collective-permute-start(f32[128,128]{1,0:T(8,128)S(1)} %get-tuple-element.67), channel_id=1, source_target_pairs={{0,26},{2,24},{4,30},{6,28},{8,18},{10,16},{12,22},{14,20},{16,10}... | collective-permute-start | bytes 196616 | tf_op jit(solution)/shard_map/ppermute | solution.py:217
  61.7 7.5 %collective-permute-start.23 = (f32[128,128]{1,0:T(8,128)S(1)}, f32[128,128]{1,0:T(8,128)S(1)}, u32[]{:S(2)}, u32[]{:S(2)}) collective-permute-start(f32[128,128]{1,0:T(8,128)S(1)} %get-tuple-element.68), channel_id=1, source_target_pairs={{0,12},{2,14},{4,8},{6,10},{8,4},{10,6},{12,0},{14,2},{16,28},{18,... | collective-permute-start | bytes 196616 | tf_op jit(solution)/shard_map/ppermute | solution.py:217
  62.4 7.8 %collective-permute-start.24 = (f32[128,128]{1,0:T(8,128)S(1)}, f32[128,128]{1,0:T(8,128)S(1)}, u32[]{:S(2)}, u32[]{:S(2)}) collective-permute-start(f32[128,128]{1,0:T(8,128)S(1)} %get-tuple-element.69), channel_id=1, source_target_pairs={{0,28},{2,30},{4,24},{6,26},{8,20},{10,22},{12,16},{14,18},{16,12}... | collective-permute-start | bytes 196616 | tf_op jit(solution)/shard_map/ppermute | solution.py:217
  65.1 6.6 %collective-permute-start.25 = (f32[128,128]{1,0:T(8,128)S(1)}, f32[128,128]{1,0:T(8,128)S(1)}, u32[]{:S(2)}, u32[]{:S(2)}) collective-permute-start(f32[128,128]{1,0:T(8,128)S(1)} %get-tuple-element.70), channel_id=1, source_target_pairs={{0,14},{2,12},{4,10},{6,8},{8,6},{10,4},{12,2},{14,0},{16,30},{18,... | collective-permute-start | bytes 196616 | tf_op jit(solution)/shard_map/ppermute | solution.py:217
  66.2 6.5 %collective-permute-start.26 = (f32[128,128]{1,0:T(8,128)S(1)}, f32[128,128]{1,0:T(8,128)S(1)}, u32[]{:S(2)}, u32[]{:S(2)}) collective-permute-start(f32[128,128]{1,0:T(8,128)S(1)} %get-tuple-element.71), channel_id=1, source_target_pairs={{0,30},{2,28},{4,26},{6,24},{8,22},{10,20},{12,18},{14,16},{16,14}... | collective-permute-start | bytes 196616 | tf_op jit(solution)/shard_map/ppermute | solution.py:217
  68.2 6.4 %collective-permute-start.27 = (f32[128,128]{1,0:T(8,128)S(1)}, f32[128,128]{1,0:T(8,128)S(1)}, u32[]{:S(2)}, u32[]{:S(2)}) collective-permute-start(f32[128,128]{1,0:T(8,128)S(1)} %get-tuple-element.72), channel_id=1, source_target_pairs={{0,4},{2,6},{4,0},{6,2},{8,12},{10,14},{12,8},{14,10},{16,20},{18,... | collective-permute-start | bytes 196616 | tf_op jit(solution)/shard_map/ppermute | solution.py:217
  69.3 6.2 %collective-permute-start.28 = (f32[128,128]{1,0:T(8,128)S(1)}, f32[128,128]{1,0:T(8,128)S(1)}, u32[]{:S(2)}, u32[]{:S(2)}) collective-permute-start(f32[128,128]{1,0:T(8,128)S(1)} %get-tuple-element.73), channel_id=1, source_target_pairs={{0,6},{2,4},{4,2},{6,0},{8,14},{10,12},{12,10},{14,8},{16,22},{18,... | collective-permute-start | bytes 196616 | tf_op jit(solution)/shard_map/ppermute | solution.py:217
  70.2 5.3 %collective-permute-start.29 = (f32[128,128]{1,0:T(8,128)S(1)}, f32[128,128]{1,0:T(8,128)S(1)}, u32[]{:S(2)}, u32[]{:S(2)}) collective-permute-start(f32[128,128]{1,0:T(8,128)S(1)} %get-tuple-element.74), channel_id=1, source_target_pairs={{0,2},{2,0},{4,6},{6,4},{8,10},{10,8},{12,14},{14,12},{16,18},{18,... | collective-permute-start | bytes 196616 | tf_op jit(solution)/shard_map/ppermute | solution.py:217
  (4 other events, 3.1 us)

commit v10 on v6

--- a/solution.py
+++ b/solution.py
@@ -17,6 +17,7 @@
 LANES = 128
 PACKED = 16
 EARLY = 5
+TILE = 128
 PAIRED = Layout(major_to_minor=(1, 0, 2))
 
 
@@ -54,7 +55,7 @@
 
 def tables_kernel(wide, ks, spect, narrow, x_hbm, re_hbm, im_hbm, order_ref, pair_ref, angle_ref, *rest):
     sends = rest[: len(ks)]
-    high_ref, low_ref, turn_ref, gates, block_sem, gate_sem = rest[len(ks) :]
+    gate_ref, turn_ref, gates, block_sem, gate_sem = rest[len(ks) :]
     copies = [pltpu.make_async_copy(block_of(x_hbm, k, wide), sends[i], block_sem.at[i]) for i, k in enumerate(ks)]
     gate_copies = [
         pltpu.make_async_copy(hbm, gates.at[part], gate_sem.at[part]) for part, hbm in enumerate((re_hbm, im_hbm))
@@ -65,6 +66,8 @@
     row = lax.broadcasted_iota(jnp.int32, (spect, LOW), 0)
     lane = lax.broadcasted_iota(jnp.int32, (spect, LOW), 1)
     r = lax.axis_index("wide") * (spect // narrow) + row // narrow
+    turn_ref[0, 0] = jnp.ones((spect, LOW), jnp.float32)
+    turn_ref[0, 1] = jnp.zeros((spect, LOW), jnp.float32)
     for layer in range(LAYERS):
         b = lax.axis_index("narrow") if layer % 2 == 0 else row % narrow
         u = ((r * narrow + b) * LOW + lane) & (2**PHASE_BITS - 1)
@@ -73,8 +76,8 @@
             first = u >> jnp.full((spect, LOW), pair_ref[layer, 0, gate], jnp.int32)
             second = u >> jnp.full((spect, LOW), pair_ref[layer, 1, gate], jnp.int32)
             phase = phase + jnp.where((first & second & 1) == 1, angle_ref[layer, gate], 0.0)
-        turn_ref[layer, 0] = jnp.cos(phase)
-        turn_ref[layer, 1] = jnp.sin(phase)
+        turn_ref[layer + 1, 0] = jnp.cos(phase)
+        turn_ref[layer + 1, 1] = jnp.sin(phase)
 
     for copy in gate_copies:
         copy.wait()
@@ -88,43 +91,27 @@
             source = source + (((t >> bit) & 1) << jnp.full((8, LOW), order_ref[layer, bit], jnp.int32))
         hot = jnp.where(position == source[None], 1.0, 0.0).reshape(LOW, LOW).astype(jnp.bfloat16)
         for part in range(2):
-            for out_ref, piece in zip((high_ref, low_ref), split(gates[part, layer])):
+            for which, piece in enumerate(split(gates[part, layer])):
                 for e in range(2):
                     moved = lax.dot_general(
                         hot[:, e * GATE : (e + 1) * GATE], piece, contract, preferred_element_type=jnp.float32
-                    ).astype(jnp.bfloat16)
-                    lanes = slice(e * GATE, (e + 1) * GATE)
-                    shifted = slice(LOW + e * GATE, LOW + (e + 1) * GATE)
-                    if part == 0:
-                        out_ref[layer, :LOW, lanes] = moved
-                        out_ref[layer, LOW:, shifted] = moved
-                    else:
-                        out_ref[layer, :LOW, shifted] = moved
-                        out_ref[layer, LOW:, lanes] = -moved
+                    )
+                    start = part * LOW + e * GATE
+                    gate_ref[layer, which, :, start : start + GATE] = moved.astype(jnp.bfloat16)
     for copy in copies:
         copy.wait()
 
 
 def exchange_modes(rows, span):
-    rows = list(rows)
-    lane = lax.broadcasted_iota(jnp.int32, rows[0].shape, 1)
+    count = len(rows)
+    group = lax.broadcasted_iota(jnp.int32, rows[0].shape, 1) // span
+    rows = [pltpu.roll(row, m * span, 1) if m else row for m, row in enumerate(rows)]
     step = 1
-    while step < len(rows):
-        shift = step * span
-        upper = (lane & shift) != 0
-        for m in range(len(rows)):
-            if m & step:
-                continue
-            x0, x1 = rows[m], rows[m + step]
-            if 2 * shift == LANES:
-                crossing = pltpu.roll(jnp.where(upper, x0, x1), shift, 1)
-                rows[m] = jnp.where(upper, crossing, x0)
-                rows[m + step] = jnp.where(upper, x1, crossing)
-            else:
-                rows[m] = jnp.where(upper, pltpu.roll(x1, shift, 1), x0)
-                rows[m + step] = jnp.where(upper, x1, pltpu.roll(x0, LANES - shift, 1))
+    while step < count:
+        taken = (group & step) != 0
+        rows = [jnp.where(taken, rows[(y + step) % count], rows[y]) for y in range(count)]
         step *= 2
-    return rows
+    return [pltpu.roll(rows[-r % count], LANES - r * span, 1) if r else rows[0] for r in range(count)]
 
 
 def place_kernel(wide, *rest):
@@ -141,59 +128,73 @@
 
 def layers_kernel(wide, spect, *rest):
     received = rest[:wide]
-    high_ref, low_ref, turn_ref = rest[wide : wide + 3]
-    outs = rest[wide + 3 : 2 * wide + 3]
-    state, left_high, left_low = rest[2 * wide + 3 :]
+    gate, turn = rest[wide : wide + 2]
+    outs = rest[wide + 2 : 2 * wide + 2]
+    state, left_high, left_low, minus_imag = rest[2 * wide + 2 :]
     me = lax.axis_index("wide")
+    count = wide * spect
     span = LOW // wide
     half = wide // 2
-    joined = max(1, PACKED // spect)
+    rows_at_once = min(spect, PACKED)
+    joined = PACKED // rows_at_once
+    tile = min(TILE, count)
 
     for i, k in enumerate(exchange_order(wide)):
         rows = pl.ds(pl.multiple_of((me ^ k) * spect, spect), spect)
         for part in range(2):
             for lanes in range(2):
-                state[part, rows, lanes * LANES : (lanes + 1) * LANES] = received[i][
+                state[0, part, rows, lanes * LANES : (lanes + 1) * LANES] = received[i][
                     pl.ds(2 * lanes + part, spect, stride=4), :
                 ]
 
-    def one_layer(layer, carry):
-        for part in range(2):
+    def turned(slot, entry, first, size, offset, lanes):
+        rows, lanes = pl.ds(first + offset, size), slice(lanes * LANES, (lanes + 1) * LANES)
+        real, imag = state[slot, 0, rows, lanes], state[slot, 1, rows, lanes]
+        cosine, sine = turn[entry, 0, offset : offset + size, lanes], turn[entry, 1, offset : offset + size, lanes]
+        return real * cosine - imag * sine, real * sine + imag * cosine
+
+    def one_layer(layer, slot):
+        for which in range(2):
+            minus_imag[which] = -gate[layer, which, :, LOW:]
+
+        for lanes in range(2):
             for top in range(2):
-                for lanes in range(2):
-                    first = top * half * spect
-                    piece = state[part, first : first + half * spect, lanes * LANES : (lanes + 1) * LANES]
-                    rows = exchange_modes([piece[m * spect : (m + 1) * spect] for m in range(half)], span)
-                    for g in range(0, half, joined):
-                        at = (lanes * half + g) * spect
+                for offset in range(0, spect, rows_at_once):
+                    pieces = [
+                        turned(slot, layer, (top * half + m) * spect, rows_at_once, offset, lanes) for m in range(half)
+                    ]
+                    for part in range(2):
+                        rows = exchange_modes([piece[part] for piece in pieces], span)
                         column = part * LOW + top * LANES
-                        high, low = split(jnp.concatenate(rows[g : g + joined], axis=0))
-                        left_high[at : at + joined * spect, column : column + LANES] = high
-                        left_low[at : at + joined * spect, column : column + LANES] = low
-
-        cosine = turn_ref[layer, 0][None]
-        sine = turn_ref[layer, 1][None]
-        for block in range(2):
-            rows = slice(block * half * spect, (block + 1) * half * spect)
-            dot = partial(jnp.dot, preferred_element_type=jnp.float32)
-            gated = dot(left_high[rows], high_ref[layer])
-            gated = gated + dot(left_low[rows], high_ref[layer])
-            gated = gated + dot(left_high[rows], low_ref[layer])
-            real = gated[:, :LOW].reshape(half, spect, LOW)
-            imag = gated[:, LOW:].reshape(half, spect, LOW)
-            state[0, rows] = (real * cosine - imag * sine).reshape(half * spect, LOW)
-            state[1, rows] = (real * sine + imag * cosine).reshape(half * spect, LOW)
+                        for g in range(0, half, joined):
+                            at = (lanes * half + g) * spect + offset
+                            high, low = split(jnp.concatenate(rows[g : g + joined], axis=0))
+                            left_high[at : at + PACKED, column : column + LANES] = high
+                            left_low[at : at + PACKED, column : column + LANES] = low
+
+        factors = []
+        for which in range(2):
+            real, imag = gate[layer, which, :, :LOW], gate[layer, which, :, LOW:]
+            factors.append([[real, minus_imag[which]], [imag, real]])
+        for first in range(0, count, tile):
+            rows = slice(first, first + tile)
+            terms = jnp.concatenate([left_high[rows], left_low[rows], left_high[rows]], axis=1)
+            for part in range(2):
+                square = jnp.concatenate(factors[0][part] + factors[0][part] + factors[1][part], axis=0)
+                state[1 - slot, part, rows] = jnp.dot(terms, square, preferred_element_type=jnp.float32)
+
+    def two_layers(step, carry):
+        one_layer(2 * step, 0)
+        one_layer(2 * step + 1, 1)
         return carry
 
-    lax.fori_loop(0, LAYERS, one_layer, 0)
+    lax.fori_loop(0, LAYERS // 2, two_layers, 0)
 
     for i, k in enumerate(exchange_order(wide)):
-        rows = pl.ds(pl.multiple_of((me ^ k) * spect, spect), spect)
-        for part in range(2):
-            for lanes in range(2):
-                outs[i][pl.ds(2 * lanes + part, spect, stride=4), :] = state[
-                    part, rows, lanes * LANES : (lanes + 1) * LANES
-                ]
+        first = pl.multiple_of((me ^ k) * spect, spect)
+        for lanes in range(2):
+            for part, piece in enumerate(turned(0, LAYERS, first, spect, 0, lanes)):
+                outs[i][pl.ds(2 * lanes + part, spect, stride=4), :] = piece
 
 
 def local(state, gate_re, gate_im, bit_orders, phase_pairs, phase_angles):
@@ -230,13 +231,13 @@
     )(rows)
     received = swap(sends, early)
 
-    square = jax.ShapeDtypeStruct((LAYERS, 2 * LOW, 2 * LOW), jnp.bfloat16)
-    *sends, high, low, turn = pl.pallas_call(
+    gates = jax.ShapeDtypeStruct((LAYERS, 2, LOW, 2 * LOW), jnp.bfloat16)
+    turns = jax.ShapeDtypeStruct((LAYERS + 1, 2, spect, LOW), jnp.float32)
+    *sends, gate, turn = pl.pallas_call(
         partial(tables_kernel, wide, late, spect, narrow),
         in_specs=[in_hbm, in_hbm, in_hbm, in_smem, in_smem, in_smem],
-        out_specs=[in_vmem] * (len(late) + 3),
-        out_shape=[piece] * len(late)
-        + [square, square, jax.ShapeDtypeStruct((LAYERS, 2, spect, LOW), jnp.float32)],
+        out_specs=[in_vmem] * (len(late) + 2),
+        out_shape=[piece] * len(late) + [gates, turns],
         scratch_shapes=[
             pltpu.VMEM((2,) + gate_re.shape, jnp.float32),
             pltpu.SemaphoreType.DMA((len(late),)),
@@ -251,18 +252,19 @@
 
     done = pl.pallas_call(
         partial(layers_kernel, wide, spect),
-        in_specs=[in_vmem] * (wide + 3),
+        in_specs=[in_vmem] * (wide + 2),
         out_specs=[in_vmem] * wide,
         out_shape=[piece] * wide,
         scratch_shapes=[
-            pltpu.VMEM((2, count, LOW), jnp.float32),
+            pltpu.VMEM((2, 2, count, LOW), jnp.float32),
             pltpu.VMEM((count, 2 * LOW), jnp.bfloat16),
             pltpu.VMEM((count, 2 * LOW), jnp.bfloat16),
+            pltpu.VMEM((2, LOW, LOW), jnp.bfloat16),
         ],
         compiler_params=part_of_vmem,
         cost_estimate=pl.CostEstimate(flops=5 * 10**9, bytes_accessed=10**7, transcendentals=0),
         name="layers",
-    )(*received, high, low, turn)
+    )(*received, gate, turn)
 
     back = pl.pallas_call(
         partial(place_kernel, wide),

time: 75.8 us -> 74.9 us (0.988)
  Pallas kernels: 14.8 us -> 13.8 us
    pallas_call x1, Pallas kernels: 8.31 us -> 7.44 us  [local(): pl.pallas_call(partial(layers_kernel, wide, spect), in_specs=[in_vmem] *...]
where the time goes in v10:
time: 74.9 us; the launch traced here: 74.5 us
  starting transfers between devices  41.2 us (55%)
  waiting for transfers between devices  14.1 us (19%)
  Pallas kernels  13.8 us (18%)
  local copies, waits for them, and re-layouts  5.28 us (7%)
    ppermute x30, starting transfers between devices, swap(): lax.ppermute(block, 'wide', [(i, i ^ k) for i in range(wide)])  41.2 us
    ppermute x30, waiting for transfers between devices, swap(): lax.ppermute(block, 'wide', [(i, i ^ k) for i in range(wide)])  14.1 us
    pallas_call x1, Pallas kernels, local(): pl.pallas_call(partial(layers_kernel, wide, spect), in_specs=[in_vmem] *...  7.44 us
    unnamed x12, local copies, waits for them, and re-layouts  5.28 us
    pallas_call x1, Pallas kernels, local(): pl.pallas_call(partial(tables_kernel, wide, late, spect, narrow), in_spec...  4.86 us
  transfers between devices with their start and end apart: 30, of which 13 were waited for; matrix products, arithmetic and copies ran while one was open for 0% of the time, Pallas kernels for 7%

profile of v10, /device:TPU:0, one launch (start us, length us, event | category | flops | bytes accessed | tf_op | source)
XLA Modules:
  0.0 74.5 jit_solution(17138149896315806835)
XLA Ops:
  0.0 1.2 %copy-done = f32[2,131072]{1,0:T(2,128)S(1)} copy-done((f32[2,131072]{1,0:T(2,128)S(1)}, f32[2,131072]{1,0:T(2,128)}, u32[]{:S(2)}) %copy-start) | copy-done | bytes 1048600
  1.7 4.1 %collective-permute-start = (f32[128,128]{1,0:T(8,128)S(1)}, f32[128,128]{1,0:T(8,128)S(1)}, u32[]{:S(2)}, u32[]{:S(2)}) collective-permute-start(f32[128,128]{1,0:T(8,128)S(1)} %get-tuple-element.40), channel_id=1, source_target_pairs={{0,16},{2,18},{4,20},{6,22},{8,24},{10,26},{12,28},{14,30},{16,0},... | collective-permute-start | bytes 196616 | tf_op jit(solution)/shard_map/ppermute | solution.py:219
  5.8 1.6 %collective-permute-start.2 = (f32[128,128]{1,0:T(8,128)S(1)}, f32[128,128]{1,0:T(8,128)S(1)}, u32[]{:S(2)}, u32[]{:S(2)}) collective-permute-start(f32[128,128]{1,0:T(8,128)S(1)} %get-tuple-element.42), channel_id=1, source_target_pairs={{0,8},{2,10},{4,12},{6,14},{8,0},{10,2},{12,4},{14,6},{16,24},{18,... | collective-permute-start | bytes 196616 | tf_op jit(solution)/shard_map/ppermute | solution.py:219
  7.4 3.7 %collective-permute-start.4 = (f32[128,128]{1,0:T(8,128)S(1)}, f32[128,128]{1,0:T(8,128)S(1)}, u32[]{:S(2)}, u32[]{:S(2)}) collective-permute-start(f32[128,128]{1,0:T(8,128)S(1)} %get-tuple-element.44), channel_id=1, source_target_pairs={{0,20},{2,22},{4,16},{6,18},{8,28},{10,30},{12,24},{14,26},{16,4},... | collective-permute-start | bytes 196616 | tf_op jit(solution)/shard_map/ppermute | solution.py:219
  11.1 1.0 %copy-done.1 = f32[6,128,128]{2,1,0:T(8,128)S(1)} copy-done((f32[6,128,128]{2,1,0:T(8,128)S(1)}, f32[6,128,128]{2,1,0:T(8,128)}, u32[]{:S(2)}) %copy-start.1) | copy-done | bytes 393240
  12.1 1.0 %copy-done.2 = f32[6,128,128]{2,1,0:T(8,128)S(1)} copy-done((f32[6,128,128]{2,1,0:T(8,128)S(1)}, f32[6,128,128]{2,1,0:T(8,128)}, u32[]{:S(2)}) %copy-start.2) | copy-done | bytes 393240
  15.2 4.9 %tables.1 = (f32[128,128]{1,0:T(8,128)S(1)}, f32[128,128]{1,0:T(8,128)S(1)}, f32[128,128]{1,0:T(8,128)S(1)}, f32[128,128]{1,0:T(8,128)S(1)}, f32[128,128]{1,0:T(...) custom-call(f32[2048,128]{1,0:T(8,128)S(1)} %bitcast.12, ...), custom_call_target="tpu_custom_call" | custom-call | flops 1000000000 | bytes 8000000 | tf_op jit(solution)/shard_map/tables/pallas_call | solution.py:236
  20.1 2.5 %collective-permute-start.6 = (f32[128,128]{1,0:T(8,128)S(1)}, f32[128,128]{1,0:T(8,128)S(1)}, u32[]{:S(2)}, u32[]{:S(2)}) collective-permute-start(f32[128,128]{1,0:T(8,128)S(1)} %get-tuple-element.46), channel_id=1, source_target_pairs={{0,12},{2,14},{4,8},{6,10},{8,4},{10,6},{12,0},{14,2},{16,28},{18,... | collective-permute-start | bytes 196616 | tf_op jit(solution)/shard_map/ppermute | solution.py:219
  22.7 3.6 %collective-permute-start.8 = (f32[128,128]{1,0:T(8,128)S(1)}, f32[128,128]{1,0:T(8,128)S(1)}, u32[]{:S(2)}, u32[]{:S(2)}) collective-permute-start(f32[128,128]{1,0:T(8,128)S(1)} %get-tuple-element.48), channel_id=1, source_target_pairs={{0,24},{2,26},{4,28},{6,30},{8,16},{10,18},{12,20},{14,22},{16,8},... | collective-permute-start | bytes 196616 | tf_op jit(solution)/shard_map/ppermute | solution.py:219
  26.4 1.2 %collective-permute-done.5.rest_6_ = f32[128,128]{1,0:T(8,128)S(1)} collective-permute-done((f32[128,128]{1,0:T(8,128)S(1)}, f32[128,128]{1,0:T(8,128)S(1)}, u32[]{:S(2)}, u32[]{:S(2)}) %collective-permute-start.5) | collective-permute-done | bytes 65568 | tf_op jit(solution)/shard_map/ppermute | solution.py:219
  27.7 2.7 %collective-permute-start.10 = (f32[128,128]{1,0:T(8,128)S(1)}, f32[128,128]{1,0:T(8,128)S(1)}, u32[]{:S(2)}, u32[]{:S(2)}) collective-permute-start(f32[128,128]{1,0:T(8,128)S(1)} %get-tuple-element.50), channel_id=1, source_target_pairs={{0,28},{2,30},{4,24},{6,26},{8,20},{10,22},{12,16},{14,18},{16,12}... | collective-permute-start | bytes 196616 | tf_op jit(solution)/shard_map/ppermute | solution.py:219
  30.3 1.1 %collective-permute-start.11 = (f32[128,128]{1,0:T(8,128)S(1)}, f32[128,128]{1,0:T(8,128)S(1)}, u32[]{:S(2)}, u32[]{:S(2)}) collective-permute-start(f32[128,128]{1,0:T(8,128)S(1)} %get-tuple-element.51), channel_id=1, source_target_pairs={{0,30},{2,28},{4,26},{6,24},{8,22},{10,20},{12,18},{14,16},{16,14}... | collective-permute-start | bytes 196616 | tf_op jit(solution)/shard_map/ppermute | solution.py:219
  32.3 1.6 %collective-permute-start.13 = (f32[128,128]{1,0:T(8,128)S(1)}, f32[128,128]{1,0:T(8,128)S(1)}, u32[]{:S(2)}, u32[]{:S(2)}) collective-permute-start(f32[128,128]{1,0:T(8,128)S(1)} %get-tuple-element.53), channel_id=1, source_target_pairs={{0,6},{2,4},{4,2},{6,0},{8,14},{10,12},{12,10},{14,8},{16,22},{18,... | collective-permute-start | bytes 196616 | tf_op jit(solution)/shard_map/ppermute | solution.py:219
  33.9 0.9 %collective-permute-done.10.rest_11_ = f32[128,128]{1,0:T(8,128)S(1)} collective-permute-done((f32[128,128]{1,0:T(8,128)S(1)}, f32[128,128]{1,0:T(8,128)S(1)}, u32[]{:S(2)}, u32[]{:S(2)}) %collective-permute-start.10) | collective-permute-done | bytes 65568 | tf_op jit(solution)/shard_map/ppermute | solution.py:219
  34.7 2.2 %collective-permute-done.11.rest_12_ = f32[128,128]{1,0:T(8,128)S(1)} collective-permute-done((f32[128,128]{1,0:T(8,128)S(1)}, f32[128,128]{1,0:T(8,128)S(1)}, u32[]{:S(2)}, u32[]{:S(2)}) %collective-permute-start.11) | collective-permute-done | bytes 65568 | tf_op jit(solution)/shard_map/ppermute | solution.py:219
  36.9 0.9 %collective-permute-done.12.rest_13_ = f32[128,128]{1,0:T(8,128)S(1)} collective-permute-done((f32[128,128]{1,0:T(8,128)S(1)}, f32[128,128]{1,0:T(8,128)S(1)}, u32[]{:S(2)}, u32[]{:S(2)}) %collective-permute-start.12) | collective-permute-done | bytes 65568 | tf_op jit(solution)/shard_map/ppermute | solution.py:219
  37.8 1.5 %collective-permute-done.13.rest_14_ = f32[128,128]{1,0:T(8,128)S(1)} collective-permute-done((f32[128,128]{1,0:T(8,128)S(1)}, f32[128,128]{1,0:T(8,128)S(1)}, u32[]{:S(2)}, u32[]{:S(2)}) %collective-permute-start.13) | collective-permute-done | bytes 65568 | tf_op jit(solution)/shard_map/ppermute | solution.py:219
  39.3 7.4 %layers.1 = (f32[128,128]{1,0:T(8,128)S(1)}, f32[128,128]{1,0:T(8,128)S(1)}, f32[128,128]{1,0:T(8,128)S(1)}, f32[128,128]{1,0:T(8,128)S(1)}, f32[128,128]{1,0:T(...) custom-call(f32[128,128]{1,0:T(8,128)S(1)} %get-tuple-element.39.res, ...), custom_call_target="tpu_custom_call" | custom-call | flops 5000000000 | bytes 10000000 | tf_op jit(solution)/shard_map/layers/pallas_call | solution.py:253
  47.2 1.9 %collective-permute-start.16 = (f32[128,128]{1,0:T(8,128)S(1)}, f32[128,128]{1,0:T(8,128)S(1)}, u32[]{:S(2)}, u32[]{:S(2)}) collective-permute-start(f32[128,128]{1,0:T(8,128)S(1)} %get-tuple-element.59), channel_id=1, source_target_pairs={{0,18},{2,16},{4,22},{6,20},{8,26},{10,24},{12,30},{14,28},{16,2},... | collective-permute-start | bytes 196616 | tf_op jit(solution)/shard_map/ppermute | solution.py:219
  49.6 1.6 %collective-permute-start.18 = (f32[128,128]{1,0:T(8,128)S(1)}, f32[128,128]{1,0:T(8,128)S(1)}, u32[]{:S(2)}, u32[]{:S(2)}) collective-permute-start(f32[128,128]{1,0:T(8,128)S(1)} %get-tuple-element.61), channel_id=1, source_target_pairs={{0,10},{2,8},{4,14},{6,12},{8,2},{10,0},{12,6},{14,4},{16,26},{18,... | collective-permute-start | bytes 196616 | tf_op jit(solution)/shard_map/ppermute | solution.py:219
  51.2 1.8 %collective-permute-start.19 = (f32[128,128]{1,0:T(8,128)S(1)}, f32[128,128]{1,0:T(8,128)S(1)}, u32[]{:S(2)}, u32[]{:S(2)}) collective-permute-start(f32[128,128]{1,0:T(8,128)S(1)} %get-tuple-element.62), channel_id=1, source_target_pairs={{0,20},{2,22},{4,16},{6,18},{8,28},{10,30},{12,24},{14,26},{16,4},... | collective-permute-start | bytes 196616 | tf_op jit(solution)/shard_map/ppermute | solution.py:219
  53.0 1.8 %collective-permute-done.15.rest_1_ = f32[128,128]{1,0:T(8,128)S(1)} collective-permute-done((f32[128,128]{1,0:T(8,128)S(1)}, f32[128,128]{1,0:T(8,128)S(1)}, u32[]{:S(2)}, u32[]{:S(2)}) %collective-permute-start.15) | collective-permute-done | bytes 65568 | tf_op jit(solution)/shard_map/ppermute | solution.py:219
  54.8 1.0 %collective-permute-done.16.rest_2_ = f32[128,128]{1,0:T(8,128)S(1)} collective-permute-done((f32[128,128]{1,0:T(8,128)S(1)}, f32[128,128]{1,0:T(8,128)S(1)}, u32[]{:S(2)}, u32[]{:S(2)}) %collective-permute-start.16) | collective-permute-done | bytes 65568 | tf_op jit(solution)/shard_map/ppermute | solution.py:219
  55.8 1.6 %collective-permute-start.21 = (f32[128,128]{1,0:T(8,128)S(1)}, f32[128,128]{1,0:T(8,128)S(1)}, u32[]{:S(2)}, u32[]{:S(2)}) collective-permute-start(f32[128,128]{1,0:T(8,128)S(1)} %get-tuple-element.64), channel_id=1, source_target_pairs={{0,12},{2,14},{4,8},{6,10},{8,4},{10,6},{12,0},{14,2},{16,28},{18,... | collective-permute-start | bytes 196616 | tf_op jit(solution)/shard_map/ppermute | solution.py:219
  58.3 1.7 %collective-permute-start.23 = (f32[128,128]{1,0:T(8,128)S(1)}, f32[128,128]{1,0:T(8,128)S(1)}, u32[]{:S(2)}, u32[]{:S(2)}) collective-permute-start(f32[128,128]{1,0:T(8,128)S(1)} %get-tuple-element.66), channel_id=1, source_target_pairs={{0,24},{2,26},{4,28},{6,30},{8,16},{10,18},{12,20},{14,22},{16,8},... | collective-permute-start | bytes 196616 | tf_op jit(solution)/shard_map/ppermute | solution.py:219
  60.0 1.9 %collective-permute-start.24 = (f32[128,128]{1,0:T(8,128)S(1)}, f32[128,128]{1,0:T(8,128)S(1)}, u32[]{:S(2)}, u32[]{:S(2)}) collective-permute-start(f32[128,128]{1,0:T(8,128)S(1)} %get-tuple-element.67), channel_id=1, source_target_pairs={{0,26},{2,24},{4,30},{6,28},{8,18},{10,16},{12,22},{14,20},{16,10}... | collective-permute-start | bytes 196616 | tf_op jit(solution)/shard_map/ppermute | solution.py:219
  62.2 2.2 %collective-permute-start.25 = (f32[128,128]{1,0:T(8,128)S(1)}, f32[128,128]{1,0:T(8,128)S(1)}, u32[]{:S(2)}, u32[]{:S(2)}) collective-permute-start(f32[128,128]{1,0:T(8,128)S(1)} %get-tuple-element.68), channel_id=1, source_target_pairs={{0,28},{2,30},{4,24},{6,26},{8,20},{10,22},{12,16},{14,18},{16,12}... | collective-permute-start | bytes 196616 | tf_op jit(solution)/shard_map/ppermute | solution.py:219
  64.4 2.6 %collective-permute-start.26 = (f32[128,128]{1,0:T(8,128)S(1)}, f32[128,128]{1,0:T(8,128)S(1)}, u32[]{:S(2)}, u32[]{:S(2)}) collective-permute-start(f32[128,128]{1,0:T(8,128)S(1)} %get-tuple-element.69), channel_id=1, source_target_pairs={{0,30},{2,28},{4,26},{6,24},{8,22},{10,20},{12,18},{14,16},{16,14}... | collective-permute-start | bytes 196616 | tf_op jit(solution)/shard_map/ppermute | solution.py:219
  66.9 1.4 %collective-permute-start.27 = (f32[128,128]{1,0:T(8,128)S(1)}, f32[128,128]{1,0:T(8,128)S(1)}, u32[]{:S(2)}, u32[]{:S(2)}) collective-permute-start(f32[128,128]{1,0:T(8,128)S(1)} %get-tuple-element.70), channel_id=1, source_target_pairs={{0,4},{2,6},{4,0},{6,2},{8,12},{10,14},{12,8},{14,10},{16,20},{18,... | collective-permute-start | bytes 196616 | tf_op jit(solution)/shard_map/ppermute | solution.py:219
  69.7 1.2 %collective-permute-done.26.rest_12_ = f32[128,128]{1,0:T(8,128)S(1)} collective-permute-done((f32[128,128]{1,0:T(8,128)S(1)}, f32[128,128]{1,0:T(8,128)S(1)}, u32[]{:S(2)}, u32[]{:S(2)}) %collective-permute-start.26) | collective-permute-done | bytes 65568 | tf_op jit(solution)/shard_map/ppermute | solution.py:219
  70.8 2.1 %collective-permute-done.27.rest_13_ = f32[128,128]{1,0:T(8,128)S(1)} collective-permute-done((f32[128,128]{1,0:T(8,128)S(1)}, f32[128,128]{1,0:T(8,128)S(1)}, u32[]{:S(2)}, u32[]{:S(2)}) %collective-permute-start.27) | collective-permute-done | bytes 65568 | tf_op jit(solution)/shard_map/ppermute | solution.py:219
  73.4 1.1 %place.1 = f32[2048,128]{1,0:T(8,128)} custom-call(f32[128,128]{1,0:T(8,128)S(1)} %get-tuple-element.57.rest_0_, f32[128,128]{1,0:T(8,128)S(1)} %collective-permute-done.15.rest_1_, f32[128,128]{1,0:T(8,128)S(1)} %collective-permute-done.16.rest_2_, f32[128,128]{1,0:T(8,128)S(1)} %collective-permute-done.17.rest_3_, ...), custom_call_target="tpu_custom_call" | custom-call | tf_op jit(solution)/shard_map/place/pallas_call | solution.py:269
  (44 shorter events, 7.6 us)
Async XLA Ops:
  0.0 1.2 %copy-start = (f32[2,131072]{1,0:T(2,128)S(1)}, f32[2,131072]{1,0:T(2,128)}, u32[]{:S(2)}) copy-start(f32[2,131072]{1,0:T(2,128)} %param.6) | copy-start | bytes 3145732
  1.7 18.4 %collective-permute-start = (f32[128,128]{1,0:T(8,128)S(1)}, f32[128,128]{1,0:T(8,128)S(1)}, u32[]{:S(2)}, u32[]{:S(2)}) collective-permute-start(f32[128,128]{1,0:T(8,128)S(1)} %get-tuple-element.40), channel_id=1, source_target_pairs={{0,16},{2,18},{4,20},{6,22},{8,24},{10,26},{12,28},{14,30},{16,0},... | collective-permute-start | bytes 196616 | tf_op jit(solution)/shard_map/ppermute | solution.py:219
  5.8 14.4 %collective-permute-start.1 = (f32[128,128]{1,0:T(8,128)S(1)}, f32[128,128]{1,0:T(8,128)S(1)}, u32[]{:S(2)}, u32[]{:S(2)}) collective-permute-start(f32[128,128]{1,0:T(8,128)S(1)} %get-tuple-element.41), channel_id=1, source_target_pairs={{0,18},{2,16},{4,22},{6,20},{8,26},{10,24},{12,30},{14,28},{16,2},... | collective-permute-start | bytes 196616 | tf_op jit(solution)/shard_map/ppermute | solution.py:219
  5.8 16.8 %collective-permute-start.2 = (f32[128,128]{1,0:T(8,128)S(1)}, f32[128,128]{1,0:T(8,128)S(1)}, u32[]{:S(2)}, u32[]{:S(2)}) collective-permute-start(f32[128,128]{1,0:T(8,128)S(1)} %get-tuple-element.42), channel_id=1, source_target_pairs={{0,8},{2,10},{4,12},{6,14},{8,0},{10,2},{12,4},{14,6},{16,24},{18,... | collective-permute-start | bytes 196616 | tf_op jit(solution)/shard_map/ppermute | solution.py:219
  7.4 15.4 %collective-permute-start.3 = (f32[128,128]{1,0:T(8,128)S(1)}, f32[128,128]{1,0:T(8,128)S(1)}, u32[]{:S(2)}, u32[]{:S(2)}) collective-permute-start(f32[128,128]{1,0:T(8,128)S(1)} %get-tuple-element.43), channel_id=1, source_target_pairs={{0,10},{2,8},{4,14},{6,12},{8,2},{10,0},{12,6},{14,4},{16,26},{18,... | collective-permute-start | bytes 196616 | tf_op jit(solution)/shard_map/ppermute | solution.py:219
  7.4 18.9 %collective-permute-start.4 = (f32[128,128]{1,0:T(8,128)S(1)}, f32[128,128]{1,0:T(8,128)S(1)}, u32[]{:S(2)}, u32[]{:S(2)}) collective-permute-start(f32[128,128]{1,0:T(8,128)S(1)} %get-tuple-element.44), channel_id=1, source_target_pairs={{0,20},{2,22},{4,16},{6,18},{8,28},{10,30},{12,24},{14,26},{16,4},... | collective-permute-start | bytes 196616 | tf_op jit(solution)/shard_map/ppermute | solution.py:219
  11.1 1.0 %copy-start.1 = (f32[6,128,128]{2,1,0:T(8,128)S(1)}, f32[6,128,128]{2,1,0:T(8,128)}, u32[]{:S(2)}) copy-start(f32[6,128,128]{2,1,0:T(8,128)} %re_hbm.1) | copy-start | bytes 1179652
  20.1 7.6 %collective-permute-start.5 = (f32[128,128]{1,0:T(8,128)S(1)}, f32[128,128]{1,0:T(8,128)S(1)}, u32[]{:S(2)}, u32[]{:S(2)}) collective-permute-start(f32[128,128]{1,0:T(8,128)S(1)} %get-tuple-element.45), channel_id=1, source_target_pairs={{0,22},{2,20},{4,18},{6,16},{8,30},{10,28},{12,26},{14,24},{16,6},... | collective-permute-start | bytes 196616 | tf_op jit(solution)/shard_map/ppermute | solution.py:219
  20.1 10.2 %collective-permute-start.6 = (f32[128,128]{1,0:T(8,128)S(1)}, f32[128,128]{1,0:T(8,128)S(1)}, u32[]{:S(2)}, u32[]{:S(2)}) collective-permute-start(f32[128,128]{1,0:T(8,128)S(1)} %get-tuple-element.46), channel_id=1, source_target_pairs={{0,12},{2,14},{4,8},{6,10},{8,4},{10,6},{12,0},{14,2},{16,28},{18,... | collective-permute-start | bytes 196616 | tf_op jit(solution)/shard_map/ppermute | solution.py:219
  22.6 8.9 %collective-permute-start.7 = (f32[128,128]{1,0:T(8,128)S(1)}, f32[128,128]{1,0:T(8,128)S(1)}, u32[]{:S(2)}, u32[]{:S(2)}) collective-permute-start(f32[128,128]{1,0:T(8,128)S(1)} %get-tuple-element.47), channel_id=1, source_target_pairs={{0,14},{2,12},{4,10},{6,8},{8,6},{10,4},{12,2},{14,0},{16,30},{18,... | collective-permute-start | bytes 196616 | tf_op jit(solution)/shard_map/ppermute | solution.py:219
  22.7 9.6 %collective-permute-start.8 = (f32[128,128]{1,0:T(8,128)S(1)}, f32[128,128]{1,0:T(8,128)S(1)}, u32[]{:S(2)}, u32[]{:S(2)}) collective-permute-start(f32[128,128]{1,0:T(8,128)S(1)} %get-tuple-element.48), channel_id=1, source_target_pairs={{0,24},{2,26},{4,28},{6,30},{8,16},{10,18},{12,20},{14,22},{16,8},... | collective-permute-start | bytes 196616 | tf_op jit(solution)/shard_map/ppermute | solution.py:219
  26.4 7.5 %collective-permute-start.9 = (f32[128,128]{1,0:T(8,128)S(1)}, f32[128,128]{1,0:T(8,128)S(1)}, u32[]{:S(2)}, u32[]{:S(2)}) collective-permute-start(f32[128,128]{1,0:T(8,128)S(1)} %get-tuple-element.49), channel_id=1, source_target_pairs={{0,26},{2,24},{4,30},{6,28},{8,18},{10,16},{12,22},{14,20},{16,10}... | collective-permute-start | bytes 196616 | tf_op jit(solution)/shard_map/ppermute | solution.py:219
  27.7 7.1 %collective-permute-start.10 = (f32[128,128]{1,0:T(8,128)S(1)}, f32[128,128]{1,0:T(8,128)S(1)}, u32[]{:S(2)}, u32[]{:S(2)}) collective-permute-start(f32[128,128]{1,0:T(8,128)S(1)} %get-tuple-element.50), channel_id=1, source_target_pairs={{0,28},{2,30},{4,24},{6,26},{8,20},{10,22},{12,16},{14,18},{16,12}... | collective-permute-start | bytes 196616 | tf_op jit(solution)/shard_map/ppermute | solution.py:219
  30.3 6.6 %collective-permute-start.11 = (f32[128,128]{1,0:T(8,128)S(1)}, f32[128,128]{1,0:T(8,128)S(1)}, u32[]{:S(2)}, u32[]{:S(2)}) collective-permute-start(f32[128,128]{1,0:T(8,128)S(1)} %get-tuple-element.51), channel_id=1, source_target_pairs={{0,30},{2,28},{4,26},{6,24},{8,22},{10,20},{12,18},{14,16},{16,14}... | collective-permute-start | bytes 196616 | tf_op jit(solution)/shard_map/ppermute | solution.py:219
  31.5 6.3 %collective-permute-start.12 = (f32[128,128]{1,0:T(8,128)S(1)}, f32[128,128]{1,0:T(8,128)S(1)}, u32[]{:S(2)}, u32[]{:S(2)}) collective-permute-start(f32[128,128]{1,0:T(8,128)S(1)} %get-tuple-element.52), channel_id=1, source_target_pairs={{0,4},{2,6},{4,0},{6,2},{8,12},{10,14},{12,8},{14,10},{16,20},{18,... | collective-permute-start | bytes 196616 | tf_op jit(solution)/shard_map/ppermute | solution.py:219
  32.3 7.0 %collective-permute-start.13 = (f32[128,128]{1,0:T(8,128)S(1)}, f32[128,128]{1,0:T(8,128)S(1)}, u32[]{:S(2)}, u32[]{:S(2)}) collective-permute-start(f32[128,128]{1,0:T(8,128)S(1)} %get-tuple-element.53), channel_id=1, source_target_pairs={{0,6},{2,4},{4,2},{6,0},{8,14},{10,12},{12,10},{14,8},{16,22},{18,... | collective-permute-start | bytes 196616 | tf_op jit(solution)/shard_map/ppermute | solution.py:219
  33.9 5.4 %collective-permute-start.14 = (f32[128,128]{1,0:T(8,128)S(1)}, f32[128,128]{1,0:T(8,128)S(1)}, u32[]{:S(2)}, u32[]{:S(2)}) collective-permute-start(f32[128,128]{1,0:T(8,128)S(1)} %get-tuple-element.54), channel_id=1, source_target_pairs={{0,2},{2,0},{4,6},{6,4},{8,10},{10,8},{12,14},{14,12},{16,18},{18,... | collective-permute-start | bytes 196616 | tf_op jit(solution)/shard_map/ppermute | solution.py:219
  46.7 8.1 %collective-permute-start.15 = (f32[128,128]{1,0:T(8,128)S(1)}, f32[128,128]{1,0:T(8,128)S(1)}, u32[]{:S(2)}, u32[]{:S(2)}) collective-permute-start(f32[128,128]{1,0:T(8,128)S(1)} %get-tuple-element.58), channel_id=1, source_target_pairs={{0,16},{2,18},{4,20},{6,22},{8,24},{10,26},{12,28},{14,30},{16,0},... | collective-permute-start | bytes 196616 | tf_op jit(solution)/shard_map/ppermute | solution.py:219
  47.2 8.6 %collective-permute-start.16 = (f32[128,128]{1,0:T(8,128)S(1)}, f32[128,128]{1,0:T(8,128)S(1)}, u32[]{:S(2)}, u32[]{:S(2)}) collective-permute-start(f32[128,128]{1,0:T(8,128)S(1)} %get-tuple-element.59), channel_id=1, source_target_pairs={{0,18},{2,16},{4,22},{6,20},{8,26},{10,24},{12,30},{14,28},{16,2},... | collective-permute-start | bytes 196616 | tf_op jit(solution)/shard_map/ppermute | solution.py:219
  49.1 8.3 %collective-permute-start.17 = (f32[128,128]{1,0:T(8,128)S(1)}, f32[128,128]{1,0:T(8,128)S(1)}, u32[]{:S(2)}, u32[]{:S(2)}) collective-permute-start(f32[128,128]{1,0:T(8,128)S(1)} %get-tuple-element.60), channel_id=1, source_target_pairs={{0,8},{2,10},{4,12},{6,14},{8,0},{10,2},{12,4},{14,6},{16,24},{18,... | collective-permute-start | bytes 196616 | tf_op jit(solution)/shard_map/ppermute | solution.py:219
  49.6 8.8 %collective-permute-start.18 = (f32[128,128]{1,0:T(8,128)S(1)}, f32[128,128]{1,0:T(8,128)S(1)}, u32[]{:S(2)}, u32[]{:S(2)}) collective-permute-start(f32[128,128]{1,0:T(8,128)S(1)} %get-tuple-element.61), channel_id=1, source_target_pairs={{0,10},{2,8},{4,14},{6,12},{8,2},{10,0},{12,6},{14,4},{16,26},{18,... | collective-permute-start | bytes 196616 | tf_op jit(solution)/shard_map/ppermute | solution.py:219
  51.2 8.9 %collective-permute-start.19 = (f32[128,128]{1,0:T(8,128)S(1)}, f32[128,128]{1,0:T(8,128)S(1)}, u32[]{:S(2)}, u32[]{:S(2)}) collective-permute-start(f32[128,128]{1,0:T(8,128)S(1)} %get-tuple-element.62), channel_id=1, source_target_pairs={{0,20},{2,22},{4,16},{6,18},{8,28},{10,30},{12,24},{14,26},{16,4},... | collective-permute-start | bytes 196616 | tf_op jit(solution)/shard_map/ppermute | solution.py:219
  54.8 7.4 %collective-permute-start.20 = (f32[128,128]{1,0:T(8,128)S(1)}, f32[128,128]{1,0:T(8,128)S(1)}, u32[]{:S(2)}, u32[]{:S(2)}) collective-permute-start(f32[128,128]{1,0:T(8,128)S(1)} %get-tuple-element.63), channel_id=1, source_target_pairs={{0,22},{2,20},{4,18},{6,16},{8,30},{10,28},{12,26},{14,24},{16,6},... | collective-permute-start | bytes 196616 | tf_op jit(solution)/shard_map/ppermute | solution.py:219
  55.8 8.6 %collective-permute-start.21 = (f32[128,128]{1,0:T(8,128)S(1)}, f32[128,128]{1,0:T(8,128)S(1)}, u32[]{:S(2)}, u32[]{:S(2)}) collective-permute-start(f32[128,128]{1,0:T(8,128)S(1)} %get-tuple-element.64), channel_id=1, source_target_pairs={{0,12},{2,14},{4,8},{6,10},{8,4},{10,6},{12,0},{14,2},{16,28},{18,... | collective-permute-start | bytes 196616 | tf_op jit(solution)/shard_map/ppermute | solution.py:219
  57.4 9.5 %collective-permute-start.22 = (f32[128,128]{1,0:T(8,128)S(1)}, f32[128,128]{1,0:T(8,128)S(1)}, u32[]{:S(2)}, u32[]{:S(2)}) collective-permute-start(f32[128,128]{1,0:T(8,128)S(1)} %get-tuple-element.65), channel_id=1, source_target_pairs={{0,14},{2,12},{4,10},{6,8},{8,6},{10,4},{12,2},{14,0},{16,30},{18,... | collective-permute-start | bytes 196616 | tf_op jit(solution)/shard_map/ppermute | solution.py:219
  58.3 10.0 %collective-permute-start.23 = (f32[128,128]{1,0:T(8,128)S(1)}, f32[128,128]{1,0:T(8,128)S(1)}, u32[]{:S(2)}, u32[]{:S(2)}) collective-permute-start(f32[128,128]{1,0:T(8,128)S(1)} %get-tuple-element.66), channel_id=1, source_target_pairs={{0,24},{2,26},{4,28},{6,30},{8,16},{10,18},{12,20},{14,22},{16,8},... | collective-permute-start | bytes 196616 | tf_op jit(solution)/shard_map/ppermute | solution.py:219
  60.0 8.3 %collective-permute-start.24 = (f32[128,128]{1,0:T(8,128)S(1)}, f32[128,128]{1,0:T(8,128)S(1)}, u32[]{:S(2)}, u32[]{:S(2)}) collective-permute-start(f32[128,128]{1,0:T(8,128)S(1)} %get-tuple-element.67), channel_id=1, source_target_pairs={{0,26},{2,24},{4,30},{6,28},{8,18},{10,16},{12,22},{14,20},{16,10}... | collective-permute-start | bytes 196616 | tf_op jit(solution)/shard_map/ppermute | solution.py:219
  62.2 7.5 %collective-permute-start.25 = (f32[128,128]{1,0:T(8,128)S(1)}, f32[128,128]{1,0:T(8,128)S(1)}, u32[]{:S(2)}, u32[]{:S(2)}) collective-permute-start(f32[128,128]{1,0:T(8,128)S(1)} %get-tuple-element.68), channel_id=1, source_target_pairs={{0,28},{2,30},{4,24},{6,26},{8,20},{10,22},{12,16},{14,18},{16,12}... | collective-permute-start | bytes 196616 | tf_op jit(solution)/shard_map/ppermute | solution.py:219
  64.4 6.5 %collective-permute-start.26 = (f32[128,128]{1,0:T(8,128)S(1)}, f32[128,128]{1,0:T(8,128)S(1)}, u32[]{:S(2)}, u32[]{:S(2)}) collective-permute-start(f32[128,128]{1,0:T(8,128)S(1)} %get-tuple-element.69), channel_id=1, source_target_pairs={{0,30},{2,28},{4,26},{6,24},{8,22},{10,20},{12,18},{14,16},{16,14}... | collective-permute-start | bytes 196616 | tf_op jit(solution)/shard_map/ppermute | solution.py:219
  66.9 6.0 %collective-permute-start.27 = (f32[128,128]{1,0:T(8,128)S(1)}, f32[128,128]{1,0:T(8,128)S(1)}, u32[]{:S(2)}, u32[]{:S(2)}) collective-permute-start(f32[128,128]{1,0:T(8,128)S(1)} %get-tuple-element.70), channel_id=1, source_target_pairs={{0,4},{2,6},{4,0},{6,2},{8,12},{10,14},{12,8},{14,10},{16,20},{18,... | collective-permute-start | bytes 196616 | tf_op jit(solution)/shard_map/ppermute | solution.py:219
  68.3 5.1 %collective-permute-start.28 = (f32[128,128]{1,0:T(8,128)S(1)}, f32[128,128]{1,0:T(8,128)S(1)}, u32[]{:S(2)}, u32[]{:S(2)}) collective-permute-start(f32[128,128]{1,0:T(8,128)S(1)} %get-tuple-element.71), channel_id=1, source_target_pairs={{0,6},{2,4},{4,2},{6,0},{8,14},{10,12},{12,10},{14,8},{16,22},{18,... | collective-permute-start | bytes 196616 | tf_op jit(solution)/shard_map/ppermute | solution.py:219
  68.4 5.0 %collective-permute-start.29 = (f32[128,128]{1,0:T(8,128)S(1)}, f32[128,128]{1,0:T(8,128)S(1)}, u32[]{:S(2)}, u32[]{:S(2)}) collective-permute-start(f32[128,128]{1,0:T(8,128)S(1)} %get-tuple-element.72), channel_id=1, source_target_pairs={{0,2},{2,0},{4,6},{6,4},{8,10},{10,8},{12,14},{14,12},{16,18},{18,... | collective-permute-start | bytes 196616 | tf_op jit(solution)/shard_map/ppermute | solution.py:219
  (4 other events, 3.1 us)

commit v11 on v10

--- a/solution.py
+++ b/solution.py
@@ -16,7 +16,7 @@
 PHASE_BITS = 12
 LANES = 128
 PACKED = 16
-EARLY = 5
+GROUP = 5
 TILE = 128
 PAIRED = Layout(major_to_minor=(1, 0, 2))
 
@@ -53,32 +53,15 @@
         copy.wait()
 
 
-def tables_kernel(wide, ks, spect, narrow, x_hbm, re_hbm, im_hbm, order_ref, pair_ref, angle_ref, *rest):
+def gates_kernel(wide, ks, x_hbm, re_hbm, im_hbm, order_ref, *rest):
     sends = rest[: len(ks)]
-    gate_ref, turn_ref, gates, block_sem, gate_sem = rest[len(ks) :]
+    gate_ref, gates, block_sem, gate_sem = rest[len(ks) :]
     copies = [pltpu.make_async_copy(block_of(x_hbm, k, wide), sends[i], block_sem.at[i]) for i, k in enumerate(ks)]
     gate_copies = [
         pltpu.make_async_copy(hbm, gates.at[part], gate_sem.at[part]) for part, hbm in enumerate((re_hbm, im_hbm))
     ]
     for copy in gate_copies + copies:
         copy.start()
-
-    row = lax.broadcasted_iota(jnp.int32, (spect, LOW), 0)
-    lane = lax.broadcasted_iota(jnp.int32, (spect, LOW), 1)
-    r = lax.axis_index("wide") * (spect // narrow) + row // narrow
-    turn_ref[0, 0] = jnp.ones((spect, LOW), jnp.float32)
-    turn_ref[0, 1] = jnp.zeros((spect, LOW), jnp.float32)
-    for layer in range(LAYERS):
-        b = lax.axis_index("narrow") if layer % 2 == 0 else row % narrow
-        u = ((r * narrow + b) * LOW + lane) & (2**PHASE_BITS - 1)
-        phase = jnp.zeros((spect, LOW), jnp.float32)
-        for gate in range(PHASES):
-            first = u >> jnp.full((spect, LOW), pair_ref[layer, 0, gate], jnp.int32)
-            second = u >> jnp.full((spect, LOW), pair_ref[layer, 1, gate], jnp.int32)
-            phase = phase + jnp.where((first & second & 1) == 1, angle_ref[layer, gate], 0.0)
-        turn_ref[layer + 1, 0] = jnp.cos(phase)
-        turn_ref[layer + 1, 1] = jnp.sin(phase)
-
     for copy in gate_copies:
         copy.wait()
     t = lax.broadcasted_iota(jnp.int32, (8, LOW), 1)
@@ -102,6 +85,33 @@
         copy.wait()
 
 
+def phases_kernel(wide, ks, spect, narrow, x_hbm, pair_ref, angle_ref, arrived_hbm, *rest):
+    sends = rest[: len(ks)]
+    turn_ref, block_sem = rest[len(ks) :]
+    copies = [pltpu.make_async_copy(block_of(x_hbm, k, wide), sends[i], block_sem.at[i]) for i, k in enumerate(ks)]
+    for copy in copies:
+        copy.start()
+    size = turn_ref.shape[2]
+    row = lax.broadcasted_iota(jnp.int32, (size, LOW), 0)
+    lane = lax.broadcasted_iota(jnp.int32, (size, LOW), 1)
+    r = lax.axis_index("wide") * (spect // narrow) + row // narrow
+    turn_ref[0, 0] = jnp.ones((size, LOW), jnp.float32)
+    turn_ref[0, 1] = jnp.zeros((size, LOW), jnp.float32)
+    for layer in range(LAYERS):
+        b = lax.axis_index("narrow") if layer % 2 == 0 else row % narrow
+        u = ((r * narrow + b) * LOW + lane) & (2**PHASE_BITS - 1)
+        phase = jnp.zeros((size, LOW), jnp.float32)
+        for gate in range(PHASES):
+            first = u >> jnp.full((size, LOW), pair_ref[layer, 0, gate], jnp.int32)
+            second = u >> jnp.full((size, LOW), pair_ref[layer, 1, gate], jnp.int32)
+            phase = phase + jnp.where((first & second & 1) == 1, angle_ref[layer, gate], 0.0)
+        turn_ref[layer + 1, 0] = jnp.cos(phase)
+        turn_ref[layer + 1, 1] = jnp.sin(phase)
+
+    for copy in copies:
+        copy.wait()
+
+
 def exchange_modes(rows, span):
     count = len(rows)
     group = lax.broadcasted_iota(jnp.int32, rows[0].shape, 1) // span
@@ -150,7 +160,7 @@
     def turned(slot, entry, first, size, offset, lanes):
         rows, lanes = pl.ds(first + offset, size), slice(lanes * LANES, (lanes + 1) * LANES)
         real, imag = state[slot, 0, rows, lanes], state[slot, 1, rows, lanes]
-        cosine, sine = turn[entry, 0, offset : offset + size, lanes], turn[entry, 1, offset : offset + size, lanes]
+        cosine, sine = turn[entry, 0, :, lanes], turn[entry, 1, :, lanes]
         return real * cosine - imag * sine, real * sine + imag * cosine
 
     def one_layer(layer, slot):
@@ -192,9 +202,10 @@
 
     for i, k in enumerate(exchange_order(wide)):
         first = pl.multiple_of((me ^ k) * spect, spect)
-        for lanes in range(2):
-            for part, piece in enumerate(turned(0, LAYERS, first, spect, 0, lanes)):
-                outs[i][pl.ds(2 * lanes + part, spect, stride=4), :] = piece
+        for offset in range(0, spect, rows_at_once):
+            for lanes in range(2):
+                for part, piece in enumerate(turned(0, LAYERS, first, rows_at_once, offset, lanes)):
+                    outs[i][pl.ds(4 * offset + 2 * lanes + part, rows_at_once, stride=4), :] = piece
 
 
 def local(state, gate_re, gate_im, bit_orders, phase_pairs, phase_angles):
@@ -212,7 +223,7 @@
     piece = jax.ShapeDtypeStruct((4 * spect, LANES), jnp.float32)
     part_of_vmem = pltpu.CompilerParams(vmem_limit_bytes=24 * 2**20)
     order = exchange_order(wide)
-    early, late = order[1 : 1 + EARLY], order[1 + EARLY :] + order[:1]
+    early, middle, late = order[1 : 1 + GROUP], order[1 + GROUP : 1 + 2 * GROUP], order[1 + 2 * GROUP :] + order[:1]
 
     def swap(blocks, ks):
         return [
@@ -231,22 +242,33 @@
     )(rows)
     received = swap(sends, early)
 
-    gates = jax.ShapeDtypeStruct((LAYERS, 2, LOW, 2 * LOW), jnp.bfloat16)
-    turns = jax.ShapeDtypeStruct((LAYERS + 1, 2, spect, LOW), jnp.float32)
-    *sends, gate, turn = pl.pallas_call(
-        partial(tables_kernel, wide, late, spect, narrow),
-        in_specs=[in_hbm, in_hbm, in_hbm, in_smem, in_smem, in_smem],
-        out_specs=[in_vmem] * (len(late) + 2),
-        out_shape=[piece] * len(late) + [gates, turns],
+    *sends, gate = pl.pallas_call(
+        partial(gates_kernel, wide, middle),
+        in_specs=[in_hbm, in_hbm, in_hbm, in_smem],
+        out_specs=[in_vmem] * (len(middle) + 1),
+        out_shape=[piece] * len(middle) + [jax.ShapeDtypeStruct((LAYERS, 2, LOW, 2 * LOW), jnp.bfloat16)],
         scratch_shapes=[
             pltpu.VMEM((2,) + gate_re.shape, jnp.float32),
-            pltpu.SemaphoreType.DMA((len(late),)),
+            pltpu.SemaphoreType.DMA((len(middle),)),
             pltpu.SemaphoreType.DMA((2,)),
         ],
         compiler_params=part_of_vmem,
-        cost_estimate=pl.CostEstimate(flops=10**9, bytes_accessed=8 * 10**6, transcendentals=10**5),
-        name="tables",
-    )(rows, gate_re, gate_im, bit_orders, phase_pairs.transpose(0, 2, 1), phase_angles)
+        cost_estimate=pl.CostEstimate(flops=10**9, bytes_accessed=4 * 10**6, transcendentals=0),
+        name="gates",
+    )(rows, gate_re, gate_im, bit_orders)
+    received = received + swap(sends, middle)
+
+    distinct = min(spect, 2 ** (PHASE_BITS - LOW_BITS))
+    *sends, turn = pl.pallas_call(
+        partial(phases_kernel, wide, late, spect, narrow),
+        in_specs=[in_hbm, in_smem, in_smem, in_hbm],
+        out_specs=[in_vmem] * (len(late) + 1),
+        out_shape=[piece] * len(late) + [jax.ShapeDtypeStruct((LAYERS + 1, 2, distinct, LOW), jnp.float32)],
+        scratch_shapes=[pltpu.SemaphoreType.DMA((len(late),))],
+        compiler_params=part_of_vmem,
+        cost_estimate=pl.CostEstimate(flops=10**8, bytes_accessed=4 * 10**6, transcendentals=10**5),
+        name="phases",
+    )(rows, phase_pairs.transpose(0, 2, 1), phase_angles, received[0])
     received = received + swap(sends, late)
     received = received[-1:] + received[:-1]
 

time: 74.9 us -> 73.1 us (0.976)
  starting transfers between devices: 41.2 us -> 45.2 us
  waiting for transfers between devices: 14.1 us -> 10.2 us
  local copies, waits for them, and re-layouts: 5.28 us -> 3.91 us
    ppermute x30, starting transfers between devices: 41.2 us -> 45.2 us  [swap(): lax.ppermute(block, 'wide', [(i, i ^ k) for i in range(wide)])]
    ppermute x30, waiting for transfers between devices: 14.1 us -> 10.2 us  [swap(): lax.ppermute(block, 'wide', [(i, i ^ k) for i in range(wide)])]
    unnamed x12, local copies, waits for them, and re-layouts: 5.28 us -> 3.91 us
    pallas_call x1 -> x2, Pallas kernels: 4.86 us -> 4.51 us  [the longest x1 2.47 us: local(): pl.pallas_call(partial(gates_kernel, wide, middle), in_specs=[in_hbm, in_...]
  transfers between devices with their start and end apart: 30 -> 30, of which waited for: 13 -> 8; matrix products, arithmetic and copies ran while one was open for 0% -> 0% of each run, Pallas kernels for 7% -> 6%
where the time goes in v11:
time: 73.1 us; the launch traced here: 72.9 us
  starting transfers between devices  45.2 us (62%)
  Pallas kernels  13.5 us (18%)
  waiting for transfers between devices  10.2 us (14%)
  local copies, waits for them, and re-layouts  3.91 us (5%)
    ppermute x30, starting transfers between devices, swap(): lax.ppermute(block, 'wide', [(i, i ^ k) for i in range(wide)])  45.2 us
    ppermute x30, waiting for transfers between devices, swap(): lax.ppermute(block, 'wide', [(i, i ^ k) for i in range(wide)])  10.2 us
    pallas_call x1, Pallas kernels, local(): pl.pallas_call(partial(layers_kernel, wide, spect), in_specs=[in_vmem] *...  7.42 us
    unnamed x12, local copies, waits for them, and re-layouts  3.91 us
    pallas_call x1, Pallas kernels, local(): pl.pallas_call(partial(gates_kernel, wide, middle), in_specs=[in_hbm, in_...  2.47 us
    pallas_call x1, Pallas kernels, local(): pl.pallas_call(partial(phases_kernel, wide, late, spect, narrow), in_spec...  2.05 us
  transfers between devices with their start and end apart: 30, of which 8 were waited for; matrix products, arithmetic and copies ran while one was open for 0% of the time, Pallas kernels for 6%

profile of v11, /device:TPU:0, one launch (start us, length us, event | category | flops | bytes accessed | tf_op | source)
XLA Modules:
  0.0 72.9 jit_solution(12413776251665268418)
XLA Ops:
  0.0 1.2 %copy-done = f32[2,131072]{1,0:T(2,128)S(1)} copy-done((f32[2,131072]{1,0:T(2,128)S(1)}, f32[2,131072]{1,0:T(2,128)}, u32[]{:S(2)}) %copy-start) | copy-done | bytes 1048600
  1.7 4.1 %collective-permute-start = (f32[128,128]{1,0:T(8,128)S(1)}, f32[128,128]{1,0:T(8,128)S(1)}, u32[]{:S(2)}, u32[]{:S(2)}) collective-permute-start(f32[128,128]{1,0:T(8,128)S(1)} %get-tuple-element.39), channel_id=1, source_target_pairs={{0,16},{2,18},{4,20},{6,22},{8,24},{10,26},{12,28},{14,30},{16,0},... | collective-permute-start | bytes 196616 | tf_op jit(solution)/shard_map/ppermute | solution.py:230
  5.8 1.6 %collective-permute-start.2 = (f32[128,128]{1,0:T(8,128)S(1)}, f32[128,128]{1,0:T(8,128)S(1)}, u32[]{:S(2)}, u32[]{:S(2)}) collective-permute-start(f32[128,128]{1,0:T(8,128)S(1)} %get-tuple-element.42), channel_id=1, source_target_pairs={{0,8},{2,10},{4,12},{6,14},{8,0},{10,2},{12,4},{14,6},{16,24},{18,... | collective-permute-start | bytes 196616 | tf_op jit(solution)/shard_map/ppermute | solution.py:230
  7.5 3.7 %collective-permute-start.4 = (f32[128,128]{1,0:T(8,128)S(1)}, f32[128,128]{1,0:T(8,128)S(1)}, u32[]{:S(2)}, u32[]{:S(2)}) collective-permute-start(f32[128,128]{1,0:T(8,128)S(1)} %get-tuple-element.44), channel_id=1, source_target_pairs={{0,20},{2,22},{4,16},{6,18},{8,28},{10,30},{12,24},{14,26},{16,4},... | collective-permute-start | bytes 196616 | tf_op jit(solution)/shard_map/ppermute | solution.py:230
  11.1 1.0 %copy-done.3 = f32[6,128,128]{2,1,0:T(8,128)S(1)} copy-done((f32[6,128,128]{2,1,0:T(8,128)S(1)}, f32[6,128,128]{2,1,0:T(8,128)}, u32[]{:S(2)}) %copy-start.3) | copy-done | bytes 393240
  12.1 1.0 %copy-done.4 = f32[6,128,128]{2,1,0:T(8,128)S(1)} copy-done((f32[6,128,128]{2,1,0:T(8,128)S(1)}, f32[6,128,128]{2,1,0:T(8,128)}, u32[]{:S(2)}) %copy-start.4) | copy-done | bytes 393240
  13.1 0.7 copy-done.5
  13.8 2.5 %gates.1 = (f32[128,128]{1,0:T(8,128)S(1)}, f32[128,128]{1,0:T(8,128)S(1)}, f32[128,128]{1,0:T(8,128)S(1)}, f32[128,128]{1,0:T(8,128)S(1)}, f32[128,128]{1,0:T(8...) custom-call(f32[2048,128]{1,0:T(8,128)S(1)} %bitcast.12, f32[6,128,128]{2,1,0:T(8,128)S(1)} %copy-done.3, ...), custom_call_target="tpu_custom_call" | custom-call | flops 1000000000 | bytes 4000000 | tf_op jit(solution)/shard_map/gates/pallas_call | solution.py:245
  16.4 2.5 %collective-permute-start.6 = (f32[128,128]{1,0:T(8,128)S(1)}, f32[128,128]{1,0:T(8,128)S(1)}, u32[]{:S(2)}, u32[]{:S(2)}) collective-permute-start(f32[128,128]{1,0:T(8,128)S(1)} %get-tuple-element.46), channel_id=1, source_target_pairs={{0,12},{2,14},{4,8},{6,10},{8,4},{10,6},{12,0},{14,2},{16,28},{18,... | collective-permute-start | bytes 196616 | tf_op jit(solution)/shard_map/ppermute | solution.py:230
  19.0 3.6 %collective-permute-start.8 = (f32[128,128]{1,0:T(8,128)S(1)}, f32[128,128]{1,0:T(8,128)S(1)}, u32[]{:S(2)}, u32[]{:S(2)}) collective-permute-start(f32[128,128]{1,0:T(8,128)S(1)} %get-tuple-element.48), channel_id=1, source_target_pairs={{0,24},{2,26},{4,28},{6,30},{8,16},{10,18},{12,20},{14,22},{16,8},... | collective-permute-start | bytes 196616 | tf_op jit(solution)/shard_map/ppermute | solution.py:230
  22.7 2.0 %phases.1 = (f32[128,128]{1,0:T(8,128)S(1)}, f32[128,128]{1,0:T(8,128)S(1)}, f32[128,128]{1,0:T(8,128)S(1)}, f32[128,128]{1,0:T(8,128)S(1)}, f32[128,128]{1,0:T(...) custom-call(f32[2048,128]{1,0:T(8,128)S(1)} %bitcast.13, s32[6,2,16]{2,1,0:T(2,128)S(1)} %bitcast.14, ...), custom_call_target="tpu_custom_call" | custom-call | flops 100000000 | bytes 4000000 | tf_op jit(solution)/shard_map/phases/pallas_call | solution.py:262
  24.8 4.0 %collective-permute-start.10 = (f32[128,128]{1,0:T(8,128)S(1)}, f32[128,128]{1,0:T(8,128)S(1)}, u32[]{:S(2)}, u32[]{:S(2)}) collective-permute-start(f32[128,128]{1,0:T(8,128)S(1)} %get-tuple-element.50), channel_id=1, source_target_pairs={{0,28},{2,30},{4,24},{6,26},{8,20},{10,22},{12,16},{14,18},{16,12}... | collective-permute-start | bytes 196616 | tf_op jit(solution)/shard_map/ppermute | solution.py:230
  29.4 1.3 %collective-permute-start.12 = (f32[128,128]{1,0:T(8,128)S(1)}, f32[128,128]{1,0:T(8,128)S(1)}, u32[]{:S(2)}, u32[]{:S(2)}) collective-permute-start(f32[128,128]{1,0:T(8,128)S(1)} %get-tuple-element.52), channel_id=1, source_target_pairs={{0,4},{2,6},{4,0},{6,2},{8,12},{10,14},{12,8},{14,10},{16,20},{18,... | collective-permute-start | bytes 196616 | tf_op jit(solution)/shard_map/ppermute | solution.py:230
  32.0 3.2 %collective-permute-done.11.rest_12_ = f32[128,128]{1,0:T(8,128)S(1)} collective-permute-done((f32[128,128]{1,0:T(8,128)S(1)}, f32[128,128]{1,0:T(8,128)S(1)}, u32[]{:S(2)}, u32[]{:S(2)}) %collective-permute-start.11) | collective-permute-done | bytes 65568 | tf_op jit(solution)/shard_map/ppermute | solution.py:230
  35.2 1.0 %collective-permute-done.13.rest_14_ = f32[128,128]{1,0:T(8,128)S(1)} collective-permute-done((f32[128,128]{1,0:T(8,128)S(1)}, f32[128,128]{1,0:T(8,128)S(1)}, u32[]{:S(2)}, u32[]{:S(2)}) %collective-permute-start.13) | collective-permute-done | bytes 65568 | tf_op jit(solution)/shard_map/ppermute | solution.py:230
  36.2 7.4 %layers.1 = (f32[128,128]{1,0:T(8,128)S(1)}, f32[128,128]{1,0:T(8,128)S(1)}, f32[128,128]{1,0:T(8,128)S(1)}, f32[128,128]{1,0:T(8,128)S(1)}, f32[128,128]{1,0:T(...) custom-call(f32[128,128]{1,0:T(8,128)S(1)} %get-tuple-element.40.res, ...), custom_call_target="tpu_custom_call" | custom-call | flops 5000000000 | bytes 10000000 | tf_op jit(solution)/shard_map/layers/pallas_call | solution.py:275
  43.7 2.3 %collective-permute-start.16 = (f32[128,128]{1,0:T(8,128)S(1)}, f32[128,128]{1,0:T(8,128)S(1)}, u32[]{:S(2)}, u32[]{:S(2)}) collective-permute-start(f32[128,128]{1,0:T(8,128)S(1)} %get-tuple-element.59), channel_id=1, source_target_pairs={{0,18},{2,16},{4,22},{6,20},{8,26},{10,24},{12,30},{14,28},{16,2},... | collective-permute-start | bytes 196616 | tf_op jit(solution)/shard_map/ppermute | solution.py:230
  46.1 1.6 %collective-permute-start.17 = (f32[128,128]{1,0:T(8,128)S(1)}, f32[128,128]{1,0:T(8,128)S(1)}, u32[]{:S(2)}, u32[]{:S(2)}) collective-permute-start(f32[128,128]{1,0:T(8,128)S(1)} %get-tuple-element.60), channel_id=1, source_target_pairs={{0,8},{2,10},{4,12},{6,14},{8,0},{10,2},{12,4},{14,6},{16,24},{18,... | collective-permute-start | bytes 196616 | tf_op jit(solution)/shard_map/ppermute | solution.py:230
  48.1 3.1 %collective-permute-start.19 = (f32[128,128]{1,0:T(8,128)S(1)}, f32[128,128]{1,0:T(8,128)S(1)}, u32[]{:S(2)}, u32[]{:S(2)}) collective-permute-start(f32[128,128]{1,0:T(8,128)S(1)} %get-tuple-element.62), channel_id=1, source_target_pairs={{0,20},{2,22},{4,16},{6,18},{8,28},{10,30},{12,24},{14,26},{16,4},... | collective-permute-start | bytes 196616 | tf_op jit(solution)/shard_map/ppermute | solution.py:230
  51.4 2.5 %collective-permute-start.21 = (f32[128,128]{1,0:T(8,128)S(1)}, f32[128,128]{1,0:T(8,128)S(1)}, u32[]{:S(2)}, u32[]{:S(2)}) collective-permute-start(f32[128,128]{1,0:T(8,128)S(1)} %get-tuple-element.64), channel_id=1, source_target_pairs={{0,12},{2,14},{4,8},{6,10},{8,4},{10,6},{12,0},{14,2},{16,28},{18,... | collective-permute-start | bytes 196616 | tf_op jit(solution)/shard_map/ppermute | solution.py:230
  53.9 1.7 %collective-permute-start.22 = (f32[128,128]{1,0:T(8,128)S(1)}, f32[128,128]{1,0:T(8,128)S(1)}, u32[]{:S(2)}, u32[]{:S(2)}) collective-permute-start(f32[128,128]{1,0:T(8,128)S(1)} %get-tuple-element.65), channel_id=1, source_target_pairs={{0,14},{2,12},{4,10},{6,8},{8,6},{10,4},{12,2},{14,0},{16,30},{18,... | collective-permute-start | bytes 196616 | tf_op jit(solution)/shard_map/ppermute | solution.py:230
  55.6 2.2 %collective-permute-start.23 = (f32[128,128]{1,0:T(8,128)S(1)}, f32[128,128]{1,0:T(8,128)S(1)}, u32[]{:S(2)}, u32[]{:S(2)}) collective-permute-start(f32[128,128]{1,0:T(8,128)S(1)} %get-tuple-element.66), channel_id=1, source_target_pairs={{0,24},{2,26},{4,28},{6,30},{8,16},{10,18},{12,20},{14,22},{16,8},... | collective-permute-start | bytes 196616 | tf_op jit(solution)/shard_map/ppermute | solution.py:230
  57.8 1.7 %collective-permute-start.24 = (f32[128,128]{1,0:T(8,128)S(1)}, f32[128,128]{1,0:T(8,128)S(1)}, u32[]{:S(2)}, u32[]{:S(2)}) collective-permute-start(f32[128,128]{1,0:T(8,128)S(1)} %get-tuple-element.67), channel_id=1, source_target_pairs={{0,26},{2,24},{4,30},{6,28},{8,18},{10,16},{12,22},{14,20},{16,10}... | collective-permute-start | bytes 196616 | tf_op jit(solution)/shard_map/ppermute | solution.py:230
  59.4 0.8 %collective-permute-done.20.rest_6_ = f32[128,128]{1,0:T(8,128)S(1)} collective-permute-done((f32[128,128]{1,0:T(8,128)S(1)}, f32[128,128]{1,0:T(8,128)S(1)}, u32[]{:S(2)}, u32[]{:S(2)}) %collective-permute-start.20) | collective-permute-done | bytes 65568 | tf_op jit(solution)/shard_map/ppermute | solution.py:230
  60.2 1.9 %collective-permute-start.25 = (f32[128,128]{1,0:T(8,128)S(1)}, f32[128,128]{1,0:T(8,128)S(1)}, u32[]{:S(2)}, u32[]{:S(2)}) collective-permute-start(f32[128,128]{1,0:T(8,128)S(1)} %get-tuple-element.68), channel_id=1, source_target_pairs={{0,28},{2,30},{4,24},{6,26},{8,20},{10,22},{12,16},{14,18},{16,12}... | collective-permute-start | bytes 196616 | tf_op jit(solution)/shard_map/ppermute | solution.py:230
  62.1 2.9 %collective-permute-start.26 = (f32[128,128]{1,0:T(8,128)S(1)}, f32[128,128]{1,0:T(8,128)S(1)}, u32[]{:S(2)}, u32[]{:S(2)}) collective-permute-start(f32[128,128]{1,0:T(8,128)S(1)} %get-tuple-element.69), channel_id=1, source_target_pairs={{0,30},{2,28},{4,26},{6,24},{8,22},{10,20},{12,18},{14,16},{16,14}... | collective-permute-start | bytes 196616 | tf_op jit(solution)/shard_map/ppermute | solution.py:230
  65.0 0.8 %collective-permute-start.27 = (f32[128,128]{1,0:T(8,128)S(1)}, f32[128,128]{1,0:T(8,128)S(1)}, u32[]{:S(2)}, u32[]{:S(2)}) collective-permute-start(f32[128,128]{1,0:T(8,128)S(1)} %get-tuple-element.70), channel_id=1, source_target_pairs={{0,4},{2,6},{4,0},{6,2},{8,12},{10,14},{12,8},{14,10},{16,20},{18,... | collective-permute-start | bytes 196616 | tf_op jit(solution)/shard_map/ppermute | solution.py:230
  66.4 0.7 collective-permute-start.29
  67.7 1.1 %collective-permute-done.26.rest_12_ = f32[128,128]{1,0:T(8,128)S(1)} collective-permute-done((f32[128,128]{1,0:T(8,128)S(1)}, f32[128,128]{1,0:T(8,128)S(1)}, u32[]{:S(2)}, u32[]{:S(2)}) %collective-permute-start.26) | collective-permute-done | bytes 65568 | tf_op jit(solution)/shard_map/ppermute | solution.py:230
  68.8 1.9 %collective-permute-done.27.rest_13_ = f32[128,128]{1,0:T(8,128)S(1)} collective-permute-done((f32[128,128]{1,0:T(8,128)S(1)}, f32[128,128]{1,0:T(8,128)S(1)}, u32[]{:S(2)}, u32[]{:S(2)}) %collective-permute-start.27) | collective-permute-done | bytes 65568 | tf_op jit(solution)/shard_map/ppermute | solution.py:230
  70.7 1.1 %collective-permute-done.28.rest_14_ = f32[128,128]{1,0:T(8,128)S(1)} collective-permute-done((f32[128,128]{1,0:T(8,128)S(1)}, f32[128,128]{1,0:T(8,128)S(1)}, u32[]{:S(2)}, u32[]{:S(2)}) %collective-permute-start.28) | collective-permute-done | bytes 65568 | tf_op jit(solution)/shard_map/ppermute | solution.py:230
  71.8 1.1 %place.1 = f32[2048,128]{1,0:T(8,128)} custom-call(f32[128,128]{1,0:T(8,128)S(1)} %get-tuple-element.57.rest_0_, f32[128,128]{1,0:T(8,128)S(1)} %collective-permute-done.15.rest_1_, f32[128,128]{1,0:T(8,128)S(1)} %collective-permute-done.16.rest_2_, f32[128,128]{1,0:T(8,128)S(1)} %collective-permute-done.17.rest_3_, ...), custom_call_target="tpu_custom_call" | custom-call | tf_op jit(solution)/shard_map/place/pallas_call | solution.py:291
  (45 shorter events, 4.7 us)
Async XLA Ops:
  1.2 21.5 %copy-start.1 = (s32[6,16,2]{1,2,0:T(2,128)S(1)}, s32[6,16,2]{1,2,0:T(2,128)}, u32[]{:S(2)}) copy-start(s32[6,16,2]{1,2,0:T(2,128)} %param.10) | copy-start | bytes 2308
  1.2 21.5 %copy-start.2 = (f32[6,16]{1,0:T(8,128)S(1)}, f32[6,16]{1,0:T(8,128)}, u32[]{:S(2)}) copy-start(f32[6,16]{1,0:T(8,128)} %angle_ref.1) | copy-start | bytes 1156
  1.7 14.6 %collective-permute-start = (f32[128,128]{1,0:T(8,128)S(1)}, f32[128,128]{1,0:T(8,128)S(1)}, u32[]{:S(2)}, u32[]{:S(2)}) collective-permute-start(f32[128,128]{1,0:T(8,128)S(1)} %get-tuple-element.39), channel_id=1, source_target_pairs={{0,16},{2,18},{4,20},{6,22},{8,24},{10,26},{12,28},{14,30},{16,0},... | collective-permute-start | bytes 196616 | tf_op jit(solution)/shard_map/ppermute | solution.py:230
  5.8 10.6 %collective-permute-start.1 = (f32[128,128]{1,0:T(8,128)S(1)}, f32[128,128]{1,0:T(8,128)S(1)}, u32[]{:S(2)}, u32[]{:S(2)}) collective-permute-start(f32[128,128]{1,0:T(8,128)S(1)} %get-tuple-element.41), channel_id=1, source_target_pairs={{0,18},{2,16},{4,22},{6,20},{8,26},{10,24},{12,30},{14,28},{16,2},... | collective-permute-start | bytes 196616 | tf_op jit(solution)/shard_map/ppermute | solution.py:230
  5.8 13.1 %collective-permute-start.2 = (f32[128,128]{1,0:T(8,128)S(1)}, f32[128,128]{1,0:T(8,128)S(1)}, u32[]{:S(2)}, u32[]{:S(2)}) collective-permute-start(f32[128,128]{1,0:T(8,128)S(1)} %get-tuple-element.42), channel_id=1, source_target_pairs={{0,8},{2,10},{4,12},{6,14},{8,0},{10,2},{12,4},{14,6},{16,24},{18,... | collective-permute-start | bytes 196616 | tf_op jit(solution)/shard_map/ppermute | solution.py:230
  7.4 11.6 %collective-permute-start.3 = (f32[128,128]{1,0:T(8,128)S(1)}, f32[128,128]{1,0:T(8,128)S(1)}, u32[]{:S(2)}, u32[]{:S(2)}) collective-permute-start(f32[128,128]{1,0:T(8,128)S(1)} %get-tuple-element.43), channel_id=1, source_target_pairs={{0,10},{2,8},{4,14},{6,12},{8,2},{10,0},{12,6},{14,4},{16,26},{18,... | collective-permute-start | bytes 196616 | tf_op jit(solution)/shard_map/ppermute | solution.py:230
  7.5 15.2 %collective-permute-start.4 = (f32[128,128]{1,0:T(8,128)S(1)}, f32[128,128]{1,0:T(8,128)S(1)}, u32[]{:S(2)}, u32[]{:S(2)}) collective-permute-start(f32[128,128]{1,0:T(8,128)S(1)} %get-tuple-element.44), channel_id=1, source_target_pairs={{0,20},{2,22},{4,16},{6,18},{8,28},{10,30},{12,24},{14,26},{16,4},... | collective-permute-start | bytes 196616 | tf_op jit(solution)/shard_map/ppermute | solution.py:230
  16.3 8.4 %collective-permute-start.5 = (f32[128,128]{1,0:T(8,128)S(1)}, f32[128,128]{1,0:T(8,128)S(1)}, u32[]{:S(2)}, u32[]{:S(2)}) collective-permute-start(f32[128,128]{1,0:T(8,128)S(1)} %get-tuple-element.45), channel_id=1, source_target_pairs={{0,22},{2,20},{4,18},{6,16},{8,30},{10,28},{12,26},{14,24},{16,6},... | collective-permute-start | bytes 196616 | tf_op jit(solution)/shard_map/ppermute | solution.py:230
  16.4 12.3 %collective-permute-start.6 = (f32[128,128]{1,0:T(8,128)S(1)}, f32[128,128]{1,0:T(8,128)S(1)}, u32[]{:S(2)}, u32[]{:S(2)}) collective-permute-start(f32[128,128]{1,0:T(8,128)S(1)} %get-tuple-element.46), channel_id=1, source_target_pairs={{0,12},{2,14},{4,8},{6,10},{8,4},{10,6},{12,0},{14,2},{16,28},{18,... | collective-permute-start | bytes 196616 | tf_op jit(solution)/shard_map/ppermute | solution.py:230
  18.9 10.5 %collective-permute-start.7 = (f32[128,128]{1,0:T(8,128)S(1)}, f32[128,128]{1,0:T(8,128)S(1)}, u32[]{:S(2)}, u32[]{:S(2)}) collective-permute-start(f32[128,128]{1,0:T(8,128)S(1)} %get-tuple-element.47), channel_id=1, source_target_pairs={{0,14},{2,12},{4,10},{6,8},{8,6},{10,4},{12,2},{14,0},{16,30},{18,... | collective-permute-start | bytes 196616 | tf_op jit(solution)/shard_map/ppermute | solution.py:230
  19.0 11.7 %collective-permute-start.8 = (f32[128,128]{1,0:T(8,128)S(1)}, f32[128,128]{1,0:T(8,128)S(1)}, u32[]{:S(2)}, u32[]{:S(2)}) collective-permute-start(f32[128,128]{1,0:T(8,128)S(1)} %get-tuple-element.48), channel_id=1, source_target_pairs={{0,24},{2,26},{4,28},{6,30},{8,16},{10,18},{12,20},{14,22},{16,8},... | collective-permute-start | bytes 196616 | tf_op jit(solution)/shard_map/ppermute | solution.py:230
  22.6 8.4 %collective-permute-start.9 = (f32[128,128]{1,0:T(8,128)S(1)}, f32[128,128]{1,0:T(8,128)S(1)}, u32[]{:S(2)}, u32[]{:S(2)}) collective-permute-start(f32[128,128]{1,0:T(8,128)S(1)} %get-tuple-element.49), channel_id=1, source_target_pairs={{0,26},{2,24},{4,30},{6,28},{8,18},{10,16},{12,22},{14,20},{16,10}... | collective-permute-start | bytes 196616 | tf_op jit(solution)/shard_map/ppermute | solution.py:230
  24.8 7.3 %collective-permute-start.10 = (f32[128,128]{1,0:T(8,128)S(1)}, f32[128,128]{1,0:T(8,128)S(1)}, u32[]{:S(2)}, u32[]{:S(2)}) collective-permute-start(f32[128,128]{1,0:T(8,128)S(1)} %get-tuple-element.50), channel_id=1, source_target_pairs={{0,28},{2,30},{4,24},{6,26},{8,20},{10,22},{12,16},{14,18},{16,12}... | collective-permute-start | bytes 196616 | tf_op jit(solution)/shard_map/ppermute | solution.py:230
  28.7 6.5 %collective-permute-start.11 = (f32[128,128]{1,0:T(8,128)S(1)}, f32[128,128]{1,0:T(8,128)S(1)}, u32[]{:S(2)}, u32[]{:S(2)}) collective-permute-start(f32[128,128]{1,0:T(8,128)S(1)} %get-tuple-element.51), channel_id=1, source_target_pairs={{0,30},{2,28},{4,26},{6,24},{8,22},{10,20},{12,18},{14,16},{16,14}... | collective-permute-start | bytes 196616 | tf_op jit(solution)/shard_map/ppermute | solution.py:230
  29.4 5.9 %collective-permute-start.12 = (f32[128,128]{1,0:T(8,128)S(1)}, f32[128,128]{1,0:T(8,128)S(1)}, u32[]{:S(2)}, u32[]{:S(2)}) collective-permute-start(f32[128,128]{1,0:T(8,128)S(1)} %get-tuple-element.52), channel_id=1, source_target_pairs={{0,4},{2,6},{4,0},{6,2},{8,12},{10,14},{12,8},{14,10},{16,20},{18,... | collective-permute-start | bytes 196616 | tf_op jit(solution)/shard_map/ppermute | solution.py:230
  30.7 5.5 %collective-permute-start.13 = (f32[128,128]{1,0:T(8,128)S(1)}, f32[128,128]{1,0:T(8,128)S(1)}, u32[]{:S(2)}, u32[]{:S(2)}) collective-permute-start(f32[128,128]{1,0:T(8,128)S(1)} %get-tuple-element.53), channel_id=1, source_target_pairs={{0,6},{2,4},{4,2},{6,0},{8,14},{10,12},{12,10},{14,8},{16,22},{18,... | collective-permute-start | bytes 196616 | tf_op jit(solution)/shard_map/ppermute | solution.py:230
  31.0 5.2 %collective-permute-start.14 = (f32[128,128]{1,0:T(8,128)S(1)}, f32[128,128]{1,0:T(8,128)S(1)}, u32[]{:S(2)}, u32[]{:S(2)}) collective-permute-start(f32[128,128]{1,0:T(8,128)S(1)} %get-tuple-element.54), channel_id=1, source_target_pairs={{0,2},{2,0},{4,6},{6,4},{8,10},{10,8},{12,14},{14,12},{16,18},{18,... | collective-permute-start | bytes 196616 | tf_op jit(solution)/shard_map/ppermute | solution.py:230
  43.6 7.6 %collective-permute-start.15 = (f32[128,128]{1,0:T(8,128)S(1)}, f32[128,128]{1,0:T(8,128)S(1)}, u32[]{:S(2)}, u32[]{:S(2)}) collective-permute-start(f32[128,128]{1,0:T(8,128)S(1)} %get-tuple-element.58), channel_id=1, source_target_pairs={{0,16},{2,18},{4,20},{6,22},{8,24},{10,26},{12,28},{14,30},{16,0},... | collective-permute-start | bytes 196616 | tf_op jit(solution)/shard_map/ppermute | solution.py:230
  43.7 7.6 %collective-permute-start.16 = (f32[128,128]{1,0:T(8,128)S(1)}, f32[128,128]{1,0:T(8,128)S(1)}, u32[]{:S(2)}, u32[]{:S(2)}) collective-permute-start(f32[128,128]{1,0:T(8,128)S(1)} %get-tuple-element.59), channel_id=1, source_target_pairs={{0,18},{2,16},{4,22},{6,20},{8,26},{10,24},{12,30},{14,28},{16,2},... | collective-permute-start | bytes 196616 | tf_op jit(solution)/shard_map/ppermute | solution.py:230
  46.1 7.8 %collective-permute-start.17 = (f32[128,128]{1,0:T(8,128)S(1)}, f32[128,128]{1,0:T(8,128)S(1)}, u32[]{:S(2)}, u32[]{:S(2)}) collective-permute-start(f32[128,128]{1,0:T(8,128)S(1)} %get-tuple-element.60), channel_id=1, source_target_pairs={{0,8},{2,10},{4,12},{6,14},{8,0},{10,2},{12,4},{14,6},{16,24},{18,... | collective-permute-start | bytes 196616 | tf_op jit(solution)/shard_map/ppermute | solution.py:230
  47.7 7.9 %collective-permute-start.18 = (f32[128,128]{1,0:T(8,128)S(1)}, f32[128,128]{1,0:T(8,128)S(1)}, u32[]{:S(2)}, u32[]{:S(2)}) collective-permute-start(f32[128,128]{1,0:T(8,128)S(1)} %get-tuple-element.61), channel_id=1, source_target_pairs={{0,10},{2,8},{4,14},{6,12},{8,2},{10,0},{12,6},{14,4},{16,26},{18,... | collective-permute-start | bytes 196616 | tf_op jit(solution)/shard_map/ppermute | solution.py:230
  48.1 9.6 %collective-permute-start.19 = (f32[128,128]{1,0:T(8,128)S(1)}, f32[128,128]{1,0:T(8,128)S(1)}, u32[]{:S(2)}, u32[]{:S(2)}) collective-permute-start(f32[128,128]{1,0:T(8,128)S(1)} %get-tuple-element.62), channel_id=1, source_target_pairs={{0,20},{2,22},{4,16},{6,18},{8,28},{10,30},{12,24},{14,26},{16,4},... | collective-permute-start | bytes 196616 | tf_op jit(solution)/shard_map/ppermute | solution.py:230
  51.2 9.0 %collective-permute-start.20 = (f32[128,128]{1,0:T(8,128)S(1)}, f32[128,128]{1,0:T(8,128)S(1)}, u32[]{:S(2)}, u32[]{:S(2)}) collective-permute-start(f32[128,128]{1,0:T(8,128)S(1)} %get-tuple-element.63), channel_id=1, source_target_pairs={{0,22},{2,20},{4,18},{6,16},{8,30},{10,28},{12,26},{14,24},{16,6},... | collective-permute-start | bytes 196616 | tf_op jit(solution)/shard_map/ppermute | solution.py:230
  51.4 10.7 %collective-permute-start.21 = (f32[128,128]{1,0:T(8,128)S(1)}, f32[128,128]{1,0:T(8,128)S(1)}, u32[]{:S(2)}, u32[]{:S(2)}) collective-permute-start(f32[128,128]{1,0:T(8,128)S(1)} %get-tuple-element.64), channel_id=1, source_target_pairs={{0,12},{2,14},{4,8},{6,10},{8,4},{10,6},{12,0},{14,2},{16,28},{18,... | collective-permute-start | bytes 196616 | tf_op jit(solution)/shard_map/ppermute | solution.py:230
  53.9 11.1 %collective-permute-start.22 = (f32[128,128]{1,0:T(8,128)S(1)}, f32[128,128]{1,0:T(8,128)S(1)}, u32[]{:S(2)}, u32[]{:S(2)}) collective-permute-start(f32[128,128]{1,0:T(8,128)S(1)} %get-tuple-element.65), channel_id=1, source_target_pairs={{0,14},{2,12},{4,10},{6,8},{8,6},{10,4},{12,2},{14,0},{16,30},{18,... | collective-permute-start | bytes 196616 | tf_op jit(solution)/shard_map/ppermute | solution.py:230
  55.6 10.2 %collective-permute-start.23 = (f32[128,128]{1,0:T(8,128)S(1)}, f32[128,128]{1,0:T(8,128)S(1)}, u32[]{:S(2)}, u32[]{:S(2)}) collective-permute-start(f32[128,128]{1,0:T(8,128)S(1)} %get-tuple-element.66), channel_id=1, source_target_pairs={{0,24},{2,26},{4,28},{6,30},{8,16},{10,18},{12,20},{14,22},{16,8},... | collective-permute-start | bytes 196616 | tf_op jit(solution)/shard_map/ppermute | solution.py:230
  57.8 8.7 %collective-permute-start.24 = (f32[128,128]{1,0:T(8,128)S(1)}, f32[128,128]{1,0:T(8,128)S(1)}, u32[]{:S(2)}, u32[]{:S(2)}) collective-permute-start(f32[128,128]{1,0:T(8,128)S(1)} %get-tuple-element.67), channel_id=1, source_target_pairs={{0,26},{2,24},{4,30},{6,28},{8,18},{10,16},{12,22},{14,20},{16,10}... | collective-permute-start | bytes 196616 | tf_op jit(solution)/shard_map/ppermute | solution.py:230
  60.2 7.5 %collective-permute-start.25 = (f32[128,128]{1,0:T(8,128)S(1)}, f32[128,128]{1,0:T(8,128)S(1)}, u32[]{:S(2)}, u32[]{:S(2)}) collective-permute-start(f32[128,128]{1,0:T(8,128)S(1)} %get-tuple-element.68), channel_id=1, source_target_pairs={{0,28},{2,30},{4,24},{6,26},{8,20},{10,22},{12,16},{14,18},{16,12}... | collective-permute-start | bytes 196616 | tf_op jit(solution)/shard_map/ppermute | solution.py:230
  62.1 6.7 %collective-permute-start.26 = (f32[128,128]{1,0:T(8,128)S(1)}, f32[128,128]{1,0:T(8,128)S(1)}, u32[]{:S(2)}, u32[]{:S(2)}) collective-permute-start(f32[128,128]{1,0:T(8,128)S(1)} %get-tuple-element.69), channel_id=1, source_target_pairs={{0,30},{2,28},{4,26},{6,24},{8,22},{10,20},{12,18},{14,16},{16,14}... | collective-permute-start | bytes 196616 | tf_op jit(solution)/shard_map/ppermute | solution.py:230
  65.0 5.7 %collective-permute-start.27 = (f32[128,128]{1,0:T(8,128)S(1)}, f32[128,128]{1,0:T(8,128)S(1)}, u32[]{:S(2)}, u32[]{:S(2)}) collective-permute-start(f32[128,128]{1,0:T(8,128)S(1)} %get-tuple-element.70), channel_id=1, source_target_pairs={{0,4},{2,6},{4,0},{6,2},{8,12},{10,14},{12,8},{14,10},{16,20},{18,... | collective-permute-start | bytes 196616 | tf_op jit(solution)/shard_map/ppermute | solution.py:230
  65.8 6.0 %collective-permute-start.28 = (f32[128,128]{1,0:T(8,128)S(1)}, f32[128,128]{1,0:T(8,128)S(1)}, u32[]{:S(2)}, u32[]{:S(2)}) collective-permute-start(f32[128,128]{1,0:T(8,128)S(1)} %get-tuple-element.71), channel_id=1, source_target_pairs={{0,6},{2,4},{4,2},{6,0},{8,14},{10,12},{12,10},{14,8},{16,22},{18,... | collective-permute-start | bytes 196616 | tf_op jit(solution)/shard_map/ppermute | solution.py:230
  66.4 5.3 %collective-permute-start.29 = (f32[128,128]{1,0:T(8,128)S(1)}, f32[128,128]{1,0:T(8,128)S(1)}, u32[]{:S(2)}, u32[]{:S(2)}) collective-permute-start(f32[128,128]{1,0:T(8,128)S(1)} %get-tuple-element.72), channel_id=1, source_target_pairs={{0,2},{2,0},{4,6},{6,4},{8,10},{10,8},{12,14},{14,12},{16,18},{18,... | collective-permute-start | bytes 196616 | tf_op jit(solution)/shard_map/ppermute | solution.py:230
  (4 other events, 3.9 us)

commit v12 on v10

--- a/solution.py
+++ b/solution.py
@@ -16,7 +16,7 @@
 PHASE_BITS = 12
 LANES = 128
 PACKED = 16
-EARLY = 5
+SPARE = 34
 TILE = 128
 PAIRED = Layout(major_to_minor=(1, 0, 2))
 
@@ -44,42 +44,33 @@
     return ref.at[pl.ds(pl.multiple_of(start, rows), rows)]
 
 
-def pick_kernel(wide, ks, x_hbm, *rest):
-    sends, sem = rest[:-1], rest[-1]
-    copies = [pltpu.make_async_copy(block_of(x_hbm, k, wide), sends[i], sem.at[i]) for i, k in enumerate(ks)]
+def tables_kernel(
+    spect, narrow, re_hbm, im_hbm, order_ref, pair_ref, angle_ref, gate_hbm, turn_hbm, gate_ref, turn_ref, gates, sem
+):
+    copies = [pltpu.make_async_copy(hbm, gates.at[part], sem.at[part]) for part, hbm in enumerate((re_hbm, im_hbm))]
     for copy in copies:
         copy.start()
-    for copy in copies:
-        copy.wait()
-
-
-def tables_kernel(wide, ks, spect, narrow, x_hbm, re_hbm, im_hbm, order_ref, pair_ref, angle_ref, *rest):
-    sends = rest[: len(ks)]
-    gate_ref, turn_ref, gates, block_sem, gate_sem = rest[len(ks) :]
-    copies = [pltpu.make_async_copy(block_of(x_hbm, k, wide), sends[i], block_sem.at[i]) for i, k in enumerate(ks)]
-    gate_copies = [
-        pltpu.make_async_copy(hbm, gates.at[part], gate_sem.at[part]) for part, hbm in enumerate((re_hbm, im_hbm))
-    ]
-    for copy in gate_copies + copies:
-        copy.start()
-
-    row = lax.broadcasted_iota(jnp.int32, (spect, LOW), 0)
-    lane = lax.broadcasted_iota(jnp.int32, (spect, LOW), 1)
+    size = turn_ref.shape[2]
+    row = lax.broadcasted_iota(jnp.int32, (size, LOW), 0)
+    lane = lax.broadcasted_iota(jnp.int32, (size, LOW), 1)
     r = lax.axis_index("wide") * (spect // narrow) + row // narrow
-    turn_ref[0, 0] = jnp.ones((spect, LOW), jnp.float32)
-    turn_ref[0, 1] = jnp.zeros((spect, LOW), jnp.float32)
+    turn_ref[0, 0] = jnp.ones((size, LOW), jnp.float32)
+    turn_ref[0, 1] = jnp.zeros((size, LOW), jnp.float32)
     for layer in range(LAYERS):
         b = lax.axis_index("narrow") if layer % 2 == 0 else row % narrow
         u = ((r * narrow + b) * LOW + lane) & (2**PHASE_BITS - 1)
-        phase = jnp.zeros((spect, LOW), jnp.float32)
+        phase = jnp.zeros((size, LOW), jnp.float32)
         for gate in range(PHASES):
-            first = u >> jnp.full((spect, LOW), pair_ref[layer, 0, gate], jnp.int32)
-            second = u >> jnp.full((spect, LOW), pair_ref[layer, 1, gate], jnp.int32)
+            first = u >> jnp.full((size, LOW), pair_ref[layer, 0, gate], jnp.int32)
+            second = u >> jnp.full((size, LOW), pair_ref[layer, 1, gate], jnp.int32)
             phase = phase + jnp.where((first & second & 1) == 1, angle_ref[layer, gate], 0.0)
         turn_ref[layer + 1, 0] = jnp.cos(phase)
         turn_ref[layer + 1, 1] = jnp.sin(phase)
 
-    for copy in gate_copies:
+    turn_copy = pltpu.make_async_copy(turn_ref, turn_hbm, sem.at[2])
+    turn_copy.start()
+
+    for copy in copies:
         copy.wait()
     t = lax.broadcasted_iota(jnp.int32, (8, LOW), 1)
     position = lax.broadcasted_iota(jnp.int32, (LOW // 8, 8, LOW), 0) * 8
@@ -98,8 +89,10 @@
                     )
                     start = part * LOW + e * GATE
                     gate_ref[layer, which, :, start : start + GATE] = moved.astype(jnp.bfloat16)
-    for copy in copies:
-        copy.wait()
+    gate_copy = pltpu.make_async_copy(gate_ref, gate_hbm.at[pl.ds(0, LAYERS)], sem.at[3])
+    gate_copy.start()
+    turn_copy.wait()
+    gate_copy.wait()
 
 
 def exchange_modes(rows, span):
@@ -126,11 +119,9 @@
         copy.wait()
 
 
-def layers_kernel(wide, spect, *rest):
-    received = rest[:wide]
-    gate, turn = rest[wide : wide + 2]
-    outs = rest[wide + 2 : 2 * wide + 2]
-    state, left_high, left_low, minus_imag = rest[2 * wide + 2 :]
+def layers_kernel(wide, spect, x, gate_hbm, turn_hbm, *rest):
+    outs = rest[:wide]
+    gate, turn, state, left_high, left_low, minus_imag, gate_sem, turn_sem = rest[wide:]
     me = lax.axis_index("wide")
     count = wide * spect
     span = LOW // wide
@@ -139,24 +130,25 @@
     joined = PACKED // rows_at_once
     tile = min(TILE, count)
 
-    for i, k in enumerate(exchange_order(wide)):
-        rows = pl.ds(pl.multiple_of((me ^ k) * spect, spect), spect)
-        for part in range(2):
-            for lanes in range(2):
-                state[0, part, rows, lanes * LANES : (lanes + 1) * LANES] = received[i][
-                    pl.ds(2 * lanes + part, spect, stride=4), :
-                ]
+    def gate_copy(layer):
+        return pltpu.make_async_copy(gate_hbm.at[layer], gate.at[layer], gate_sem.at[layer])
+
+    turn_copy = pltpu.make_async_copy(turn_hbm, turn, turn_sem.at[0])
+    turn_copy.start()
+    for layer in range(LAYERS):
+        gate_copy(layer).start()
+    for part in range(2):
+        for lanes in range(2):
+            state[0, part, :, lanes * LANES : (lanes + 1) * LANES] = x[pl.ds(2 * lanes + part, count, stride=4), :]
+    turn_copy.wait()
 
     def turned(slot, entry, first, size, offset, lanes):
         rows, lanes = pl.ds(first + offset, size), slice(lanes * LANES, (lanes + 1) * LANES)
         real, imag = state[slot, 0, rows, lanes], state[slot, 1, rows, lanes]
-        cosine, sine = turn[entry, 0, offset : offset + size, lanes], turn[entry, 1, offset : offset + size, lanes]
+        cosine, sine = turn[entry, 0, :, lanes], turn[entry, 1, :, lanes]
         return real * cosine - imag * sine, real * sine + imag * cosine
 
     def one_layer(layer, slot):
-        for which in range(2):
-            minus_imag[which] = -gate[layer, which, :, LOW:]
-
         for lanes in range(2):
             for top in range(2):
                 for offset in range(0, spect, rows_at_once):
@@ -172,6 +164,10 @@
                             left_high[at : at + PACKED, column : column + LANES] = high
                             left_low[at : at + PACKED, column : column + LANES] = low
 
+        gate_copy(layer).wait()
+        for which in range(2):
+            minus_imag[which] = -gate[layer, which, :, LOW:]
+
         factors = []
         for which in range(2):
             real, imag = gate[layer, which, :, :LOW], gate[layer, which, :, LOW:]
@@ -192,9 +188,10 @@
 
     for i, k in enumerate(exchange_order(wide)):
         first = pl.multiple_of((me ^ k) * spect, spect)
-        for lanes in range(2):
-            for part, piece in enumerate(turned(0, LAYERS, first, spect, 0, lanes)):
-                outs[i][pl.ds(2 * lanes + part, spect, stride=4), :] = piece
+        for offset in range(0, spect, rows_at_once):
+            for lanes in range(2):
+                for part, piece in enumerate(turned(0, LAYERS, first, rows_at_once, offset, lanes)):
+                    outs[i][pl.ds(4 * offset + 2 * lanes + part, rows_at_once, stride=4), :] = piece
 
 
 def local(state, gate_re, gate_im, bit_orders, phase_pairs, phase_angles):
@@ -206,13 +203,36 @@
 
     view = with_layout_constraint(state.reshape(2, amps // LANES, LANES), PAIRED)
     rows = view.transpose(1, 0, 2).reshape(2 * amps // LANES, LANES)
+    gathered = lax.all_to_all(rows, "wide", split_axis=0, concat_axis=0, tiled=True)
+
     in_hbm = pl.BlockSpec(memory_space=pltpu.HBM)
     in_vmem = pl.BlockSpec(memory_space=pltpu.VMEM)
     in_smem = pl.BlockSpec(memory_space=pltpu.SMEM)
     piece = jax.ShapeDtypeStruct((4 * spect, LANES), jnp.float32)
     part_of_vmem = pltpu.CompilerParams(vmem_limit_bytes=24 * 2**20)
+    most_of_vmem = pltpu.CompilerParams(vmem_limit_bytes=52 * 2**20)
     order = exchange_order(wide)
-    early, late = order[1 : 1 + EARLY], order[1 + EARLY :] + order[:1]
+
+    gates = (LAYERS, 2, LOW, 2 * LOW)
+    turns = (LAYERS + 1, 2, min(spect, 2 ** (PHASE_BITS - LOW_BITS)), LOW)
+    gate, turn = pl.pallas_call(
+        partial(tables_kernel, spect, narrow),
+        in_specs=[in_hbm, in_hbm, in_smem, in_smem, in_smem],
+        out_specs=[in_hbm, in_hbm],
+        out_shape=[
+            jax.ShapeDtypeStruct((LAYERS + SPARE,) + gates[1:], jnp.bfloat16),
+            jax.ShapeDtypeStruct(turns, jnp.float32),
+        ],
+        scratch_shapes=[
+            pltpu.VMEM(gates, jnp.bfloat16),
+            pltpu.VMEM(turns, jnp.float32),
+            pltpu.VMEM((2,) + gate_re.shape, jnp.float32),
+            pltpu.SemaphoreType.DMA((4,)),
+        ],
+        compiler_params=most_of_vmem,
+        cost_estimate=pl.CostEstimate(flops=10**9, bytes_accessed=8 * 10**6, transcendentals=10**5),
+        name="tables",
+    )(gate_re, gate_im, bit_orders, phase_pairs.transpose(0, 2, 1), phase_angles)
 
     def swap(blocks, ks):
         return [
@@ -220,51 +240,25 @@
             for block, k in zip(blocks, ks)
         ]
 
-    sends = pl.pallas_call(
-        partial(pick_kernel, wide, early),
-        in_specs=[in_hbm],
-        out_specs=[in_vmem] * len(early),
-        out_shape=[piece] * len(early),
-        scratch_shapes=[pltpu.SemaphoreType.DMA((len(early),))],
-        compiler_params=part_of_vmem,
-        name="pick",
-    )(rows)
-    received = swap(sends, early)
-
-    gates = jax.ShapeDtypeStruct((LAYERS, 2, LOW, 2 * LOW), jnp.bfloat16)
-    turns = jax.ShapeDtypeStruct((LAYERS + 1, 2, spect, LOW), jnp.float32)
-    *sends, gate, turn = pl.pallas_call(
-        partial(tables_kernel, wide, late, spect, narrow),
-        in_specs=[in_hbm, in_hbm, in_hbm, in_smem, in_smem, in_smem],
-        out_specs=[in_vmem] * (len(late) + 2),
-        out_shape=[piece] * len(late) + [gates, turns],
-        scratch_shapes=[
-            pltpu.VMEM((2,) + gate_re.shape, jnp.float32),
-            pltpu.SemaphoreType.DMA((len(late),)),
-            pltpu.SemaphoreType.DMA((2,)),
-        ],
-        compiler_params=part_of_vmem,
-        cost_estimate=pl.CostEstimate(flops=10**9, bytes_accessed=8 * 10**6, transcendentals=10**5),
-        name="tables",
-    )(rows, gate_re, gate_im, bit_orders, phase_pairs.transpose(0, 2, 1), phase_angles)
-    received = received + swap(sends, late)
-    received = received[-1:] + received[:-1]
-
     done = pl.pallas_call(
         partial(layers_kernel, wide, spect),
-        in_specs=[in_vmem] * (wide + 2),
+        in_specs=[in_vmem, in_hbm, in_hbm],
         out_specs=[in_vmem] * wide,
         out_shape=[piece] * wide,
         scratch_shapes=[
+            pltpu.VMEM(gates, jnp.bfloat16),
+            pltpu.VMEM(turns, jnp.float32),
             pltpu.VMEM((2, 2, count, LOW), jnp.float32),
             pltpu.VMEM((count, 2 * LOW), jnp.bfloat16),
             pltpu.VMEM((count, 2 * LOW), jnp.bfloat16),
             pltpu.VMEM((2, LOW, LOW), jnp.bfloat16),
+            pltpu.SemaphoreType.DMA((LAYERS,)),
+            pltpu.SemaphoreType.DMA((1,)),
         ],
-        compiler_params=part_of_vmem,
+        compiler_params=most_of_vmem,
         cost_estimate=pl.CostEstimate(flops=5 * 10**9, bytes_accessed=10**7, transcendentals=0),
         name="layers",
-    )(*received, gate, turn)
+    )(gathered, gate, turn)
 
     back = pl.pallas_call(
         partial(place_kernel, wide),

time: 74.9 us -> 74.7 us (level)
  starting transfers between devices: 41.2 us -> 29.6 us
  waiting for transfers between devices: 14.1 us -> 21.2 us
  Pallas kernels: 13.8 us -> 18.4 us
    ppermute x30 -> x15, starting transfers between devices: 41.2 us -> 22.2 us  [swap(): lax.ppermute(block, 'wide', [(i, i ^ k) for i in range(wide)])]
    all_to_all x0 -> x1, waiting for transfers between devices: none -> 14 us  [local(): lax.all_to_all(rows, 'wide', split_axis=0, concat_axis=0, tiled=True)]
    all_to_all x0 -> x1, starting transfers between devices: none -> 7.38 us  [local(): lax.all_to_all(rows, 'wide', split_axis=0, concat_axis=0, tiled=True)]
    ppermute x30 -> x15, waiting for transfers between devices: 14.1 us -> 7.17 us  [swap(): lax.ppermute(block, 'wide', [(i, i ^ k) for i in range(wide)])]
    pallas_call x3 -> x2, Pallas kernels: 12.7 us -> 17.4 us  [the longest x1 12.5 us: local(): pl.pallas_call(partial(layers_kernel, wide, spect), in_specs=[in_vmem, in...]
  transfers between devices with their start and end apart: 30 -> 16, of which waited for: 13 -> 8; matrix products, arithmetic and copies ran while one was open for 0% -> 0% of each run, Pallas kernels for 7% -> 7%
where the time goes in v12:
time: 74.7 us; the launch traced here: 74.3 us
  starting transfers between devices  29.6 us (40%)
  waiting for transfers between devices  21.2 us (28%)
  Pallas kernels  18.4 us (25%)
  local copies, waits for them, and re-layouts  5.02 us (7%)
    ppermute x15, starting transfers between devices, swap(): lax.ppermute(block, 'wide', [(i, i ^ k) for i in range(wide)])  22.2 us
    all_to_all x1, waiting for transfers between devices, local(): lax.all_to_all(rows, 'wide', split_axis=0, concat_axis=0, tiled=True)  14 us
    pallas_call x1, Pallas kernels, local(): pl.pallas_call(partial(layers_kernel, wide, spect), in_specs=[in_vmem, in...  12.5 us
    all_to_all x1, starting transfers between devices, local(): lax.all_to_all(rows, 'wide', split_axis=0, concat_axis=0, tiled=True)  7.38 us
    ppermute x15, waiting for transfers between devices, swap(): lax.ppermute(block, 'wide', [(i, i ^ k) for i in range(wide)])  7.17 us
    unnamed x12, local copies, waits for them, and re-layouts  5.02 us
    pallas_call x1, Pallas kernels, local(): pl.pallas_call(partial(tables_kernel, spect, narrow), in_specs=[in_hbm, i...  4.86 us
  transfers between devices with their start and end apart: 16, of which 8 were waited for; matrix products, arithmetic and copies ran while one was open for 0% of the time, Pallas kernels for 7%

profile of v12, /device:TPU:0, one launch (start us, length us, event | category | flops | bytes accessed | tf_op | source)
XLA Modules:
  0.0 74.3 jit_solution(18260453998042427987)
XLA Ops:
  0.0 7.4 %all-to-all-start = ((f32[16,128,128]{2,1,0:T(8,128)}), f32[16,128,128]{2,1,0:T(8,128)S(1)}, u32[]{:S(2)}, u32[]{:S(2)}) async-start(f32[16,128,128]{2,1,0:T(8,128)} %bitcast.14), calls=%async_computation | async-start | bytes 2097152 | tf_op jit(solution)/shard_map/all_to_all | solution.py:206
  7.4 0.0 copy-start
  7.4 1.0 %copy-done = f32[6,128,128]{2,1,0:T(8,128)S(1)} copy-done((f32[6,128,128]{2,1,0:T(8,128)S(1)}, f32[6,128,128]{2,1,0:T(8,128)}, u32[]{:S(2)}) %copy-start) | copy-done | bytes 393240
  8.4 1.0 %copy-done.1 = f32[6,128,128]{2,1,0:T(8,128)S(1)} copy-done((f32[6,128,128]{2,1,0:T(8,128)S(1)}, f32[6,128,128]{2,1,0:T(8,128)}, u32[]{:S(2)}) %copy-start.1) | copy-done | bytes 393240
  9.4 0.7 copy-done.2
  10.1 0.7 copy-done.3
  10.8 0.7 copy-done.4
  11.5 4.9 %tables.1 = (bf16[40,2,256,512]{3,2,1,0:T(8,128)(2,1)}, f32[7,2,16,256]{3,2,1,0:T(8,128)S(1)}) custom-call(f32[6,128,128]{2,1,0:T(8,128)S(1)} %copy-done, f32[6,128,128]{2,1,0:T(8,128)S(1)} %copy-done.1, s32[6,8]{1,0:T(8,128)S(1)} %copy-done.3, s32[6,2,16]{2,1,0:T(2,128)S(1)} %bitcast.12, f32[6,16]{1,0:T(8,128)S(1)} %copy-done.4), custom_call_target="tpu_custom_call" | custom-call | flops 1000000000 | bytes 8000000 | tf_op jit(solution)/shard_map/tables/pallas_call | solution.py:218
  16.3 14.0 %all-to-all-done = f32[16,128,128]{2,1,0:T(8,128)S(1)} async-done(((f32[16,128,128]{2,1,0:T(8,128)}), f32[16,128,128]{2,1,0:T(8,128)S(1)}, u32[]{:S(2)}, u32[]{:S(2)}) %all-to-all-start) | async-done | bytes 1048608 | tf_op jit(solution)/shard_map/all_to_all | solution.py:206
  30.3 1.0 %copy-done.5 = f32[16,128,128]{2,1,0:T(8,128)} copy-done((f32[16,128,128]{2,1,0:T(8,128)}, f32[16,128,128]{2,1,0:T(8,128)S(1)}, u32[]{:S(2)}) %copy-start.5) | copy-done | bytes 1048600
  31.3 12.5 %layers.1 = (f32[128,128]{1,0:T(8,128)S(1)}, f32[128,128]{1,0:T(8,128)S(1)}, f32[128,128]{1,0:T(8,128)S(1)}, f32[128,128]{1,0:T(8,128)S(1)}, f32[128,128]{1,0:T(...) custom-call(f32[2048,128]{1,0:T(8,128)} %bitcast.13, ...), custom_call_target="tpu_custom_call" | custom-call | flops 5000000000 | bytes 10000000 | tf_op jit(solution)/shard_map/layers/pallas_call | solution.py:243
  43.8 5.1 %collective-permute-start = (f32[128,128]{1,0:T(8,128)S(1)}, f32[128,128]{1,0:T(8,128)S(1)}, u32[]{:S(2)}, u32[]{:S(2)}) collective-permute-start(f32[128,128]{1,0:T(8,128)S(1)} %get-tuple-element.26), channel_id=1, source_target_pairs={{0,16},{2,18},{4,20},{6,22},{8,24},{10,26},{12,28},{14,30},{16,0},... | collective-permute-start | bytes 196616 | tf_op jit(solution)/shard_map/ppermute | solution.py:239
  49.0 1.2 %collective-permute-start.2 = (f32[128,128]{1,0:T(8,128)S(1)}, f32[128,128]{1,0:T(8,128)S(1)}, u32[]{:S(2)}, u32[]{:S(2)}) collective-permute-start(f32[128,128]{1,0:T(8,128)S(1)} %get-tuple-element.28), channel_id=1, source_target_pairs={{0,8},{2,10},{4,12},{6,14},{8,0},{10,2},{12,4},{14,6},{16,24},{18,... | collective-permute-start | bytes 196616 | tf_op jit(solution)/shard_map/ppermute | solution.py:239
  50.1 0.4 collective-permute-start.3
  50.5 2.1 %collective-permute-start.4 = (f32[128,128]{1,0:T(8,128)S(1)}, f32[128,128]{1,0:T(8,128)S(1)}, u32[]{:S(2)}, u32[]{:S(2)}) collective-permute-start(f32[128,128]{1,0:T(8,128)S(1)} %get-tuple-element.30), channel_id=1, source_target_pairs={{0,20},{2,22},{4,16},{6,18},{8,28},{10,30},{12,24},{14,26},{16,4},... | collective-permute-start | bytes 196616 | tf_op jit(solution)/shard_map/ppermute | solution.py:239
  52.6 1.7 %collective-permute-done.rest_1_ = f32[128,128]{1,0:T(8,128)S(1)} collective-permute-done((f32[128,128]{1,0:T(8,128)S(1)}, f32[128,128]{1,0:T(8,128)S(1)}, u32[]{:S(2)}, u32[]{:S(2)}) %collective-permute-start) | collective-permute-done | bytes 65568 | tf_op jit(solution)/shard_map/ppermute | solution.py:239
  54.4 0.9 %collective-permute-done.1.rest_2_ = f32[128,128]{1,0:T(8,128)S(1)} collective-permute-done((f32[128,128]{1,0:T(8,128)S(1)}, f32[128,128]{1,0:T(8,128)S(1)}, u32[]{:S(2)}, u32[]{:S(2)}) %collective-permute-start.1) | collective-permute-done | bytes 65568 | tf_op jit(solution)/shard_map/ppermute | solution.py:239
  55.3 1.1 %collective-permute-start.6 = (f32[128,128]{1,0:T(8,128)S(1)}, f32[128,128]{1,0:T(8,128)S(1)}, u32[]{:S(2)}, u32[]{:S(2)}) collective-permute-start(f32[128,128]{1,0:T(8,128)S(1)} %get-tuple-element.32), channel_id=1, source_target_pairs={{0,12},{2,14},{4,8},{6,10},{8,4},{10,6},{12,0},{14,2},{16,28},{18,... | collective-permute-start | bytes 196616 | tf_op jit(solution)/shard_map/ppermute | solution.py:239
  56.4 1.5 %collective-permute-start.7 = (f32[128,128]{1,0:T(8,128)S(1)}, f32[128,128]{1,0:T(8,128)S(1)}, u32[]{:S(2)}, u32[]{:S(2)}) collective-permute-start(f32[128,128]{1,0:T(8,128)S(1)} %get-tuple-element.33), channel_id=1, source_target_pairs={{0,14},{2,12},{4,10},{6,8},{8,6},{10,4},{12,2},{14,0},{16,30},{18,... | collective-permute-start | bytes 196616 | tf_op jit(solution)/shard_map/ppermute | solution.py:239
  57.8 1.6 %collective-permute-start.8 = (f32[128,128]{1,0:T(8,128)S(1)}, f32[128,128]{1,0:T(8,128)S(1)}, u32[]{:S(2)}, u32[]{:S(2)}) collective-permute-start(f32[128,128]{1,0:T(8,128)S(1)} %get-tuple-element.34), channel_id=1, source_target_pairs={{0,24},{2,26},{4,28},{6,30},{8,16},{10,18},{12,20},{14,22},{16,8},... | collective-permute-start | bytes 196616 | tf_op jit(solution)/shard_map/ppermute | solution.py:239
  59.4 2.0 %collective-permute-start.9 = (f32[128,128]{1,0:T(8,128)S(1)}, f32[128,128]{1,0:T(8,128)S(1)}, u32[]{:S(2)}, u32[]{:S(2)}) collective-permute-start(f32[128,128]{1,0:T(8,128)S(1)} %get-tuple-element.35), channel_id=1, source_target_pairs={{0,26},{2,24},{4,30},{6,28},{8,18},{10,16},{12,22},{14,20},{16,10}... | collective-permute-start | bytes 196616 | tf_op jit(solution)/shard_map/ppermute | solution.py:239
  61.5 0.2 collective-permute-done.5.rest_6_
  61.7 3.4 %collective-permute-start.10 = (f32[128,128]{1,0:T(8,128)S(1)}, f32[128,128]{1,0:T(8,128)S(1)}, u32[]{:S(2)}, u32[]{:S(2)}) collective-permute-start(f32[128,128]{1,0:T(8,128)S(1)} %get-tuple-element.36), channel_id=1, source_target_pairs={{0,28},{2,30},{4,24},{6,26},{8,20},{10,22},{12,16},{14,18},{16,12}... | collective-permute-start | bytes 196616 | tf_op jit(solution)/shard_map/ppermute | solution.py:239
  65.1 1.7 %collective-permute-start.11 = (f32[128,128]{1,0:T(8,128)S(1)}, f32[128,128]{1,0:T(8,128)S(1)}, u32[]{:S(2)}, u32[]{:S(2)}) collective-permute-start(f32[128,128]{1,0:T(8,128)S(1)} %get-tuple-element.37), channel_id=1, source_target_pairs={{0,30},{2,28},{4,26},{6,24},{8,22},{10,20},{12,18},{14,16},{16,14}... | collective-permute-start | bytes 196616 | tf_op jit(solution)/shard_map/ppermute | solution.py:239
  66.7 0.7 collective-permute-start.12
  67.4 0.4 collective-permute-start.13
  67.9 1.0 %collective-permute-start.14 = (f32[128,128]{1,0:T(8,128)S(1)}, f32[128,128]{1,0:T(8,128)S(1)}, u32[]{:S(2)}, u32[]{:S(2)}) collective-permute-start(f32[128,128]{1,0:T(8,128)S(1)} %get-tuple-element.40), channel_id=1, source_target_pairs={{0,2},{2,0},{4,6},{6,4},{8,10},{10,8},{12,14},{14,12},{16,18},{18,... | collective-permute-start | bytes 196616 | tf_op jit(solution)/shard_map/ppermute | solution.py:239
  68.9 0.4 collective-permute-done.10.rest_11_
  69.3 2.9 %collective-permute-done.11.rest_12_ = f32[128,128]{1,0:T(8,128)S(1)} collective-permute-done((f32[128,128]{1,0:T(8,128)S(1)}, f32[128,128]{1,0:T(8,128)S(1)}, u32[]{:S(2)}, u32[]{:S(2)}) %collective-permute-start.11) | collective-permute-done | bytes 65568 | tf_op jit(solution)/shard_map/ppermute | solution.py:239
  72.2 0.9 %collective-permute-done.12.rest_13_ = f32[128,128]{1,0:T(8,128)S(1)} collective-permute-done((f32[128,128]{1,0:T(8,128)S(1)}, f32[128,128]{1,0:T(8,128)S(1)}, u32[]{:S(2)}, u32[]{:S(2)}) %collective-permute-start.12) | collective-permute-done | bytes 65568 | tf_op jit(solution)/shard_map/ppermute | solution.py:239
  73.0 0.2 collective-permute-done.13.rest_14_
  73.2 1.1 %place.1 = f32[2048,128]{1,0:T(8,128)} custom-call(f32[128,128]{1,0:T(8,128)S(1)} %get-tuple-element.25.rest_0_, f32[128,128]{1,0:T(8,128)S(1)} %collective-permute-done.rest_1_, f32[128,128]{1,0:T(8,128)S(1)} %collective-permute-done.1.rest_2_, f32[128,128]{1,0:T(8,128)S(1)} %collective-permute-done.2.rest_3_, ...), custom_call_target="tpu_custom_call" | custom-call | tf_op jit(solution)/shard_map/place/pallas_call | solution.py:263
  (15 shorter events, 0.0 us)
Async XLA Ops:
  0.0 30.3 %all-to-all-start = ((f32[16,128,128]{2,1,0:T(8,128)}), f32[16,128,128]{2,1,0:T(8,128)S(1)}, u32[]{:S(2)}, u32[]{:S(2)}) async-start(f32[16,128,128]{2,1,0:T(8,128)} %bitcast.14), calls=%async_computation | async-start | bytes 2097152 | tf_op jit(solution)/shard_map/all_to_all | solution.py:206
  7.4 1.0 %copy-start = (f32[6,128,128]{2,1,0:T(8,128)S(1)}, f32[6,128,128]{2,1,0:T(8,128)}, u32[]{:S(2)}) copy-start(f32[6,128,128]{2,1,0:T(8,128)} %re_hbm.1) | copy-start | bytes 1179652
  8.4 1.0 %copy-start.1 = (f32[6,128,128]{2,1,0:T(8,128)S(1)}, f32[6,128,128]{2,1,0:T(8,128)}, u32[]{:S(2)}) copy-start(f32[6,128,128]{2,1,0:T(8,128)} %im_hbm.1) | copy-start | bytes 1179652
  9.4 0.7 copy-start.2
  10.1 0.7 copy-start.3
  10.8 0.7 copy-start.4
  30.3 1.0 %copy-start.5 = (f32[16,128,128]{2,1,0:T(8,128)}, f32[16,128,128]{2,1,0:T(8,128)S(1)}, u32[]{:S(2)}) copy-start(f32[16,128,128]{2,1,0:T(8,128)S(1)} %all-to-all-done) | copy-start | bytes 3145732
  43.8 10.5 %collective-permute-start = (f32[128,128]{1,0:T(8,128)S(1)}, f32[128,128]{1,0:T(8,128)S(1)}, u32[]{:S(2)}, u32[]{:S(2)}) collective-permute-start(f32[128,128]{1,0:T(8,128)S(1)} %get-tuple-element.26), channel_id=1, source_target_pairs={{0,16},{2,18},{4,20},{6,22},{8,24},{10,26},{12,28},{14,30},{16,0},... | collective-permute-start | bytes 196616 | tf_op jit(solution)/shard_map/ppermute | solution.py:239
  49.0 6.3 %collective-permute-start.1 = (f32[128,128]{1,0:T(8,128)S(1)}, f32[128,128]{1,0:T(8,128)S(1)}, u32[]{:S(2)}, u32[]{:S(2)}) collective-permute-start(f32[128,128]{1,0:T(8,128)S(1)} %get-tuple-element.27), channel_id=1, source_target_pairs={{0,18},{2,16},{4,22},{6,20},{8,26},{10,24},{12,30},{14,28},{16,2},... | collective-permute-start | bytes 196616 | tf_op jit(solution)/shard_map/ppermute | solution.py:239
  49.0 7.4 %collective-permute-start.2 = (f32[128,128]{1,0:T(8,128)S(1)}, f32[128,128]{1,0:T(8,128)S(1)}, u32[]{:S(2)}, u32[]{:S(2)}) collective-permute-start(f32[128,128]{1,0:T(8,128)S(1)} %get-tuple-element.28), channel_id=1, source_target_pairs={{0,8},{2,10},{4,12},{6,14},{8,0},{10,2},{12,4},{14,6},{16,24},{18,... | collective-permute-start | bytes 196616 | tf_op jit(solution)/shard_map/ppermute | solution.py:239
  50.1 7.7 %collective-permute-start.3 = (f32[128,128]{1,0:T(8,128)S(1)}, f32[128,128]{1,0:T(8,128)S(1)}, u32[]{:S(2)}, u32[]{:S(2)}) collective-permute-start(f32[128,128]{1,0:T(8,128)S(1)} %get-tuple-element.29), channel_id=1, source_target_pairs={{0,10},{2,8},{4,14},{6,12},{8,2},{10,0},{12,6},{14,4},{16,26},{18,... | collective-permute-start | bytes 196616 | tf_op jit(solution)/shard_map/ppermute | solution.py:239
  50.5 8.9 %collective-permute-start.4 = (f32[128,128]{1,0:T(8,128)S(1)}, f32[128,128]{1,0:T(8,128)S(1)}, u32[]{:S(2)}, u32[]{:S(2)}) collective-permute-start(f32[128,128]{1,0:T(8,128)S(1)} %get-tuple-element.30), channel_id=1, source_target_pairs={{0,20},{2,22},{4,16},{6,18},{8,28},{10,30},{12,24},{14,26},{16,4},... | collective-permute-start | bytes 196616 | tf_op jit(solution)/shard_map/ppermute | solution.py:239
  54.4 7.3 %collective-permute-start.5 = (f32[128,128]{1,0:T(8,128)S(1)}, f32[128,128]{1,0:T(8,128)S(1)}, u32[]{:S(2)}, u32[]{:S(2)}) collective-permute-start(f32[128,128]{1,0:T(8,128)S(1)} %get-tuple-element.31), channel_id=1, source_target_pairs={{0,22},{2,20},{4,18},{6,16},{8,30},{10,28},{12,26},{14,24},{16,6},... | collective-permute-start | bytes 196616 | tf_op jit(solution)/shard_map/ppermute | solution.py:239
  55.3 9.8 %collective-permute-start.6 = (f32[128,128]{1,0:T(8,128)S(1)}, f32[128,128]{1,0:T(8,128)S(1)}, u32[]{:S(2)}, u32[]{:S(2)}) collective-permute-start(f32[128,128]{1,0:T(8,128)S(1)} %get-tuple-element.32), channel_id=1, source_target_pairs={{0,12},{2,14},{4,8},{6,10},{8,4},{10,6},{12,0},{14,2},{16,28},{18,... | collective-permute-start | bytes 196616 | tf_op jit(solution)/shard_map/ppermute | solution.py:239
  56.4 10.4 %collective-permute-start.7 = (f32[128,128]{1,0:T(8,128)S(1)}, f32[128,128]{1,0:T(8,128)S(1)}, u32[]{:S(2)}, u32[]{:S(2)}) collective-permute-start(f32[128,128]{1,0:T(8,128)S(1)} %get-tuple-element.33), channel_id=1, source_target_pairs={{0,14},{2,12},{4,10},{6,8},{8,6},{10,4},{12,2},{14,0},{16,30},{18,... | collective-permute-start | bytes 196616 | tf_op jit(solution)/shard_map/ppermute | solution.py:239
  57.8 9.6 %collective-permute-start.8 = (f32[128,128]{1,0:T(8,128)S(1)}, f32[128,128]{1,0:T(8,128)S(1)}, u32[]{:S(2)}, u32[]{:S(2)}) collective-permute-start(f32[128,128]{1,0:T(8,128)S(1)} %get-tuple-element.34), channel_id=1, source_target_pairs={{0,24},{2,26},{4,28},{6,30},{8,16},{10,18},{12,20},{14,22},{16,8},... | collective-permute-start | bytes 196616 | tf_op jit(solution)/shard_map/ppermute | solution.py:239
  59.4 8.4 %collective-permute-start.9 = (f32[128,128]{1,0:T(8,128)S(1)}, f32[128,128]{1,0:T(8,128)S(1)}, u32[]{:S(2)}, u32[]{:S(2)}) collective-permute-start(f32[128,128]{1,0:T(8,128)S(1)} %get-tuple-element.35), channel_id=1, source_target_pairs={{0,26},{2,24},{4,30},{6,28},{8,18},{10,16},{12,22},{14,20},{16,10}... | collective-permute-start | bytes 196616 | tf_op jit(solution)/shard_map/ppermute | solution.py:239
  61.7 7.6 %collective-permute-start.10 = (f32[128,128]{1,0:T(8,128)S(1)}, f32[128,128]{1,0:T(8,128)S(1)}, u32[]{:S(2)}, u32[]{:S(2)}) collective-permute-start(f32[128,128]{1,0:T(8,128)S(1)} %get-tuple-element.36), channel_id=1, source_target_pairs={{0,28},{2,30},{4,24},{6,26},{8,20},{10,22},{12,16},{14,18},{16,12}... | collective-permute-start | bytes 196616 | tf_op jit(solution)/shard_map/ppermute | solution.py:239
  65.1 7.1 %collective-permute-start.11 = (f32[128,128]{1,0:T(8,128)S(1)}, f32[128,128]{1,0:T(8,128)S(1)}, u32[]{:S(2)}, u32[]{:S(2)}) collective-permute-start(f32[128,128]{1,0:T(8,128)S(1)} %get-tuple-element.37), channel_id=1, source_target_pairs={{0,30},{2,28},{4,26},{6,24},{8,22},{10,20},{12,18},{14,16},{16,14}... | collective-permute-start | bytes 196616 | tf_op jit(solution)/shard_map/ppermute | solution.py:239
  66.7 6.3 %collective-permute-start.12 = (f32[128,128]{1,0:T(8,128)S(1)}, f32[128,128]{1,0:T(8,128)S(1)}, u32[]{:S(2)}, u32[]{:S(2)}) collective-permute-start(f32[128,128]{1,0:T(8,128)S(1)} %get-tuple-element.38), channel_id=1, source_target_pairs={{0,4},{2,6},{4,0},{6,2},{8,12},{10,14},{12,8},{14,10},{16,20},{18,... | collective-permute-start | bytes 196616 | tf_op jit(solution)/shard_map/ppermute | solution.py:239
  67.4 5.8 %collective-permute-start.13 = (f32[128,128]{1,0:T(8,128)S(1)}, f32[128,128]{1,0:T(8,128)S(1)}, u32[]{:S(2)}, u32[]{:S(2)}) collective-permute-start(f32[128,128]{1,0:T(8,128)S(1)} %get-tuple-element.39), channel_id=1, source_target_pairs={{0,6},{2,4},{4,2},{6,0},{8,14},{10,12},{12,10},{14,8},{16,22},{18,... | collective-permute-start | bytes 196616 | tf_op jit(solution)/shard_map/ppermute | solution.py:239
  67.9 5.3 %collective-permute-start.14 = (f32[128,128]{1,0:T(8,128)S(1)}, f32[128,128]{1,0:T(8,128)S(1)}, u32[]{:S(2)}, u32[]{:S(2)}) collective-permute-start(f32[128,128]{1,0:T(8,128)S(1)} %get-tuple-element.40), channel_id=1, source_target_pairs={{0,2},{2,0},{4,6},{6,4},{8,10},{10,8},{12,14},{14,12},{16,18},{18,... | collective-permute-start | bytes 196616 | tf_op jit(solution)/shard_map/ppermute | solution.py:239

commit v13 on v12

--- a/solution.py
+++ b/solution.py
@@ -16,7 +16,6 @@
 PHASE_BITS = 12
 LANES = 128
 PACKED = 16
-SPARE = 34
 TILE = 128
 PAIRED = Layout(major_to_minor=(1, 0, 2))
 
@@ -44,12 +43,7 @@
     return ref.at[pl.ds(pl.multiple_of(start, rows), rows)]
 
 
-def tables_kernel(
-    spect, narrow, re_hbm, im_hbm, order_ref, pair_ref, angle_ref, gate_hbm, turn_hbm, gate_ref, turn_ref, gates, sem
-):
-    copies = [pltpu.make_async_copy(hbm, gates.at[part], sem.at[part]) for part, hbm in enumerate((re_hbm, im_hbm))]
-    for copy in copies:
-        copy.start()
+def tables_kernel(spect, narrow, re_ref, im_ref, order_ref, pair_ref, angle_ref, gate_ref, half_ref, turn_ref):
     size = turn_ref.shape[2]
     row = lax.broadcasted_iota(jnp.int32, (size, LOW), 0)
     lane = lax.broadcasted_iota(jnp.int32, (size, LOW), 1)
@@ -67,32 +61,21 @@
         turn_ref[layer + 1, 0] = jnp.cos(phase)
         turn_ref[layer + 1, 1] = jnp.sin(phase)
 
-    turn_copy = pltpu.make_async_copy(turn_ref, turn_hbm, sem.at[2])
-    turn_copy.start()
-
-    for copy in copies:
-        copy.wait()
-    t = lax.broadcasted_iota(jnp.int32, (8, LOW), 1)
-    position = lax.broadcasted_iota(jnp.int32, (LOW // 8, 8, LOW), 0) * 8
-    position = position + lax.broadcasted_iota(jnp.int32, (LOW // 8, 8, LOW), 1)
+    t = lax.broadcasted_iota(jnp.int32, (8, GATE), 1)
+    position = lax.broadcasted_iota(jnp.int32, (LOW // 8, 8, GATE), 0) * 8
+    position = position + lax.broadcasted_iota(jnp.int32, (LOW // 8, 8, GATE), 1)
     contract = (((1,), (1,)), ((), ()))
     for layer in range(LAYERS):
-        source = jnp.zeros((8, LOW), jnp.int32)
-        for bit in range(LOW_BITS):
-            source = source + (((t >> bit) & 1) << jnp.full((8, LOW), order_ref[layer, bit], jnp.int32))
-        hot = jnp.where(position == source[None], 1.0, 0.0).reshape(LOW, LOW).astype(jnp.bfloat16)
-        for part in range(2):
-            for which, piece in enumerate(split(gates[part, layer])):
-                for e in range(2):
-                    moved = lax.dot_general(
-                        hot[:, e * GATE : (e + 1) * GATE], piece, contract, preferred_element_type=jnp.float32
-                    )
-                    start = part * LOW + e * GATE
-                    gate_ref[layer, which, :, start : start + GATE] = moved.astype(jnp.bfloat16)
-    gate_copy = pltpu.make_async_copy(gate_ref, gate_hbm.at[pl.ds(0, LAYERS)], sem.at[3])
-    gate_copy.start()
-    turn_copy.wait()
-    gate_copy.wait()
+        source = jnp.zeros((8, GATE), jnp.int32)
+        for bit in range(LOW_BITS - 1):
+            source = source + (((t >> bit) & 1) << jnp.full((8, GATE), order_ref[layer, bit], jnp.int32))
+        half = jnp.int32(1) << order_ref[layer, LOW_BITS - 1]
+        hot = jnp.where((position & ~half) == source[None], 1.0, 0.0).reshape(LOW, GATE).astype(jnp.bfloat16)
+        half_ref[layer] = jnp.where((position & half) == 0, 1.0, 0.0).reshape(LOW, GATE).astype(jnp.bfloat16)
+        for part, ref in enumerate((re_ref, im_ref)):
+            for which, piece in enumerate(split(ref[layer])):
+                moved = lax.dot_general(hot, piece, contract, preferred_element_type=jnp.float32)
+                gate_ref[layer, which, :, part * GATE : (part + 1) * GATE] = moved.astype(jnp.bfloat16)
 
 
 def exchange_modes(rows, span):
@@ -119,9 +102,9 @@
         copy.wait()
 
 
-def layers_kernel(wide, spect, x, gate_hbm, turn_hbm, *rest):
+def layers_kernel(wide, spect, x, gate, first_half, turn, *rest):
     outs = rest[:wide]
-    gate, turn, state, left_high, left_low, minus_imag, gate_sem, turn_sem = rest[wide:]
+    state, left_high, left_low, spread = rest[wide:]
     me = lax.axis_index("wide")
     count = wide * spect
     span = LOW // wide
@@ -130,18 +113,9 @@
     joined = PACKED // rows_at_once
     tile = min(TILE, count)
 
-    def gate_copy(layer):
-        return pltpu.make_async_copy(gate_hbm.at[layer], gate.at[layer], gate_sem.at[layer])
-
-    turn_copy = pltpu.make_async_copy(turn_hbm, turn, turn_sem.at[0])
-    turn_copy.start()
-    for layer in range(LAYERS):
-        gate_copy(layer).start()
     for part in range(2):
         for lanes in range(2):
             state[0, part, :, lanes * LANES : (lanes + 1) * LANES] = x[pl.ds(2 * lanes + part, count, stride=4), :]
-    turn_copy.wait()
-
     def turned(slot, entry, first, size, offset, lanes):
         rows, lanes = pl.ds(first + offset, size), slice(lanes * LANES, (lanes + 1) * LANES)
         real, imag = state[slot, 0, rows, lanes], state[slot, 1, rows, lanes]
@@ -164,14 +138,17 @@
                             left_high[at : at + PACKED, column : column + LANES] = high
                             left_low[at : at + PACKED, column : column + LANES] = low
 
-        gate_copy(layer).wait()
+        kept = first_half[layer]
         for which in range(2):
-            minus_imag[which] = -gate[layer, which, :, LOW:]
-
-        factors = []
-        for which in range(2):
-            real, imag = gate[layer, which, :, :LOW], gate[layer, which, :, LOW:]
-            factors.append([[real, minus_imag[which]], [imag, real]])
+            for part in range(2):
+                piece = gate[layer, which, :, part * GATE : (part + 1) * GATE]
+                first = piece * kept
+                both = jnp.concatenate([first, piece - first], axis=1)
+                spread[which, part] = both
+                if part:
+                    spread[which, 2] = -both
+        factors = [[[spread[which, 0], spread[which, 2]], [spread[which, 1], spread[which, 0]]] for which in range(2)]
+
         for first in range(0, count, tile):
             rows = slice(first, first + tile)
             terms = jnp.concatenate([left_high[rows], left_low[rows], left_high[rows]], axis=1)
@@ -210,26 +187,19 @@
     in_smem = pl.BlockSpec(memory_space=pltpu.SMEM)
     piece = jax.ShapeDtypeStruct((4 * spect, LANES), jnp.float32)
     part_of_vmem = pltpu.CompilerParams(vmem_limit_bytes=24 * 2**20)
-    most_of_vmem = pltpu.CompilerParams(vmem_limit_bytes=52 * 2**20)
     order = exchange_order(wide)
 
-    gates = (LAYERS, 2, LOW, 2 * LOW)
     turns = (LAYERS + 1, 2, min(spect, 2 ** (PHASE_BITS - LOW_BITS)), LOW)
-    gate, turn = pl.pallas_call(
+    tables = pl.pallas_call(
         partial(tables_kernel, spect, narrow),
-        in_specs=[in_hbm, in_hbm, in_smem, in_smem, in_smem],
-        out_specs=[in_hbm, in_hbm],
+        in_specs=[in_vmem, in_vmem, in_smem, in_smem, in_smem],
+        out_specs=[in_vmem] * 3,
         out_shape=[
-            jax.ShapeDtypeStruct((LAYERS + SPARE,) + gates[1:], jnp.bfloat16),
+            jax.ShapeDtypeStruct((LAYERS, 2, LOW, 2 * GATE), jnp.bfloat16),
+            jax.ShapeDtypeStruct((LAYERS, LOW, GATE), jnp.bfloat16),
             jax.ShapeDtypeStruct(turns, jnp.float32),
         ],
-        scratch_shapes=[
-            pltpu.VMEM(gates, jnp.bfloat16),
-            pltpu.VMEM(turns, jnp.float32),
-            pltpu.VMEM((2,) + gate_re.shape, jnp.float32),
-            pltpu.SemaphoreType.DMA((4,)),
-        ],
-        compiler_params=most_of_vmem,
+        compiler_params=part_of_vmem,
         cost_estimate=pl.CostEstimate(flops=10**9, bytes_accessed=8 * 10**6, transcendentals=10**5),
         name="tables",
     )(gate_re, gate_im, bit_orders, phase_pairs.transpose(0, 2, 1), phase_angles)
@@ -242,23 +212,19 @@
 
     done = pl.pallas_call(
         partial(layers_kernel, wide, spect),
-        in_specs=[in_vmem, in_hbm, in_hbm],
+        in_specs=[in_vmem] * 4,
         out_specs=[in_vmem] * wide,
         out_shape=[piece] * wide,
         scratch_shapes=[
-            pltpu.VMEM(gates, jnp.bfloat16),
-            pltpu.VMEM(turns, jnp.float32),
             pltpu.VMEM((2, 2, count, LOW), jnp.float32),
             pltpu.VMEM((count, 2 * LOW), jnp.bfloat16),
             pltpu.VMEM((count, 2 * LOW), jnp.bfloat16),
-            pltpu.VMEM((2, LOW, LOW), jnp.bfloat16),
-            pltpu.SemaphoreType.DMA((LAYERS,)),
-            pltpu.SemaphoreType.DMA((1,)),
+            pltpu.VMEM((2, 3, LOW, LOW), jnp.bfloat16),
         ],
-        compiler_params=most_of_vmem,
+        compiler_params=part_of_vmem,
         cost_estimate=pl.CostEstimate(flops=5 * 10**9, bytes_accessed=10**7, transcendentals=0),
         name="layers",
-    )(gathered, gate, turn)
+    )(gathered, *tables)
 
     back = pl.pallas_call(
         partial(place_kernel, wide),

time: 74.7 us -> 70.7 us (0.946)
  Pallas kernels: 18.4 us -> 10.7 us
  waiting for transfers between devices: 21.2 us -> 26.4 us
  local copies, waits for them, and re-layouts: 5.02 us -> 3.38 us
    pallas_call x2, Pallas kernels: 17.4 us -> 9.62 us  [the longest x1 7.45 us: local(): pl.pallas_call(partial(layers_kernel, wide, spect), in_specs=[in_vmem] *...]
    all_to_all x1, waiting for transfers between devices: 14 us -> 19.3 us  [local(): lax.all_to_all(rows, 'wide', split_axis=0, concat_axis=0, tiled=True)]
    unnamed x12 -> x18, local copies, waits for them, and re-layouts: 5.02 us -> 3.38 us
  transfers between devices with their start and end apart: 16 -> 16, of which waited for: 8 -> 8; matrix products, arithmetic and copies ran while one was open for 0% -> 0% of each run, Pallas kernels for 7% -> 3%
where the time goes in v13:
time: 70.7 us; the launch traced here: 70.4 us
  starting transfers between devices  29.8 us (42%)
  waiting for transfers between devices  26.4 us (37%)
  Pallas kernels  10.7 us (15%)
  local copies, waits for them, and re-layouts  3.38 us (5%)
    ppermute x15, starting transfers between devices, swap(): lax.ppermute(block, 'wide', [(i, i ^ k) for i in range(wide)])  22.3 us
    all_to_all x1, waiting for transfers between devices, local(): lax.all_to_all(rows, 'wide', split_axis=0, concat_axis=0, tiled=True)  19.3 us
    all_to_all x1, starting transfers between devices, local(): lax.all_to_all(rows, 'wide', split_axis=0, concat_axis=0, tiled=True)  7.54 us
    pallas_call x1, Pallas kernels, local(): pl.pallas_call(partial(layers_kernel, wide, spect), in_specs=[in_vmem] *...  7.45 us
    ppermute x15, waiting for transfers between devices, swap(): lax.ppermute(block, 'wide', [(i, i ^ k) for i in range(wide)])  7.12 us
    unnamed x18, local copies, waits for them, and re-layouts  3.38 us
    pallas_call x1, Pallas kernels, local(): pl.pallas_call(partial(tables_kernel, spect, narrow), in_specs=[in_vmem,...  2.16 us
  transfers between devices with their start and end apart: 16, of which 8 were waited for; matrix products, arithmetic and copies ran while one was open for 0% of the time, Pallas kernels for 3%

profile of v13, /device:TPU:0, one launch (start us, length us, event | category | flops | bytes accessed | tf_op | source)
XLA Modules:
  0.0 70.4 jit_solution(13429085042275920832)
XLA Ops:
  0.0 7.5 %all-to-all-start = ((f32[16,128,128]{2,1,0:T(8,128)}), f32[16,128,128]{2,1,0:T(8,128)S(1)}, u32[]{:S(2)}, u32[]{:S(2)}) async-start(f32[16,128,128]{2,1,0:T(8,128)} %bitcast.14), calls=%async_computation | async-start | bytes 2097152 | tf_op jit(solution)/shard_map/all_to_all | solution.py:183
  7.6 2.2 %tables.1 = (bf16[6,2,256,256]{3,2,1,0:T(8,128)(2,1)S(1)}, bf16[6,256,128]{2,1,0:T(8,128)(2,1)S(1)}, f32[7,2,16,256]{3,2,1,0:T(8,128)S(1)}) custom-call(f32[6,128,128]{2,1,0:T(8,128)S(1)} %copy-done, f32[6,128,128]{2,1,0:T(8,128)S(1)} %copy-done.1, s32[6,8]{1,0:T(8,128)S(1)} %copy-done.3, s32[6,2,16]{2,1,0:T(2,128)S(1)} %bitcast.13, f32[6,16]{1,0:T(8,128)S(1)} %copy-done.4), custom_call_target="tpu_custom_call" | custom-call | flops 1000000000 | bytes 8000000 | tf_op jit(solution)/shard_map/tables/pallas_call | solution.py:193
  9.8 0.0 copy-start.5
  9.8 0.7 %copy-done.5 = bf16[6,256,128]{2,1,0:T(8,128)(2,1)} copy-done((bf16[6,256,128]{2,1,0:T(8,128)(2,1)}, bf16[6,256,128]{2,1,0:T(8,128)(2,1)S(1)}, u32[]{:S(2)}) %copy-start.5) | copy-done | bytes 393240
  10.5 0.7 copy-done.7
  11.2 19.3 %all-to-all-done = f32[16,128,128]{2,1,0:T(8,128)S(1)} async-done(((f32[16,128,128]{2,1,0:T(8,128)}), f32[16,128,128]{2,1,0:T(8,128)S(1)}, u32[]{:S(2)}, u32[]{:S(2)}) %all-to-all-start) | async-done | bytes 1048608 | tf_op jit(solution)/shard_map/all_to_all | solution.py:183
  30.5 1.0 %copy-done.6 = bf16[6,256,128]{2,1,0:T(8,128)(2,1)S(1)} copy-done((bf16[6,256,128]{2,1,0:T(8,128)(2,1)S(1)}, bf16[6,256,128]{2,1,0:T(8,128)(2,1)}, u32[]{:S(2)}) %copy-start.6) | copy-done | bytes 393240
  31.5 0.9 %copy-done.8 = f32[7,2,16,256]{3,2,1,0:T(8,128)S(1)} copy-done((f32[7,2,16,256]{3,2,1,0:T(8,128)S(1)}, f32[7,2,16,256]{3,2,1,0:T(8,128)}, u32[]{:S(2)}) %copy-start.8) | copy-done | bytes 229400
  32.4 7.5 %layers.1 = (f32[128,128]{1,0:T(8,128)S(1)}, f32[128,128]{1,0:T(8,128)S(1)}, f32[128,128]{1,0:T(8,128)S(1)}, f32[128,128]{1,0:T(8,128)S(1)}, f32[128,128]{1,0:T(...) custom-call(f32[2048,128]{1,0:T(8,128)S(1)} %bitcast.12, ...), custom_call_target="tpu_custom_call" | custom-call | flops 5000000000 | bytes 10000000 | tf_op jit(solution)/shard_map/layers/pallas_call | solution.py:213
  39.9 5.1 %collective-permute-start = (f32[128,128]{1,0:T(8,128)S(1)}, f32[128,128]{1,0:T(8,128)S(1)}, u32[]{:S(2)}, u32[]{:S(2)}) collective-permute-start(f32[128,128]{1,0:T(8,128)S(1)} %get-tuple-element.28), channel_id=1, source_target_pairs={{0,16},{2,18},{4,20},{6,22},{8,24},{10,26},{12,28},{14,30},{16,0},... | collective-permute-start | bytes 196616 | tf_op jit(solution)/shard_map/ppermute | solution.py:209
  45.0 0.0 collective-permute-start.1
  45.0 1.2 %collective-permute-start.2 = (f32[128,128]{1,0:T(8,128)S(1)}, f32[128,128]{1,0:T(8,128)S(1)}, u32[]{:S(2)}, u32[]{:S(2)}) collective-permute-start(f32[128,128]{1,0:T(8,128)S(1)} %get-tuple-element.30), channel_id=1, source_target_pairs={{0,8},{2,10},{4,12},{6,14},{8,0},{10,2},{12,4},{14,6},{16,24},{18,... | collective-permute-start | bytes 196616 | tf_op jit(solution)/shard_map/ppermute | solution.py:209
  46.2 0.4 collective-permute-start.3
  46.6 2.1 %collective-permute-start.4 = (f32[128,128]{1,0:T(8,128)S(1)}, f32[128,128]{1,0:T(8,128)S(1)}, u32[]{:S(2)}, u32[]{:S(2)}) collective-permute-start(f32[128,128]{1,0:T(8,128)S(1)} %get-tuple-element.32), channel_id=1, source_target_pairs={{0,20},{2,22},{4,16},{6,18},{8,28},{10,30},{12,24},{14,26},{16,4},... | collective-permute-start | bytes 196616 | tf_op jit(solution)/shard_map/ppermute | solution.py:209
  48.7 1.7 %collective-permute-done.rest_1_ = f32[128,128]{1,0:T(8,128)S(1)} collective-permute-done((f32[128,128]{1,0:T(8,128)S(1)}, f32[128,128]{1,0:T(8,128)S(1)}, u32[]{:S(2)}, u32[]{:S(2)}) %collective-permute-start) | collective-permute-done | bytes 65568 | tf_op jit(solution)/shard_map/ppermute | solution.py:209
  50.4 0.0 collective-permute-start.5
  50.4 0.9 %collective-permute-done.1.rest_2_ = f32[128,128]{1,0:T(8,128)S(1)} collective-permute-done((f32[128,128]{1,0:T(8,128)S(1)}, f32[128,128]{1,0:T(8,128)S(1)}, u32[]{:S(2)}, u32[]{:S(2)}) %collective-permute-start.1) | collective-permute-done | bytes 65568 | tf_op jit(solution)/shard_map/ppermute | solution.py:209
  51.4 1.1 %collective-permute-start.6 = (f32[128,128]{1,0:T(8,128)S(1)}, f32[128,128]{1,0:T(8,128)S(1)}, u32[]{:S(2)}, u32[]{:S(2)}) collective-permute-start(f32[128,128]{1,0:T(8,128)S(1)} %get-tuple-element.34), channel_id=1, source_target_pairs={{0,12},{2,14},{4,8},{6,10},{8,4},{10,6},{12,0},{14,2},{16,28},{18,... | collective-permute-start | bytes 196616 | tf_op jit(solution)/shard_map/ppermute | solution.py:209
  52.4 1.5 %collective-permute-start.7 = (f32[128,128]{1,0:T(8,128)S(1)}, f32[128,128]{1,0:T(8,128)S(1)}, u32[]{:S(2)}, u32[]{:S(2)}) collective-permute-start(f32[128,128]{1,0:T(8,128)S(1)} %get-tuple-element.35), channel_id=1, source_target_pairs={{0,14},{2,12},{4,10},{6,8},{8,6},{10,4},{12,2},{14,0},{16,30},{18,... | collective-permute-start | bytes 196616 | tf_op jit(solution)/shard_map/ppermute | solution.py:209
  53.9 1.6 %collective-permute-start.8 = (f32[128,128]{1,0:T(8,128)S(1)}, f32[128,128]{1,0:T(8,128)S(1)}, u32[]{:S(2)}, u32[]{:S(2)}) collective-permute-start(f32[128,128]{1,0:T(8,128)S(1)} %get-tuple-element.36), channel_id=1, source_target_pairs={{0,24},{2,26},{4,28},{6,30},{8,16},{10,18},{12,20},{14,22},{16,8},... | collective-permute-start | bytes 196616 | tf_op jit(solution)/shard_map/ppermute | solution.py:209
  55.5 2.0 %collective-permute-start.9 = (f32[128,128]{1,0:T(8,128)S(1)}, f32[128,128]{1,0:T(8,128)S(1)}, u32[]{:S(2)}, u32[]{:S(2)}) collective-permute-start(f32[128,128]{1,0:T(8,128)S(1)} %get-tuple-element.37), channel_id=1, source_target_pairs={{0,26},{2,24},{4,30},{6,28},{8,18},{10,16},{12,22},{14,20},{16,10}... | collective-permute-start | bytes 196616 | tf_op jit(solution)/shard_map/ppermute | solution.py:209
  57.6 0.2 collective-permute-done.5.rest_6_
  57.7 3.4 %collective-permute-start.10 = (f32[128,128]{1,0:T(8,128)S(1)}, f32[128,128]{1,0:T(8,128)S(1)}, u32[]{:S(2)}, u32[]{:S(2)}) collective-permute-start(f32[128,128]{1,0:T(8,128)S(1)} %get-tuple-element.38), channel_id=1, source_target_pairs={{0,28},{2,30},{4,24},{6,26},{8,20},{10,22},{12,16},{14,18},{16,12}... | collective-permute-start | bytes 196616 | tf_op jit(solution)/shard_map/ppermute | solution.py:209
  61.1 1.7 %collective-permute-start.11 = (f32[128,128]{1,0:T(8,128)S(1)}, f32[128,128]{1,0:T(8,128)S(1)}, u32[]{:S(2)}, u32[]{:S(2)}) collective-permute-start(f32[128,128]{1,0:T(8,128)S(1)} %get-tuple-element.39), channel_id=1, source_target_pairs={{0,30},{2,28},{4,26},{6,24},{8,22},{10,20},{12,18},{14,16},{16,14}... | collective-permute-start | bytes 196616 | tf_op jit(solution)/shard_map/ppermute | solution.py:209
  62.8 0.7 collective-permute-start.12
  63.5 0.4 collective-permute-start.13
  63.9 1.1 %collective-permute-start.14 = (f32[128,128]{1,0:T(8,128)S(1)}, f32[128,128]{1,0:T(8,128)S(1)}, u32[]{:S(2)}, u32[]{:S(2)}) collective-permute-start(f32[128,128]{1,0:T(8,128)S(1)} %get-tuple-element.42), channel_id=1, source_target_pairs={{0,2},{2,0},{4,6},{6,4},{8,10},{10,8},{12,14},{14,12},{16,18},{18,... | collective-permute-start | bytes 196616 | tf_op jit(solution)/shard_map/ppermute | solution.py:209
  65.0 0.3 collective-permute-done.10.rest_11_
  65.3 3.0 %collective-permute-done.11.rest_12_ = f32[128,128]{1,0:T(8,128)S(1)} collective-permute-done((f32[128,128]{1,0:T(8,128)S(1)}, f32[128,128]{1,0:T(8,128)S(1)}, u32[]{:S(2)}, u32[]{:S(2)}) %collective-permute-start.11) | collective-permute-done | bytes 65568 | tf_op jit(solution)/shard_map/ppermute | solution.py:209
  68.3 0.9 %collective-permute-done.12.rest_13_ = f32[128,128]{1,0:T(8,128)S(1)} collective-permute-done((f32[128,128]{1,0:T(8,128)S(1)}, f32[128,128]{1,0:T(8,128)S(1)}, u32[]{:S(2)}, u32[]{:S(2)}) %collective-permute-start.12) | collective-permute-done | bytes 65568 | tf_op jit(solution)/shard_map/ppermute | solution.py:209
  69.2 0.1 collective-permute-done.13.rest_14_
  69.3 1.1 %place.1 = f32[2048,128]{1,0:T(8,128)} custom-call(f32[128,128]{1,0:T(8,128)S(1)} %get-tuple-element.27.rest_0_, f32[128,128]{1,0:T(8,128)S(1)} %collective-permute-done.rest_1_, f32[128,128]{1,0:T(8,128)S(1)} %collective-permute-done.1.rest_2_, f32[128,128]{1,0:T(8,128)S(1)} %collective-permute-done.2.rest_3_, ...), custom_call_target="tpu_custom_call" | custom-call | tf_op jit(solution)/shard_map/place/pallas_call | solution.py:229
  (21 shorter events, 0.0 us)
Async XLA Ops:
  0.0 7.6 %copy-start.4 = (f32[6,16]{1,0:T(8,128)S(1)}, f32[6,16]{1,0:T(8,128)}, u32[]{:S(2)}) copy-start(f32[6,16]{1,0:T(8,128)} %angle_ref.1) | copy-start | bytes 1156
  0.0 7.6 %copy-start.2 = (s32[6,16,2]{1,2,0:T(2,128)S(1)}, s32[6,16,2]{1,2,0:T(2,128)}, u32[]{:S(2)}) copy-start(s32[6,16,2]{1,2,0:T(2,128)} %param.10) | copy-start | bytes 2308
  0.0 7.6 %copy-start.3 = (s32[6,8]{1,0:T(8,128)S(1)}, s32[6,8]{1,0:T(8,128)}, u32[]{:S(2)}) copy-start(s32[6,8]{1,0:T(8,128)} %order_ref.1) | copy-start | bytes 580
  0.0 7.6 %copy-start.1 = (f32[6,128,128]{2,1,0:T(8,128)S(1)}, f32[6,128,128]{2,1,0:T(8,128)}, u32[]{:S(2)}) copy-start(f32[6,128,128]{2,1,0:T(8,128)} %im_ref.1) | copy-start | bytes 1179652
  0.0 7.6 %copy-start = (f32[6,128,128]{2,1,0:T(8,128)S(1)}, f32[6,128,128]{2,1,0:T(8,128)}, u32[]{:S(2)}) copy-start(f32[6,128,128]{2,1,0:T(8,128)} %re_ref.1) | copy-start | bytes 1179652
  0.0 30.5 %all-to-all-start = ((f32[16,128,128]{2,1,0:T(8,128)}), f32[16,128,128]{2,1,0:T(8,128)S(1)}, u32[]{:S(2)}, u32[]{:S(2)}) async-start(f32[16,128,128]{2,1,0:T(8,128)} %bitcast.14), calls=%async_computation | async-start | bytes 2097152 | tf_op jit(solution)/shard_map/all_to_all | solution.py:183
  9.8 0.7 %copy-start.5 = (bf16[6,256,128]{2,1,0:T(8,128)(2,1)}, bf16[6,256,128]{2,1,0:T(8,128)(2,1)S(1)}, u32[]{:S(2)}) copy-start(bf16[6,256,128]{2,1,0:T(8,128)(2,1)S(1)} %get-tuple-element.25.first_half) | copy-start | bytes 1179652
  10.5 0.7 copy-start.7
  30.5 1.0 %copy-start.6 = (bf16[6,256,128]{2,1,0:T(8,128)(2,1)S(1)}, bf16[6,256,128]{2,1,0:T(8,128)(2,1)}, u32[]{:S(2)}) copy-start(bf16[6,256,128]{2,1,0:T(8,128)(2,1)} %copy-done.5) | copy-start | bytes 1179652
  31.5 0.9 %copy-start.8 = (f32[7,2,16,256]{3,2,1,0:T(8,128)S(1)}, f32[7,2,16,256]{3,2,1,0:T(8,128)}, u32[]{:S(2)}) copy-start(f32[7,2,16,256]{3,2,1,0:T(8,128)} %copy-done.7) | copy-start | bytes 688132
  39.9 10.5 %collective-permute-start = (f32[128,128]{1,0:T(8,128)S(1)}, f32[128,128]{1,0:T(8,128)S(1)}, u32[]{:S(2)}, u32[]{:S(2)}) collective-permute-start(f32[128,128]{1,0:T(8,128)S(1)} %get-tuple-element.28), channel_id=1, source_target_pairs={{0,16},{2,18},{4,20},{6,22},{8,24},{10,26},{12,28},{14,30},{16,0},... | collective-permute-start | bytes 196616 | tf_op jit(solution)/shard_map/ppermute | solution.py:209
  45.0 6.3 %collective-permute-start.1 = (f32[128,128]{1,0:T(8,128)S(1)}, f32[128,128]{1,0:T(8,128)S(1)}, u32[]{:S(2)}, u32[]{:S(2)}) collective-permute-start(f32[128,128]{1,0:T(8,128)S(1)} %get-tuple-element.29), channel_id=1, source_target_pairs={{0,18},{2,16},{4,22},{6,20},{8,26},{10,24},{12,30},{14,28},{16,2},... | collective-permute-start | bytes 196616 | tf_op jit(solution)/shard_map/ppermute | solution.py:209
  45.0 7.4 %collective-permute-start.2 = (f32[128,128]{1,0:T(8,128)S(1)}, f32[128,128]{1,0:T(8,128)S(1)}, u32[]{:S(2)}, u32[]{:S(2)}) collective-permute-start(f32[128,128]{1,0:T(8,128)S(1)} %get-tuple-element.30), channel_id=1, source_target_pairs={{0,8},{2,10},{4,12},{6,14},{8,0},{10,2},{12,4},{14,6},{16,24},{18,... | collective-permute-start | bytes 196616 | tf_op jit(solution)/shard_map/ppermute | solution.py:209
  46.2 7.7 %collective-permute-start.3 = (f32[128,128]{1,0:T(8,128)S(1)}, f32[128,128]{1,0:T(8,128)S(1)}, u32[]{:S(2)}, u32[]{:S(2)}) collective-permute-start(f32[128,128]{1,0:T(8,128)S(1)} %get-tuple-element.31), channel_id=1, source_target_pairs={{0,10},{2,8},{4,14},{6,12},{8,2},{10,0},{12,6},{14,4},{16,26},{18,... | collective-permute-start | bytes 196616 | tf_op jit(solution)/shard_map/ppermute | solution.py:209
  46.6 8.9 %collective-permute-start.4 = (f32[128,128]{1,0:T(8,128)S(1)}, f32[128,128]{1,0:T(8,128)S(1)}, u32[]{:S(2)}, u32[]{:S(2)}) collective-permute-start(f32[128,128]{1,0:T(8,128)S(1)} %get-tuple-element.32), channel_id=1, source_target_pairs={{0,20},{2,22},{4,16},{6,18},{8,28},{10,30},{12,24},{14,26},{16,4},... | collective-permute-start | bytes 196616 | tf_op jit(solution)/shard_map/ppermute | solution.py:209
  50.4 7.3 %collective-permute-start.5 = (f32[128,128]{1,0:T(8,128)S(1)}, f32[128,128]{1,0:T(8,128)S(1)}, u32[]{:S(2)}, u32[]{:S(2)}) collective-permute-start(f32[128,128]{1,0:T(8,128)S(1)} %get-tuple-element.33), channel_id=1, source_target_pairs={{0,22},{2,20},{4,18},{6,16},{8,30},{10,28},{12,26},{14,24},{16,6},... | collective-permute-start | bytes 196616 | tf_op jit(solution)/shard_map/ppermute | solution.py:209
  51.4 9.8 %collective-permute-start.6 = (f32[128,128]{1,0:T(8,128)S(1)}, f32[128,128]{1,0:T(8,128)S(1)}, u32[]{:S(2)}, u32[]{:S(2)}) collective-permute-start(f32[128,128]{1,0:T(8,128)S(1)} %get-tuple-element.34), channel_id=1, source_target_pairs={{0,12},{2,14},{4,8},{6,10},{8,4},{10,6},{12,0},{14,2},{16,28},{18,... | collective-permute-start | bytes 196616 | tf_op jit(solution)/shard_map/ppermute | solution.py:209
  52.4 10.4 %collective-permute-start.7 = (f32[128,128]{1,0:T(8,128)S(1)}, f32[128,128]{1,0:T(8,128)S(1)}, u32[]{:S(2)}, u32[]{:S(2)}) collective-permute-start(f32[128,128]{1,0:T(8,128)S(1)} %get-tuple-element.35), channel_id=1, source_target_pairs={{0,14},{2,12},{4,10},{6,8},{8,6},{10,4},{12,2},{14,0},{16,30},{18,... | collective-permute-start | bytes 196616 | tf_op jit(solution)/shard_map/ppermute | solution.py:209
  53.9 9.6 %collective-permute-start.8 = (f32[128,128]{1,0:T(8,128)S(1)}, f32[128,128]{1,0:T(8,128)S(1)}, u32[]{:S(2)}, u32[]{:S(2)}) collective-permute-start(f32[128,128]{1,0:T(8,128)S(1)} %get-tuple-element.36), channel_id=1, source_target_pairs={{0,24},{2,26},{4,28},{6,30},{8,16},{10,18},{12,20},{14,22},{16,8},... | collective-permute-start | bytes 196616 | tf_op jit(solution)/shard_map/ppermute | solution.py:209
  55.5 8.4 %collective-permute-start.9 = (f32[128,128]{1,0:T(8,128)S(1)}, f32[128,128]{1,0:T(8,128)S(1)}, u32[]{:S(2)}, u32[]{:S(2)}) collective-permute-start(f32[128,128]{1,0:T(8,128)S(1)} %get-tuple-element.37), channel_id=1, source_target_pairs={{0,26},{2,24},{4,30},{6,28},{8,18},{10,16},{12,22},{14,20},{16,10}... | collective-permute-start | bytes 196616 | tf_op jit(solution)/shard_map/ppermute | solution.py:209
  57.7 7.6 %collective-permute-start.10 = (f32[128,128]{1,0:T(8,128)S(1)}, f32[128,128]{1,0:T(8,128)S(1)}, u32[]{:S(2)}, u32[]{:S(2)}) collective-permute-start(f32[128,128]{1,0:T(8,128)S(1)} %get-tuple-element.38), channel_id=1, source_target_pairs={{0,28},{2,30},{4,24},{6,26},{8,20},{10,22},{12,16},{14,18},{16,12}... | collective-permute-start | bytes 196616 | tf_op jit(solution)/shard_map/ppermute | solution.py:209
  61.1 7.1 %collective-permute-start.11 = (f32[128,128]{1,0:T(8,128)S(1)}, f32[128,128]{1,0:T(8,128)S(1)}, u32[]{:S(2)}, u32[]{:S(2)}) collective-permute-start(f32[128,128]{1,0:T(8,128)S(1)} %get-tuple-element.39), channel_id=1, source_target_pairs={{0,30},{2,28},{4,26},{6,24},{8,22},{10,20},{12,18},{14,16},{16,14}... | collective-permute-start | bytes 196616 | tf_op jit(solution)/shard_map/ppermute | solution.py:209
  62.8 6.3 %collective-permute-start.12 = (f32[128,128]{1,0:T(8,128)S(1)}, f32[128,128]{1,0:T(8,128)S(1)}, u32[]{:S(2)}, u32[]{:S(2)}) collective-permute-start(f32[128,128]{1,0:T(8,128)S(1)} %get-tuple-element.40), channel_id=1, source_target_pairs={{0,4},{2,6},{4,0},{6,2},{8,12},{10,14},{12,8},{14,10},{16,20},{18,... | collective-permute-start | bytes 196616 | tf_op jit(solution)/shard_map/ppermute | solution.py:209
  63.5 5.8 %collective-permute-start.13 = (f32[128,128]{1,0:T(8,128)S(1)}, f32[128,128]{1,0:T(8,128)S(1)}, u32[]{:S(2)}, u32[]{:S(2)}) collective-permute-start(f32[128,128]{1,0:T(8,128)S(1)} %get-tuple-element.41), channel_id=1, source_target_pairs={{0,6},{2,4},{4,2},{6,0},{8,14},{10,12},{12,10},{14,8},{16,22},{18,... | collective-permute-start | bytes 196616 | tf_op jit(solution)/shard_map/ppermute | solution.py:209
  63.9 5.4 %collective-permute-start.14 = (f32[128,128]{1,0:T(8,128)S(1)}, f32[128,128]{1,0:T(8,128)S(1)}, u32[]{:S(2)}, u32[]{:S(2)}) collective-permute-start(f32[128,128]{1,0:T(8,128)S(1)} %get-tuple-element.42), channel_id=1, source_target_pairs={{0,2},{2,0},{4,6},{6,4},{8,10},{10,8},{12,14},{14,12},{16,18},{18,... | collective-permute-start | bytes 196616 | tf_op jit(solution)/shard_map/ppermute | solution.py:209

commit v14 on v13

--- a/solution.py
+++ b/solution.py
@@ -16,7 +16,7 @@
 PHASE_BITS = 12
 LANES = 128
 PACKED = 16
-TILE = 128
+TILE = 256
 PAIRED = Layout(major_to_minor=(1, 0, 2))
 
 
@@ -43,7 +43,7 @@
     return ref.at[pl.ds(pl.multiple_of(start, rows), rows)]
 
 
-def tables_kernel(spect, narrow, re_ref, im_ref, order_ref, pair_ref, angle_ref, gate_ref, half_ref, turn_ref):
+def tables_kernel(spect, narrow, re_ref, im_ref, order_ref, pair_ref, angle_ref, gate_ref, turn_ref):
     size = turn_ref.shape[2]
     row = lax.broadcasted_iota(jnp.int32, (size, LOW), 0)
     lane = lax.broadcasted_iota(jnp.int32, (size, LOW), 1)
@@ -71,7 +71,6 @@
             source = source + (((t >> bit) & 1) << jnp.full((8, GATE), order_ref[layer, bit], jnp.int32))
         half = jnp.int32(1) << order_ref[layer, LOW_BITS - 1]
         hot = jnp.where((position & ~half) == source[None], 1.0, 0.0).reshape(LOW, GATE).astype(jnp.bfloat16)
-        half_ref[layer] = jnp.where((position & half) == 0, 1.0, 0.0).reshape(LOW, GATE).astype(jnp.bfloat16)
         for part, ref in enumerate((re_ref, im_ref)):
             for which, piece in enumerate(split(ref[layer])):
                 moved = lax.dot_general(hot, piece, contract, preferred_element_type=jnp.float32)
@@ -102,7 +101,7 @@
         copy.wait()
 
 
-def layers_kernel(wide, spect, x, gate, first_half, turn, *rest):
+def layers_kernel(wide, spect, order_ref, x, gate, turn, *rest):
     outs = rest[:wide]
     state, left_high, left_low, spread = rest[wide:]
     me = lax.axis_index("wide")
@@ -138,7 +137,9 @@
                             left_high[at : at + PACKED, column : column + LANES] = high
                             left_low[at : at + PACKED, column : column + LANES] = low
 
-        kept = first_half[layer]
+        half_bit = jnp.int32(1) << order_ref[layer, LOW_BITS - 1]
+        position = lax.broadcasted_iota(jnp.int32, (LOW, GATE), 0)
+        kept = jnp.where((position & half_bit) == 0, 1.0, 0.0).astype(jnp.bfloat16)
         for which in range(2):
             for part in range(2):
                 piece = gate[layer, which, :, part * GATE : (part + 1) * GATE]
@@ -193,10 +194,9 @@
     tables = pl.pallas_call(
         partial(tables_kernel, spect, narrow),
         in_specs=[in_vmem, in_vmem, in_smem, in_smem, in_smem],
-        out_specs=[in_vmem] * 3,
+        out_specs=[in_vmem] * 2,
         out_shape=[
             jax.ShapeDtypeStruct((LAYERS, 2, LOW, 2 * GATE), jnp.bfloat16),
-            jax.ShapeDtypeStruct((LAYERS, LOW, GATE), jnp.bfloat16),
             jax.ShapeDtypeStruct(turns, jnp.float32),
         ],
         compiler_params=part_of_vmem,
@@ -212,7 +212,7 @@
 
     done = pl.pallas_call(
         partial(layers_kernel, wide, spect),
-        in_specs=[in_vmem] * 4,
+        in_specs=[in_smem] + [in_vmem] * 3,
         out_specs=[in_vmem] * wide,
         out_shape=[piece] * wide,
         scratch_shapes=[
@@ -224,7 +224,7 @@
         compiler_params=part_of_vmem,
         cost_estimate=pl.CostEstimate(flops=5 * 10**9, bytes_accessed=10**7, transcendentals=0),
         name="layers",
-    )(gathered, *tables)
+    )(bit_orders, gathered, *tables)
 
     back = pl.pallas_call(
         partial(place_kernel, wide),

time: 70.7 us -> 70.5 us (level)
  local copies, waits for them, and re-layouts: 3.38 us -> 1.64 us
  waiting for transfers between devices: 26.4 us -> 27.3 us
  Pallas kernels: 10.7 us -> 11.5 us
    unnamed x18 -> x14, local copies, waits for them, and re-layouts: 3.38 us -> 1.64 us
    pallas_call x1, Pallas kernels: 7.45 us -> 8.31 us  [local(): pl.pallas_call(partial(layers_kernel, wide, spect), in_specs=[in_smem] +...]
    all_to_all x1, waiting for transfers between devices: 19.3 us -> 20.1 us  [local(): lax.all_to_all(rows, 'wide', split_axis=0, concat_axis=0, tiled=True)]
where the time goes in v14:
time: 70.5 us; the launch traced here: 70.3 us
  starting transfers between devices  29.8 us (42%)
  waiting for transfers between devices  27.3 us (39%)
  Pallas kernels  11.5 us (16%)
  local copies, waits for them, and re-layouts  1.64 us (2%)
    ppermute x15, starting transfers between devices, swap(): lax.ppermute(block, 'wide', [(i, i ^ k) for i in range(wide)])  22.3 us
    all_to_all x1, waiting for transfers between devices, local(): lax.all_to_all(rows, 'wide', split_axis=0, concat_axis=0, tiled=True)  20.1 us
    pallas_call x1, Pallas kernels, local(): pl.pallas_call(partial(layers_kernel, wide, spect), in_specs=[in_smem] +...  8.31 us
    all_to_all x1, starting transfers between devices, local(): lax.all_to_all(rows, 'wide', split_axis=0, concat_axis=0, tiled=True)  7.54 us
    ppermute x15, waiting for transfers between devices, swap(): lax.ppermute(block, 'wide', [(i, i ^ k) for i in range(wide)])  7.12 us
    pallas_call x1, Pallas kernels, local(): pl.pallas_call(partial(tables_kernel, spect, narrow), in_specs=[in_vmem,...  2.06 us
    unnamed x14, local copies, waits for them, and re-layouts  1.64 us
  transfers between devices with their start and end apart: 16, of which 8 were waited for; matrix products, arithmetic and copies ran while one was open for 0% of the time, Pallas kernels for 3%

profile of v14, /device:TPU:0, one launch (start us, length us, event | category | flops | bytes accessed | tf_op | source)
XLA Modules:
  0.0 70.3 jit_solution(13625006320911233228)
XLA Ops:
  0.0 7.5 %all-to-all-start = ((f32[16,128,128]{2,1,0:T(8,128)}), f32[16,128,128]{2,1,0:T(8,128)S(1)}, u32[]{:S(2)}, u32[]{:S(2)}) async-start(f32[16,128,128]{2,1,0:T(8,128)} %bitcast.14), calls=%async_computation | async-start | bytes 2097152 | tf_op jit(solution)/shard_map/all_to_all | solution.py:184
  7.6 2.1 %tables.1 = (bf16[6,2,256,256]{3,2,1,0:T(8,128)(2,1)S(1)}, f32[7,2,16,256]{3,2,1,0:T(8,128)S(1)}) custom-call(f32[6,128,128]{2,1,0:T(8,128)S(1)} %copy-done, f32[6,128,128]{2,1,0:T(8,128)S(1)} %copy-done.1, s32[6,8]{1,0:T(8,128)S(1)} %copy-done.4, s32[6,2,16]{2,1,0:T(2,128)S(1)} %bitcast.13, f32[6,16]{1,0:T(8,128)S(1)} %copy-done.3), custom_call_target="tpu_custom_call" | custom-call | flops 1000000000 | bytes 8000000 | tf_op jit(solution)/shard_map/tables/pallas_call | solution.py:194
  9.7 0.0 copy-start.5
  9.7 0.7 copy-done.5
  10.4 20.1 %all-to-all-done = f32[16,128,128]{2,1,0:T(8,128)S(1)} async-done(((f32[16,128,128]{2,1,0:T(8,128)}), f32[16,128,128]{2,1,0:T(8,128)S(1)}, u32[]{:S(2)}, u32[]{:S(2)}) %all-to-all-start) | async-done | bytes 1048608 | tf_op jit(solution)/shard_map/all_to_all | solution.py:184
  30.5 0.9 %copy-done.6 = f32[7,2,16,256]{3,2,1,0:T(8,128)S(1)} copy-done((f32[7,2,16,256]{3,2,1,0:T(8,128)S(1)}, f32[7,2,16,256]{3,2,1,0:T(8,128)}, u32[]{:S(2)}) %copy-start.6) | copy-done | bytes 229400
  31.4 8.3 %layers.1 = (f32[128,128]{1,0:T(8,128)S(1)}, f32[128,128]{1,0:T(8,128)S(1)}, f32[128,128]{1,0:T(8,128)S(1)}, f32[128,128]{1,0:T(8,128)S(1)}, f32[128,128]{1,0:T(...) custom-call(s32[6,8]{1,0:T(8,128)S(1)} %copy-done.4, ...), custom_call_target="tpu_custom_call" | custom-call | flops 5000000000 | bytes 10000000 | tf_op jit(solution)/shard_map/layers/pallas_call | solution.py:213
  39.8 5.1 %collective-permute-start = (f32[128,128]{1,0:T(8,128)S(1)}, f32[128,128]{1,0:T(8,128)S(1)}, u32[]{:S(2)}, u32[]{:S(2)}) collective-permute-start(f32[128,128]{1,0:T(8,128)S(1)} %get-tuple-element.26), channel_id=1, source_target_pairs={{0,16},{2,18},{4,20},{6,22},{8,24},{10,26},{12,28},{14,30},{16,0},... | collective-permute-start | bytes 196616 | tf_op jit(solution)/shard_map/ppermute | solution.py:209
  44.9 1.2 %collective-permute-start.2 = (f32[128,128]{1,0:T(8,128)S(1)}, f32[128,128]{1,0:T(8,128)S(1)}, u32[]{:S(2)}, u32[]{:S(2)}) collective-permute-start(f32[128,128]{1,0:T(8,128)S(1)} %get-tuple-element.28), channel_id=1, source_target_pairs={{0,8},{2,10},{4,12},{6,14},{8,0},{10,2},{12,4},{14,6},{16,24},{18,... | collective-permute-start | bytes 196616 | tf_op jit(solution)/shard_map/ppermute | solution.py:209
  46.1 0.4 collective-permute-start.3
  46.4 2.1 %collective-permute-start.4 = (f32[128,128]{1,0:T(8,128)S(1)}, f32[128,128]{1,0:T(8,128)S(1)}, u32[]{:S(2)}, u32[]{:S(2)}) collective-permute-start(f32[128,128]{1,0:T(8,128)S(1)} %get-tuple-element.30), channel_id=1, source_target_pairs={{0,20},{2,22},{4,16},{6,18},{8,28},{10,30},{12,24},{14,26},{16,4},... | collective-permute-start | bytes 196616 | tf_op jit(solution)/shard_map/ppermute | solution.py:209
  48.6 1.7 %collective-permute-done.rest_1_ = f32[128,128]{1,0:T(8,128)S(1)} collective-permute-done((f32[128,128]{1,0:T(8,128)S(1)}, f32[128,128]{1,0:T(8,128)S(1)}, u32[]{:S(2)}, u32[]{:S(2)}) %collective-permute-start) | collective-permute-done | bytes 65568 | tf_op jit(solution)/shard_map/ppermute | solution.py:209
  50.3 0.0 collective-permute-start.5
  50.3 0.9 %collective-permute-done.1.rest_2_ = f32[128,128]{1,0:T(8,128)S(1)} collective-permute-done((f32[128,128]{1,0:T(8,128)S(1)}, f32[128,128]{1,0:T(8,128)S(1)}, u32[]{:S(2)}, u32[]{:S(2)}) %collective-permute-start.1) | collective-permute-done | bytes 65568 | tf_op jit(solution)/shard_map/ppermute | solution.py:209
  51.2 1.1 %collective-permute-start.6 = (f32[128,128]{1,0:T(8,128)S(1)}, f32[128,128]{1,0:T(8,128)S(1)}, u32[]{:S(2)}, u32[]{:S(2)}) collective-permute-start(f32[128,128]{1,0:T(8,128)S(1)} %get-tuple-element.32), channel_id=1, source_target_pairs={{0,12},{2,14},{4,8},{6,10},{8,4},{10,6},{12,0},{14,2},{16,28},{18,... | collective-permute-start | bytes 196616 | tf_op jit(solution)/shard_map/ppermute | solution.py:209
  52.3 0.0 collective-permute-done.2.rest_3_
  52.3 1.5 %collective-permute-start.7 = (f32[128,128]{1,0:T(8,128)S(1)}, f32[128,128]{1,0:T(8,128)S(1)}, u32[]{:S(2)}, u32[]{:S(2)}) collective-permute-start(f32[128,128]{1,0:T(8,128)S(1)} %get-tuple-element.33), channel_id=1, source_target_pairs={{0,14},{2,12},{4,10},{6,8},{8,6},{10,4},{12,2},{14,0},{16,30},{18,... | collective-permute-start | bytes 196616 | tf_op jit(solution)/shard_map/ppermute | solution.py:209
  53.8 1.6 %collective-permute-start.8 = (f32[128,128]{1,0:T(8,128)S(1)}, f32[128,128]{1,0:T(8,128)S(1)}, u32[]{:S(2)}, u32[]{:S(2)}) collective-permute-start(f32[128,128]{1,0:T(8,128)S(1)} %get-tuple-element.34), channel_id=1, source_target_pairs={{0,24},{2,26},{4,28},{6,30},{8,16},{10,18},{12,20},{14,22},{16,8},... | collective-permute-start | bytes 196616 | tf_op jit(solution)/shard_map/ppermute | solution.py:209
  55.4 0.0 collective-permute-done.4.rest_5_
  55.4 2.0 %collective-permute-start.9 = (f32[128,128]{1,0:T(8,128)S(1)}, f32[128,128]{1,0:T(8,128)S(1)}, u32[]{:S(2)}, u32[]{:S(2)}) collective-permute-start(f32[128,128]{1,0:T(8,128)S(1)} %get-tuple-element.35), channel_id=1, source_target_pairs={{0,26},{2,24},{4,30},{6,28},{8,18},{10,16},{12,22},{14,20},{16,10}... | collective-permute-start | bytes 196616 | tf_op jit(solution)/shard_map/ppermute | solution.py:209
  57.4 0.2 collective-permute-done.5.rest_6_
  57.6 3.4 %collective-permute-start.10 = (f32[128,128]{1,0:T(8,128)S(1)}, f32[128,128]{1,0:T(8,128)S(1)}, u32[]{:S(2)}, u32[]{:S(2)}) collective-permute-start(f32[128,128]{1,0:T(8,128)S(1)} %get-tuple-element.36), channel_id=1, source_target_pairs={{0,28},{2,30},{4,24},{6,26},{8,20},{10,22},{12,16},{14,18},{16,12}... | collective-permute-start | bytes 196616 | tf_op jit(solution)/shard_map/ppermute | solution.py:209
  61.0 0.0 collective-permute-done.6.rest_7_
  61.0 1.7 %collective-permute-start.11 = (f32[128,128]{1,0:T(8,128)S(1)}, f32[128,128]{1,0:T(8,128)S(1)}, u32[]{:S(2)}, u32[]{:S(2)}) collective-permute-start(f32[128,128]{1,0:T(8,128)S(1)} %get-tuple-element.37), channel_id=1, source_target_pairs={{0,30},{2,28},{4,26},{6,24},{8,22},{10,20},{12,18},{14,16},{16,14}... | collective-permute-start | bytes 196616 | tf_op jit(solution)/shard_map/ppermute | solution.py:209
  62.7 0.6 collective-permute-start.12
  63.4 0.4 collective-permute-start.13
  63.8 1.1 %collective-permute-start.14 = (f32[128,128]{1,0:T(8,128)S(1)}, f32[128,128]{1,0:T(8,128)S(1)}, u32[]{:S(2)}, u32[]{:S(2)}) collective-permute-start(f32[128,128]{1,0:T(8,128)S(1)} %get-tuple-element.40), channel_id=1, source_target_pairs={{0,2},{2,0},{4,6},{6,4},{8,10},{10,8},{12,14},{14,12},{16,18},{18,... | collective-permute-start | bytes 196616 | tf_op jit(solution)/shard_map/ppermute | solution.py:209
  64.9 0.3 collective-permute-done.10.rest_11_
  65.2 3.0 %collective-permute-done.11.rest_12_ = f32[128,128]{1,0:T(8,128)S(1)} collective-permute-done((f32[128,128]{1,0:T(8,128)S(1)}, f32[128,128]{1,0:T(8,128)S(1)}, u32[]{:S(2)}, u32[]{:S(2)}) %collective-permute-start.11) | collective-permute-done | bytes 65568 | tf_op jit(solution)/shard_map/ppermute | solution.py:209
  68.1 0.9 %collective-permute-done.12.rest_13_ = f32[128,128]{1,0:T(8,128)S(1)} collective-permute-done((f32[128,128]{1,0:T(8,128)S(1)}, f32[128,128]{1,0:T(8,128)S(1)}, u32[]{:S(2)}, u32[]{:S(2)}) %collective-permute-start.12) | collective-permute-done | bytes 65568 | tf_op jit(solution)/shard_map/ppermute | solution.py:209
  69.1 0.1 collective-permute-done.13.rest_14_
  69.2 1.1 %place.1 = f32[2048,128]{1,0:T(8,128)} custom-call(f32[128,128]{1,0:T(8,128)S(1)} %get-tuple-element.25.rest_0_, f32[128,128]{1,0:T(8,128)S(1)} %collective-permute-done.rest_1_, f32[128,128]{1,0:T(8,128)S(1)} %collective-permute-done.1.rest_2_, f32[128,128]{1,0:T(8,128)S(1)} %collective-permute-done.2.rest_3_, ...), custom_call_target="tpu_custom_call" | custom-call | tf_op jit(solution)/shard_map/place/pallas_call | solution.py:229
  (17 shorter events, 0.0 us)
Async XLA Ops:
  0.0 7.6 %copy-start.4 = (s32[6,8]{1,0:T(8,128)S(1)}, s32[6,8]{1,0:T(8,128)}, u32[]{:S(2)}) copy-start(s32[6,8]{1,0:T(8,128)} %order_ref.3) | copy-start | bytes 580
  0.0 7.6 %copy-start.3 = (f32[6,16]{1,0:T(8,128)S(1)}, f32[6,16]{1,0:T(8,128)}, u32[]{:S(2)}) copy-start(f32[6,16]{1,0:T(8,128)} %angle_ref.1) | copy-start | bytes 1156
  0.0 7.6 %copy-start.2 = (s32[6,16,2]{1,2,0:T(2,128)S(1)}, s32[6,16,2]{1,2,0:T(2,128)}, u32[]{:S(2)}) copy-start(s32[6,16,2]{1,2,0:T(2,128)} %param.10) | copy-start | bytes 2308
  0.0 7.6 %copy-start.1 = (f32[6,128,128]{2,1,0:T(8,128)S(1)}, f32[6,128,128]{2,1,0:T(8,128)}, u32[]{:S(2)}) copy-start(f32[6,128,128]{2,1,0:T(8,128)} %im_ref.1) | copy-start | bytes 1179652
  0.0 7.6 %copy-start = (f32[6,128,128]{2,1,0:T(8,128)S(1)}, f32[6,128,128]{2,1,0:T(8,128)}, u32[]{:S(2)}) copy-start(f32[6,128,128]{2,1,0:T(8,128)} %re_ref.1) | copy-start | bytes 1179652
  0.0 30.5 %all-to-all-start = ((f32[16,128,128]{2,1,0:T(8,128)}), f32[16,128,128]{2,1,0:T(8,128)S(1)}, u32[]{:S(2)}, u32[]{:S(2)}) async-start(f32[16,128,128]{2,1,0:T(8,128)} %bitcast.14), calls=%async_computation | async-start | bytes 2097152 | tf_op jit(solution)/shard_map/all_to_all | solution.py:184
  9.7 0.7 copy-start.5
  30.5 0.9 %copy-start.6 = (f32[7,2,16,256]{3,2,1,0:T(8,128)S(1)}, f32[7,2,16,256]{3,2,1,0:T(8,128)}, u32[]{:S(2)}) copy-start(f32[7,2,16,256]{3,2,1,0:T(8,128)} %copy-done.5) | copy-start | bytes 688132
  39.8 10.5 %collective-permute-start = (f32[128,128]{1,0:T(8,128)S(1)}, f32[128,128]{1,0:T(8,128)S(1)}, u32[]{:S(2)}, u32[]{:S(2)}) collective-permute-start(f32[128,128]{1,0:T(8,128)S(1)} %get-tuple-element.26), channel_id=1, source_target_pairs={{0,16},{2,18},{4,20},{6,22},{8,24},{10,26},{12,28},{14,30},{16,0},... | collective-permute-start | bytes 196616 | tf_op jit(solution)/shard_map/ppermute | solution.py:209
  44.9 6.3 %collective-permute-start.1 = (f32[128,128]{1,0:T(8,128)S(1)}, f32[128,128]{1,0:T(8,128)S(1)}, u32[]{:S(2)}, u32[]{:S(2)}) collective-permute-start(f32[128,128]{1,0:T(8,128)S(1)} %get-tuple-element.27), channel_id=1, source_target_pairs={{0,18},{2,16},{4,22},{6,20},{8,26},{10,24},{12,30},{14,28},{16,2},... | collective-permute-start | bytes 196616 | tf_op jit(solution)/shard_map/ppermute | solution.py:209
  44.9 7.4 %collective-permute-start.2 = (f32[128,128]{1,0:T(8,128)S(1)}, f32[128,128]{1,0:T(8,128)S(1)}, u32[]{:S(2)}, u32[]{:S(2)}) collective-permute-start(f32[128,128]{1,0:T(8,128)S(1)} %get-tuple-element.28), channel_id=1, source_target_pairs={{0,8},{2,10},{4,12},{6,14},{8,0},{10,2},{12,4},{14,6},{16,24},{18,... | collective-permute-start | bytes 196616 | tf_op jit(solution)/shard_map/ppermute | solution.py:209
  46.1 7.7 %collective-permute-start.3 = (f32[128,128]{1,0:T(8,128)S(1)}, f32[128,128]{1,0:T(8,128)S(1)}, u32[]{:S(2)}, u32[]{:S(2)}) collective-permute-start(f32[128,128]{1,0:T(8,128)S(1)} %get-tuple-element.29), channel_id=1, source_target_pairs={{0,10},{2,8},{4,14},{6,12},{8,2},{10,0},{12,6},{14,4},{16,26},{18,... | collective-permute-start | bytes 196616 | tf_op jit(solution)/shard_map/ppermute | solution.py:209
  46.4 8.9 %collective-permute-start.4 = (f32[128,128]{1,0:T(8,128)S(1)}, f32[128,128]{1,0:T(8,128)S(1)}, u32[]{:S(2)}, u32[]{:S(2)}) collective-permute-start(f32[128,128]{1,0:T(8,128)S(1)} %get-tuple-element.30), channel_id=1, source_target_pairs={{0,20},{2,22},{4,16},{6,18},{8,28},{10,30},{12,24},{14,26},{16,4},... | collective-permute-start | bytes 196616 | tf_op jit(solution)/shard_map/ppermute | solution.py:209
  50.3 7.3 %collective-permute-start.5 = (f32[128,128]{1,0:T(8,128)S(1)}, f32[128,128]{1,0:T(8,128)S(1)}, u32[]{:S(2)}, u32[]{:S(2)}) collective-permute-start(f32[128,128]{1,0:T(8,128)S(1)} %get-tuple-element.31), channel_id=1, source_target_pairs={{0,22},{2,20},{4,18},{6,16},{8,30},{10,28},{12,26},{14,24},{16,6},... | collective-permute-start | bytes 196616 | tf_op jit(solution)/shard_map/ppermute | solution.py:209
  51.2 9.8 %collective-permute-start.6 = (f32[128,128]{1,0:T(8,128)S(1)}, f32[128,128]{1,0:T(8,128)S(1)}, u32[]{:S(2)}, u32[]{:S(2)}) collective-permute-start(f32[128,128]{1,0:T(8,128)S(1)} %get-tuple-element.32), channel_id=1, source_target_pairs={{0,12},{2,14},{4,8},{6,10},{8,4},{10,6},{12,0},{14,2},{16,28},{18,... | collective-permute-start | bytes 196616 | tf_op jit(solution)/shard_map/ppermute | solution.py:209
  52.3 10.4 %collective-permute-start.7 = (f32[128,128]{1,0:T(8,128)S(1)}, f32[128,128]{1,0:T(8,128)S(1)}, u32[]{:S(2)}, u32[]{:S(2)}) collective-permute-start(f32[128,128]{1,0:T(8,128)S(1)} %get-tuple-element.33), channel_id=1, source_target_pairs={{0,14},{2,12},{4,10},{6,8},{8,6},{10,4},{12,2},{14,0},{16,30},{18,... | collective-permute-start | bytes 196616 | tf_op jit(solution)/shard_map/ppermute | solution.py:209
  53.8 9.6 %collective-permute-start.8 = (f32[128,128]{1,0:T(8,128)S(1)}, f32[128,128]{1,0:T(8,128)S(1)}, u32[]{:S(2)}, u32[]{:S(2)}) collective-permute-start(f32[128,128]{1,0:T(8,128)S(1)} %get-tuple-element.34), channel_id=1, source_target_pairs={{0,24},{2,26},{4,28},{6,30},{8,16},{10,18},{12,20},{14,22},{16,8},... | collective-permute-start | bytes 196616 | tf_op jit(solution)/shard_map/ppermute | solution.py:209
  55.4 8.4 %collective-permute-start.9 = (f32[128,128]{1,0:T(8,128)S(1)}, f32[128,128]{1,0:T(8,128)S(1)}, u32[]{:S(2)}, u32[]{:S(2)}) collective-permute-start(f32[128,128]{1,0:T(8,128)S(1)} %get-tuple-element.35), channel_id=1, source_target_pairs={{0,26},{2,24},{4,30},{6,28},{8,18},{10,16},{12,22},{14,20},{16,10}... | collective-permute-start | bytes 196616 | tf_op jit(solution)/shard_map/ppermute | solution.py:209
  57.6 7.6 %collective-permute-start.10 = (f32[128,128]{1,0:T(8,128)S(1)}, f32[128,128]{1,0:T(8,128)S(1)}, u32[]{:S(2)}, u32[]{:S(2)}) collective-permute-start(f32[128,128]{1,0:T(8,128)S(1)} %get-tuple-element.36), channel_id=1, source_target_pairs={{0,28},{2,30},{4,24},{6,26},{8,20},{10,22},{12,16},{14,18},{16,12}... | collective-permute-start | bytes 196616 | tf_op jit(solution)/shard_map/ppermute | solution.py:209
  61.0 7.1 %collective-permute-start.11 = (f32[128,128]{1,0:T(8,128)S(1)}, f32[128,128]{1,0:T(8,128)S(1)}, u32[]{:S(2)}, u32[]{:S(2)}) collective-permute-start(f32[128,128]{1,0:T(8,128)S(1)} %get-tuple-element.37), channel_id=1, source_target_pairs={{0,30},{2,28},{4,26},{6,24},{8,22},{10,20},{12,18},{14,16},{16,14}... | collective-permute-start | bytes 196616 | tf_op jit(solution)/shard_map/ppermute | solution.py:209
  62.7 6.3 %collective-permute-start.12 = (f32[128,128]{1,0:T(8,128)S(1)}, f32[128,128]{1,0:T(8,128)S(1)}, u32[]{:S(2)}, u32[]{:S(2)}) collective-permute-start(f32[128,128]{1,0:T(8,128)S(1)} %get-tuple-element.38), channel_id=1, source_target_pairs={{0,4},{2,6},{4,0},{6,2},{8,12},{10,14},{12,8},{14,10},{16,20},{18,... | collective-permute-start | bytes 196616 | tf_op jit(solution)/shard_map/ppermute | solution.py:209
  63.4 5.8 %collective-permute-start.13 = (f32[128,128]{1,0:T(8,128)S(1)}, f32[128,128]{1,0:T(8,128)S(1)}, u32[]{:S(2)}, u32[]{:S(2)}) collective-permute-start(f32[128,128]{1,0:T(8,128)S(1)} %get-tuple-element.39), channel_id=1, source_target_pairs={{0,6},{2,4},{4,2},{6,0},{8,14},{10,12},{12,10},{14,8},{16,22},{18,... | collective-permute-start | bytes 196616 | tf_op jit(solution)/shard_map/ppermute | solution.py:209
  63.8 5.4 %collective-permute-start.14 = (f32[128,128]{1,0:T(8,128)S(1)}, f32[128,128]{1,0:T(8,128)S(1)}, u32[]{:S(2)}, u32[]{:S(2)}) collective-permute-start(f32[128,128]{1,0:T(8,128)S(1)} %get-tuple-element.40), channel_id=1, source_target_pairs={{0,2},{2,0},{4,6},{6,4},{8,10},{10,8},{12,14},{14,12},{16,18},{18,... | collective-permute-start | bytes 196616 | tf_op jit(solution)/shard_map/ppermute | solution.py:209

commit v15 on v13

--- a/solution.py
+++ b/solution.py
@@ -70,8 +70,8 @@
         for bit in range(LOW_BITS - 1):
             source = source + (((t >> bit) & 1) << jnp.full((8, GATE), order_ref[layer, bit], jnp.int32))
         half = jnp.int32(1) << order_ref[layer, LOW_BITS - 1]
+        half_ref[layer] = jnp.full((8, GATE), half, jnp.int32)
         hot = jnp.where((position & ~half) == source[None], 1.0, 0.0).reshape(LOW, GATE).astype(jnp.bfloat16)
-        half_ref[layer] = jnp.where((position & half) == 0, 1.0, 0.0).reshape(LOW, GATE).astype(jnp.bfloat16)
         for part, ref in enumerate((re_ref, im_ref)):
             for which, piece in enumerate(split(ref[layer])):
                 moved = lax.dot_general(hot, piece, contract, preferred_element_type=jnp.float32)
@@ -102,7 +102,7 @@
         copy.wait()
 
 
-def layers_kernel(wide, spect, x, gate, first_half, turn, *rest):
+def layers_kernel(wide, spect, x, gate, half_bit, turn, *rest):
     outs = rest[:wide]
     state, left_high, left_low, spread = rest[wide:]
     me = lax.axis_index("wide")
@@ -111,7 +111,7 @@
     half = wide // 2
     rows_at_once = min(spect, PACKED)
     joined = PACKED // rows_at_once
-    tile = min(TILE, count)
+    tile = min(TILE, count // 2)
 
     for part in range(2):
         for lanes in range(2):
@@ -123,22 +123,9 @@
         return real * cosine - imag * sine, real * sine + imag * cosine
 
     def one_layer(layer, slot):
-        for lanes in range(2):
-            for top in range(2):
-                for offset in range(0, spect, rows_at_once):
-                    pieces = [
-                        turned(slot, layer, (top * half + m) * spect, rows_at_once, offset, lanes) for m in range(half)
-                    ]
-                    for part in range(2):
-                        rows = exchange_modes([piece[part] for piece in pieces], span)
-                        column = part * LOW + top * LANES
-                        for g in range(0, half, joined):
-                            at = (lanes * half + g) * spect + offset
-                            high, low = split(jnp.concatenate(rows[g : g + joined], axis=0))
-                            left_high[at : at + PACKED, column : column + LANES] = high
-                            left_low[at : at + PACKED, column : column + LANES] = low
-
-        kept = first_half[layer]
+        position = lax.broadcasted_iota(jnp.int32, (LOW // 8, 8, GATE), 0) * 8
+        position = position + lax.broadcasted_iota(jnp.int32, (LOW // 8, 8, GATE), 1)
+        kept = jnp.where((position & half_bit[layer][None]) == 0, 1.0, 0.0).reshape(LOW, GATE).astype(jnp.bfloat16)
         for which in range(2):
             for part in range(2):
                 piece = gate[layer, which, :, part * GATE : (part + 1) * GATE]
@@ -149,12 +136,35 @@
                     spread[which, 2] = -both
         factors = [[[spread[which, 0], spread[which, 2]], [spread[which, 1], spread[which, 0]]] for which in range(2)]
 
-        for first in range(0, count, tile):
+        def load(lanes, top, offset):
+            pieces = [turned(slot, layer, (top * half + m) * spect, rows_at_once, offset, lanes) for m in range(half)]
+            for part in range(2):
+                rows = exchange_modes([piece[part] for piece in pieces], span)
+                column = part * LOW + top * LANES
+                for g in range(0, half, joined):
+                    at = (lanes * half + g) * spect + offset
+                    high, low = split(jnp.concatenate(rows[g : g + joined], axis=0))
+                    left_high[at : at + PACKED, column : column + LANES] = high
+                    left_low[at : at + PACKED, column : column + LANES] = low
+
+        def multiply(first, part):
             rows = slice(first, first + tile)
             terms = jnp.concatenate([left_high[rows], left_low[rows], left_high[rows]], axis=1)
-            for part in range(2):
-                square = jnp.concatenate(factors[0][part] + factors[0][part] + factors[1][part], axis=0)
-                state[1 - slot, part, rows] = jnp.dot(terms, square, preferred_element_type=jnp.float32)
+            square = jnp.concatenate(factors[0][part] + factors[0][part] + factors[1][part], axis=0)
+            state[1 - slot, part, rows] = jnp.dot(terms, square, preferred_element_type=jnp.float32)
+
+        loads = [[(lanes, top, offset) for offset in range(0, spect, rows_at_once) for top in range(2)] for lanes in range(2)]
+        products = [(first, part) for first in range(0, count, tile) for part in range(2)]
+        middle = len(products) // 2
+        for args in loads[0]:
+            load(*args)
+        for i in range(max(middle, len(loads[1]))):
+            if i < middle:
+                multiply(*products[i])
+            if i < len(loads[1]):
+                load(*loads[1][i])
+        for args in products[middle:]:
+            multiply(*args)
 
     def two_layers(step, carry):
         one_layer(2 * step, 0)
@@ -196,7 +206,7 @@
         out_specs=[in_vmem] * 3,
         out_shape=[
             jax.ShapeDtypeStruct((LAYERS, 2, LOW, 2 * GATE), jnp.bfloat16),
-            jax.ShapeDtypeStruct((LAYERS, LOW, GATE), jnp.bfloat16),
+            jax.ShapeDtypeStruct((LAYERS, 8, GATE), jnp.int32),
             jax.ShapeDtypeStruct(turns, jnp.float32),
         ],
         compiler_params=part_of_vmem,

time: 70.7 us -> 69.8 us (0.987)
  local copies, waits for them, and re-layouts: 3.38 us -> 1.64 us
  waiting for transfers between devices: 26.4 us -> 27.3 us
    unnamed x18 -> x14, local copies, waits for them, and re-layouts: 3.38 us -> 1.64 us
    all_to_all x1, waiting for transfers between devices: 19.3 us -> 20.1 us  [local(): lax.all_to_all(rows, 'wide', split_axis=0, concat_axis=0, tiled=True)]
where the time goes in v15:
time: 69.8 us; the launch traced here: 69.6 us
  starting transfers between devices  29.8 us (43%)
  waiting for transfers between devices  27.3 us (39%)
  Pallas kernels  10.8 us (15%)
  local copies, waits for them, and re-layouts  1.64 us (2%)
    ppermute x15, starting transfers between devices, swap(): lax.ppermute(block, 'wide', [(i, i ^ k) for i in range(wide)])  22.3 us
    all_to_all x1, waiting for transfers between devices, local(): lax.all_to_all(rows, 'wide', split_axis=0, concat_axis=0, tiled=True)  20.1 us
    pallas_call x1, Pallas kernels, local(): pl.pallas_call(partial(layers_kernel, wide, spect), in_specs=[in_vmem] *...  7.62 us
    all_to_all x1, starting transfers between devices, local(): lax.all_to_all(rows, 'wide', split_axis=0, concat_axis=0, tiled=True)  7.54 us
    ppermute x15, waiting for transfers between devices, swap(): lax.ppermute(block, 'wide', [(i, i ^ k) for i in range(wide)])  7.12 us
    pallas_call x1, Pallas kernels, local(): pl.pallas_call(partial(tables_kernel, spect, narrow), in_specs=[in_vmem,...  2.06 us
    unnamed x14, local copies, waits for them, and re-layouts  1.64 us
  transfers between devices with their start and end apart: 16, of which 8 were waited for; matrix products, arithmetic and copies ran while one was open for 0% of the time, Pallas kernels for 3%

profile of v15, /device:TPU:0, one launch (start us, length us, event | category | flops | bytes accessed | tf_op | source)
XLA Modules:
  0.0 69.6 jit_solution(17453563046385768626)
XLA Ops:
  0.0 7.5 %all-to-all-start = ((f32[16,128,128]{2,1,0:T(8,128)}), f32[16,128,128]{2,1,0:T(8,128)S(1)}, u32[]{:S(2)}, u32[]{:S(2)}) async-start(f32[16,128,128]{2,1,0:T(8,128)} %bitcast.14), calls=%async_computation | async-start | bytes 2097152 | tf_op jit(solution)/shard_map/all_to_all | solution.py:193
  7.6 2.1 %tables.1 = (bf16[6,2,256,256]{3,2,1,0:T(8,128)(2,1)S(1)}, s32[6,8,128]{2,1,0:T(8,128)S(1)}, f32[7,2,16,256]{3,2,1,0:T(8,128)S(1)}) custom-call(f32[6,128,128]{2,1,0:T(8,128)S(1)} %copy-done, f32[6,128,128]{2,1,0:T(8,128)S(1)} %copy-done.1, s32[6,8]{1,0:T(8,128)S(1)} %copy-done.3, s32[6,2,16]{2,1,0:T(2,128)S(1)} %bitcast.13, f32[6,16]{1,0:T(8,128)S(1)} %copy-done.4), custom_call_target="tpu_custom_call" | custom-call | flops 1000000000 | bytes 8000000 | tf_op jit(solution)/shard_map/tables/pallas_call | solution.py:203
  9.7 0.0 copy-start.5
  9.7 0.7 copy-done.5
  10.4 20.1 %all-to-all-done = f32[16,128,128]{2,1,0:T(8,128)S(1)} async-done(((f32[16,128,128]{2,1,0:T(8,128)}), f32[16,128,128]{2,1,0:T(8,128)S(1)}, u32[]{:S(2)}, u32[]{:S(2)}) %all-to-all-start) | async-done | bytes 1048608 | tf_op jit(solution)/shard_map/all_to_all | solution.py:193
  30.5 0.9 %copy-done.6 = f32[7,2,16,256]{3,2,1,0:T(8,128)S(1)} copy-done((f32[7,2,16,256]{3,2,1,0:T(8,128)S(1)}, f32[7,2,16,256]{3,2,1,0:T(8,128)}, u32[]{:S(2)}) %copy-start.6) | copy-done | bytes 229400
  31.4 7.6 %layers.1 = (f32[128,128]{1,0:T(8,128)S(1)}, f32[128,128]{1,0:T(8,128)S(1)}, f32[128,128]{1,0:T(8,128)S(1)}, f32[128,128]{1,0:T(8,128)S(1)}, f32[128,128]{1,0:T(...) custom-call(f32[2048,128]{1,0:T(8,128)S(1)} %bitcast.12, ...), custom_call_target="tpu_custom_call" | custom-call | flops 5000000000 | bytes 10000000 | tf_op jit(solution)/shard_map/layers/pallas_call | solution.py:223
  39.1 5.1 %collective-permute-start = (f32[128,128]{1,0:T(8,128)S(1)}, f32[128,128]{1,0:T(8,128)S(1)}, u32[]{:S(2)}, u32[]{:S(2)}) collective-permute-start(f32[128,128]{1,0:T(8,128)S(1)} %get-tuple-element.28), channel_id=1, source_target_pairs={{0,16},{2,18},{4,20},{6,22},{8,24},{10,26},{12,28},{14,30},{16,0},... | collective-permute-start | bytes 196616 | tf_op jit(solution)/shard_map/ppermute | solution.py:219
  44.2 1.2 %collective-permute-start.2 = (f32[128,128]{1,0:T(8,128)S(1)}, f32[128,128]{1,0:T(8,128)S(1)}, u32[]{:S(2)}, u32[]{:S(2)}) collective-permute-start(f32[128,128]{1,0:T(8,128)S(1)} %get-tuple-element.30), channel_id=1, source_target_pairs={{0,8},{2,10},{4,12},{6,14},{8,0},{10,2},{12,4},{14,6},{16,24},{18,... | collective-permute-start | bytes 196616 | tf_op jit(solution)/shard_map/ppermute | solution.py:219
  45.4 0.4 collective-permute-start.3
  45.8 2.1 %collective-permute-start.4 = (f32[128,128]{1,0:T(8,128)S(1)}, f32[128,128]{1,0:T(8,128)S(1)}, u32[]{:S(2)}, u32[]{:S(2)}) collective-permute-start(f32[128,128]{1,0:T(8,128)S(1)} %get-tuple-element.32), channel_id=1, source_target_pairs={{0,20},{2,22},{4,16},{6,18},{8,28},{10,30},{12,24},{14,26},{16,4},... | collective-permute-start | bytes 196616 | tf_op jit(solution)/shard_map/ppermute | solution.py:219
  47.9 1.7 %collective-permute-done.rest_1_ = f32[128,128]{1,0:T(8,128)S(1)} collective-permute-done((f32[128,128]{1,0:T(8,128)S(1)}, f32[128,128]{1,0:T(8,128)S(1)}, u32[]{:S(2)}, u32[]{:S(2)}) %collective-permute-start) | collective-permute-done | bytes 65568 | tf_op jit(solution)/shard_map/ppermute | solution.py:219
  49.6 0.9 %collective-permute-done.1.rest_2_ = f32[128,128]{1,0:T(8,128)S(1)} collective-permute-done((f32[128,128]{1,0:T(8,128)S(1)}, f32[128,128]{1,0:T(8,128)S(1)}, u32[]{:S(2)}, u32[]{:S(2)}) %collective-permute-start.1) | collective-permute-done | bytes 65568 | tf_op jit(solution)/shard_map/ppermute | solution.py:219
  50.5 1.1 %collective-permute-start.6 = (f32[128,128]{1,0:T(8,128)S(1)}, f32[128,128]{1,0:T(8,128)S(1)}, u32[]{:S(2)}, u32[]{:S(2)}) collective-permute-start(f32[128,128]{1,0:T(8,128)S(1)} %get-tuple-element.34), channel_id=1, source_target_pairs={{0,12},{2,14},{4,8},{6,10},{8,4},{10,6},{12,0},{14,2},{16,28},{18,... | collective-permute-start | bytes 196616 | tf_op jit(solution)/shard_map/ppermute | solution.py:219
  51.6 0.0 collective-permute-done.2.rest_3_
  51.6 1.5 %collective-permute-start.7 = (f32[128,128]{1,0:T(8,128)S(1)}, f32[128,128]{1,0:T(8,128)S(1)}, u32[]{:S(2)}, u32[]{:S(2)}) collective-permute-start(f32[128,128]{1,0:T(8,128)S(1)} %get-tuple-element.35), channel_id=1, source_target_pairs={{0,14},{2,12},{4,10},{6,8},{8,6},{10,4},{12,2},{14,0},{16,30},{18,... | collective-permute-start | bytes 196616 | tf_op jit(solution)/shard_map/ppermute | solution.py:219
  53.1 0.0 collective-permute-done.3.rest_4_
  53.1 1.6 %collective-permute-start.8 = (f32[128,128]{1,0:T(8,128)S(1)}, f32[128,128]{1,0:T(8,128)S(1)}, u32[]{:S(2)}, u32[]{:S(2)}) collective-permute-start(f32[128,128]{1,0:T(8,128)S(1)} %get-tuple-element.36), channel_id=1, source_target_pairs={{0,24},{2,26},{4,28},{6,30},{8,16},{10,18},{12,20},{14,22},{16,8},... | collective-permute-start | bytes 196616 | tf_op jit(solution)/shard_map/ppermute | solution.py:219
  54.7 0.0 collective-permute-done.4.rest_5_
  54.7 2.0 %collective-permute-start.9 = (f32[128,128]{1,0:T(8,128)S(1)}, f32[128,128]{1,0:T(8,128)S(1)}, u32[]{:S(2)}, u32[]{:S(2)}) collective-permute-start(f32[128,128]{1,0:T(8,128)S(1)} %get-tuple-element.37), channel_id=1, source_target_pairs={{0,26},{2,24},{4,30},{6,28},{8,18},{10,16},{12,22},{14,20},{16,10}... | collective-permute-start | bytes 196616 | tf_op jit(solution)/shard_map/ppermute | solution.py:219
  56.7 0.2 collective-permute-done.5.rest_6_
  56.9 3.4 %collective-permute-start.10 = (f32[128,128]{1,0:T(8,128)S(1)}, f32[128,128]{1,0:T(8,128)S(1)}, u32[]{:S(2)}, u32[]{:S(2)}) collective-permute-start(f32[128,128]{1,0:T(8,128)S(1)} %get-tuple-element.38), channel_id=1, source_target_pairs={{0,28},{2,30},{4,24},{6,26},{8,20},{10,22},{12,16},{14,18},{16,12}... | collective-permute-start | bytes 196616 | tf_op jit(solution)/shard_map/ppermute | solution.py:219
  60.3 0.0 collective-permute-done.6.rest_7_
  60.3 1.7 %collective-permute-start.11 = (f32[128,128]{1,0:T(8,128)S(1)}, f32[128,128]{1,0:T(8,128)S(1)}, u32[]{:S(2)}, u32[]{:S(2)}) collective-permute-start(f32[128,128]{1,0:T(8,128)S(1)} %get-tuple-element.39), channel_id=1, source_target_pairs={{0,30},{2,28},{4,26},{6,24},{8,22},{10,20},{12,18},{14,16},{16,14}... | collective-permute-start | bytes 196616 | tf_op jit(solution)/shard_map/ppermute | solution.py:219
  62.0 0.6 collective-permute-start.12
  62.7 0.4 collective-permute-start.13
  63.1 1.1 %collective-permute-start.14 = (f32[128,128]{1,0:T(8,128)S(1)}, f32[128,128]{1,0:T(8,128)S(1)}, u32[]{:S(2)}, u32[]{:S(2)}) collective-permute-start(f32[128,128]{1,0:T(8,128)S(1)} %get-tuple-element.42), channel_id=1, source_target_pairs={{0,2},{2,0},{4,6},{6,4},{8,10},{10,8},{12,14},{14,12},{16,18},{18,... | collective-permute-start | bytes 196616 | tf_op jit(solution)/shard_map/ppermute | solution.py:219
  64.2 0.3 collective-permute-done.10.rest_11_
  64.5 2.9 %collective-permute-done.11.rest_12_ = f32[128,128]{1,0:T(8,128)S(1)} collective-permute-done((f32[128,128]{1,0:T(8,128)S(1)}, f32[128,128]{1,0:T(8,128)S(1)}, u32[]{:S(2)}, u32[]{:S(2)}) %collective-permute-start.11) | collective-permute-done | bytes 65568 | tf_op jit(solution)/shard_map/ppermute | solution.py:219
  67.4 0.9 %collective-permute-done.12.rest_13_ = f32[128,128]{1,0:T(8,128)S(1)} collective-permute-done((f32[128,128]{1,0:T(8,128)S(1)}, f32[128,128]{1,0:T(8,128)S(1)}, u32[]{:S(2)}, u32[]{:S(2)}) %collective-permute-start.12) | collective-permute-done | bytes 65568 | tf_op jit(solution)/shard_map/ppermute | solution.py:219
  68.4 0.1 collective-permute-done.13.rest_14_
  68.5 1.1 %place.1 = f32[2048,128]{1,0:T(8,128)} custom-call(f32[128,128]{1,0:T(8,128)S(1)} %get-tuple-element.27.rest_0_, f32[128,128]{1,0:T(8,128)S(1)} %collective-permute-done.rest_1_, f32[128,128]{1,0:T(8,128)S(1)} %collective-permute-done.1.rest_2_, f32[128,128]{1,0:T(8,128)S(1)} %collective-permute-done.2.rest_3_, ...), custom_call_target="tpu_custom_call" | custom-call | tf_op jit(solution)/shard_map/place/pallas_call | solution.py:239
  (17 shorter events, 0.0 us)
Async XLA Ops:
  0.0 7.6 %copy-start.4 = (f32[6,16]{1,0:T(8,128)S(1)}, f32[6,16]{1,0:T(8,128)}, u32[]{:S(2)}) copy-start(f32[6,16]{1,0:T(8,128)} %angle_ref.1) | copy-start | bytes 1156
  0.0 7.6 %copy-start.2 = (s32[6,16,2]{1,2,0:T(2,128)S(1)}, s32[6,16,2]{1,2,0:T(2,128)}, u32[]{:S(2)}) copy-start(s32[6,16,2]{1,2,0:T(2,128)} %param.10) | copy-start | bytes 2308
  0.0 7.6 %copy-start.3 = (s32[6,8]{1,0:T(8,128)S(1)}, s32[6,8]{1,0:T(8,128)}, u32[]{:S(2)}) copy-start(s32[6,8]{1,0:T(8,128)} %order_ref.1) | copy-start | bytes 580
  0.0 7.6 %copy-start.1 = (f32[6,128,128]{2,1,0:T(8,128)S(1)}, f32[6,128,128]{2,1,0:T(8,128)}, u32[]{:S(2)}) copy-start(f32[6,128,128]{2,1,0:T(8,128)} %im_ref.1) | copy-start | bytes 1179652
  0.0 7.6 %copy-start = (f32[6,128,128]{2,1,0:T(8,128)S(1)}, f32[6,128,128]{2,1,0:T(8,128)}, u32[]{:S(2)}) copy-start(f32[6,128,128]{2,1,0:T(8,128)} %re_ref.1) | copy-start | bytes 1179652
  0.0 30.5 %all-to-all-start = ((f32[16,128,128]{2,1,0:T(8,128)}), f32[16,128,128]{2,1,0:T(8,128)S(1)}, u32[]{:S(2)}, u32[]{:S(2)}) async-start(f32[16,128,128]{2,1,0:T(8,128)} %bitcast.14), calls=%async_computation | async-start | bytes 2097152 | tf_op jit(solution)/shard_map/all_to_all | solution.py:193
  9.7 0.7 copy-start.5
  30.5 0.9 %copy-start.6 = (f32[7,2,16,256]{3,2,1,0:T(8,128)S(1)}, f32[7,2,16,256]{3,2,1,0:T(8,128)}, u32[]{:S(2)}) copy-start(f32[7,2,16,256]{3,2,1,0:T(8,128)} %copy-done.5) | copy-start | bytes 688132
  39.1 10.5 %collective-permute-start = (f32[128,128]{1,0:T(8,128)S(1)}, f32[128,128]{1,0:T(8,128)S(1)}, u32[]{:S(2)}, u32[]{:S(2)}) collective-permute-start(f32[128,128]{1,0:T(8,128)S(1)} %get-tuple-element.28), channel_id=1, source_target_pairs={{0,16},{2,18},{4,20},{6,22},{8,24},{10,26},{12,28},{14,30},{16,0},... | collective-permute-start | bytes 196616 | tf_op jit(solution)/shard_map/ppermute | solution.py:219
  44.2 6.3 %collective-permute-start.1 = (f32[128,128]{1,0:T(8,128)S(1)}, f32[128,128]{1,0:T(8,128)S(1)}, u32[]{:S(2)}, u32[]{:S(2)}) collective-permute-start(f32[128,128]{1,0:T(8,128)S(1)} %get-tuple-element.29), channel_id=1, source_target_pairs={{0,18},{2,16},{4,22},{6,20},{8,26},{10,24},{12,30},{14,28},{16,2},... | collective-permute-start | bytes 196616 | tf_op jit(solution)/shard_map/ppermute | solution.py:219
  44.2 7.4 %collective-permute-start.2 = (f32[128,128]{1,0:T(8,128)S(1)}, f32[128,128]{1,0:T(8,128)S(1)}, u32[]{:S(2)}, u32[]{:S(2)}) collective-permute-start(f32[128,128]{1,0:T(8,128)S(1)} %get-tuple-element.30), channel_id=1, source_target_pairs={{0,8},{2,10},{4,12},{6,14},{8,0},{10,2},{12,4},{14,6},{16,24},{18,... | collective-permute-start | bytes 196616 | tf_op jit(solution)/shard_map/ppermute | solution.py:219
  45.4 7.7 %collective-permute-start.3 = (f32[128,128]{1,0:T(8,128)S(1)}, f32[128,128]{1,0:T(8,128)S(1)}, u32[]{:S(2)}, u32[]{:S(2)}) collective-permute-start(f32[128,128]{1,0:T(8,128)S(1)} %get-tuple-element.31), channel_id=1, source_target_pairs={{0,10},{2,8},{4,14},{6,12},{8,2},{10,0},{12,6},{14,4},{16,26},{18,... | collective-permute-start | bytes 196616 | tf_op jit(solution)/shard_map/ppermute | solution.py:219
  45.8 8.9 %collective-permute-start.4 = (f32[128,128]{1,0:T(8,128)S(1)}, f32[128,128]{1,0:T(8,128)S(1)}, u32[]{:S(2)}, u32[]{:S(2)}) collective-permute-start(f32[128,128]{1,0:T(8,128)S(1)} %get-tuple-element.32), channel_id=1, source_target_pairs={{0,20},{2,22},{4,16},{6,18},{8,28},{10,30},{12,24},{14,26},{16,4},... | collective-permute-start | bytes 196616 | tf_op jit(solution)/shard_map/ppermute | solution.py:219
  49.6 7.3 %collective-permute-start.5 = (f32[128,128]{1,0:T(8,128)S(1)}, f32[128,128]{1,0:T(8,128)S(1)}, u32[]{:S(2)}, u32[]{:S(2)}) collective-permute-start(f32[128,128]{1,0:T(8,128)S(1)} %get-tuple-element.33), channel_id=1, source_target_pairs={{0,22},{2,20},{4,18},{6,16},{8,30},{10,28},{12,26},{14,24},{16,6},... | collective-permute-start | bytes 196616 | tf_op jit(solution)/shard_map/ppermute | solution.py:219
  50.5 9.8 %collective-permute-start.6 = (f32[128,128]{1,0:T(8,128)S(1)}, f32[128,128]{1,0:T(8,128)S(1)}, u32[]{:S(2)}, u32[]{:S(2)}) collective-permute-start(f32[128,128]{1,0:T(8,128)S(1)} %get-tuple-element.34), channel_id=1, source_target_pairs={{0,12},{2,14},{4,8},{6,10},{8,4},{10,6},{12,0},{14,2},{16,28},{18,... | collective-permute-start | bytes 196616 | tf_op jit(solution)/shard_map/ppermute | solution.py:219
  51.6 10.4 %collective-permute-start.7 = (f32[128,128]{1,0:T(8,128)S(1)}, f32[128,128]{1,0:T(8,128)S(1)}, u32[]{:S(2)}, u32[]{:S(2)}) collective-permute-start(f32[128,128]{1,0:T(8,128)S(1)} %get-tuple-element.35), channel_id=1, source_target_pairs={{0,14},{2,12},{4,10},{6,8},{8,6},{10,4},{12,2},{14,0},{16,30},{18,... | collective-permute-start | bytes 196616 | tf_op jit(solution)/shard_map/ppermute | solution.py:219
  53.1 9.6 %collective-permute-start.8 = (f32[128,128]{1,0:T(8,128)S(1)}, f32[128,128]{1,0:T(8,128)S(1)}, u32[]{:S(2)}, u32[]{:S(2)}) collective-permute-start(f32[128,128]{1,0:T(8,128)S(1)} %get-tuple-element.36), channel_id=1, source_target_pairs={{0,24},{2,26},{4,28},{6,30},{8,16},{10,18},{12,20},{14,22},{16,8},... | collective-permute-start | bytes 196616 | tf_op jit(solution)/shard_map/ppermute | solution.py:219
  54.7 8.4 %collective-permute-start.9 = (f32[128,128]{1,0:T(8,128)S(1)}, f32[128,128]{1,0:T(8,128)S(1)}, u32[]{:S(2)}, u32[]{:S(2)}) collective-permute-start(f32[128,128]{1,0:T(8,128)S(1)} %get-tuple-element.37), channel_id=1, source_target_pairs={{0,26},{2,24},{4,30},{6,28},{8,18},{10,16},{12,22},{14,20},{16,10}... | collective-permute-start | bytes 196616 | tf_op jit(solution)/shard_map/ppermute | solution.py:219
  56.9 7.6 %collective-permute-start.10 = (f32[128,128]{1,0:T(8,128)S(1)}, f32[128,128]{1,0:T(8,128)S(1)}, u32[]{:S(2)}, u32[]{:S(2)}) collective-permute-start(f32[128,128]{1,0:T(8,128)S(1)} %get-tuple-element.38), channel_id=1, source_target_pairs={{0,28},{2,30},{4,24},{6,26},{8,20},{10,22},{12,16},{14,18},{16,12}... | collective-permute-start | bytes 196616 | tf_op jit(solution)/shard_map/ppermute | solution.py:219
  60.3 7.1 %collective-permute-start.11 = (f32[128,128]{1,0:T(8,128)S(1)}, f32[128,128]{1,0:T(8,128)S(1)}, u32[]{:S(2)}, u32[]{:S(2)}) collective-permute-start(f32[128,128]{1,0:T(8,128)S(1)} %get-tuple-element.39), channel_id=1, source_target_pairs={{0,30},{2,28},{4,26},{6,24},{8,22},{10,20},{12,18},{14,16},{16,14}... | collective-permute-start | bytes 196616 | tf_op jit(solution)/shard_map/ppermute | solution.py:219
  62.0 6.3 %collective-permute-start.12 = (f32[128,128]{1,0:T(8,128)S(1)}, f32[128,128]{1,0:T(8,128)S(1)}, u32[]{:S(2)}, u32[]{:S(2)}) collective-permute-start(f32[128,128]{1,0:T(8,128)S(1)} %get-tuple-element.40), channel_id=1, source_target_pairs={{0,4},{2,6},{4,0},{6,2},{8,12},{10,14},{12,8},{14,10},{16,20},{18,... | collective-permute-start | bytes 196616 | tf_op jit(solution)/shard_map/ppermute | solution.py:219
  62.7 5.8 %collective-permute-start.13 = (f32[128,128]{1,0:T(8,128)S(1)}, f32[128,128]{1,0:T(8,128)S(1)}, u32[]{:S(2)}, u32[]{:S(2)}) collective-permute-start(f32[128,128]{1,0:T(8,128)S(1)} %get-tuple-element.41), channel_id=1, source_target_pairs={{0,6},{2,4},{4,2},{6,0},{8,14},{10,12},{12,10},{14,8},{16,22},{18,... | collective-permute-start | bytes 196616 | tf_op jit(solution)/shard_map/ppermute | solution.py:219
  63.1 5.4 %collective-permute-start.14 = (f32[128,128]{1,0:T(8,128)S(1)}, f32[128,128]{1,0:T(8,128)S(1)}, u32[]{:S(2)}, u32[]{:S(2)}) collective-permute-start(f32[128,128]{1,0:T(8,128)S(1)} %get-tuple-element.42), channel_id=1, source_target_pairs={{0,2},{2,0},{4,6},{6,4},{8,10},{10,8},{12,14},{14,12},{16,18},{18,... | collective-permute-start | bytes 196616 | tf_op jit(solution)/shard_map/ppermute | solution.py:219

commit v16 on v15

--- a/solution.py
+++ b/solution.py
@@ -16,7 +16,7 @@
 PHASE_BITS = 12
 LANES = 128
 PACKED = 16
-TILE = 128
+TILE = 256
 PAIRED = Layout(major_to_minor=(1, 0, 2))
 
 
@@ -43,7 +43,25 @@
     return ref.at[pl.ds(pl.multiple_of(start, rows), rows)]
 
 
-def tables_kernel(spect, narrow, re_ref, im_ref, order_ref, pair_ref, angle_ref, gate_ref, half_ref, turn_ref):
+def gates_kernel(re_ref, im_ref, order_ref, gate_ref, half_ref):
+    t = lax.broadcasted_iota(jnp.int32, (8, GATE), 1)
+    position = lax.broadcasted_iota(jnp.int32, (LOW // 8, 8, GATE), 0) * 8
+    position = position + lax.broadcasted_iota(jnp.int32, (LOW // 8, 8, GATE), 1)
+    contract = (((1,), (1,)), ((), ()))
+    for layer in range(LAYERS):
+        source = jnp.zeros((8, GATE), jnp.int32)
+        for bit in range(LOW_BITS - 1):
+            source = source + (((t >> bit) & 1) << jnp.full((8, GATE), order_ref[layer, bit], jnp.int32))
+        half = jnp.int32(1) << order_ref[layer, LOW_BITS - 1]
+        half_ref[layer] = jnp.full((8, GATE), half, jnp.int32)
+        hot = jnp.where((position & ~half) == source[None], 1.0, 0.0).reshape(LOW, GATE).astype(jnp.bfloat16)
+        for part, ref in enumerate((re_ref, im_ref)):
+            for which, piece in enumerate(split(ref[layer])):
+                moved = lax.dot_general(hot, piece, contract, preferred_element_type=jnp.float32)
+                gate_ref[layer, which, :, part * GATE : (part + 1) * GATE] = moved.astype(jnp.bfloat16)
+
+
+def phases_kernel(spect, narrow, pair_ref, angle_ref, half_ref, turn_ref):
     size = turn_ref.shape[2]
     row = lax.broadcasted_iota(jnp.int32, (size, LOW), 0)
     lane = lax.broadcasted_iota(jnp.int32, (size, LOW), 1)
@@ -61,22 +79,6 @@
         turn_ref[layer + 1, 0] = jnp.cos(phase)
         turn_ref[layer + 1, 1] = jnp.sin(phase)
 
-    t = lax.broadcasted_iota(jnp.int32, (8, GATE), 1)
-    position = lax.broadcasted_iota(jnp.int32, (LOW // 8, 8, GATE), 0) * 8
-    position = position + lax.broadcasted_iota(jnp.int32, (LOW // 8, 8, GATE), 1)
-    contract = (((1,), (1,)), ((), ()))
-    for layer in range(LAYERS):
-        source = jnp.zeros((8, GATE), jnp.int32)
-        for bit in range(LOW_BITS - 1):
-            source = source + (((t >> bit) & 1) << jnp.full((8, GATE), order_ref[layer, bit], jnp.int32))
-        half = jnp.int32(1) << order_ref[layer, LOW_BITS - 1]
-        half_ref[layer] = jnp.full((8, GATE), half, jnp.int32)
-        hot = jnp.where((position & ~half) == source[None], 1.0, 0.0).reshape(LOW, GATE).astype(jnp.bfloat16)
-        for part, ref in enumerate((re_ref, im_ref)):
-            for which, piece in enumerate(split(ref[layer])):
-                moved = lax.dot_general(hot, piece, contract, preferred_element_type=jnp.float32)
-                gate_ref[layer, which, :, part * GATE : (part + 1) * GATE] = moved.astype(jnp.bfloat16)
-
 
 def exchange_modes(rows, span):
     count = len(rows)
@@ -200,19 +202,27 @@
     order = exchange_order(wide)
 
     turns = (LAYERS + 1, 2, min(spect, 2 ** (PHASE_BITS - LOW_BITS)), LOW)
-    tables = pl.pallas_call(
-        partial(tables_kernel, spect, narrow),
-        in_specs=[in_vmem, in_vmem, in_smem, in_smem, in_smem],
-        out_specs=[in_vmem] * 3,
+    gate, half_bit = pl.pallas_call(
+        gates_kernel,
+        in_specs=[in_vmem, in_vmem, in_smem],
+        out_specs=[in_vmem] * 2,
         out_shape=[
             jax.ShapeDtypeStruct((LAYERS, 2, LOW, 2 * GATE), jnp.bfloat16),
             jax.ShapeDtypeStruct((LAYERS, 8, GATE), jnp.int32),
-            jax.ShapeDtypeStruct(turns, jnp.float32),
         ],
         compiler_params=part_of_vmem,
-        cost_estimate=pl.CostEstimate(flops=10**9, bytes_accessed=8 * 10**6, transcendentals=10**5),
-        name="tables",
-    )(gate_re, gate_im, bit_orders, phase_pairs.transpose(0, 2, 1), phase_angles)
+        cost_estimate=pl.CostEstimate(flops=10**9, bytes_accessed=4 * 10**6, transcendentals=0),
+        name="gates",
+    )(gate_re, gate_im, bit_orders)
+    turn = pl.pallas_call(
+        partial(phases_kernel, spect, narrow),
+        in_specs=[in_smem, in_smem, in_vmem],
+        out_specs=in_vmem,
+        out_shape=jax.ShapeDtypeStruct(turns, jnp.float32),
+        compiler_params=part_of_vmem,
+        cost_estimate=pl.CostEstimate(flops=10**8, bytes_accessed=10**6, transcendentals=10**5),
+        name="phases",
+    )(phase_pairs.transpose(0, 2, 1), phase_angles, half_bit)
 
     def swap(blocks, ks):
         return [
@@ -234,7 +244,7 @@
         compiler_params=part_of_vmem,
         cost_estimate=pl.CostEstimate(flops=5 * 10**9, bytes_accessed=10**7, transcendentals=0),
         name="layers",
-    )(gathered, *tables)
+    )(gathered, gate, half_bit, turn)
 
     back = pl.pallas_call(
         partial(place_kernel, wide),

time: 69.8 us -> 68.9 us (0.987)
  local copies, waits for them, and re-layouts: 1.64 us -> 0.02 us
  Pallas kernels: 10.8 us -> 11.5 us
    unnamed x14 -> x10, local copies, waits for them, and re-layouts: 1.64 us -> 0.02 us
    pallas_call x1 -> x2, Pallas kernels: 2.06 us -> 2.64 us  [the longest x1 1.47 us: local(): pl.pallas_call(partial(phases_kernel, spect, narrow), in_specs=[in_smem,...]
  transfers between devices with their start and end apart: 16 -> 16, of which waited for: 8 -> 8; matrix products, arithmetic and copies ran while one was open for 0% -> 0% of each run, Pallas kernels for 3% -> 4%
where the time goes in v16:
time: 68.9 us; the launch traced here: 68.7 us
  starting transfers between devices  29.8 us (43%)
  waiting for transfers between devices  27.4 us (40%)
  Pallas kernels  11.5 us (17%)
    ppermute x15, starting transfers between devices, swap(): lax.ppermute(block, 'wide', [(i, i ^ k) for i in range(wide)])  22.2 us
    all_to_all x1, waiting for transfers between devices, local(): lax.all_to_all(rows, 'wide', split_axis=0, concat_axis=0, tiled=True)  20.2 us
    pallas_call x1, Pallas kernels, local(): pl.pallas_call(partial(layers_kernel, wide, spect), in_specs=[in_vmem] *...  7.76 us
    all_to_all x1, starting transfers between devices, local(): lax.all_to_all(rows, 'wide', split_axis=0, concat_axis=0, tiled=True)  7.53 us
    ppermute x15, waiting for transfers between devices, swap(): lax.ppermute(block, 'wide', [(i, i ^ k) for i in range(wide)])  7.16 us
    pallas_call x1, Pallas kernels, local(): pl.pallas_call(partial(phases_kernel, spect, narrow), in_specs=[in_smem,...  1.47 us
  transfers between devices with their start and end apart: 16, of which 8 were waited for; matrix products, arithmetic and copies ran while one was open for 0% of the time, Pallas kernels for 4%

profile of v16, /device:TPU:0, one launch (start us, length us, event | category | flops | bytes accessed | tf_op | source)
XLA Modules:
  0.0 68.7 jit_solution(4793629542218218835)
XLA Ops:
  0.0 7.5 %all-to-all-start = ((f32[16,128,128]{2,1,0:T(8,128)}), f32[16,128,128]{2,1,0:T(8,128)S(1)}, u32[]{:S(2)}, u32[]{:S(2)}) async-start(f32[16,128,128]{2,1,0:T(8,128)} %bitcast.14), calls=%async_computation | async-start | bytes 2097152 | tf_op jit(solution)/shard_map/all_to_all | solution.py:195
  7.6 0.0 copy-start.2
  7.6 0.0 copy-start.4
  7.6 1.2 %gates.1 = (bf16[6,2,256,256]{3,2,1,0:T(8,128)(2,1)S(1)}, s32[6,8,128]{2,1,0:T(8,128)S(1)}) custom-call(f32[6,128,128]{2,1,0:T(8,128)S(1)} %copy-done, f32[6,128,128]{2,1,0:T(8,128)S(1)} %copy-done.1, s32[6,8]{1,0:T(8,128)S(1)} %copy-done.3), custom_call_target="tpu_custom_call" | custom-call | flops 1000000000 | bytes 4000000 | tf_op jit(solution)/shard_map/gates/pallas_call | solution.py:205
  8.8 1.5 %phases.1.turn = f32[7,2,16,256]{3,2,1,0:T(8,128)S(1)} custom-call(s32[6,2,16]{2,1,0:T(2,128)S(1)} %bitcast.13, f32[6,16]{1,0:T(8,128)S(1)} %copy-done.4, s32[6,8,128]{2,1,0:T(8,128)S(1)} %get-tuple-element.24.half_ref.half_bit), custom_call_target="tpu_custom_call" | custom-call | flops 100000000 | bytes 1000000 | tf_op jit(solution)/shard_map/phases/pallas_call | solution.py:217
  10.3 20.2 %all-to-all-done = f32[16,128,128]{2,1,0:T(8,128)S(1)} async-done(((f32[16,128,128]{2,1,0:T(8,128)}), f32[16,128,128]{2,1,0:T(8,128)S(1)}, u32[]{:S(2)}, u32[]{:S(2)}) %all-to-all-start) | async-done | bytes 1048608 | tf_op jit(solution)/shard_map/all_to_all | solution.py:195
  30.5 7.8 %layers.1 = (f32[128,128]{1,0:T(8,128)S(1)}, f32[128,128]{1,0:T(8,128)S(1)}, f32[128,128]{1,0:T(8,128)S(1)}, f32[128,128]{1,0:T(8,128)S(1)}, f32[128,128]{1,0:T(...) custom-call(f32[2048,128]{1,0:T(8,128)S(1)} %bitcast.12, ...), custom_call_target="tpu_custom_call" | custom-call | flops 5000000000 | bytes 10000000 | tf_op jit(solution)/shard_map/layers/pallas_call | solution.py:233
  38.3 5.1 %collective-permute-start = (f32[128,128]{1,0:T(8,128)S(1)}, f32[128,128]{1,0:T(8,128)S(1)}, u32[]{:S(2)}, u32[]{:S(2)}) collective-permute-start(f32[128,128]{1,0:T(8,128)S(1)} %get-tuple-element.26), channel_id=1, source_target_pairs={{0,16},{2,18},{4,20},{6,22},{8,24},{10,26},{12,28},{14,30},{16,0},... | collective-permute-start | bytes 196616 | tf_op jit(solution)/shard_map/ppermute | solution.py:229
  43.4 1.2 %collective-permute-start.2 = (f32[128,128]{1,0:T(8,128)S(1)}, f32[128,128]{1,0:T(8,128)S(1)}, u32[]{:S(2)}, u32[]{:S(2)}) collective-permute-start(f32[128,128]{1,0:T(8,128)S(1)} %get-tuple-element.28), channel_id=1, source_target_pairs={{0,8},{2,10},{4,12},{6,14},{8,0},{10,2},{12,4},{14,6},{16,24},{18,... | collective-permute-start | bytes 196616 | tf_op jit(solution)/shard_map/ppermute | solution.py:229
  44.6 0.4 collective-permute-start.3
  44.9 2.1 %collective-permute-start.4 = (f32[128,128]{1,0:T(8,128)S(1)}, f32[128,128]{1,0:T(8,128)S(1)}, u32[]{:S(2)}, u32[]{:S(2)}) collective-permute-start(f32[128,128]{1,0:T(8,128)S(1)} %get-tuple-element.30), channel_id=1, source_target_pairs={{0,20},{2,22},{4,16},{6,18},{8,28},{10,30},{12,24},{14,26},{16,4},... | collective-permute-start | bytes 196616 | tf_op jit(solution)/shard_map/ppermute | solution.py:229
  47.1 1.7 %collective-permute-done.rest_1_ = f32[128,128]{1,0:T(8,128)S(1)} collective-permute-done((f32[128,128]{1,0:T(8,128)S(1)}, f32[128,128]{1,0:T(8,128)S(1)}, u32[]{:S(2)}, u32[]{:S(2)}) %collective-permute-start) | collective-permute-done | bytes 65568 | tf_op jit(solution)/shard_map/ppermute | solution.py:229
  48.8 0.0 collective-permute-start.5
  48.8 0.9 %collective-permute-done.1.rest_2_ = f32[128,128]{1,0:T(8,128)S(1)} collective-permute-done((f32[128,128]{1,0:T(8,128)S(1)}, f32[128,128]{1,0:T(8,128)S(1)}, u32[]{:S(2)}, u32[]{:S(2)}) %collective-permute-start.1) | collective-permute-done | bytes 65568 | tf_op jit(solution)/shard_map/ppermute | solution.py:229
  49.7 1.1 %collective-permute-start.6 = (f32[128,128]{1,0:T(8,128)S(1)}, f32[128,128]{1,0:T(8,128)S(1)}, u32[]{:S(2)}, u32[]{:S(2)}) collective-permute-start(f32[128,128]{1,0:T(8,128)S(1)} %get-tuple-element.32), channel_id=1, source_target_pairs={{0,12},{2,14},{4,8},{6,10},{8,4},{10,6},{12,0},{14,2},{16,28},{18,... | collective-permute-start | bytes 196616 | tf_op jit(solution)/shard_map/ppermute | solution.py:229
  50.8 0.0 collective-permute-done.2.rest_3_
  50.8 1.5 %collective-permute-start.7 = (f32[128,128]{1,0:T(8,128)S(1)}, f32[128,128]{1,0:T(8,128)S(1)}, u32[]{:S(2)}, u32[]{:S(2)}) collective-permute-start(f32[128,128]{1,0:T(8,128)S(1)} %get-tuple-element.33), channel_id=1, source_target_pairs={{0,14},{2,12},{4,10},{6,8},{8,6},{10,4},{12,2},{14,0},{16,30},{18,... | collective-permute-start | bytes 196616 | tf_op jit(solution)/shard_map/ppermute | solution.py:229
  52.3 0.0 collective-permute-done.3.rest_4_
  52.3 1.6 %collective-permute-start.8 = (f32[128,128]{1,0:T(8,128)S(1)}, f32[128,128]{1,0:T(8,128)S(1)}, u32[]{:S(2)}, u32[]{:S(2)}) collective-permute-start(f32[128,128]{1,0:T(8,128)S(1)} %get-tuple-element.34), channel_id=1, source_target_pairs={{0,24},{2,26},{4,28},{6,30},{8,16},{10,18},{12,20},{14,22},{16,8},... | collective-permute-start | bytes 196616 | tf_op jit(solution)/shard_map/ppermute | solution.py:229
  53.9 0.0 collective-permute-done.4.rest_5_
  53.9 2.0 %collective-permute-start.9 = (f32[128,128]{1,0:T(8,128)S(1)}, f32[128,128]{1,0:T(8,128)S(1)}, u32[]{:S(2)}, u32[]{:S(2)}) collective-permute-start(f32[128,128]{1,0:T(8,128)S(1)} %get-tuple-element.35), channel_id=1, source_target_pairs={{0,26},{2,24},{4,30},{6,28},{8,18},{10,16},{12,22},{14,20},{16,10}... | collective-permute-start | bytes 196616 | tf_op jit(solution)/shard_map/ppermute | solution.py:229
  55.9 0.2 collective-permute-done.5.rest_6_
  56.1 3.4 %collective-permute-start.10 = (f32[128,128]{1,0:T(8,128)S(1)}, f32[128,128]{1,0:T(8,128)S(1)}, u32[]{:S(2)}, u32[]{:S(2)}) collective-permute-start(f32[128,128]{1,0:T(8,128)S(1)} %get-tuple-element.36), channel_id=1, source_target_pairs={{0,28},{2,30},{4,24},{6,26},{8,20},{10,22},{12,16},{14,18},{16,12}... | collective-permute-start | bytes 196616 | tf_op jit(solution)/shard_map/ppermute | solution.py:229
  59.5 1.7 %collective-permute-start.11 = (f32[128,128]{1,0:T(8,128)S(1)}, f32[128,128]{1,0:T(8,128)S(1)}, u32[]{:S(2)}, u32[]{:S(2)}) collective-permute-start(f32[128,128]{1,0:T(8,128)S(1)} %get-tuple-element.37), channel_id=1, source_target_pairs={{0,30},{2,28},{4,26},{6,24},{8,22},{10,20},{12,18},{14,16},{16,14}... | collective-permute-start | bytes 196616 | tf_op jit(solution)/shard_map/ppermute | solution.py:229
  61.2 0.7 collective-permute-start.12
  61.9 0.4 collective-permute-start.13
  62.3 1.0 %collective-permute-start.14 = (f32[128,128]{1,0:T(8,128)S(1)}, f32[128,128]{1,0:T(8,128)S(1)}, u32[]{:S(2)}, u32[]{:S(2)}) collective-permute-start(f32[128,128]{1,0:T(8,128)S(1)} %get-tuple-element.40), channel_id=1, source_target_pairs={{0,2},{2,0},{4,6},{6,4},{8,10},{10,8},{12,14},{14,12},{16,18},{18,... | collective-permute-start | bytes 196616 | tf_op jit(solution)/shard_map/ppermute | solution.py:229
  63.3 0.4 collective-permute-done.10.rest_11_
  63.7 2.9 %collective-permute-done.11.rest_12_ = f32[128,128]{1,0:T(8,128)S(1)} collective-permute-done((f32[128,128]{1,0:T(8,128)S(1)}, f32[128,128]{1,0:T(8,128)S(1)}, u32[]{:S(2)}, u32[]{:S(2)}) %collective-permute-start.11) | collective-permute-done | bytes 65568 | tf_op jit(solution)/shard_map/ppermute | solution.py:229
  66.6 0.9 %collective-permute-done.12.rest_13_ = f32[128,128]{1,0:T(8,128)S(1)} collective-permute-done((f32[128,128]{1,0:T(8,128)S(1)}, f32[128,128]{1,0:T(8,128)S(1)}, u32[]{:S(2)}, u32[]{:S(2)}) %collective-permute-start.12) | collective-permute-done | bytes 65568 | tf_op jit(solution)/shard_map/ppermute | solution.py:229
  67.5 0.2 collective-permute-done.13.rest_14_
  67.7 1.1 %place.1 = f32[2048,128]{1,0:T(8,128)} custom-call(f32[128,128]{1,0:T(8,128)S(1)} %get-tuple-element.25.rest_0_, f32[128,128]{1,0:T(8,128)S(1)} %collective-permute-done.rest_1_, f32[128,128]{1,0:T(8,128)S(1)} %collective-permute-done.1.rest_2_, f32[128,128]{1,0:T(8,128)S(1)} %collective-permute-done.2.rest_3_, ...), custom_call_target="tpu_custom_call" | custom-call | tf_op jit(solution)/shard_map/place/pallas_call | solution.py:249
  (14 shorter events, 0.0 us)
Async XLA Ops:
  0.0 7.5 %copy-start.3 = (s32[6,8]{1,0:T(8,128)S(1)}, s32[6,8]{1,0:T(8,128)}, u32[]{:S(2)}) copy-start(s32[6,8]{1,0:T(8,128)} %order_ref.1) | copy-start | bytes 580
  0.0 7.6 %copy-start.1 = (f32[6,128,128]{2,1,0:T(8,128)S(1)}, f32[6,128,128]{2,1,0:T(8,128)}, u32[]{:S(2)}) copy-start(f32[6,128,128]{2,1,0:T(8,128)} %im_ref.1) | copy-start | bytes 1179652
  0.0 7.6 %copy-start = (f32[6,128,128]{2,1,0:T(8,128)S(1)}, f32[6,128,128]{2,1,0:T(8,128)}, u32[]{:S(2)}) copy-start(f32[6,128,128]{2,1,0:T(8,128)} %re_ref.1) | copy-start | bytes 1179652
  0.0 30.5 %all-to-all-start = ((f32[16,128,128]{2,1,0:T(8,128)}), f32[16,128,128]{2,1,0:T(8,128)S(1)}, u32[]{:S(2)}, u32[]{:S(2)}) async-start(f32[16,128,128]{2,1,0:T(8,128)} %bitcast.14), calls=%async_computation | async-start | bytes 2097152 | tf_op jit(solution)/shard_map/all_to_all | solution.py:195
  7.6 1.2 %copy-start.2 = (s32[6,16,2]{1,2,0:T(2,128)S(1)}, s32[6,16,2]{1,2,0:T(2,128)}, u32[]{:S(2)}) copy-start(s32[6,16,2]{1,2,0:T(2,128)} %param.10) | copy-start | bytes 2308
  7.6 1.2 %copy-start.4 = (f32[6,16]{1,0:T(8,128)S(1)}, f32[6,16]{1,0:T(8,128)}, u32[]{:S(2)}) copy-start(f32[6,16]{1,0:T(8,128)} %angle_ref.1) | copy-start | bytes 1156
  38.3 10.5 %collective-permute-start = (f32[128,128]{1,0:T(8,128)S(1)}, f32[128,128]{1,0:T(8,128)S(1)}, u32[]{:S(2)}, u32[]{:S(2)}) collective-permute-start(f32[128,128]{1,0:T(8,128)S(1)} %get-tuple-element.26), channel_id=1, source_target_pairs={{0,16},{2,18},{4,20},{6,22},{8,24},{10,26},{12,28},{14,30},{16,0},... | collective-permute-start | bytes 196616 | tf_op jit(solution)/shard_map/ppermute | solution.py:229
  43.4 6.3 %collective-permute-start.1 = (f32[128,128]{1,0:T(8,128)S(1)}, f32[128,128]{1,0:T(8,128)S(1)}, u32[]{:S(2)}, u32[]{:S(2)}) collective-permute-start(f32[128,128]{1,0:T(8,128)S(1)} %get-tuple-element.27), channel_id=1, source_target_pairs={{0,18},{2,16},{4,22},{6,20},{8,26},{10,24},{12,30},{14,28},{16,2},... | collective-permute-start | bytes 196616 | tf_op jit(solution)/shard_map/ppermute | solution.py:229
  43.4 7.4 %collective-permute-start.2 = (f32[128,128]{1,0:T(8,128)S(1)}, f32[128,128]{1,0:T(8,128)S(1)}, u32[]{:S(2)}, u32[]{:S(2)}) collective-permute-start(f32[128,128]{1,0:T(8,128)S(1)} %get-tuple-element.28), channel_id=1, source_target_pairs={{0,8},{2,10},{4,12},{6,14},{8,0},{10,2},{12,4},{14,6},{16,24},{18,... | collective-permute-start | bytes 196616 | tf_op jit(solution)/shard_map/ppermute | solution.py:229
  44.6 7.7 %collective-permute-start.3 = (f32[128,128]{1,0:T(8,128)S(1)}, f32[128,128]{1,0:T(8,128)S(1)}, u32[]{:S(2)}, u32[]{:S(2)}) collective-permute-start(f32[128,128]{1,0:T(8,128)S(1)} %get-tuple-element.29), channel_id=1, source_target_pairs={{0,10},{2,8},{4,14},{6,12},{8,2},{10,0},{12,6},{14,4},{16,26},{18,... | collective-permute-start | bytes 196616 | tf_op jit(solution)/shard_map/ppermute | solution.py:229
  44.9 8.9 %collective-permute-start.4 = (f32[128,128]{1,0:T(8,128)S(1)}, f32[128,128]{1,0:T(8,128)S(1)}, u32[]{:S(2)}, u32[]{:S(2)}) collective-permute-start(f32[128,128]{1,0:T(8,128)S(1)} %get-tuple-element.30), channel_id=1, source_target_pairs={{0,20},{2,22},{4,16},{6,18},{8,28},{10,30},{12,24},{14,26},{16,4},... | collective-permute-start | bytes 196616 | tf_op jit(solution)/shard_map/ppermute | solution.py:229
  48.8 7.3 %collective-permute-start.5 = (f32[128,128]{1,0:T(8,128)S(1)}, f32[128,128]{1,0:T(8,128)S(1)}, u32[]{:S(2)}, u32[]{:S(2)}) collective-permute-start(f32[128,128]{1,0:T(8,128)S(1)} %get-tuple-element.31), channel_id=1, source_target_pairs={{0,22},{2,20},{4,18},{6,16},{8,30},{10,28},{12,26},{14,24},{16,6},... | collective-permute-start | bytes 196616 | tf_op jit(solution)/shard_map/ppermute | solution.py:229
  49.7 9.8 %collective-permute-start.6 = (f32[128,128]{1,0:T(8,128)S(1)}, f32[128,128]{1,0:T(8,128)S(1)}, u32[]{:S(2)}, u32[]{:S(2)}) collective-permute-start(f32[128,128]{1,0:T(8,128)S(1)} %get-tuple-element.32), channel_id=1, source_target_pairs={{0,12},{2,14},{4,8},{6,10},{8,4},{10,6},{12,0},{14,2},{16,28},{18,... | collective-permute-start | bytes 196616 | tf_op jit(solution)/shard_map/ppermute | solution.py:229
  50.8 10.4 %collective-permute-start.7 = (f32[128,128]{1,0:T(8,128)S(1)}, f32[128,128]{1,0:T(8,128)S(1)}, u32[]{:S(2)}, u32[]{:S(2)}) collective-permute-start(f32[128,128]{1,0:T(8,128)S(1)} %get-tuple-element.33), channel_id=1, source_target_pairs={{0,14},{2,12},{4,10},{6,8},{8,6},{10,4},{12,2},{14,0},{16,30},{18,... | collective-permute-start | bytes 196616 | tf_op jit(solution)/shard_map/ppermute | solution.py:229
  52.3 9.6 %collective-permute-start.8 = (f32[128,128]{1,0:T(8,128)S(1)}, f32[128,128]{1,0:T(8,128)S(1)}, u32[]{:S(2)}, u32[]{:S(2)}) collective-permute-start(f32[128,128]{1,0:T(8,128)S(1)} %get-tuple-element.34), channel_id=1, source_target_pairs={{0,24},{2,26},{4,28},{6,30},{8,16},{10,18},{12,20},{14,22},{16,8},... | collective-permute-start | bytes 196616 | tf_op jit(solution)/shard_map/ppermute | solution.py:229
  53.9 8.4 %collective-permute-start.9 = (f32[128,128]{1,0:T(8,128)S(1)}, f32[128,128]{1,0:T(8,128)S(1)}, u32[]{:S(2)}, u32[]{:S(2)}) collective-permute-start(f32[128,128]{1,0:T(8,128)S(1)} %get-tuple-element.35), channel_id=1, source_target_pairs={{0,26},{2,24},{4,30},{6,28},{8,18},{10,16},{12,22},{14,20},{16,10}... | collective-permute-start | bytes 196616 | tf_op jit(solution)/shard_map/ppermute | solution.py:229
  56.1 7.6 %collective-permute-start.10 = (f32[128,128]{1,0:T(8,128)S(1)}, f32[128,128]{1,0:T(8,128)S(1)}, u32[]{:S(2)}, u32[]{:S(2)}) collective-permute-start(f32[128,128]{1,0:T(8,128)S(1)} %get-tuple-element.36), channel_id=1, source_target_pairs={{0,28},{2,30},{4,24},{6,26},{8,20},{10,22},{12,16},{14,18},{16,12}... | collective-permute-start | bytes 196616 | tf_op jit(solution)/shard_map/ppermute | solution.py:229
  59.5 7.1 %collective-permute-start.11 = (f32[128,128]{1,0:T(8,128)S(1)}, f32[128,128]{1,0:T(8,128)S(1)}, u32[]{:S(2)}, u32[]{:S(2)}) collective-permute-start(f32[128,128]{1,0:T(8,128)S(1)} %get-tuple-element.37), channel_id=1, source_target_pairs={{0,30},{2,28},{4,26},{6,24},{8,22},{10,20},{12,18},{14,16},{16,14}... | collective-permute-start | bytes 196616 | tf_op jit(solution)/shard_map/ppermute | solution.py:229
  61.2 6.3 %collective-permute-start.12 = (f32[128,128]{1,0:T(8,128)S(1)}, f32[128,128]{1,0:T(8,128)S(1)}, u32[]{:S(2)}, u32[]{:S(2)}) collective-permute-start(f32[128,128]{1,0:T(8,128)S(1)} %get-tuple-element.38), channel_id=1, source_target_pairs={{0,4},{2,6},{4,0},{6,2},{8,12},{10,14},{12,8},{14,10},{16,20},{18,... | collective-permute-start | bytes 196616 | tf_op jit(solution)/shard_map/ppermute | solution.py:229
  61.9 5.8 %collective-permute-start.13 = (f32[128,128]{1,0:T(8,128)S(1)}, f32[128,128]{1,0:T(8,128)S(1)}, u32[]{:S(2)}, u32[]{:S(2)}) collective-permute-start(f32[128,128]{1,0:T(8,128)S(1)} %get-tuple-element.39), channel_id=1, source_target_pairs={{0,6},{2,4},{4,2},{6,0},{8,14},{10,12},{12,10},{14,8},{16,22},{18,... | collective-permute-start | bytes 196616 | tf_op jit(solution)/shard_map/ppermute | solution.py:229
  62.3 5.4 %collective-permute-start.14 = (f32[128,128]{1,0:T(8,128)S(1)}, f32[128,128]{1,0:T(8,128)S(1)}, u32[]{:S(2)}, u32[]{:S(2)}) collective-permute-start(f32[128,128]{1,0:T(8,128)S(1)} %get-tuple-element.40), channel_id=1, source_target_pairs={{0,2},{2,0},{4,6},{6,4},{8,10},{10,8},{12,14},{14,12},{16,18},{18,... | collective-permute-start | bytes 196616 | tf_op jit(solution)/shard_map/ppermute | solution.py:229

commit v17 on v8

--- a/solution.py
+++ b/solution.py
@@ -27,11 +27,14 @@
 
 
 def exchange_order(wide):
-    far = range(wide // 2, wide, 2)
-    near = list(range(wide // 4, wide // 2, 2))
-    near = [k for pair in zip(near, list(range(2, wide // 4, 2)) + [None]) for k in pair if k]
-    pairs = [k for pair in zip(far, near) for k in pair]
-    return [0] + [k + j for k in pairs for j in range(2)] + [1, wide - 2, wide - 1]
+    far = list(range(wide // 2, wide, 2))
+    near = [k for top in (wide // 4, wide // 8) for k in range(top, 2 * top, 2) if top > 1]
+    near += [k for k in range(wide // 2 - 2, 0, -2) if k not in near]
+    pairs = []
+    for i, k in enumerate(far):
+        pairs += [k] + near[i : i + 1] * (i < len(near) - 1)
+    pairs += near[-1:]
+    return [0] + [k + j for k in pairs for j in range(2)] + [1]
 
 
 def block_of(ref, k, wide):
@@ -40,21 +43,7 @@
     return ref.at[pl.ds(pl.multiple_of(start, rows), rows)]
 
 
-def tables_kernel(spect, narrow, re_ref, im_ref, order_ref, pair_ref, angle_ref, gate_ref, turn_ref):
-    row = lax.broadcasted_iota(jnp.int32, (spect, LOW), 0)
-    lane = lax.broadcasted_iota(jnp.int32, (spect, LOW), 1)
-    r = lax.axis_index("wide") * (spect // narrow) + row // narrow
-    for layer in range(LAYERS):
-        b = lax.axis_index("narrow") if layer % 2 == 0 else row % narrow
-        u = ((r * narrow + b) * LOW + lane) & (2**PHASE_BITS - 1)
-        phase = jnp.zeros((spect, LOW), jnp.float32)
-        for gate in range(PHASES):
-            first = u >> jnp.full((spect, LOW), pair_ref[layer, 0, gate], jnp.int32)
-            second = u >> jnp.full((spect, LOW), pair_ref[layer, 1, gate], jnp.int32)
-            phase = phase + jnp.where((first & second & 1) == 1, angle_ref[layer, gate], 0.0)
-        turn_ref[layer, 0] = jnp.cos(phase)
-        turn_ref[layer, 1] = jnp.sin(phase)
-
+def gates_kernel(re_ref, im_ref, order_ref, gate_ref):
     j = lax.broadcasted_iota(jnp.int32, (8, GATE), 1)
     position = lax.broadcasted_iota(jnp.int32, (GATE // 8, 8, GATE), 0) * 8
     position = position + lax.broadcasted_iota(jnp.int32, (GATE // 8, 8, GATE), 1)
@@ -73,26 +62,33 @@
                 gate_ref[layer, which, :, part * GATE : (part + 1) * GATE] = moved.astype(jnp.bfloat16)
 
 
+def phases_kernel(spect, narrow, pair_ref, angle_ref, turn_ref):
+    size = turn_ref.shape[2]
+    row = lax.broadcasted_iota(jnp.int32, (size, LOW), 0)
+    lane = lax.broadcasted_iota(jnp.int32, (size, LOW), 1)
+    r = lax.axis_index("wide") * (spect // narrow) + row // narrow
+    for layer in range(LAYERS):
+        b = lax.axis_index("narrow") if layer % 2 == 0 else row % narrow
+        u = ((r * narrow + b) * LOW + lane) & (2**PHASE_BITS - 1)
+        phase = jnp.zeros((size, LOW), jnp.float32)
+        for gate in range(PHASES):
+            first = u >> jnp.full((size, LOW), pair_ref[layer, 0, gate], jnp.int32)
+            second = u >> jnp.full((size, LOW), pair_ref[layer, 1, gate], jnp.int32)
+            phase = phase + jnp.where((first & second & 1) == 1, angle_ref[layer, gate], 0.0)
+        turn_ref[layer, 0] = jnp.cos(phase)
+        turn_ref[layer, 1] = jnp.sin(phase)
+
+
 def exchange_modes(rows, span):
-    rows = list(rows)
-    lane = lax.broadcasted_iota(jnp.int32, rows[0].shape, 1)
+    count = len(rows)
+    group = lax.broadcasted_iota(jnp.int32, rows[0].shape, 1) // span
+    rows = [pltpu.roll(row, m * span, 1) if m else row for m, row in enumerate(rows)]
     step = 1
-    while step < len(rows):
-        shift = step * span
-        upper = (lane & shift) != 0
-        for m in range(len(rows)):
-            if m & step:
-                continue
-            x0, x1 = rows[m], rows[m + step]
-            if 2 * shift == LANES:
-                crossing = pltpu.roll(jnp.where(upper, x0, x1), shift, 1)
-                rows[m] = jnp.where(upper, crossing, x0)
-                rows[m + step] = jnp.where(upper, x1, crossing)
-            else:
-                rows[m] = jnp.where(upper, pltpu.roll(x1, shift, 1), x0)
-                rows[m + step] = jnp.where(upper, x1, pltpu.roll(x0, LANES - shift, 1))
+    while step < count:
+        taken = (group & step) != 0
+        rows = [jnp.where(taken, rows[(y + step) % count], rows[y]) for y in range(count)]
         step *= 2
-    return rows
+    return [pltpu.roll(rows[-r % count], LANES - r * span, 1) if r else rows[0] for r in range(count)]
 
 
 def place_kernel(wide, *rest):
@@ -124,6 +120,7 @@
     rows_at_once = min(spect, PACKED)
     joined = PACKED // rows_at_once
     tile = min(TILE, count)
+    distinct = turn.shape[2]
 
     for part in range(2):
         for lanes in range(2):
@@ -160,15 +157,14 @@
                             left_high[e, at : at + PACKED, part * LANES : (part + 1) * LANES] = high
                             left_low[e, at : at + PACKED, part * LANES : (part + 1) * LANES] = low
 
-        dot = partial(jnp.dot, preferred_element_type=jnp.float32)
+        square = jnp.concatenate([factor[0], factor[0], factor[1]], axis=0)
         for first in range(0, count, tile):
             rows = slice(first, first + tile)
             for e in range(2):
-                gated = dot(left_high[e, rows], factor[0])
-                gated = gated + dot(left_low[e, rows], factor[0])
-                gated = gated + dot(left_high[e, rows], factor[1])
-                real = gated[:, :LANES].reshape(tile // spect, spect, LANES)
-                imag = gated[:, LANES:].reshape(tile // spect, spect, LANES)
+                terms = jnp.concatenate([left_high[e, rows], left_low[e, rows], left_high[e, rows]], axis=1)
+                gated = jnp.dot(terms, square, preferred_element_type=jnp.float32)
+                real = gated[:, :LANES].reshape(tile // distinct, distinct, LANES)
+                imag = gated[:, LANES:].reshape(tile // distinct, distinct, LANES)
                 lanes = slice(e * LANES, (e + 1) * LANES)
                 cosine, sine = turn[layer, 0, :, lanes][None], turn[layer, 1, :, lanes][None]
                 state[1 - slot, 0, rows, lanes] = (real * cosine - imag * sine).reshape(tile, LANES)
@@ -208,17 +204,31 @@
     part_of_vmem = pltpu.CompilerParams(vmem_limit_bytes=24 * 2**20)
     order = exchange_order(wide)
 
-    gates = (LAYERS, 2, GATE, 2 * GATE)
-    turns = (LAYERS, 2, spect, LOW)
-    gate, turn = pl.pallas_call(
-        partial(tables_kernel, spect, narrow),
-        in_specs=[in_vmem, in_vmem, in_smem, in_smem, in_smem],
-        out_specs=[in_vmem, in_vmem],
-        out_shape=[jax.ShapeDtypeStruct(gates, jnp.bfloat16), jax.ShapeDtypeStruct(turns, jnp.float32)],
-        compiler_params=part_of_vmem,
-        cost_estimate=pl.CostEstimate(flops=10**9, bytes_accessed=8 * 10**6, transcendentals=10**5),
-        name="tables",
-    )(gate_re, gate_im, bit_orders, phase_pairs.transpose(0, 2, 1), phase_angles)
+    turns = (LAYERS, 2, min(spect, 2 ** (PHASE_BITS - LOW_BITS)), LOW)
+    gate = pl.pallas_call(
+        gates_kernel,
+        in_specs=[in_vmem, in_vmem, in_smem],
+        out_specs=in_vmem,
+        out_shape=jax.ShapeDtypeStruct((LAYERS, 2, GATE, 2 * GATE), jnp.bfloat16),
+        compiler_params=part_of_vmem,
+        cost_estimate=pl.CostEstimate(flops=10**9, bytes_accessed=4 * 10**6, transcendentals=0),
+        name="gates",
+    )(gate_re, gate_im, bit_orders)
+    turn = pl.pallas_call(
+        partial(phases_kernel, spect, narrow),
+        in_specs=[in_smem, in_smem],
+        out_specs=in_vmem,
+        out_shape=jax.ShapeDtypeStruct(turns, jnp.float32),
+        compiler_params=part_of_vmem,
+        cost_estimate=pl.CostEstimate(flops=10**8, bytes_accessed=10**6, transcendentals=10**5),
+        name="phases",
+    )(phase_pairs.transpose(0, 2, 1), phase_angles)
+
+    def swap(blocks, ks):
+        return [
+            lax.ppermute(block, "wide", [(i, i ^ k) for i in range(wide)]) if k else block
+            for block, k in zip(blocks, ks)
+        ]
 
     done = pl.pallas_call(
         partial(layers_kernel, wide, spect),
@@ -236,12 +246,6 @@
         name="layers",
     )(bit_orders, gathered, gate, turn)
 
-    def swap(blocks, ks):
-        return [
-            lax.ppermute(block, "wide", [(i, i ^ k) for i in range(wide)]) if k else block
-            for block, k in zip(blocks, ks)
-        ]
-
     back = pl.pallas_call(
         partial(place_kernel, wide),
         in_specs=[in_vmem] * wide,

time: 78.5 us -> 71.7 us (0.913)
  Pallas kernels: 19.6 us -> 14.3 us
  waiting for transfers between devices: 29.5 us -> 27.2 us
    pallas_call x1, Pallas kernels: 15.6 us -> 10.5 us  [local(): pl.pallas_call(partial(layers_kernel, wide, spect), in_specs=[in_smem] +...]
    ppermute x15, waiting for transfers between devices: 9.47 us -> 7.09 us  [swap(): lax.ppermute(block, 'wide', [(i, i ^ k) for i in range(wide)])]
    pallas_call x1 -> x2, Pallas kernels: 2.82 us -> 2.73 us  [the longest x1 1.47 us: local(): pl.pallas_call(partial(phases_kernel, spect, narrow), in_specs=[in_smem,...]
where the time goes in v17:
time: 71.7 us; the launch traced here: 71.5 us
  starting transfers between devices  29.8 us (42%)
  waiting for transfers between devices  27.2 us (38%)
  Pallas kernels  14.3 us (20%)
    ppermute x15, starting transfers between devices, swap(): lax.ppermute(block, 'wide', [(i, i ^ k) for i in range(wide)])  22.3 us
    all_to_all x1, waiting for transfers between devices, local(): lax.all_to_all(rows, 'wide', split_axis=0, concat_axis=0, tiled=True)  20.1 us
    pallas_call x1, Pallas kernels, local(): pl.pallas_call(partial(layers_kernel, wide, spect), in_specs=[in_smem] +...  10.5 us
    all_to_all x1, starting transfers between devices, local(): lax.all_to_all(rows, 'wide', split_axis=0, concat_axis=0, tiled=True)  7.54 us
    ppermute x15, waiting for transfers between devices, swap(): lax.ppermute(block, 'wide', [(i, i ^ k) for i in range(wide)])  7.09 us
    pallas_call x1, Pallas kernels, local(): pl.pallas_call(partial(phases_kernel, spect, narrow), in_specs=[in_smem,...  1.47 us
  transfers between devices with their start and end apart: 16, of which 8 were waited for; matrix products, arithmetic and copies ran while one was open for 0% of the time, Pallas kernels for 4%

profile of v17, /device:TPU:0, one launch (start us, length us, event | category | flops | bytes accessed | tf_op | source)
XLA Modules:
  0.0 71.5 jit_solution(13621082257382292918)
XLA Ops:
  0.0 7.5 %all-to-all-start = ((f32[16,128,128]{2,1,0:T(8,128)}), f32[16,128,128]{2,1,0:T(8,128)S(1)}, u32[]{:S(2)}, u32[]{:S(2)}) async-start(f32[16,128,128]{2,1,0:T(8,128)} %bitcast.14), calls=%async_computation | async-start | bytes 2097152 | tf_op jit(solution)/shard_map/all_to_all | solution.py:198
  7.6 0.0 copy-start.4
  7.6 1.5 %phases.1.turn = f32[6,2,16,256]{3,2,1,0:T(8,128)S(1)} custom-call(s32[6,2,16]{2,1,0:T(2,128)S(1)} %bitcast.13, f32[6,16]{1,0:T(8,128)S(1)} %copy-done.3), custom_call_target="tpu_custom_call" | custom-call | flops 100000000 | bytes 1000000 | tf_op jit(solution)/shard_map/phases/pallas_call | solution.py:217
  9.1 1.3 %gates.1.gate = bf16[6,2,128,256]{3,2,1,0:T(8,128)(2,1)S(1)} custom-call(f32[6,128,128]{2,1,0:T(8,128)S(1)} %copy-done, f32[6,128,128]{2,1,0:T(8,128)S(1)} %copy-done.1, s32[6,8]{1,0:T(8,128)S(1)} %copy-done.4), custom_call_target="tpu_custom_call" | custom-call | flops 1000000000 | bytes 4000000 | tf_op jit(solution)/shard_map/gates/pallas_call | solution.py:208
  10.4 20.1 %all-to-all-done = f32[16,128,128]{2,1,0:T(8,128)S(1)} async-done(((f32[16,128,128]{2,1,0:T(8,128)}), f32[16,128,128]{2,1,0:T(8,128)S(1)}, u32[]{:S(2)}, u32[]{:S(2)}) %all-to-all-start) | async-done | bytes 1048608 | tf_op jit(solution)/shard_map/all_to_all | solution.py:198
  30.5 10.5 %layers.1 = (f32[128,128]{1,0:T(8,128)S(1)}, f32[128,128]{1,0:T(8,128)S(1)}, f32[128,128]{1,0:T(8,128)S(1)}, f32[128,128]{1,0:T(8,128)S(1)}, f32[128,128]{1,0:T(...) custom-call(s32[6,8]{1,0:T(8,128)S(1)} %copy-done.4, ...), custom_call_target="tpu_custom_call" | custom-call | flops 5000000000 | bytes 10000000 | tf_op jit(solution)/shard_map/layers/pallas_call | solution.py:233
  41.0 5.1 %collective-permute-start = (f32[128,128]{1,0:T(8,128)S(1)}, f32[128,128]{1,0:T(8,128)S(1)}, u32[]{:S(2)}, u32[]{:S(2)}) collective-permute-start(f32[128,128]{1,0:T(8,128)S(1)} %get-tuple-element.22), channel_id=1, source_target_pairs={{0,16},{2,18},{4,20},{6,22},{8,24},{10,26},{12,28},{14,30},{16,0},... | collective-permute-start | bytes 196616 | tf_op jit(solution)/shard_map/ppermute | solution.py:229
  46.1 0.0 collective-permute-start.1
  46.1 1.2 %collective-permute-start.2 = (f32[128,128]{1,0:T(8,128)S(1)}, f32[128,128]{1,0:T(8,128)S(1)}, u32[]{:S(2)}, u32[]{:S(2)}) collective-permute-start(f32[128,128]{1,0:T(8,128)S(1)} %get-tuple-element.24), channel_id=1, source_target_pairs={{0,8},{2,10},{4,12},{6,14},{8,0},{10,2},{12,4},{14,6},{16,24},{18,... | collective-permute-start | bytes 196616 | tf_op jit(solution)/shard_map/ppermute | solution.py:229
  47.3 0.4 collective-permute-start.3
  47.6 2.1 %collective-permute-start.4 = (f32[128,128]{1,0:T(8,128)S(1)}, f32[128,128]{1,0:T(8,128)S(1)}, u32[]{:S(2)}, u32[]{:S(2)}) collective-permute-start(f32[128,128]{1,0:T(8,128)S(1)} %get-tuple-element.26), channel_id=1, source_target_pairs={{0,20},{2,22},{4,16},{6,18},{8,28},{10,30},{12,24},{14,26},{16,4},... | collective-permute-start | bytes 196616 | tf_op jit(solution)/shard_map/ppermute | solution.py:229
  49.8 1.7 %collective-permute-done.rest_1_ = f32[128,128]{1,0:T(8,128)S(1)} collective-permute-done((f32[128,128]{1,0:T(8,128)S(1)}, f32[128,128]{1,0:T(8,128)S(1)}, u32[]{:S(2)}, u32[]{:S(2)}) %collective-permute-start) | collective-permute-done | bytes 65568 | tf_op jit(solution)/shard_map/ppermute | solution.py:229
  51.5 0.0 collective-permute-start.5
  51.5 0.9 %collective-permute-done.1.rest_2_ = f32[128,128]{1,0:T(8,128)S(1)} collective-permute-done((f32[128,128]{1,0:T(8,128)S(1)}, f32[128,128]{1,0:T(8,128)S(1)}, u32[]{:S(2)}, u32[]{:S(2)}) %collective-permute-start.1) | collective-permute-done | bytes 65568 | tf_op jit(solution)/shard_map/ppermute | solution.py:229
  52.4 1.1 %collective-permute-start.6 = (f32[128,128]{1,0:T(8,128)S(1)}, f32[128,128]{1,0:T(8,128)S(1)}, u32[]{:S(2)}, u32[]{:S(2)}) collective-permute-start(f32[128,128]{1,0:T(8,128)S(1)} %get-tuple-element.28), channel_id=1, source_target_pairs={{0,12},{2,14},{4,8},{6,10},{8,4},{10,6},{12,0},{14,2},{16,28},{18,... | collective-permute-start | bytes 196616 | tf_op jit(solution)/shard_map/ppermute | solution.py:229
  53.5 1.5 %collective-permute-start.7 = (f32[128,128]{1,0:T(8,128)S(1)}, f32[128,128]{1,0:T(8,128)S(1)}, u32[]{:S(2)}, u32[]{:S(2)}) collective-permute-start(f32[128,128]{1,0:T(8,128)S(1)} %get-tuple-element.29), channel_id=1, source_target_pairs={{0,14},{2,12},{4,10},{6,8},{8,6},{10,4},{12,2},{14,0},{16,30},{18,... | collective-permute-start | bytes 196616 | tf_op jit(solution)/shard_map/ppermute | solution.py:229
  55.0 1.6 %collective-permute-start.8 = (f32[128,128]{1,0:T(8,128)S(1)}, f32[128,128]{1,0:T(8,128)S(1)}, u32[]{:S(2)}, u32[]{:S(2)}) collective-permute-start(f32[128,128]{1,0:T(8,128)S(1)} %get-tuple-element.30), channel_id=1, source_target_pairs={{0,24},{2,26},{4,28},{6,30},{8,16},{10,18},{12,20},{14,22},{16,8},... | collective-permute-start | bytes 196616 | tf_op jit(solution)/shard_map/ppermute | solution.py:229
  56.6 0.0 collective-permute-done.4.rest_5_
  56.6 2.0 %collective-permute-start.9 = (f32[128,128]{1,0:T(8,128)S(1)}, f32[128,128]{1,0:T(8,128)S(1)}, u32[]{:S(2)}, u32[]{:S(2)}) collective-permute-start(f32[128,128]{1,0:T(8,128)S(1)} %get-tuple-element.31), channel_id=1, source_target_pairs={{0,26},{2,24},{4,30},{6,28},{8,18},{10,16},{12,22},{14,20},{16,10}... | collective-permute-start | bytes 196616 | tf_op jit(solution)/shard_map/ppermute | solution.py:229
  58.6 0.2 collective-permute-done.5.rest_6_
  58.8 3.4 %collective-permute-start.10 = (f32[128,128]{1,0:T(8,128)S(1)}, f32[128,128]{1,0:T(8,128)S(1)}, u32[]{:S(2)}, u32[]{:S(2)}) collective-permute-start(f32[128,128]{1,0:T(8,128)S(1)} %get-tuple-element.32), channel_id=1, source_target_pairs={{0,28},{2,30},{4,24},{6,26},{8,20},{10,22},{12,16},{14,18},{16,12}... | collective-permute-start | bytes 196616 | tf_op jit(solution)/shard_map/ppermute | solution.py:229
  62.2 1.8 %collective-permute-start.11 = (f32[128,128]{1,0:T(8,128)S(1)}, f32[128,128]{1,0:T(8,128)S(1)}, u32[]{:S(2)}, u32[]{:S(2)}) collective-permute-start(f32[128,128]{1,0:T(8,128)S(1)} %get-tuple-element.33), channel_id=1, source_target_pairs={{0,30},{2,28},{4,26},{6,24},{8,22},{10,20},{12,18},{14,16},{16,14}... | collective-permute-start | bytes 196616 | tf_op jit(solution)/shard_map/ppermute | solution.py:229
  64.0 0.0 collective-permute-done.7.rest_8_
  64.0 0.6 collective-permute-start.12
  64.6 0.4 collective-permute-start.13
  65.0 0.0 collective-permute-done.9.rest_10_
  65.0 1.1 %collective-permute-start.14 = (f32[128,128]{1,0:T(8,128)S(1)}, f32[128,128]{1,0:T(8,128)S(1)}, u32[]{:S(2)}, u32[]{:S(2)}) collective-permute-start(f32[128,128]{1,0:T(8,128)S(1)} %get-tuple-element.36), channel_id=1, source_target_pairs={{0,2},{2,0},{4,6},{6,4},{8,10},{10,8},{12,14},{14,12},{16,18},{18,... | collective-permute-start | bytes 196616 | tf_op jit(solution)/shard_map/ppermute | solution.py:229
  66.1 0.2 collective-permute-done.10.rest_11_
  66.3 3.1 %collective-permute-done.11.rest_12_ = f32[128,128]{1,0:T(8,128)S(1)} collective-permute-done((f32[128,128]{1,0:T(8,128)S(1)}, f32[128,128]{1,0:T(8,128)S(1)}, u32[]{:S(2)}, u32[]{:S(2)}) %collective-permute-start.11) | collective-permute-done | bytes 65568 | tf_op jit(solution)/shard_map/ppermute | solution.py:229
  69.4 0.9 %collective-permute-done.12.rest_13_ = f32[128,128]{1,0:T(8,128)S(1)} collective-permute-done((f32[128,128]{1,0:T(8,128)S(1)}, f32[128,128]{1,0:T(8,128)S(1)}, u32[]{:S(2)}, u32[]{:S(2)}) %collective-permute-start.12) | collective-permute-done | bytes 65568 | tf_op jit(solution)/shard_map/ppermute | solution.py:229
  70.3 0.1 collective-permute-done.13.rest_14_
  70.4 1.1 %place.1 = f32[2048,128]{1,0:T(8,128)} custom-call(f32[128,128]{1,0:T(8,128)S(1)} %get-tuple-element.21.rest_0_, f32[128,128]{1,0:T(8,128)S(1)} %collective-permute-done.rest_1_, f32[128,128]{1,0:T(8,128)S(1)} %collective-permute-done.1.rest_2_, f32[128,128]{1,0:T(8,128)S(1)} %collective-permute-done.2.rest_3_, ...), custom_call_target="tpu_custom_call" | custom-call | tf_op jit(solution)/shard_map/place/pallas_call | solution.py:249
  (14 shorter events, 0.0 us)
Async XLA Ops:
  0.0 7.6 %copy-start.2 = (s32[6,16,2]{1,2,0:T(2,128)S(1)}, s32[6,16,2]{1,2,0:T(2,128)}, u32[]{:S(2)}) copy-start(s32[6,16,2]{1,2,0:T(2,128)} %param.10) | copy-start | bytes 2308
  0.0 7.6 %copy-start.3 = (f32[6,16]{1,0:T(8,128)S(1)}, f32[6,16]{1,0:T(8,128)}, u32[]{:S(2)}) copy-start(f32[6,16]{1,0:T(8,128)} %angle_ref.1) | copy-start | bytes 1156
  0.0 9.1 %copy-start = (f32[6,128,128]{2,1,0:T(8,128)S(1)}, f32[6,128,128]{2,1,0:T(8,128)}, u32[]{:S(2)}) copy-start(f32[6,128,128]{2,1,0:T(8,128)} %re_ref.1) | copy-start | bytes 1179652
  0.0 9.1 %copy-start.1 = (f32[6,128,128]{2,1,0:T(8,128)S(1)}, f32[6,128,128]{2,1,0:T(8,128)}, u32[]{:S(2)}) copy-start(f32[6,128,128]{2,1,0:T(8,128)} %im_ref.1) | copy-start | bytes 1179652
  0.0 30.5 %all-to-all-start = ((f32[16,128,128]{2,1,0:T(8,128)}), f32[16,128,128]{2,1,0:T(8,128)S(1)}, u32[]{:S(2)}, u32[]{:S(2)}) async-start(f32[16,128,128]{2,1,0:T(8,128)} %bitcast.14), calls=%async_computation | async-start | bytes 2097152 | tf_op jit(solution)/shard_map/all_to_all | solution.py:198
  7.6 1.5 %copy-start.4 = (s32[6,8]{1,0:T(8,128)S(1)}, s32[6,8]{1,0:T(8,128)}, u32[]{:S(2)}) copy-start(s32[6,8]{1,0:T(8,128)} %order_ref.3) | copy-start | bytes 580
  41.0 10.5 %collective-permute-start = (f32[128,128]{1,0:T(8,128)S(1)}, f32[128,128]{1,0:T(8,128)S(1)}, u32[]{:S(2)}, u32[]{:S(2)}) collective-permute-start(f32[128,128]{1,0:T(8,128)S(1)} %get-tuple-element.22), channel_id=1, source_target_pairs={{0,16},{2,18},{4,20},{6,22},{8,24},{10,26},{12,28},{14,30},{16,0},... | collective-permute-start | bytes 196616 | tf_op jit(solution)/shard_map/ppermute | solution.py:229
  46.1 6.3 %collective-permute-start.1 = (f32[128,128]{1,0:T(8,128)S(1)}, f32[128,128]{1,0:T(8,128)S(1)}, u32[]{:S(2)}, u32[]{:S(2)}) collective-permute-start(f32[128,128]{1,0:T(8,128)S(1)} %get-tuple-element.23), channel_id=1, source_target_pairs={{0,18},{2,16},{4,22},{6,20},{8,26},{10,24},{12,30},{14,28},{16,2},... | collective-permute-start | bytes 196616 | tf_op jit(solution)/shard_map/ppermute | solution.py:229
  46.1 7.4 %collective-permute-start.2 = (f32[128,128]{1,0:T(8,128)S(1)}, f32[128,128]{1,0:T(8,128)S(1)}, u32[]{:S(2)}, u32[]{:S(2)}) collective-permute-start(f32[128,128]{1,0:T(8,128)S(1)} %get-tuple-element.24), channel_id=1, source_target_pairs={{0,8},{2,10},{4,12},{6,14},{8,0},{10,2},{12,4},{14,6},{16,24},{18,... | collective-permute-start | bytes 196616 | tf_op jit(solution)/shard_map/ppermute | solution.py:229
  47.3 7.7 %collective-permute-start.3 = (f32[128,128]{1,0:T(8,128)S(1)}, f32[128,128]{1,0:T(8,128)S(1)}, u32[]{:S(2)}, u32[]{:S(2)}) collective-permute-start(f32[128,128]{1,0:T(8,128)S(1)} %get-tuple-element.25), channel_id=1, source_target_pairs={{0,10},{2,8},{4,14},{6,12},{8,2},{10,0},{12,6},{14,4},{16,26},{18,... | collective-permute-start | bytes 196616 | tf_op jit(solution)/shard_map/ppermute | solution.py:229
  47.6 8.9 %collective-permute-start.4 = (f32[128,128]{1,0:T(8,128)S(1)}, f32[128,128]{1,0:T(8,128)S(1)}, u32[]{:S(2)}, u32[]{:S(2)}) collective-permute-start(f32[128,128]{1,0:T(8,128)S(1)} %get-tuple-element.26), channel_id=1, source_target_pairs={{0,20},{2,22},{4,16},{6,18},{8,28},{10,30},{12,24},{14,26},{16,4},... | collective-permute-start | bytes 196616 | tf_op jit(solution)/shard_map/ppermute | solution.py:229
  51.5 7.3 %collective-permute-start.5 = (f32[128,128]{1,0:T(8,128)S(1)}, f32[128,128]{1,0:T(8,128)S(1)}, u32[]{:S(2)}, u32[]{:S(2)}) collective-permute-start(f32[128,128]{1,0:T(8,128)S(1)} %get-tuple-element.27), channel_id=1, source_target_pairs={{0,22},{2,20},{4,18},{6,16},{8,30},{10,28},{12,26},{14,24},{16,6},... | collective-permute-start | bytes 196616 | tf_op jit(solution)/shard_map/ppermute | solution.py:229
  52.4 9.8 %collective-permute-start.6 = (f32[128,128]{1,0:T(8,128)S(1)}, f32[128,128]{1,0:T(8,128)S(1)}, u32[]{:S(2)}, u32[]{:S(2)}) collective-permute-start(f32[128,128]{1,0:T(8,128)S(1)} %get-tuple-element.28), channel_id=1, source_target_pairs={{0,12},{2,14},{4,8},{6,10},{8,4},{10,6},{12,0},{14,2},{16,28},{18,... | collective-permute-start | bytes 196616 | tf_op jit(solution)/shard_map/ppermute | solution.py:229
  53.5 10.5 %collective-permute-start.7 = (f32[128,128]{1,0:T(8,128)S(1)}, f32[128,128]{1,0:T(8,128)S(1)}, u32[]{:S(2)}, u32[]{:S(2)}) collective-permute-start(f32[128,128]{1,0:T(8,128)S(1)} %get-tuple-element.29), channel_id=1, source_target_pairs={{0,14},{2,12},{4,10},{6,8},{8,6},{10,4},{12,2},{14,0},{16,30},{18,... | collective-permute-start | bytes 196616 | tf_op jit(solution)/shard_map/ppermute | solution.py:229
  55.0 9.6 %collective-permute-start.8 = (f32[128,128]{1,0:T(8,128)S(1)}, f32[128,128]{1,0:T(8,128)S(1)}, u32[]{:S(2)}, u32[]{:S(2)}) collective-permute-start(f32[128,128]{1,0:T(8,128)S(1)} %get-tuple-element.30), channel_id=1, source_target_pairs={{0,24},{2,26},{4,28},{6,30},{8,16},{10,18},{12,20},{14,22},{16,8},... | collective-permute-start | bytes 196616 | tf_op jit(solution)/shard_map/ppermute | solution.py:229
  56.6 8.4 %collective-permute-start.9 = (f32[128,128]{1,0:T(8,128)S(1)}, f32[128,128]{1,0:T(8,128)S(1)}, u32[]{:S(2)}, u32[]{:S(2)}) collective-permute-start(f32[128,128]{1,0:T(8,128)S(1)} %get-tuple-element.31), channel_id=1, source_target_pairs={{0,26},{2,24},{4,30},{6,28},{8,18},{10,16},{12,22},{14,20},{16,10}... | collective-permute-start | bytes 196616 | tf_op jit(solution)/shard_map/ppermute | solution.py:229
  58.8 7.5 %collective-permute-start.10 = (f32[128,128]{1,0:T(8,128)S(1)}, f32[128,128]{1,0:T(8,128)S(1)}, u32[]{:S(2)}, u32[]{:S(2)}) collective-permute-start(f32[128,128]{1,0:T(8,128)S(1)} %get-tuple-element.32), channel_id=1, source_target_pairs={{0,28},{2,30},{4,24},{6,26},{8,20},{10,22},{12,16},{14,18},{16,12}... | collective-permute-start | bytes 196616 | tf_op jit(solution)/shard_map/ppermute | solution.py:229
  62.2 7.2 %collective-permute-start.11 = (f32[128,128]{1,0:T(8,128)S(1)}, f32[128,128]{1,0:T(8,128)S(1)}, u32[]{:S(2)}, u32[]{:S(2)}) collective-permute-start(f32[128,128]{1,0:T(8,128)S(1)} %get-tuple-element.33), channel_id=1, source_target_pairs={{0,30},{2,28},{4,26},{6,24},{8,22},{10,20},{12,18},{14,16},{16,14}... | collective-permute-start | bytes 196616 | tf_op jit(solution)/shard_map/ppermute | solution.py:229
  64.0 6.3 %collective-permute-start.12 = (f32[128,128]{1,0:T(8,128)S(1)}, f32[128,128]{1,0:T(8,128)S(1)}, u32[]{:S(2)}, u32[]{:S(2)}) collective-permute-start(f32[128,128]{1,0:T(8,128)S(1)} %get-tuple-element.34), channel_id=1, source_target_pairs={{0,4},{2,6},{4,0},{6,2},{8,12},{10,14},{12,8},{14,10},{16,20},{18,... | collective-permute-start | bytes 196616 | tf_op jit(solution)/shard_map/ppermute | solution.py:229
  64.6 5.8 %collective-permute-start.13 = (f32[128,128]{1,0:T(8,128)S(1)}, f32[128,128]{1,0:T(8,128)S(1)}, u32[]{:S(2)}, u32[]{:S(2)}) collective-permute-start(f32[128,128]{1,0:T(8,128)S(1)} %get-tuple-element.35), channel_id=1, source_target_pairs={{0,6},{2,4},{4,2},{6,0},{8,14},{10,12},{12,10},{14,8},{16,22},{18,... | collective-permute-start | bytes 196616 | tf_op jit(solution)/shard_map/ppermute | solution.py:229
  65.0 5.4 %collective-permute-start.14 = (f32[128,128]{1,0:T(8,128)S(1)}, f32[128,128]{1,0:T(8,128)S(1)}, u32[]{:S(2)}, u32[]{:S(2)}) collective-permute-start(f32[128,128]{1,0:T(8,128)S(1)} %get-tuple-element.36), channel_id=1, source_target_pairs={{0,2},{2,0},{4,6},{6,4},{8,10},{10,8},{12,14},{14,12},{16,18},{18,... | collective-permute-start | bytes 196616 | tf_op jit(solution)/shard_map/ppermute | solution.py:229

commit v18 on v16

--- a/solution.py
+++ b/solution.py
@@ -16,7 +16,7 @@
 PHASE_BITS = 12
 LANES = 128
 PACKED = 16
-TILE = 256
+TILE = 128
 PAIRED = Layout(major_to_minor=(1, 0, 2))
 
 
@@ -128,35 +128,39 @@
         position = lax.broadcasted_iota(jnp.int32, (LOW // 8, 8, GATE), 0) * 8
         position = position + lax.broadcasted_iota(jnp.int32, (LOW // 8, 8, GATE), 1)
         kept = jnp.where((position & half_bit[layer][None]) == 0, 1.0, 0.0).reshape(LOW, GATE).astype(jnp.bfloat16)
-        for which in range(2):
-            for part in range(2):
-                piece = gate[layer, which, :, part * GATE : (part + 1) * GATE]
-                first = piece * kept
-                both = jnp.concatenate([first, piece - first], axis=1)
-                spread[which, part] = both
-                if part:
-                    spread[which, 2] = -both
-        factors = [[[spread[which, 0], spread[which, 2]], [spread[which, 1], spread[which, 0]]] for which in range(2)]
+        parts = [[gate[layer, which, :, part * GATE : (part + 1) * GATE] for part in range(2)] for which in range(2)]
+        total = parts[0][0].astype(jnp.float32) + parts[0][1].astype(jnp.float32)
+        total = total + (parts[1][0].astype(jnp.float32) + parts[1][1].astype(jnp.float32))
+        for which, piece in enumerate(split(total)):
+            for i, values in enumerate(parts[which] + [piece]):
+                first = values * kept
+                spread[which, i] = jnp.concatenate([first, values - first], axis=1)
 
         def load(lanes, top, offset):
             pieces = [turned(slot, layer, (top * half + m) * spect, rows_at_once, offset, lanes) for m in range(half)]
-            for part in range(2):
-                rows = exchange_modes([piece[part] for piece in pieces], span)
-                column = part * LOW + top * LANES
-                for g in range(0, half, joined):
-                    at = (lanes * half + g) * spect + offset
-                    high, low = split(jnp.concatenate(rows[g : g + joined], axis=0))
-                    left_high[at : at + PACKED, column : column + LANES] = high
-                    left_low[at : at + PACKED, column : column + LANES] = low
-
-        def multiply(first, part):
+            reals, imags = (exchange_modes([piece[part] for piece in pieces], span) for part in range(2))
+            for g in range(0, half, joined):
+                at = (lanes * half + g) * spect + offset
+                real = jnp.concatenate(reals[g : g + joined], axis=0)
+                imag = jnp.concatenate(imags[g : g + joined], axis=0)
+                for i, values in enumerate((real, imag, real + imag)):
+                    high, low = split(values)
+                    left_high[i, at : at + PACKED, top * LANES : (top + 1) * LANES] = high
+                    left_low[i, at : at + PACKED, top * LANES : (top + 1) * LANES] = low
+
+        def product(i, rows):
+            terms = jnp.concatenate([left_high[i, rows], left_low[i, rows], left_high[i, rows]], axis=1)
+            square = jnp.concatenate([spread[0, i], spread[0, i], spread[1, i]], axis=0)
+            return jnp.dot(terms, square, preferred_element_type=jnp.float32)
+
+        def multiply(first):
             rows = slice(first, first + tile)
-            terms = jnp.concatenate([left_high[rows], left_low[rows], left_high[rows]], axis=1)
-            square = jnp.concatenate(factors[0][part] + factors[0][part] + factors[1][part], axis=0)
-            state[1 - slot, part, rows] = jnp.dot(terms, square, preferred_element_type=jnp.float32)
+            real, imag = product(0, rows), product(1, rows)
+            state[1 - slot, 0, rows] = real - imag
+            state[1 - slot, 1, rows] = product(2, rows) - (real + imag)
 
         loads = [[(lanes, top, offset) for offset in range(0, spect, rows_at_once) for top in range(2)] for lanes in range(2)]
-        products = [(first, part) for first in range(0, count, tile) for part in range(2)]
+        products = [(first,) for first in range(0, count, tile)]
         middle = len(products) // 2
         for args in loads[0]:
             load(*args)
@@ -237,8 +241,8 @@
         out_shape=[piece] * wide,
         scratch_shapes=[
             pltpu.VMEM((2, 2, count, LOW), jnp.float32),
-            pltpu.VMEM((count, 2 * LOW), jnp.bfloat16),
-            pltpu.VMEM((count, 2 * LOW), jnp.bfloat16),
+            pltpu.VMEM((3, count, LOW), jnp.bfloat16),
+            pltpu.VMEM((3, count, LOW), jnp.bfloat16),
             pltpu.VMEM((2, 3, LOW, LOW), jnp.bfloat16),
         ],
         compiler_params=part_of_vmem,

time: 68.9 us -> 68.4 us (level)
  no operation moved by 1% of the time
where the time goes in v18:
time: 68.4 us; the launch traced here: 68.2 us
  starting transfers between devices  29.8 us (44%)
  waiting for transfers between devices  27.3 us (40%)
  Pallas kernels  10.9 us (16%)
    ppermute x15, starting transfers between devices, swap(): lax.ppermute(block, 'wide', [(i, i ^ k) for i in range(wide)])  22.3 us
    all_to_all x1, waiting for transfers between devices, local(): lax.all_to_all(rows, 'wide', split_axis=0, concat_axis=0, tiled=True)  20.2 us
    all_to_all x1, starting transfers between devices, local(): lax.all_to_all(rows, 'wide', split_axis=0, concat_axis=0, tiled=True)  7.53 us
    pallas_call x1, Pallas kernels, local(): pl.pallas_call(partial(layers_kernel, wide, spect), in_specs=[in_vmem] *...  7.2 us
    ppermute x15, waiting for transfers between devices, swap(): lax.ppermute(block, 'wide', [(i, i ^ k) for i in range(wide)])  7.12 us
    pallas_call x1, Pallas kernels, local(): pl.pallas_call(partial(phases_kernel, spect, narrow), in_specs=[in_smem,...  1.47 us
  transfers between devices with their start and end apart: 16, of which 8 were waited for; matrix products, arithmetic and copies ran while one was open for 0% of the time, Pallas kernels for 4%

profile of v18, /device:TPU:0, one launch (start us, length us, event | category | flops | bytes accessed | tf_op | source)
XLA Modules:
  0.0 68.2 jit_solution(2646037194058931531)
XLA Ops:
  0.0 7.5 %all-to-all-start = ((f32[16,128,128]{2,1,0:T(8,128)}), f32[16,128,128]{2,1,0:T(8,128)S(1)}, u32[]{:S(2)}, u32[]{:S(2)}) async-start(f32[16,128,128]{2,1,0:T(8,128)} %bitcast.14), calls=%async_computation | async-start | bytes 2097152 | tf_op jit(solution)/shard_map/all_to_all | solution.py:199
  7.6 0.0 copy-start.2
  7.6 0.0 copy-start.4
  7.6 1.2 %gates.1 = (bf16[6,2,256,256]{3,2,1,0:T(8,128)(2,1)S(1)}, s32[6,8,128]{2,1,0:T(8,128)S(1)}) custom-call(f32[6,128,128]{2,1,0:T(8,128)S(1)} %copy-done, f32[6,128,128]{2,1,0:T(8,128)S(1)} %copy-done.1, s32[6,8]{1,0:T(8,128)S(1)} %copy-done.3), custom_call_target="tpu_custom_call" | custom-call | flops 1000000000 | bytes 4000000 | tf_op jit(solution)/shard_map/gates/pallas_call | solution.py:209
  8.8 1.5 %phases.1.turn = f32[7,2,16,256]{3,2,1,0:T(8,128)S(1)} custom-call(s32[6,2,16]{2,1,0:T(2,128)S(1)} %bitcast.13, f32[6,16]{1,0:T(8,128)S(1)} %copy-done.4, s32[6,8,128]{2,1,0:T(8,128)S(1)} %get-tuple-element.24.half_ref.half_bit), custom_call_target="tpu_custom_call" | custom-call | flops 100000000 | bytes 1000000 | tf_op jit(solution)/shard_map/phases/pallas_call | solution.py:221
  10.3 20.2 %all-to-all-done = f32[16,128,128]{2,1,0:T(8,128)S(1)} async-done(((f32[16,128,128]{2,1,0:T(8,128)}), f32[16,128,128]{2,1,0:T(8,128)S(1)}, u32[]{:S(2)}, u32[]{:S(2)}) %all-to-all-start) | async-done | bytes 1048608 | tf_op jit(solution)/shard_map/all_to_all | solution.py:199
  30.5 7.2 %layers.1 = (f32[128,128]{1,0:T(8,128)S(1)}, f32[128,128]{1,0:T(8,128)S(1)}, f32[128,128]{1,0:T(8,128)S(1)}, f32[128,128]{1,0:T(8,128)S(1)}, f32[128,128]{1,0:T(...) custom-call(f32[2048,128]{1,0:T(8,128)S(1)} %bitcast.12, ...), custom_call_target="tpu_custom_call" | custom-call | flops 5000000000 | bytes 10000000 | tf_op jit(solution)/shard_map/layers/pallas_call | solution.py:237
  37.7 5.1 %collective-permute-start = (f32[128,128]{1,0:T(8,128)S(1)}, f32[128,128]{1,0:T(8,128)S(1)}, u32[]{:S(2)}, u32[]{:S(2)}) collective-permute-start(f32[128,128]{1,0:T(8,128)S(1)} %get-tuple-element.26), channel_id=1, source_target_pairs={{0,16},{2,18},{4,20},{6,22},{8,24},{10,26},{12,28},{14,30},{16,0},... | collective-permute-start | bytes 196616 | tf_op jit(solution)/shard_map/ppermute | solution.py:233
  42.8 0.0 collective-permute-start.1
  42.8 1.2 %collective-permute-start.2 = (f32[128,128]{1,0:T(8,128)S(1)}, f32[128,128]{1,0:T(8,128)S(1)}, u32[]{:S(2)}, u32[]{:S(2)}) collective-permute-start(f32[128,128]{1,0:T(8,128)S(1)} %get-tuple-element.28), channel_id=1, source_target_pairs={{0,8},{2,10},{4,12},{6,14},{8,0},{10,2},{12,4},{14,6},{16,24},{18,... | collective-permute-start | bytes 196616 | tf_op jit(solution)/shard_map/ppermute | solution.py:233
  44.0 0.4 collective-permute-start.3
  44.4 2.1 %collective-permute-start.4 = (f32[128,128]{1,0:T(8,128)S(1)}, f32[128,128]{1,0:T(8,128)S(1)}, u32[]{:S(2)}, u32[]{:S(2)}) collective-permute-start(f32[128,128]{1,0:T(8,128)S(1)} %get-tuple-element.30), channel_id=1, source_target_pairs={{0,20},{2,22},{4,16},{6,18},{8,28},{10,30},{12,24},{14,26},{16,4},... | collective-permute-start | bytes 196616 | tf_op jit(solution)/shard_map/ppermute | solution.py:233
  46.5 1.7 %collective-permute-done.rest_1_ = f32[128,128]{1,0:T(8,128)S(1)} collective-permute-done((f32[128,128]{1,0:T(8,128)S(1)}, f32[128,128]{1,0:T(8,128)S(1)}, u32[]{:S(2)}, u32[]{:S(2)}) %collective-permute-start) | collective-permute-done | bytes 65568 | tf_op jit(solution)/shard_map/ppermute | solution.py:233
  48.2 0.9 %collective-permute-done.1.rest_2_ = f32[128,128]{1,0:T(8,128)S(1)} collective-permute-done((f32[128,128]{1,0:T(8,128)S(1)}, f32[128,128]{1,0:T(8,128)S(1)}, u32[]{:S(2)}, u32[]{:S(2)}) %collective-permute-start.1) | collective-permute-done | bytes 65568 | tf_op jit(solution)/shard_map/ppermute | solution.py:233
  49.1 1.1 %collective-permute-start.6 = (f32[128,128]{1,0:T(8,128)S(1)}, f32[128,128]{1,0:T(8,128)S(1)}, u32[]{:S(2)}, u32[]{:S(2)}) collective-permute-start(f32[128,128]{1,0:T(8,128)S(1)} %get-tuple-element.32), channel_id=1, source_target_pairs={{0,12},{2,14},{4,8},{6,10},{8,4},{10,6},{12,0},{14,2},{16,28},{18,... | collective-permute-start | bytes 196616 | tf_op jit(solution)/shard_map/ppermute | solution.py:233
  50.2 0.0 collective-permute-done.2.rest_3_
  50.2 1.5 %collective-permute-start.7 = (f32[128,128]{1,0:T(8,128)S(1)}, f32[128,128]{1,0:T(8,128)S(1)}, u32[]{:S(2)}, u32[]{:S(2)}) collective-permute-start(f32[128,128]{1,0:T(8,128)S(1)} %get-tuple-element.33), channel_id=1, source_target_pairs={{0,14},{2,12},{4,10},{6,8},{8,6},{10,4},{12,2},{14,0},{16,30},{18,... | collective-permute-start | bytes 196616 | tf_op jit(solution)/shard_map/ppermute | solution.py:233
  51.7 0.0 collective-permute-done.3.rest_4_
  51.7 1.6 %collective-permute-start.8 = (f32[128,128]{1,0:T(8,128)S(1)}, f32[128,128]{1,0:T(8,128)S(1)}, u32[]{:S(2)}, u32[]{:S(2)}) collective-permute-start(f32[128,128]{1,0:T(8,128)S(1)} %get-tuple-element.34), channel_id=1, source_target_pairs={{0,24},{2,26},{4,28},{6,30},{8,16},{10,18},{12,20},{14,22},{16,8},... | collective-permute-start | bytes 196616 | tf_op jit(solution)/shard_map/ppermute | solution.py:233
  53.3 2.0 %collective-permute-start.9 = (f32[128,128]{1,0:T(8,128)S(1)}, f32[128,128]{1,0:T(8,128)S(1)}, u32[]{:S(2)}, u32[]{:S(2)}) collective-permute-start(f32[128,128]{1,0:T(8,128)S(1)} %get-tuple-element.35), channel_id=1, source_target_pairs={{0,26},{2,24},{4,30},{6,28},{8,18},{10,16},{12,22},{14,20},{16,10}... | collective-permute-start | bytes 196616 | tf_op jit(solution)/shard_map/ppermute | solution.py:233
  55.4 0.2 collective-permute-done.5.rest_6_
  55.5 3.4 %collective-permute-start.10 = (f32[128,128]{1,0:T(8,128)S(1)}, f32[128,128]{1,0:T(8,128)S(1)}, u32[]{:S(2)}, u32[]{:S(2)}) collective-permute-start(f32[128,128]{1,0:T(8,128)S(1)} %get-tuple-element.36), channel_id=1, source_target_pairs={{0,28},{2,30},{4,24},{6,26},{8,20},{10,22},{12,16},{14,18},{16,12}... | collective-permute-start | bytes 196616 | tf_op jit(solution)/shard_map/ppermute | solution.py:233
  58.9 0.0 collective-permute-done.6.rest_7_
  58.9 1.7 %collective-permute-start.11 = (f32[128,128]{1,0:T(8,128)S(1)}, f32[128,128]{1,0:T(8,128)S(1)}, u32[]{:S(2)}, u32[]{:S(2)}) collective-permute-start(f32[128,128]{1,0:T(8,128)S(1)} %get-tuple-element.37), channel_id=1, source_target_pairs={{0,30},{2,28},{4,26},{6,24},{8,22},{10,20},{12,18},{14,16},{16,14}... | collective-permute-start | bytes 196616 | tf_op jit(solution)/shard_map/ppermute | solution.py:233
  60.6 0.7 collective-permute-start.12
  61.3 0.4 collective-permute-start.13
  61.7 1.1 %collective-permute-start.14 = (f32[128,128]{1,0:T(8,128)S(1)}, f32[128,128]{1,0:T(8,128)S(1)}, u32[]{:S(2)}, u32[]{:S(2)}) collective-permute-start(f32[128,128]{1,0:T(8,128)S(1)} %get-tuple-element.40), channel_id=1, source_target_pairs={{0,2},{2,0},{4,6},{6,4},{8,10},{10,8},{12,14},{14,12},{16,18},{18,... | collective-permute-start | bytes 196616 | tf_op jit(solution)/shard_map/ppermute | solution.py:233
  62.8 0.3 collective-permute-done.10.rest_11_
  63.1 3.0 %collective-permute-done.11.rest_12_ = f32[128,128]{1,0:T(8,128)S(1)} collective-permute-done((f32[128,128]{1,0:T(8,128)S(1)}, f32[128,128]{1,0:T(8,128)S(1)}, u32[]{:S(2)}, u32[]{:S(2)}) %collective-permute-start.11) | collective-permute-done | bytes 65568 | tf_op jit(solution)/shard_map/ppermute | solution.py:233
  66.1 0.9 %collective-permute-done.12.rest_13_ = f32[128,128]{1,0:T(8,128)S(1)} collective-permute-done((f32[128,128]{1,0:T(8,128)S(1)}, f32[128,128]{1,0:T(8,128)S(1)}, u32[]{:S(2)}, u32[]{:S(2)}) %collective-permute-start.12) | collective-permute-done | bytes 65568 | tf_op jit(solution)/shard_map/ppermute | solution.py:233
  67.0 0.1 collective-permute-done.13.rest_14_
  67.1 1.1 %place.1 = f32[2048,128]{1,0:T(8,128)} custom-call(f32[128,128]{1,0:T(8,128)S(1)} %get-tuple-element.25.rest_0_, f32[128,128]{1,0:T(8,128)S(1)} %collective-permute-done.rest_1_, f32[128,128]{1,0:T(8,128)S(1)} %collective-permute-done.1.rest_2_, f32[128,128]{1,0:T(8,128)S(1)} %collective-permute-done.2.rest_3_, ...), custom_call_target="tpu_custom_call" | custom-call | tf_op jit(solution)/shard_map/place/pallas_call | solution.py:253
  (14 shorter events, 0.0 us)
Async XLA Ops:
  0.0 7.5 %copy-start.3 = (s32[6,8]{1,0:T(8,128)S(1)}, s32[6,8]{1,0:T(8,128)}, u32[]{:S(2)}) copy-start(s32[6,8]{1,0:T(8,128)} %order_ref.1) | copy-start | bytes 580
  0.0 7.6 %copy-start.1 = (f32[6,128,128]{2,1,0:T(8,128)S(1)}, f32[6,128,128]{2,1,0:T(8,128)}, u32[]{:S(2)}) copy-start(f32[6,128,128]{2,1,0:T(8,128)} %im_ref.1) | copy-start | bytes 1179652
  0.0 7.6 %copy-start = (f32[6,128,128]{2,1,0:T(8,128)S(1)}, f32[6,128,128]{2,1,0:T(8,128)}, u32[]{:S(2)}) copy-start(f32[6,128,128]{2,1,0:T(8,128)} %re_ref.1) | copy-start | bytes 1179652
  0.0 30.5 %all-to-all-start = ((f32[16,128,128]{2,1,0:T(8,128)}), f32[16,128,128]{2,1,0:T(8,128)S(1)}, u32[]{:S(2)}, u32[]{:S(2)}) async-start(f32[16,128,128]{2,1,0:T(8,128)} %bitcast.14), calls=%async_computation | async-start | bytes 2097152 | tf_op jit(solution)/shard_map/all_to_all | solution.py:199
  7.6 1.2 %copy-start.2 = (s32[6,16,2]{1,2,0:T(2,128)S(1)}, s32[6,16,2]{1,2,0:T(2,128)}, u32[]{:S(2)}) copy-start(s32[6,16,2]{1,2,0:T(2,128)} %param.10) | copy-start | bytes 2308
  7.6 1.2 %copy-start.4 = (f32[6,16]{1,0:T(8,128)S(1)}, f32[6,16]{1,0:T(8,128)}, u32[]{:S(2)}) copy-start(f32[6,16]{1,0:T(8,128)} %angle_ref.1) | copy-start | bytes 1156
  37.7 10.5 %collective-permute-start = (f32[128,128]{1,0:T(8,128)S(1)}, f32[128,128]{1,0:T(8,128)S(1)}, u32[]{:S(2)}, u32[]{:S(2)}) collective-permute-start(f32[128,128]{1,0:T(8,128)S(1)} %get-tuple-element.26), channel_id=1, source_target_pairs={{0,16},{2,18},{4,20},{6,22},{8,24},{10,26},{12,28},{14,30},{16,0},... | collective-permute-start | bytes 196616 | tf_op jit(solution)/shard_map/ppermute | solution.py:233
  42.8 6.3 %collective-permute-start.1 = (f32[128,128]{1,0:T(8,128)S(1)}, f32[128,128]{1,0:T(8,128)S(1)}, u32[]{:S(2)}, u32[]{:S(2)}) collective-permute-start(f32[128,128]{1,0:T(8,128)S(1)} %get-tuple-element.27), channel_id=1, source_target_pairs={{0,18},{2,16},{4,22},{6,20},{8,26},{10,24},{12,30},{14,28},{16,2},... | collective-permute-start | bytes 196616 | tf_op jit(solution)/shard_map/ppermute | solution.py:233
  42.8 7.4 %collective-permute-start.2 = (f32[128,128]{1,0:T(8,128)S(1)}, f32[128,128]{1,0:T(8,128)S(1)}, u32[]{:S(2)}, u32[]{:S(2)}) collective-permute-start(f32[128,128]{1,0:T(8,128)S(1)} %get-tuple-element.28), channel_id=1, source_target_pairs={{0,8},{2,10},{4,12},{6,14},{8,0},{10,2},{12,4},{14,6},{16,24},{18,... | collective-permute-start | bytes 196616 | tf_op jit(solution)/shard_map/ppermute | solution.py:233
  44.0 7.7 %collective-permute-start.3 = (f32[128,128]{1,0:T(8,128)S(1)}, f32[128,128]{1,0:T(8,128)S(1)}, u32[]{:S(2)}, u32[]{:S(2)}) collective-permute-start(f32[128,128]{1,0:T(8,128)S(1)} %get-tuple-element.29), channel_id=1, source_target_pairs={{0,10},{2,8},{4,14},{6,12},{8,2},{10,0},{12,6},{14,4},{16,26},{18,... | collective-permute-start | bytes 196616 | tf_op jit(solution)/shard_map/ppermute | solution.py:233
  44.4 8.9 %collective-permute-start.4 = (f32[128,128]{1,0:T(8,128)S(1)}, f32[128,128]{1,0:T(8,128)S(1)}, u32[]{:S(2)}, u32[]{:S(2)}) collective-permute-start(f32[128,128]{1,0:T(8,128)S(1)} %get-tuple-element.30), channel_id=1, source_target_pairs={{0,20},{2,22},{4,16},{6,18},{8,28},{10,30},{12,24},{14,26},{16,4},... | collective-permute-start | bytes 196616 | tf_op jit(solution)/shard_map/ppermute | solution.py:233
  48.2 7.3 %collective-permute-start.5 = (f32[128,128]{1,0:T(8,128)S(1)}, f32[128,128]{1,0:T(8,128)S(1)}, u32[]{:S(2)}, u32[]{:S(2)}) collective-permute-start(f32[128,128]{1,0:T(8,128)S(1)} %get-tuple-element.31), channel_id=1, source_target_pairs={{0,22},{2,20},{4,18},{6,16},{8,30},{10,28},{12,26},{14,24},{16,6},... | collective-permute-start | bytes 196616 | tf_op jit(solution)/shard_map/ppermute | solution.py:233
  49.1 9.8 %collective-permute-start.6 = (f32[128,128]{1,0:T(8,128)S(1)}, f32[128,128]{1,0:T(8,128)S(1)}, u32[]{:S(2)}, u32[]{:S(2)}) collective-permute-start(f32[128,128]{1,0:T(8,128)S(1)} %get-tuple-element.32), channel_id=1, source_target_pairs={{0,12},{2,14},{4,8},{6,10},{8,4},{10,6},{12,0},{14,2},{16,28},{18,... | collective-permute-start | bytes 196616 | tf_op jit(solution)/shard_map/ppermute | solution.py:233
  50.2 10.4 %collective-permute-start.7 = (f32[128,128]{1,0:T(8,128)S(1)}, f32[128,128]{1,0:T(8,128)S(1)}, u32[]{:S(2)}, u32[]{:S(2)}) collective-permute-start(f32[128,128]{1,0:T(8,128)S(1)} %get-tuple-element.33), channel_id=1, source_target_pairs={{0,14},{2,12},{4,10},{6,8},{8,6},{10,4},{12,2},{14,0},{16,30},{18,... | collective-permute-start | bytes 196616 | tf_op jit(solution)/shard_map/ppermute | solution.py:233
  51.7 9.6 %collective-permute-start.8 = (f32[128,128]{1,0:T(8,128)S(1)}, f32[128,128]{1,0:T(8,128)S(1)}, u32[]{:S(2)}, u32[]{:S(2)}) collective-permute-start(f32[128,128]{1,0:T(8,128)S(1)} %get-tuple-element.34), channel_id=1, source_target_pairs={{0,24},{2,26},{4,28},{6,30},{8,16},{10,18},{12,20},{14,22},{16,8},... | collective-permute-start | bytes 196616 | tf_op jit(solution)/shard_map/ppermute | solution.py:233
  53.3 8.4 %collective-permute-start.9 = (f32[128,128]{1,0:T(8,128)S(1)}, f32[128,128]{1,0:T(8,128)S(1)}, u32[]{:S(2)}, u32[]{:S(2)}) collective-permute-start(f32[128,128]{1,0:T(8,128)S(1)} %get-tuple-element.35), channel_id=1, source_target_pairs={{0,26},{2,24},{4,30},{6,28},{8,18},{10,16},{12,22},{14,20},{16,10}... | collective-permute-start | bytes 196616 | tf_op jit(solution)/shard_map/ppermute | solution.py:233
  55.5 7.6 %collective-permute-start.10 = (f32[128,128]{1,0:T(8,128)S(1)}, f32[128,128]{1,0:T(8,128)S(1)}, u32[]{:S(2)}, u32[]{:S(2)}) collective-permute-start(f32[128,128]{1,0:T(8,128)S(1)} %get-tuple-element.36), channel_id=1, source_target_pairs={{0,28},{2,30},{4,24},{6,26},{8,20},{10,22},{12,16},{14,18},{16,12}... | collective-permute-start | bytes 196616 | tf_op jit(solution)/shard_map/ppermute | solution.py:233
  58.9 7.1 %collective-permute-start.11 = (f32[128,128]{1,0:T(8,128)S(1)}, f32[128,128]{1,0:T(8,128)S(1)}, u32[]{:S(2)}, u32[]{:S(2)}) collective-permute-start(f32[128,128]{1,0:T(8,128)S(1)} %get-tuple-element.37), channel_id=1, source_target_pairs={{0,30},{2,28},{4,26},{6,24},{8,22},{10,20},{12,18},{14,16},{16,14}... | collective-permute-start | bytes 196616 | tf_op jit(solution)/shard_map/ppermute | solution.py:233
  60.6 6.3 %collective-permute-start.12 = (f32[128,128]{1,0:T(8,128)S(1)}, f32[128,128]{1,0:T(8,128)S(1)}, u32[]{:S(2)}, u32[]{:S(2)}) collective-permute-start(f32[128,128]{1,0:T(8,128)S(1)} %get-tuple-element.38), channel_id=1, source_target_pairs={{0,4},{2,6},{4,0},{6,2},{8,12},{10,14},{12,8},{14,10},{16,20},{18,... | collective-permute-start | bytes 196616 | tf_op jit(solution)/shard_map/ppermute | solution.py:233
  61.3 5.8 %collective-permute-start.13 = (f32[128,128]{1,0:T(8,128)S(1)}, f32[128,128]{1,0:T(8,128)S(1)}, u32[]{:S(2)}, u32[]{:S(2)}) collective-permute-start(f32[128,128]{1,0:T(8,128)S(1)} %get-tuple-element.39), channel_id=1, source_target_pairs={{0,6},{2,4},{4,2},{6,0},{8,14},{10,12},{12,10},{14,8},{16,22},{18,... | collective-permute-start | bytes 196616 | tf_op jit(solution)/shard_map/ppermute | solution.py:233
  61.7 5.4 %collective-permute-start.14 = (f32[128,128]{1,0:T(8,128)S(1)}, f32[128,128]{1,0:T(8,128)S(1)}, u32[]{:S(2)}, u32[]{:S(2)}) collective-permute-start(f32[128,128]{1,0:T(8,128)S(1)} %get-tuple-element.40), channel_id=1, source_target_pairs={{0,2},{2,0},{4,6},{6,4},{8,10},{10,8},{12,14},{14,12},{16,18},{18,... | collective-permute-start | bytes 196616 | tf_op jit(solution)/shard_map/ppermute | solution.py:233

commit v19 on v18

--- a/solution.py
+++ b/solution.py
@@ -28,12 +28,11 @@
 
 def exchange_order(wide):
     far = list(range(wide // 2, wide, 2))
-    near = [k for top in (wide // 4, wide // 8) for k in range(top, 2 * top, 2) if top > 1]
+    near = [k for low in (wide // 4, wide // 8) for k in range(low, 2 * low, 2) if low > 1]
     near += [k for k in range(wide // 2 - 2, 0, -2) if k not in near]
     pairs = []
     for i, k in enumerate(far):
-        pairs += [k] + near[i : i + 1] * (i < len(near) - 1)
-    pairs += near[-1:]
+        pairs += [k] + near[i : i + 1]
     return [0] + [k + j for k in pairs for j in range(2)] + [1]
 
 
@@ -80,15 +79,11 @@
         turn_ref[layer + 1, 1] = jnp.sin(phase)
 
 
-def exchange_modes(rows, span):
+def exchange_modes(rows, span, taken):
     count = len(rows)
-    group = lax.broadcasted_iota(jnp.int32, rows[0].shape, 1) // span
     rows = [pltpu.roll(row, m * span, 1) if m else row for m, row in enumerate(rows)]
-    step = 1
-    while step < count:
-        taken = (group & step) != 0
-        rows = [jnp.where(taken, rows[(y + step) % count], rows[y]) for y in range(count)]
-        step *= 2
+    for i, mask in enumerate(taken):
+        rows = [jnp.where(mask, rows[(y + (1 << i)) % count], rows[y]) for y in range(count)]
     return [pltpu.roll(rows[-r % count], LANES - r * span, 1) if r else rows[0] for r in range(count)]
 
 
@@ -118,11 +113,18 @@
     for part in range(2):
         for lanes in range(2):
             state[0, part, :, lanes * LANES : (lanes + 1) * LANES] = x[pl.ds(2 * lanes + part, count, stride=4), :]
-    def turned(slot, entry, first, size, offset, lanes):
-        rows, lanes = pl.ds(first + offset, size), slice(lanes * LANES, (lanes + 1) * LANES)
-        real, imag = state[slot, 0, rows, lanes], state[slot, 1, rows, lanes]
+    lane = lax.broadcasted_iota(jnp.int32, (rows_at_once, LANES), 1)
+    taken = [(lane & (span << i)) != 0 for i in range(half.bit_length() - 1)]
+
+    def turned(slot, entry, firsts, offset, lanes):
+        lanes = slice(lanes * LANES, (lanes + 1) * LANES)
         cosine, sine = turn[entry, 0, :, lanes], turn[entry, 1, :, lanes]
-        return real * cosine - imag * sine, real * sine + imag * cosine
+        pieces = []
+        for first in firsts:
+            rows = pl.ds(first + offset, rows_at_once)
+            real, imag = state[slot, 0, rows, lanes], state[slot, 1, rows, lanes]
+            pieces.append((real * cosine - imag * sine, real * sine + imag * cosine))
+        return pieces
 
     def one_layer(layer, slot):
         position = lax.broadcasted_iota(jnp.int32, (LOW // 8, 8, GATE), 0) * 8
@@ -137,8 +139,8 @@
                 spread[which, i] = jnp.concatenate([first, values - first], axis=1)
 
         def load(lanes, top, offset):
-            pieces = [turned(slot, layer, (top * half + m) * spect, rows_at_once, offset, lanes) for m in range(half)]
-            reals, imags = (exchange_modes([piece[part] for piece in pieces], span) for part in range(2))
+            pieces = turned(slot, layer, [(top * half + m) * spect for m in range(half)], offset, lanes)
+            reals, imags = (exchange_modes([piece[part] for piece in pieces], span, taken) for part in range(2))
             for g in range(0, half, joined):
                 at = (lanes * half + g) * spect + offset
                 real = jnp.concatenate(reals[g : g + joined], axis=0)
@@ -179,11 +181,11 @@
 
     lax.fori_loop(0, LAYERS // 2, two_layers, 0)
 
-    for i, k in enumerate(exchange_order(wide)):
-        first = pl.multiple_of((me ^ k) * spect, spect)
-        for offset in range(0, spect, rows_at_once):
-            for lanes in range(2):
-                for part, piece in enumerate(turned(0, LAYERS, first, rows_at_once, offset, lanes)):
+    firsts = [pl.multiple_of((me ^ k) * spect, spect) for k in exchange_order(wide)]
+    for offset in range(0, spect, rows_at_once):
+        for lanes in range(2):
+            for i, pieces in enumerate(turned(0, LAYERS, firsts, offset, lanes)):
+                for part, piece in enumerate(pieces):
                     outs[i][pl.ds(4 * offset + 2 * lanes + part, rows_at_once, stride=4), :] = piece
 
 

time: 68.4 us -> 69.2 us (1.012)
  waiting for transfers between devices: 27.3 us -> 28.1 us
    ppermute x15, waiting for transfers between devices: 7.12 us -> 7.89 us  [swap(): lax.ppermute(block, 'wide', [(i, i ^ k) for i in range(wide)])]
  transfers between devices with their start and end apart: 16 -> 16, of which waited for: 8 -> 6; matrix products, arithmetic and copies ran while one was open for 0% -> 0% of each run, Pallas kernels for 4% -> 4%
where the time goes in v19:
time: 69.2 us; the launch traced here: 69 us
  starting transfers between devices  29.8 us (43%)
  waiting for transfers between devices  28.1 us (41%)
  Pallas kernels  11 us (16%)
    ppermute x15, starting transfers between devices, swap(): lax.ppermute(block, 'wide', [(i, i ^ k) for i in range(wide)])  22.3 us
    all_to_all x1, waiting for transfers between devices, local(): lax.all_to_all(rows, 'wide', split_axis=0, concat_axis=0, tiled=True)  20.2 us
    ppermute x15, waiting for transfers between devices, swap(): lax.ppermute(block, 'wide', [(i, i ^ k) for i in range(wide)])  7.89 us
    all_to_all x1, starting transfers between devices, local(): lax.all_to_all(rows, 'wide', split_axis=0, concat_axis=0, tiled=True)  7.53 us
    pallas_call x1, Pallas kernels, local(): pl.pallas_call(partial(layers_kernel, wide, spect), in_specs=[in_vmem] *...  7.22 us
    pallas_call x1, Pallas kernels, local(): pl.pallas_call(partial(phases_kernel, spect, narrow), in_specs=[in_smem,...  1.47 us
  transfers between devices with their start and end apart: 16, of which 6 were waited for; matrix products, arithmetic and copies ran while one was open for 0% of the time, Pallas kernels for 4%

profile of v19, /device:TPU:0, one launch (start us, length us, event | category | flops | bytes accessed | tf_op | source)
XLA Modules:
  0.0 69.0 jit_solution(14775826602874851009)
XLA Ops:
  0.0 7.5 %all-to-all-start = ((f32[16,128,128]{2,1,0:T(8,128)}), f32[16,128,128]{2,1,0:T(8,128)S(1)}, u32[]{:S(2)}, u32[]{:S(2)}) async-start(f32[16,128,128]{2,1,0:T(8,128)} %bitcast.14), calls=%async_computation | async-start | bytes 2097152 | tf_op jit(solution)/shard_map/all_to_all | solution.py:201
  7.6 0.0 copy-start.2
  7.6 0.0 copy-start.4
  7.6 1.2 %gates.1 = (bf16[6,2,256,256]{3,2,1,0:T(8,128)(2,1)S(1)}, s32[6,8,128]{2,1,0:T(8,128)S(1)}) custom-call(f32[6,128,128]{2,1,0:T(8,128)S(1)} %copy-done, f32[6,128,128]{2,1,0:T(8,128)S(1)} %copy-done.1, s32[6,8]{1,0:T(8,128)S(1)} %copy-done.3), custom_call_target="tpu_custom_call" | custom-call | flops 1000000000 | bytes 4000000 | tf_op jit(solution)/shard_map/gates/pallas_call | solution.py:211
  8.8 1.5 %phases.1.turn = f32[7,2,16,256]{3,2,1,0:T(8,128)S(1)} custom-call(s32[6,2,16]{2,1,0:T(2,128)S(1)} %bitcast.13, f32[6,16]{1,0:T(8,128)S(1)} %copy-done.4, s32[6,8,128]{2,1,0:T(8,128)S(1)} %get-tuple-element.24.half_ref.half_bit), custom_call_target="tpu_custom_call" | custom-call | flops 100000000 | bytes 1000000 | tf_op jit(solution)/shard_map/phases/pallas_call | solution.py:223
  10.3 20.2 %all-to-all-done = f32[16,128,128]{2,1,0:T(8,128)S(1)} async-done(((f32[16,128,128]{2,1,0:T(8,128)}), f32[16,128,128]{2,1,0:T(8,128)S(1)}, u32[]{:S(2)}, u32[]{:S(2)}) %all-to-all-start) | async-done | bytes 1048608 | tf_op jit(solution)/shard_map/all_to_all | solution.py:201
  30.5 7.2 %layers.1 = (f32[128,128]{1,0:T(8,128)S(1)}, f32[128,128]{1,0:T(8,128)S(1)}, f32[128,128]{1,0:T(8,128)S(1)}, f32[128,128]{1,0:T(8,128)S(1)}, f32[128,128]{1,0:T(...) custom-call(f32[2048,128]{1,0:T(8,128)S(1)} %bitcast.12, ...), custom_call_target="tpu_custom_call" | custom-call | flops 5000000000 | bytes 10000000 | tf_op jit(solution)/shard_map/layers/pallas_call | solution.py:239
  37.7 5.1 %collective-permute-start = (f32[128,128]{1,0:T(8,128)S(1)}, f32[128,128]{1,0:T(8,128)S(1)}, u32[]{:S(2)}, u32[]{:S(2)}) collective-permute-start(f32[128,128]{1,0:T(8,128)S(1)} %get-tuple-element.26), channel_id=1, source_target_pairs={{0,16},{2,18},{4,20},{6,22},{8,24},{10,26},{12,28},{14,30},{16,0},... | collective-permute-start | bytes 196616 | tf_op jit(solution)/shard_map/ppermute | solution.py:235
  42.8 0.0 collective-permute-start.1
  42.8 1.2 %collective-permute-start.2 = (f32[128,128]{1,0:T(8,128)S(1)}, f32[128,128]{1,0:T(8,128)S(1)}, u32[]{:S(2)}, u32[]{:S(2)}) collective-permute-start(f32[128,128]{1,0:T(8,128)S(1)} %get-tuple-element.28), channel_id=1, source_target_pairs={{0,8},{2,10},{4,12},{6,14},{8,0},{10,2},{12,4},{14,6},{16,24},{18,... | collective-permute-start | bytes 196616 | tf_op jit(solution)/shard_map/ppermute | solution.py:235
  44.0 0.4 collective-permute-start.3
  44.4 2.1 %collective-permute-start.4 = (f32[128,128]{1,0:T(8,128)S(1)}, f32[128,128]{1,0:T(8,128)S(1)}, u32[]{:S(2)}, u32[]{:S(2)}) collective-permute-start(f32[128,128]{1,0:T(8,128)S(1)} %get-tuple-element.30), channel_id=1, source_target_pairs={{0,20},{2,22},{4,16},{6,18},{8,28},{10,30},{12,24},{14,26},{16,4},... | collective-permute-start | bytes 196616 | tf_op jit(solution)/shard_map/ppermute | solution.py:235
  46.5 1.7 %collective-permute-done.rest_1_ = f32[128,128]{1,0:T(8,128)S(1)} collective-permute-done((f32[128,128]{1,0:T(8,128)S(1)}, f32[128,128]{1,0:T(8,128)S(1)}, u32[]{:S(2)}, u32[]{:S(2)}) %collective-permute-start) | collective-permute-done | bytes 65568 | tf_op jit(solution)/shard_map/ppermute | solution.py:235
  48.2 0.9 %collective-permute-done.1.rest_2_ = f32[128,128]{1,0:T(8,128)S(1)} collective-permute-done((f32[128,128]{1,0:T(8,128)S(1)}, f32[128,128]{1,0:T(8,128)S(1)}, u32[]{:S(2)}, u32[]{:S(2)}) %collective-permute-start.1) | collective-permute-done | bytes 65568 | tf_op jit(solution)/shard_map/ppermute | solution.py:235
  49.2 1.1 %collective-permute-start.6 = (f32[128,128]{1,0:T(8,128)S(1)}, f32[128,128]{1,0:T(8,128)S(1)}, u32[]{:S(2)}, u32[]{:S(2)}) collective-permute-start(f32[128,128]{1,0:T(8,128)S(1)} %get-tuple-element.32), channel_id=1, source_target_pairs={{0,12},{2,14},{4,8},{6,10},{8,4},{10,6},{12,0},{14,2},{16,28},{18,... | collective-permute-start | bytes 196616 | tf_op jit(solution)/shard_map/ppermute | solution.py:235
  50.2 1.5 %collective-permute-start.7 = (f32[128,128]{1,0:T(8,128)S(1)}, f32[128,128]{1,0:T(8,128)S(1)}, u32[]{:S(2)}, u32[]{:S(2)}) collective-permute-start(f32[128,128]{1,0:T(8,128)S(1)} %get-tuple-element.33), channel_id=1, source_target_pairs={{0,14},{2,12},{4,10},{6,8},{8,6},{10,4},{12,2},{14,0},{16,30},{18,... | collective-permute-start | bytes 196616 | tf_op jit(solution)/shard_map/ppermute | solution.py:235
  51.7 0.0 collective-permute-done.3.rest_4_
  51.7 1.6 %collective-permute-start.8 = (f32[128,128]{1,0:T(8,128)S(1)}, f32[128,128]{1,0:T(8,128)S(1)}, u32[]{:S(2)}, u32[]{:S(2)}) collective-permute-start(f32[128,128]{1,0:T(8,128)S(1)} %get-tuple-element.34), channel_id=1, source_target_pairs={{0,24},{2,26},{4,28},{6,30},{8,16},{10,18},{12,20},{14,22},{16,8},... | collective-permute-start | bytes 196616 | tf_op jit(solution)/shard_map/ppermute | solution.py:235
  53.3 2.0 %collective-permute-start.9 = (f32[128,128]{1,0:T(8,128)S(1)}, f32[128,128]{1,0:T(8,128)S(1)}, u32[]{:S(2)}, u32[]{:S(2)}) collective-permute-start(f32[128,128]{1,0:T(8,128)S(1)} %get-tuple-element.35), channel_id=1, source_target_pairs={{0,26},{2,24},{4,30},{6,28},{8,18},{10,16},{12,22},{14,20},{16,10}... | collective-permute-start | bytes 196616 | tf_op jit(solution)/shard_map/ppermute | solution.py:235
  55.4 0.2 collective-permute-done.5.rest_6_
  55.5 0.9 %collective-permute-start.10 = (f32[128,128]{1,0:T(8,128)S(1)}, f32[128,128]{1,0:T(8,128)S(1)}, u32[]{:S(2)}, u32[]{:S(2)}) collective-permute-start(f32[128,128]{1,0:T(8,128)S(1)} %get-tuple-element.36), channel_id=1, source_target_pairs={{0,4},{2,6},{4,0},{6,2},{8,12},{10,14},{12,8},{14,10},{16,20},{18,... | collective-permute-start | bytes 196616 | tf_op jit(solution)/shard_map/ppermute | solution.py:235
  56.5 0.0 collective-permute-done.6.rest_7_
  56.5 1.5 %collective-permute-start.11 = (f32[128,128]{1,0:T(8,128)S(1)}, f32[128,128]{1,0:T(8,128)S(1)}, u32[]{:S(2)}, u32[]{:S(2)}) collective-permute-start(f32[128,128]{1,0:T(8,128)S(1)} %get-tuple-element.37), channel_id=1, source_target_pairs={{0,6},{2,4},{4,2},{6,0},{8,14},{10,12},{12,10},{14,8},{16,22},{18,... | collective-permute-start | bytes 196616 | tf_op jit(solution)/shard_map/ppermute | solution.py:235
  58.0 3.1 %collective-permute-start.12 = (f32[128,128]{1,0:T(8,128)S(1)}, f32[128,128]{1,0:T(8,128)S(1)}, u32[]{:S(2)}, u32[]{:S(2)}) collective-permute-start(f32[128,128]{1,0:T(8,128)S(1)} %get-tuple-element.38), channel_id=1, source_target_pairs={{0,28},{2,30},{4,24},{6,26},{8,20},{10,22},{12,16},{14,18},{16,12}... | collective-permute-start | bytes 196616 | tf_op jit(solution)/shard_map/ppermute | solution.py:235
  61.0 0.0 collective-permute-done.8.rest_9_
  61.0 0.7 %collective-permute-start.13 = (f32[128,128]{1,0:T(8,128)S(1)}, f32[128,128]{1,0:T(8,128)S(1)}, u32[]{:S(2)}, u32[]{:S(2)}) collective-permute-start(f32[128,128]{1,0:T(8,128)S(1)} %get-tuple-element.39), channel_id=1, source_target_pairs={{0,30},{2,28},{4,26},{6,24},{8,22},{10,20},{12,18},{14,16},{16,14}... | collective-permute-start | bytes 196616 | tf_op jit(solution)/shard_map/ppermute | solution.py:235
  61.7 0.0 collective-permute-done.9.rest_10_
  61.7 1.1 %collective-permute-start.14 = (f32[128,128]{1,0:T(8,128)S(1)}, f32[128,128]{1,0:T(8,128)S(1)}, u32[]{:S(2)}, u32[]{:S(2)}) collective-permute-start(f32[128,128]{1,0:T(8,128)S(1)} %get-tuple-element.40), channel_id=1, source_target_pairs={{0,2},{2,0},{4,6},{6,4},{8,10},{10,8},{12,14},{14,12},{16,18},{18,... | collective-permute-start | bytes 196616 | tf_op jit(solution)/shard_map/ppermute | solution.py:235
  62.8 0.0 collective-permute-done.10.rest_11_
  62.8 2.2 %collective-permute-done.12.rest_13_ = f32[128,128]{1,0:T(8,128)S(1)} collective-permute-done((f32[128,128]{1,0:T(8,128)S(1)}, f32[128,128]{1,0:T(8,128)S(1)}, u32[]{:S(2)}, u32[]{:S(2)}) %collective-permute-start.12) | collective-permute-done | bytes 65568 | tf_op jit(solution)/shard_map/ppermute | solution.py:235
  65.0 2.8 %collective-permute-done.13.rest_14_ = f32[128,128]{1,0:T(8,128)S(1)} collective-permute-done((f32[128,128]{1,0:T(8,128)S(1)}, f32[128,128]{1,0:T(8,128)S(1)}, u32[]{:S(2)}, u32[]{:S(2)}) %collective-permute-start.13) | collective-permute-done | bytes 65568 | tf_op jit(solution)/shard_map/ppermute | solution.py:235
  67.9 1.1 %place.1 = f32[2048,128]{1,0:T(8,128)} custom-call(f32[128,128]{1,0:T(8,128)S(1)} %get-tuple-element.25.rest_0_, f32[128,128]{1,0:T(8,128)S(1)} %collective-permute-done.rest_1_, f32[128,128]{1,0:T(8,128)S(1)} %collective-permute-done.1.rest_2_, f32[128,128]{1,0:T(8,128)S(1)} %collective-permute-done.2.rest_3_, ...), custom_call_target="tpu_custom_call" | custom-call | tf_op jit(solution)/shard_map/place/pallas_call | solution.py:255
  (14 shorter events, 0.0 us)
Async XLA Ops:
  0.0 7.5 %copy-start.3 = (s32[6,8]{1,0:T(8,128)S(1)}, s32[6,8]{1,0:T(8,128)}, u32[]{:S(2)}) copy-start(s32[6,8]{1,0:T(8,128)} %order_ref.1) | copy-start | bytes 580
  0.0 7.6 %copy-start.1 = (f32[6,128,128]{2,1,0:T(8,128)S(1)}, f32[6,128,128]{2,1,0:T(8,128)}, u32[]{:S(2)}) copy-start(f32[6,128,128]{2,1,0:T(8,128)} %im_ref.1) | copy-start | bytes 1179652
  0.0 7.6 %copy-start = (f32[6,128,128]{2,1,0:T(8,128)S(1)}, f32[6,128,128]{2,1,0:T(8,128)}, u32[]{:S(2)}) copy-start(f32[6,128,128]{2,1,0:T(8,128)} %re_ref.1) | copy-start | bytes 1179652
  0.0 30.5 %all-to-all-start = ((f32[16,128,128]{2,1,0:T(8,128)}), f32[16,128,128]{2,1,0:T(8,128)S(1)}, u32[]{:S(2)}, u32[]{:S(2)}) async-start(f32[16,128,128]{2,1,0:T(8,128)} %bitcast.14), calls=%async_computation | async-start | bytes 2097152 | tf_op jit(solution)/shard_map/all_to_all | solution.py:201
  7.6 1.2 %copy-start.2 = (s32[6,16,2]{1,2,0:T(2,128)S(1)}, s32[6,16,2]{1,2,0:T(2,128)}, u32[]{:S(2)}) copy-start(s32[6,16,2]{1,2,0:T(2,128)} %param.10) | copy-start | bytes 2308
  7.6 1.2 %copy-start.4 = (f32[6,16]{1,0:T(8,128)S(1)}, f32[6,16]{1,0:T(8,128)}, u32[]{:S(2)}) copy-start(f32[6,16]{1,0:T(8,128)} %angle_ref.1) | copy-start | bytes 1156
  37.7 10.5 %collective-permute-start = (f32[128,128]{1,0:T(8,128)S(1)}, f32[128,128]{1,0:T(8,128)S(1)}, u32[]{:S(2)}, u32[]{:S(2)}) collective-permute-start(f32[128,128]{1,0:T(8,128)S(1)} %get-tuple-element.26), channel_id=1, source_target_pairs={{0,16},{2,18},{4,20},{6,22},{8,24},{10,26},{12,28},{14,30},{16,0},... | collective-permute-start | bytes 196616 | tf_op jit(solution)/shard_map/ppermute | solution.py:235
  42.8 6.3 %collective-permute-start.1 = (f32[128,128]{1,0:T(8,128)S(1)}, f32[128,128]{1,0:T(8,128)S(1)}, u32[]{:S(2)}, u32[]{:S(2)}) collective-permute-start(f32[128,128]{1,0:T(8,128)S(1)} %get-tuple-element.27), channel_id=1, source_target_pairs={{0,18},{2,16},{4,22},{6,20},{8,26},{10,24},{12,30},{14,28},{16,2},... | collective-permute-start | bytes 196616 | tf_op jit(solution)/shard_map/ppermute | solution.py:235
  42.8 7.4 %collective-permute-start.2 = (f32[128,128]{1,0:T(8,128)S(1)}, f32[128,128]{1,0:T(8,128)S(1)}, u32[]{:S(2)}, u32[]{:S(2)}) collective-permute-start(f32[128,128]{1,0:T(8,128)S(1)} %get-tuple-element.28), channel_id=1, source_target_pairs={{0,8},{2,10},{4,12},{6,14},{8,0},{10,2},{12,4},{14,6},{16,24},{18,... | collective-permute-start | bytes 196616 | tf_op jit(solution)/shard_map/ppermute | solution.py:235
  44.0 7.7 %collective-permute-start.3 = (f32[128,128]{1,0:T(8,128)S(1)}, f32[128,128]{1,0:T(8,128)S(1)}, u32[]{:S(2)}, u32[]{:S(2)}) collective-permute-start(f32[128,128]{1,0:T(8,128)S(1)} %get-tuple-element.29), channel_id=1, source_target_pairs={{0,10},{2,8},{4,14},{6,12},{8,2},{10,0},{12,6},{14,4},{16,26},{18,... | collective-permute-start | bytes 196616 | tf_op jit(solution)/shard_map/ppermute | solution.py:235
  44.4 8.9 %collective-permute-start.4 = (f32[128,128]{1,0:T(8,128)S(1)}, f32[128,128]{1,0:T(8,128)S(1)}, u32[]{:S(2)}, u32[]{:S(2)}) collective-permute-start(f32[128,128]{1,0:T(8,128)S(1)} %get-tuple-element.30), channel_id=1, source_target_pairs={{0,20},{2,22},{4,16},{6,18},{8,28},{10,30},{12,24},{14,26},{16,4},... | collective-permute-start | bytes 196616 | tf_op jit(solution)/shard_map/ppermute | solution.py:235
  48.2 7.3 %collective-permute-start.5 = (f32[128,128]{1,0:T(8,128)S(1)}, f32[128,128]{1,0:T(8,128)S(1)}, u32[]{:S(2)}, u32[]{:S(2)}) collective-permute-start(f32[128,128]{1,0:T(8,128)S(1)} %get-tuple-element.31), channel_id=1, source_target_pairs={{0,22},{2,20},{4,18},{6,16},{8,30},{10,28},{12,26},{14,24},{16,6},... | collective-permute-start | bytes 196616 | tf_op jit(solution)/shard_map/ppermute | solution.py:235
  49.2 7.3 %collective-permute-start.6 = (f32[128,128]{1,0:T(8,128)S(1)}, f32[128,128]{1,0:T(8,128)S(1)}, u32[]{:S(2)}, u32[]{:S(2)}) collective-permute-start(f32[128,128]{1,0:T(8,128)S(1)} %get-tuple-element.32), channel_id=1, source_target_pairs={{0,12},{2,14},{4,8},{6,10},{8,4},{10,6},{12,0},{14,2},{16,28},{18,... | collective-permute-start | bytes 196616 | tf_op jit(solution)/shard_map/ppermute | solution.py:235
  50.2 7.7 %collective-permute-start.7 = (f32[128,128]{1,0:T(8,128)S(1)}, f32[128,128]{1,0:T(8,128)S(1)}, u32[]{:S(2)}, u32[]{:S(2)}) collective-permute-start(f32[128,128]{1,0:T(8,128)S(1)} %get-tuple-element.33), channel_id=1, source_target_pairs={{0,14},{2,12},{4,10},{6,8},{8,6},{10,4},{12,2},{14,0},{16,30},{18,... | collective-permute-start | bytes 196616 | tf_op jit(solution)/shard_map/ppermute | solution.py:235
  51.7 9.3 %collective-permute-start.8 = (f32[128,128]{1,0:T(8,128)S(1)}, f32[128,128]{1,0:T(8,128)S(1)}, u32[]{:S(2)}, u32[]{:S(2)}) collective-permute-start(f32[128,128]{1,0:T(8,128)S(1)} %get-tuple-element.34), channel_id=1, source_target_pairs={{0,24},{2,26},{4,28},{6,30},{8,16},{10,18},{12,20},{14,22},{16,8},... | collective-permute-start | bytes 196616 | tf_op jit(solution)/shard_map/ppermute | solution.py:235
  53.3 8.4 %collective-permute-start.9 = (f32[128,128]{1,0:T(8,128)S(1)}, f32[128,128]{1,0:T(8,128)S(1)}, u32[]{:S(2)}, u32[]{:S(2)}) collective-permute-start(f32[128,128]{1,0:T(8,128)S(1)} %get-tuple-element.35), channel_id=1, source_target_pairs={{0,26},{2,24},{4,30},{6,28},{8,18},{10,16},{12,22},{14,20},{16,10}... | collective-permute-start | bytes 196616 | tf_op jit(solution)/shard_map/ppermute | solution.py:235
  55.5 7.3 %collective-permute-start.10 = (f32[128,128]{1,0:T(8,128)S(1)}, f32[128,128]{1,0:T(8,128)S(1)}, u32[]{:S(2)}, u32[]{:S(2)}) collective-permute-start(f32[128,128]{1,0:T(8,128)S(1)} %get-tuple-element.36), channel_id=1, source_target_pairs={{0,4},{2,6},{4,0},{6,2},{8,12},{10,14},{12,8},{14,10},{16,20},{18,... | collective-permute-start | bytes 196616 | tf_op jit(solution)/shard_map/ppermute | solution.py:235
  56.5 6.3 %collective-permute-start.11 = (f32[128,128]{1,0:T(8,128)S(1)}, f32[128,128]{1,0:T(8,128)S(1)}, u32[]{:S(2)}, u32[]{:S(2)}) collective-permute-start(f32[128,128]{1,0:T(8,128)S(1)} %get-tuple-element.37), channel_id=1, source_target_pairs={{0,6},{2,4},{4,2},{6,0},{8,14},{10,12},{12,10},{14,8},{16,22},{18,... | collective-permute-start | bytes 196616 | tf_op jit(solution)/shard_map/ppermute | solution.py:235
  58.0 7.1 %collective-permute-start.12 = (f32[128,128]{1,0:T(8,128)S(1)}, f32[128,128]{1,0:T(8,128)S(1)}, u32[]{:S(2)}, u32[]{:S(2)}) collective-permute-start(f32[128,128]{1,0:T(8,128)S(1)} %get-tuple-element.38), channel_id=1, source_target_pairs={{0,28},{2,30},{4,24},{6,26},{8,20},{10,22},{12,16},{14,18},{16,12}... | collective-permute-start | bytes 196616 | tf_op jit(solution)/shard_map/ppermute | solution.py:235
  61.0 6.8 %collective-permute-start.13 = (f32[128,128]{1,0:T(8,128)S(1)}, f32[128,128]{1,0:T(8,128)S(1)}, u32[]{:S(2)}, u32[]{:S(2)}) collective-permute-start(f32[128,128]{1,0:T(8,128)S(1)} %get-tuple-element.39), channel_id=1, source_target_pairs={{0,30},{2,28},{4,26},{6,24},{8,22},{10,20},{12,18},{14,16},{16,14}... | collective-permute-start | bytes 196616 | tf_op jit(solution)/shard_map/ppermute | solution.py:235
  61.7 6.1 %collective-permute-start.14 = (f32[128,128]{1,0:T(8,128)S(1)}, f32[128,128]{1,0:T(8,128)S(1)}, u32[]{:S(2)}, u32[]{:S(2)}) collective-permute-start(f32[128,128]{1,0:T(8,128)S(1)} %get-tuple-element.40), channel_id=1, source_target_pairs={{0,2},{2,0},{4,6},{6,4},{8,10},{10,8},{12,14},{14,12},{16,18},{18,... | collective-permute-start | bytes 196616 | tf_op jit(solution)/shard_map/ppermute | solution.py:235

commit v20 on v19

--- a/solution.py
+++ b/solution.py
@@ -28,11 +28,12 @@
 
 def exchange_order(wide):
     far = list(range(wide // 2, wide, 2))
-    near = [k for low in (wide // 4, wide // 8) for k in range(low, 2 * low, 2) if low > 1]
+    near = [k for top in (wide // 4, wide // 8) for k in range(top, 2 * top, 2) if top > 1]
     near += [k for k in range(wide // 2 - 2, 0, -2) if k not in near]
     pairs = []
     for i, k in enumerate(far):
-        pairs += [k] + near[i : i + 1]
+        pairs += [k] + near[i : i + 1] * (i < len(near) - 1)
+    pairs += near[-1:]
     return [0] + [k + j for k in pairs for j in range(2)] + [1]
 
 
@@ -174,12 +175,11 @@
         for args in products[middle:]:
             multiply(*args)
 
-    def two_layers(step, carry):
-        one_layer(2 * step, 0)
-        one_layer(2 * step + 1, 1)
+    def step(layer, carry):
+        one_layer(layer, layer & 1)
         return carry
 
-    lax.fori_loop(0, LAYERS // 2, two_layers, 0)
+    lax.fori_loop(0, LAYERS, step, 0)
 
     firsts = [pl.multiple_of((me ^ k) * spect, spect) for k in exchange_order(wide)]
     for offset in range(0, spect, rows_at_once):

time: 69.2 us -> 70.5 us (1.019)
  Pallas kernels: 11 us -> 13 us
    pallas_call x1, Pallas kernels: 7.22 us -> 9.28 us  [local(): pl.pallas_call(partial(layers_kernel, wide, spect), in_specs=[in_vmem] *...]
    ppermute x15, waiting for transfers between devices: 7.89 us -> 7.16 us  [swap(): lax.ppermute(block, 'wide', [(i, i ^ k) for i in range(wide)])]
  transfers between devices with their start and end apart: 16 -> 16, of which waited for: 6 -> 8; matrix products, arithmetic and copies ran while one was open for 0% -> 0% of each run, Pallas kernels for 4% -> 4%
where the time goes in v20:
time: 70.5 us; the launch traced here: 70.3 us
  starting transfers between devices  29.8 us (42%)
  waiting for transfers between devices  27.4 us (39%)
  Pallas kernels  13 us (18%)
    ppermute x15, starting transfers between devices, swap(): lax.ppermute(block, 'wide', [(i, i ^ k) for i in range(wide)])  22.2 us
    all_to_all x1, waiting for transfers between devices, local(): lax.all_to_all(rows, 'wide', split_axis=0, concat_axis=0, tiled=True)  20.2 us
    pallas_call x1, Pallas kernels, local(): pl.pallas_call(partial(layers_kernel, wide, spect), in_specs=[in_vmem] *...  9.28 us
    all_to_all x1, starting transfers between devices, local(): lax.all_to_all(rows, 'wide', split_axis=0, concat_axis=0, tiled=True)  7.53 us
    ppermute x15, waiting for transfers between devices, swap(): lax.ppermute(block, 'wide', [(i, i ^ k) for i in range(wide)])  7.16 us
    pallas_call x1, Pallas kernels, local(): pl.pallas_call(partial(phases_kernel, spect, narrow), in_specs=[in_smem,...  1.47 us
  transfers between devices with their start and end apart: 16, of which 8 were waited for; matrix products, arithmetic and copies ran while one was open for 0% of the time, Pallas kernels for 4%

profile of v20, /device:TPU:0, one launch (start us, length us, event | category | flops | bytes accessed | tf_op | source)
XLA Modules:
  0.0 70.3 jit_solution(2583035743610953854)
XLA Ops:
  0.0 7.5 %all-to-all-start = ((f32[16,128,128]{2,1,0:T(8,128)}), f32[16,128,128]{2,1,0:T(8,128)S(1)}, u32[]{:S(2)}, u32[]{:S(2)}) async-start(f32[16,128,128]{2,1,0:T(8,128)} %bitcast.14), calls=%async_computation | async-start | bytes 2097152 | tf_op jit(solution)/shard_map/all_to_all | solution.py:201
  7.6 0.0 copy-start.2
  7.6 0.0 copy-start.4
  7.6 1.2 %gates.1 = (bf16[6,2,256,256]{3,2,1,0:T(8,128)(2,1)S(1)}, s32[6,8,128]{2,1,0:T(8,128)S(1)}) custom-call(f32[6,128,128]{2,1,0:T(8,128)S(1)} %copy-done, f32[6,128,128]{2,1,0:T(8,128)S(1)} %copy-done.1, s32[6,8]{1,0:T(8,128)S(1)} %copy-done.3), custom_call_target="tpu_custom_call" | custom-call | flops 1000000000 | bytes 4000000 | tf_op jit(solution)/shard_map/gates/pallas_call | solution.py:211
  8.8 1.5 %phases.1.turn = f32[7,2,16,256]{3,2,1,0:T(8,128)S(1)} custom-call(s32[6,2,16]{2,1,0:T(2,128)S(1)} %bitcast.13, f32[6,16]{1,0:T(8,128)S(1)} %copy-done.4, s32[6,8,128]{2,1,0:T(8,128)S(1)} %get-tuple-element.24.half_ref.half_bit), custom_call_target="tpu_custom_call" | custom-call | flops 100000000 | bytes 1000000 | tf_op jit(solution)/shard_map/phases/pallas_call | solution.py:223
  10.3 20.2 %all-to-all-done = f32[16,128,128]{2,1,0:T(8,128)S(1)} async-done(((f32[16,128,128]{2,1,0:T(8,128)}), f32[16,128,128]{2,1,0:T(8,128)S(1)}, u32[]{:S(2)}, u32[]{:S(2)}) %all-to-all-start) | async-done | bytes 1048608 | tf_op jit(solution)/shard_map/all_to_all | solution.py:201
  30.5 9.3 %layers.1 = (f32[128,128]{1,0:T(8,128)S(1)}, f32[128,128]{1,0:T(8,128)S(1)}, f32[128,128]{1,0:T(8,128)S(1)}, f32[128,128]{1,0:T(8,128)S(1)}, f32[128,128]{1,0:T(...) custom-call(f32[2048,128]{1,0:T(8,128)S(1)} %bitcast.12, ...), custom_call_target="tpu_custom_call" | custom-call | flops 5000000000 | bytes 10000000 | tf_op jit(solution)/shard_map/layers/pallas_call | solution.py:239
  39.8 5.1 %collective-permute-start = (f32[128,128]{1,0:T(8,128)S(1)}, f32[128,128]{1,0:T(8,128)S(1)}, u32[]{:S(2)}, u32[]{:S(2)}) collective-permute-start(f32[128,128]{1,0:T(8,128)S(1)} %get-tuple-element.26), channel_id=1, source_target_pairs={{0,16},{2,18},{4,20},{6,22},{8,24},{10,26},{12,28},{14,30},{16,0},... | collective-permute-start | bytes 196616 | tf_op jit(solution)/shard_map/ppermute | solution.py:235
  44.9 1.2 %collective-permute-start.2 = (f32[128,128]{1,0:T(8,128)S(1)}, f32[128,128]{1,0:T(8,128)S(1)}, u32[]{:S(2)}, u32[]{:S(2)}) collective-permute-start(f32[128,128]{1,0:T(8,128)S(1)} %get-tuple-element.28), channel_id=1, source_target_pairs={{0,8},{2,10},{4,12},{6,14},{8,0},{10,2},{12,4},{14,6},{16,24},{18,... | collective-permute-start | bytes 196616 | tf_op jit(solution)/shard_map/ppermute | solution.py:235
  46.1 0.4 collective-permute-start.3
  46.4 2.1 %collective-permute-start.4 = (f32[128,128]{1,0:T(8,128)S(1)}, f32[128,128]{1,0:T(8,128)S(1)}, u32[]{:S(2)}, u32[]{:S(2)}) collective-permute-start(f32[128,128]{1,0:T(8,128)S(1)} %get-tuple-element.30), channel_id=1, source_target_pairs={{0,20},{2,22},{4,16},{6,18},{8,28},{10,30},{12,24},{14,26},{16,4},... | collective-permute-start | bytes 196616 | tf_op jit(solution)/shard_map/ppermute | solution.py:235
  48.6 1.7 %collective-permute-done.rest_1_ = f32[128,128]{1,0:T(8,128)S(1)} collective-permute-done((f32[128,128]{1,0:T(8,128)S(1)}, f32[128,128]{1,0:T(8,128)S(1)}, u32[]{:S(2)}, u32[]{:S(2)}) %collective-permute-start) | collective-permute-done | bytes 65568 | tf_op jit(solution)/shard_map/ppermute | solution.py:235
  50.3 0.0 collective-permute-start.5
  50.3 1.0 %collective-permute-done.1.rest_2_ = f32[128,128]{1,0:T(8,128)S(1)} collective-permute-done((f32[128,128]{1,0:T(8,128)S(1)}, f32[128,128]{1,0:T(8,128)S(1)}, u32[]{:S(2)}, u32[]{:S(2)}) %collective-permute-start.1) | collective-permute-done | bytes 65568 | tf_op jit(solution)/shard_map/ppermute | solution.py:235
  51.2 1.1 %collective-permute-start.6 = (f32[128,128]{1,0:T(8,128)S(1)}, f32[128,128]{1,0:T(8,128)S(1)}, u32[]{:S(2)}, u32[]{:S(2)}) collective-permute-start(f32[128,128]{1,0:T(8,128)S(1)} %get-tuple-element.32), channel_id=1, source_target_pairs={{0,12},{2,14},{4,8},{6,10},{8,4},{10,6},{12,0},{14,2},{16,28},{18,... | collective-permute-start | bytes 196616 | tf_op jit(solution)/shard_map/ppermute | solution.py:235
  52.3 1.5 %collective-permute-start.7 = (f32[128,128]{1,0:T(8,128)S(1)}, f32[128,128]{1,0:T(8,128)S(1)}, u32[]{:S(2)}, u32[]{:S(2)}) collective-permute-start(f32[128,128]{1,0:T(8,128)S(1)} %get-tuple-element.33), channel_id=1, source_target_pairs={{0,14},{2,12},{4,10},{6,8},{8,6},{10,4},{12,2},{14,0},{16,30},{18,... | collective-permute-start | bytes 196616 | tf_op jit(solution)/shard_map/ppermute | solution.py:235
  53.8 1.6 %collective-permute-start.8 = (f32[128,128]{1,0:T(8,128)S(1)}, f32[128,128]{1,0:T(8,128)S(1)}, u32[]{:S(2)}, u32[]{:S(2)}) collective-permute-start(f32[128,128]{1,0:T(8,128)S(1)} %get-tuple-element.34), channel_id=1, source_target_pairs={{0,24},{2,26},{4,28},{6,30},{8,16},{10,18},{12,20},{14,22},{16,8},... | collective-permute-start | bytes 196616 | tf_op jit(solution)/shard_map/ppermute | solution.py:235
  55.4 2.0 %collective-permute-start.9 = (f32[128,128]{1,0:T(8,128)S(1)}, f32[128,128]{1,0:T(8,128)S(1)}, u32[]{:S(2)}, u32[]{:S(2)}) collective-permute-start(f32[128,128]{1,0:T(8,128)S(1)} %get-tuple-element.35), channel_id=1, source_target_pairs={{0,26},{2,24},{4,30},{6,28},{8,18},{10,16},{12,22},{14,20},{16,10}... | collective-permute-start | bytes 196616 | tf_op jit(solution)/shard_map/ppermute | solution.py:235
  57.4 0.2 collective-permute-done.5.rest_6_
  57.6 3.4 %collective-permute-start.10 = (f32[128,128]{1,0:T(8,128)S(1)}, f32[128,128]{1,0:T(8,128)S(1)}, u32[]{:S(2)}, u32[]{:S(2)}) collective-permute-start(f32[128,128]{1,0:T(8,128)S(1)} %get-tuple-element.36), channel_id=1, source_target_pairs={{0,28},{2,30},{4,24},{6,26},{8,20},{10,22},{12,16},{14,18},{16,12}... | collective-permute-start | bytes 196616 | tf_op jit(solution)/shard_map/ppermute | solution.py:235
  61.0 0.0 collective-permute-done.6.rest_7_
  61.0 1.7 %collective-permute-start.11 = (f32[128,128]{1,0:T(8,128)S(1)}, f32[128,128]{1,0:T(8,128)S(1)}, u32[]{:S(2)}, u32[]{:S(2)}) collective-permute-start(f32[128,128]{1,0:T(8,128)S(1)} %get-tuple-element.37), channel_id=1, source_target_pairs={{0,30},{2,28},{4,26},{6,24},{8,22},{10,20},{12,18},{14,16},{16,14}... | collective-permute-start | bytes 196616 | tf_op jit(solution)/shard_map/ppermute | solution.py:235
  62.7 0.7 collective-permute-start.12
  63.4 0.0 collective-permute-done.8.rest_9_
  63.4 0.4 collective-permute-start.13
  63.8 1.0 %collective-permute-start.14 = (f32[128,128]{1,0:T(8,128)S(1)}, f32[128,128]{1,0:T(8,128)S(1)}, u32[]{:S(2)}, u32[]{:S(2)}) collective-permute-start(f32[128,128]{1,0:T(8,128)S(1)} %get-tuple-element.40), channel_id=1, source_target_pairs={{0,2},{2,0},{4,6},{6,4},{8,10},{10,8},{12,14},{14,12},{16,18},{18,... | collective-permute-start | bytes 196616 | tf_op jit(solution)/shard_map/ppermute | solution.py:235
  64.9 0.3 collective-permute-done.10.rest_11_
  65.2 2.9 %collective-permute-done.11.rest_12_ = f32[128,128]{1,0:T(8,128)S(1)} collective-permute-done((f32[128,128]{1,0:T(8,128)S(1)}, f32[128,128]{1,0:T(8,128)S(1)}, u32[]{:S(2)}, u32[]{:S(2)}) %collective-permute-start.11) | collective-permute-done | bytes 65568 | tf_op jit(solution)/shard_map/ppermute | solution.py:235
  68.1 0.9 %collective-permute-done.12.rest_13_ = f32[128,128]{1,0:T(8,128)S(1)} collective-permute-done((f32[128,128]{1,0:T(8,128)S(1)}, f32[128,128]{1,0:T(8,128)S(1)}, u32[]{:S(2)}, u32[]{:S(2)}) %collective-permute-start.12) | collective-permute-done | bytes 65568 | tf_op jit(solution)/shard_map/ppermute | solution.py:235
  69.0 0.2 collective-permute-done.13.rest_14_
  69.2 0.0 collective-permute-done.14.rest_15_
  69.2 1.1 %place.1 = f32[2048,128]{1,0:T(8,128)} custom-call(f32[128,128]{1,0:T(8,128)S(1)} %get-tuple-element.25.rest_0_, f32[128,128]{1,0:T(8,128)S(1)} %collective-permute-done.rest_1_, f32[128,128]{1,0:T(8,128)S(1)} %collective-permute-done.1.rest_2_, f32[128,128]{1,0:T(8,128)S(1)} %collective-permute-done.2.rest_3_, ...), custom_call_target="tpu_custom_call" | custom-call | tf_op jit(solution)/shard_map/place/pallas_call | solution.py:255
  (14 shorter events, 0.0 us)
Async XLA Ops:
  0.0 7.5 %copy-start.3 = (s32[6,8]{1,0:T(8,128)S(1)}, s32[6,8]{1,0:T(8,128)}, u32[]{:S(2)}) copy-start(s32[6,8]{1,0:T(8,128)} %order_ref.1) | copy-start | bytes 580
  0.0 7.6 %copy-start.1 = (f32[6,128,128]{2,1,0:T(8,128)S(1)}, f32[6,128,128]{2,1,0:T(8,128)}, u32[]{:S(2)}) copy-start(f32[6,128,128]{2,1,0:T(8,128)} %im_ref.1) | copy-start | bytes 1179652
  0.0 7.6 %copy-start = (f32[6,128,128]{2,1,0:T(8,128)S(1)}, f32[6,128,128]{2,1,0:T(8,128)}, u32[]{:S(2)}) copy-start(f32[6,128,128]{2,1,0:T(8,128)} %re_ref.1) | copy-start | bytes 1179652
  0.0 30.5 %all-to-all-start = ((f32[16,128,128]{2,1,0:T(8,128)}), f32[16,128,128]{2,1,0:T(8,128)S(1)}, u32[]{:S(2)}, u32[]{:S(2)}) async-start(f32[16,128,128]{2,1,0:T(8,128)} %bitcast.14), calls=%async_computation | async-start | bytes 2097152 | tf_op jit(solution)/shard_map/all_to_all | solution.py:201
  7.6 1.2 %copy-start.2 = (s32[6,16,2]{1,2,0:T(2,128)S(1)}, s32[6,16,2]{1,2,0:T(2,128)}, u32[]{:S(2)}) copy-start(s32[6,16,2]{1,2,0:T(2,128)} %param.10) | copy-start | bytes 2308
  7.6 1.2 %copy-start.4 = (f32[6,16]{1,0:T(8,128)S(1)}, f32[6,16]{1,0:T(8,128)}, u32[]{:S(2)}) copy-start(f32[6,16]{1,0:T(8,128)} %angle_ref.1) | copy-start | bytes 1156
  39.8 10.5 %collective-permute-start = (f32[128,128]{1,0:T(8,128)S(1)}, f32[128,128]{1,0:T(8,128)S(1)}, u32[]{:S(2)}, u32[]{:S(2)}) collective-permute-start(f32[128,128]{1,0:T(8,128)S(1)} %get-tuple-element.26), channel_id=1, source_target_pairs={{0,16},{2,18},{4,20},{6,22},{8,24},{10,26},{12,28},{14,30},{16,0},... | collective-permute-start | bytes 196616 | tf_op jit(solution)/shard_map/ppermute | solution.py:235
  44.9 6.3 %collective-permute-start.1 = (f32[128,128]{1,0:T(8,128)S(1)}, f32[128,128]{1,0:T(8,128)S(1)}, u32[]{:S(2)}, u32[]{:S(2)}) collective-permute-start(f32[128,128]{1,0:T(8,128)S(1)} %get-tuple-element.27), channel_id=1, source_target_pairs={{0,18},{2,16},{4,22},{6,20},{8,26},{10,24},{12,30},{14,28},{16,2},... | collective-permute-start | bytes 196616 | tf_op jit(solution)/shard_map/ppermute | solution.py:235
  44.9 7.4 %collective-permute-start.2 = (f32[128,128]{1,0:T(8,128)S(1)}, f32[128,128]{1,0:T(8,128)S(1)}, u32[]{:S(2)}, u32[]{:S(2)}) collective-permute-start(f32[128,128]{1,0:T(8,128)S(1)} %get-tuple-element.28), channel_id=1, source_target_pairs={{0,8},{2,10},{4,12},{6,14},{8,0},{10,2},{12,4},{14,6},{16,24},{18,... | collective-permute-start | bytes 196616 | tf_op jit(solution)/shard_map/ppermute | solution.py:235
  46.1 7.7 %collective-permute-start.3 = (f32[128,128]{1,0:T(8,128)S(1)}, f32[128,128]{1,0:T(8,128)S(1)}, u32[]{:S(2)}, u32[]{:S(2)}) collective-permute-start(f32[128,128]{1,0:T(8,128)S(1)} %get-tuple-element.29), channel_id=1, source_target_pairs={{0,10},{2,8},{4,14},{6,12},{8,2},{10,0},{12,6},{14,4},{16,26},{18,... | collective-permute-start | bytes 196616 | tf_op jit(solution)/shard_map/ppermute | solution.py:235
  46.4 8.9 %collective-permute-start.4 = (f32[128,128]{1,0:T(8,128)S(1)}, f32[128,128]{1,0:T(8,128)S(1)}, u32[]{:S(2)}, u32[]{:S(2)}) collective-permute-start(f32[128,128]{1,0:T(8,128)S(1)} %get-tuple-element.30), channel_id=1, source_target_pairs={{0,20},{2,22},{4,16},{6,18},{8,28},{10,30},{12,24},{14,26},{16,4},... | collective-permute-start | bytes 196616 | tf_op jit(solution)/shard_map/ppermute | solution.py:235
  50.3 7.3 %collective-permute-start.5 = (f32[128,128]{1,0:T(8,128)S(1)}, f32[128,128]{1,0:T(8,128)S(1)}, u32[]{:S(2)}, u32[]{:S(2)}) collective-permute-start(f32[128,128]{1,0:T(8,128)S(1)} %get-tuple-element.31), channel_id=1, source_target_pairs={{0,22},{2,20},{4,18},{6,16},{8,30},{10,28},{12,26},{14,24},{16,6},... | collective-permute-start | bytes 196616 | tf_op jit(solution)/shard_map/ppermute | solution.py:235
  51.2 9.8 %collective-permute-start.6 = (f32[128,128]{1,0:T(8,128)S(1)}, f32[128,128]{1,0:T(8,128)S(1)}, u32[]{:S(2)}, u32[]{:S(2)}) collective-permute-start(f32[128,128]{1,0:T(8,128)S(1)} %get-tuple-element.32), channel_id=1, source_target_pairs={{0,12},{2,14},{4,8},{6,10},{8,4},{10,6},{12,0},{14,2},{16,28},{18,... | collective-permute-start | bytes 196616 | tf_op jit(solution)/shard_map/ppermute | solution.py:235
  52.3 10.4 %collective-permute-start.7 = (f32[128,128]{1,0:T(8,128)S(1)}, f32[128,128]{1,0:T(8,128)S(1)}, u32[]{:S(2)}, u32[]{:S(2)}) collective-permute-start(f32[128,128]{1,0:T(8,128)S(1)} %get-tuple-element.33), channel_id=1, source_target_pairs={{0,14},{2,12},{4,10},{6,8},{8,6},{10,4},{12,2},{14,0},{16,30},{18,... | collective-permute-start | bytes 196616 | tf_op jit(solution)/shard_map/ppermute | solution.py:235
  53.8 9.6 %collective-permute-start.8 = (f32[128,128]{1,0:T(8,128)S(1)}, f32[128,128]{1,0:T(8,128)S(1)}, u32[]{:S(2)}, u32[]{:S(2)}) collective-permute-start(f32[128,128]{1,0:T(8,128)S(1)} %get-tuple-element.34), channel_id=1, source_target_pairs={{0,24},{2,26},{4,28},{6,30},{8,16},{10,18},{12,20},{14,22},{16,8},... | collective-permute-start | bytes 196616 | tf_op jit(solution)/shard_map/ppermute | solution.py:235
  55.4 8.4 %collective-permute-start.9 = (f32[128,128]{1,0:T(8,128)S(1)}, f32[128,128]{1,0:T(8,128)S(1)}, u32[]{:S(2)}, u32[]{:S(2)}) collective-permute-start(f32[128,128]{1,0:T(8,128)S(1)} %get-tuple-element.35), channel_id=1, source_target_pairs={{0,26},{2,24},{4,30},{6,28},{8,18},{10,16},{12,22},{14,20},{16,10}... | collective-permute-start | bytes 196616 | tf_op jit(solution)/shard_map/ppermute | solution.py:235
  57.6 7.6 %collective-permute-start.10 = (f32[128,128]{1,0:T(8,128)S(1)}, f32[128,128]{1,0:T(8,128)S(1)}, u32[]{:S(2)}, u32[]{:S(2)}) collective-permute-start(f32[128,128]{1,0:T(8,128)S(1)} %get-tuple-element.36), channel_id=1, source_target_pairs={{0,28},{2,30},{4,24},{6,26},{8,20},{10,22},{12,16},{14,18},{16,12}... | collective-permute-start | bytes 196616 | tf_op jit(solution)/shard_map/ppermute | solution.py:235
  61.0 7.1 %collective-permute-start.11 = (f32[128,128]{1,0:T(8,128)S(1)}, f32[128,128]{1,0:T(8,128)S(1)}, u32[]{:S(2)}, u32[]{:S(2)}) collective-permute-start(f32[128,128]{1,0:T(8,128)S(1)} %get-tuple-element.37), channel_id=1, source_target_pairs={{0,30},{2,28},{4,26},{6,24},{8,22},{10,20},{12,18},{14,16},{16,14}... | collective-permute-start | bytes 196616 | tf_op jit(solution)/shard_map/ppermute | solution.py:235
  62.7 6.3 %collective-permute-start.12 = (f32[128,128]{1,0:T(8,128)S(1)}, f32[128,128]{1,0:T(8,128)S(1)}, u32[]{:S(2)}, u32[]{:S(2)}) collective-permute-start(f32[128,128]{1,0:T(8,128)S(1)} %get-tuple-element.38), channel_id=1, source_target_pairs={{0,4},{2,6},{4,0},{6,2},{8,12},{10,14},{12,8},{14,10},{16,20},{18,... | collective-permute-start | bytes 196616 | tf_op jit(solution)/shard_map/ppermute | solution.py:235
  63.4 5.8 %collective-permute-start.13 = (f32[128,128]{1,0:T(8,128)S(1)}, f32[128,128]{1,0:T(8,128)S(1)}, u32[]{:S(2)}, u32[]{:S(2)}) collective-permute-start(f32[128,128]{1,0:T(8,128)S(1)} %get-tuple-element.39), channel_id=1, source_target_pairs={{0,6},{2,4},{4,2},{6,0},{8,14},{10,12},{12,10},{14,8},{16,22},{18,... | collective-permute-start | bytes 196616 | tf_op jit(solution)/shard_map/ppermute | solution.py:235
  63.8 5.4 %collective-permute-start.14 = (f32[128,128]{1,0:T(8,128)S(1)}, f32[128,128]{1,0:T(8,128)S(1)}, u32[]{:S(2)}, u32[]{:S(2)}) collective-permute-start(f32[128,128]{1,0:T(8,128)S(1)} %get-tuple-element.40), channel_id=1, source_target_pairs={{0,2},{2,0},{4,6},{6,4},{8,10},{10,8},{12,14},{14,12},{16,18},{18,... | collective-permute-start | bytes 196616 | tf_op jit(solution)/shard_map/ppermute | solution.py:235

commit v21 on v20

--- a/solution.py
+++ b/solution.py
@@ -127,9 +127,10 @@
             pieces.append((real * cosine - imag * sine, real * sine + imag * cosine))
         return pieces
 
-    def one_layer(layer, slot):
-        position = lax.broadcasted_iota(jnp.int32, (LOW // 8, 8, GATE), 0) * 8
-        position = position + lax.broadcasted_iota(jnp.int32, (LOW // 8, 8, GATE), 1)
+    position = lax.broadcasted_iota(jnp.int32, (LOW // 8, 8, GATE), 0) * 8
+    position = position + lax.broadcasted_iota(jnp.int32, (LOW // 8, 8, GATE), 1)
+
+    def prepare(layer):
         kept = jnp.where((position & half_bit[layer][None]) == 0, 1.0, 0.0).reshape(LOW, GATE).astype(jnp.bfloat16)
         parts = [[gate[layer, which, :, part * GATE : (part + 1) * GATE] for part in range(2)] for which in range(2)]
         total = parts[0][0].astype(jnp.float32) + parts[0][1].astype(jnp.float32)
@@ -137,49 +138,53 @@
         for which, piece in enumerate(split(total)):
             for i, values in enumerate(parts[which] + [piece]):
                 first = values * kept
-                spread[which, i] = jnp.concatenate([first, values - first], axis=1)
-
-        def load(lanes, top, offset):
-            pieces = turned(slot, layer, [(top * half + m) * spect for m in range(half)], offset, lanes)
-            reals, imags = (exchange_modes([piece[part] for piece in pieces], span, taken) for part in range(2))
-            for g in range(0, half, joined):
-                at = (lanes * half + g) * spect + offset
-                real = jnp.concatenate(reals[g : g + joined], axis=0)
-                imag = jnp.concatenate(imags[g : g + joined], axis=0)
-                for i, values in enumerate((real, imag, real + imag)):
-                    high, low = split(values)
-                    left_high[i, at : at + PACKED, top * LANES : (top + 1) * LANES] = high
-                    left_low[i, at : at + PACKED, top * LANES : (top + 1) * LANES] = low
-
-        def product(i, rows):
-            terms = jnp.concatenate([left_high[i, rows], left_low[i, rows], left_high[i, rows]], axis=1)
-            square = jnp.concatenate([spread[0, i], spread[0, i], spread[1, i]], axis=0)
-            return jnp.dot(terms, square, preferred_element_type=jnp.float32)
-
-        def multiply(first):
-            rows = slice(first, first + tile)
-            real, imag = product(0, rows), product(1, rows)
-            state[1 - slot, 0, rows] = real - imag
-            state[1 - slot, 1, rows] = product(2, rows) - (real + imag)
-
-        loads = [[(lanes, top, offset) for offset in range(0, spect, rows_at_once) for top in range(2)] for lanes in range(2)]
-        products = [(first,) for first in range(0, count, tile)]
-        middle = len(products) // 2
-        for args in loads[0]:
-            load(*args)
-        for i in range(max(middle, len(loads[1]))):
-            if i < middle:
-                multiply(*products[i])
-            if i < len(loads[1]):
-                load(*loads[1][i])
-        for args in products[middle:]:
+                spread[layer % 2, which, i] = jnp.concatenate([first, values - first], axis=1)
+
+    def load(layer, lanes, top, offset):
+        slot = layer % 2
+        pieces = turned(slot, layer, [(top * half + m) * spect for m in range(half)], offset, lanes)
+        reals, imags = (exchange_modes([piece[part] for piece in pieces], span, taken) for part in range(2))
+        for g in range(0, half, joined):
+            at = (lanes * half + g) * spect + offset
+            real = jnp.concatenate(reals[g : g + joined], axis=0)
+            imag = jnp.concatenate(imags[g : g + joined], axis=0)
+            for i, values in enumerate((real, imag, real + imag)):
+                high, low = split(values)
+                left_high[slot, i, at : at + PACKED, top * LANES : (top + 1) * LANES] = high
+                left_low[slot, i, at : at + PACKED, top * LANES : (top + 1) * LANES] = low
+
+    def product(layer, i, rows):
+        slot = layer % 2
+        high, low = left_high[slot, i, rows], left_low[slot, i, rows]
+        square = jnp.concatenate([spread[slot, 0, i], spread[slot, 0, i], spread[slot, 1, i]], axis=0)
+        return jnp.dot(jnp.concatenate([high, low, high], axis=1), square, preferred_element_type=jnp.float32)
+
+    def multiply(layer, first):
+        rows = slice(first, first + tile)
+        real, imag = product(layer, 0, rows), product(layer, 1, rows)
+        state[1 - layer % 2, 0, rows] = real - imag
+        state[1 - layer % 2, 1, rows] = product(layer, 2, rows) - (real + imag)
+
+    def in_turn(products, loads):
+        for i, args in enumerate(products):
             multiply(*args)
-
-    def step(layer, carry):
-        one_layer(layer, layer & 1)
-        return carry
-
-    lax.fori_loop(0, LAYERS, step, 0)
+            for more in loads[i * len(loads) // len(products) : (i + 1) * len(loads) // len(products)]:
+                load(*more)
+
+    offsets = range(0, spect, rows_at_once)
+    tiles = range(0, count, tile)
+    prepare(0)
+    for args in [(0, lanes, 0, offset) for lanes in range(2) for offset in offsets]:
+        load(*args)
+    for layer in range(LAYERS):
+        for offset in offsets:
+            load(layer, 0, 1, offset)
+        in_turn([(layer, first) for first in tiles if first < count // 2], [(layer, 1, 1, offset) for offset in offsets])
+        ahead = []
+        if layer + 1 < LAYERS:
+            prepare(layer + 1)
+            ahead = [(layer + 1, lanes, 0, offset) for lanes in range(2) for offset in offsets]
+        in_turn([(layer, first) for first in tiles if first >= count // 2], ahead)
 
     firsts = [pl.multiple_of((me ^ k) * spect, spect) for k in exchange_order(wide)]
     for offset in range(0, spect, rows_at_once):
@@ -243,9 +248,9 @@
         out_shape=[piece] * wide,
         scratch_shapes=[
             pltpu.VMEM((2, 2, count, LOW), jnp.float32),
-            pltpu.VMEM((3, count, LOW), jnp.bfloat16),
-            pltpu.VMEM((3, count, LOW), jnp.bfloat16),
-            pltpu.VMEM((2, 3, LOW, LOW), jnp.bfloat16),
+            pltpu.VMEM((2, 3, count, LOW), jnp.bfloat16),
+            pltpu.VMEM((2, 3, count, LOW), jnp.bfloat16),
+            pltpu.VMEM((2, 2, 3, LOW, LOW), jnp.bfloat16),
         ],
         compiler_params=part_of_vmem,
         cost_estimate=pl.CostEstimate(flops=5 * 10**9, bytes_accessed=10**7, transcendentals=0),

time: 70.5 us -> 68.1 us (0.966)
  Pallas kernels: 13 us -> 10.6 us
    pallas_call x1, Pallas kernels: 9.28 us -> 6.85 us  [local(): pl.pallas_call(partial(layers_kernel, wide, spect), in_specs=[in_vmem] *...]
where the time goes in v21:
time: 68.1 us; the launch traced here: 67.8 us
  starting transfers between devices  29.8 us (44%)
  waiting for transfers between devices  27.3 us (40%)
  Pallas kernels  10.6 us (16%)
    ppermute x15, starting transfers between devices, swap(): lax.ppermute(block, 'wide', [(i, i ^ k) for i in range(wide)])  22.3 us
    all_to_all x1, waiting for transfers between devices, local(): lax.all_to_all(rows, 'wide', split_axis=0, concat_axis=0, tiled=True)  20.2 us
    all_to_all x1, starting transfers between devices, local(): lax.all_to_all(rows, 'wide', split_axis=0, concat_axis=0, tiled=True)  7.53 us
    ppermute x15, waiting for transfers between devices, swap(): lax.ppermute(block, 'wide', [(i, i ^ k) for i in range(wide)])  7.12 us
    pallas_call x1, Pallas kernels, local(): pl.pallas_call(partial(layers_kernel, wide, spect), in_specs=[in_vmem] *...  6.85 us
    pallas_call x1, Pallas kernels, local(): pl.pallas_call(partial(phases_kernel, spect, narrow), in_specs=[in_smem,...  1.47 us
  transfers between devices with their start and end apart: 16, of which 8 were waited for; matrix products, arithmetic and copies ran while one was open for 0% of the time, Pallas kernels for 4%

profile of v21, /device:TPU:0, one launch (start us, length us, event | category | flops | bytes accessed | tf_op | source)
XLA Modules:
  0.0 67.8 jit_solution(10396316015821115622)
XLA Ops:
  0.0 7.5 %all-to-all-start = ((f32[16,128,128]{2,1,0:T(8,128)}), f32[16,128,128]{2,1,0:T(8,128)S(1)}, u32[]{:S(2)}, u32[]{:S(2)}) async-start(f32[16,128,128]{2,1,0:T(8,128)} %bitcast.14), calls=%async_computation | async-start | bytes 2097152 | tf_op jit(solution)/shard_map/all_to_all | solution.py:206
  7.6 0.0 copy-start.2
  7.6 0.0 copy-start.4
  7.6 1.2 %gates.1 = (bf16[6,2,256,256]{3,2,1,0:T(8,128)(2,1)S(1)}, s32[6,8,128]{2,1,0:T(8,128)S(1)}) custom-call(f32[6,128,128]{2,1,0:T(8,128)S(1)} %copy-done, f32[6,128,128]{2,1,0:T(8,128)S(1)} %copy-done.1, s32[6,8]{1,0:T(8,128)S(1)} %copy-done.3), custom_call_target="tpu_custom_call" | custom-call | flops 1000000000 | bytes 4000000 | tf_op jit(solution)/shard_map/gates/pallas_call | solution.py:216
  8.8 1.5 %phases.1.turn = f32[7,2,16,256]{3,2,1,0:T(8,128)S(1)} custom-call(s32[6,2,16]{2,1,0:T(2,128)S(1)} %bitcast.13, f32[6,16]{1,0:T(8,128)S(1)} %copy-done.4, s32[6,8,128]{2,1,0:T(8,128)S(1)} %get-tuple-element.24.half_ref.half_bit), custom_call_target="tpu_custom_call" | custom-call | flops 100000000 | bytes 1000000 | tf_op jit(solution)/shard_map/phases/pallas_call | solution.py:228
  10.3 20.2 %all-to-all-done = f32[16,128,128]{2,1,0:T(8,128)S(1)} async-done(((f32[16,128,128]{2,1,0:T(8,128)}), f32[16,128,128]{2,1,0:T(8,128)S(1)}, u32[]{:S(2)}, u32[]{:S(2)}) %all-to-all-start) | async-done | bytes 1048608 | tf_op jit(solution)/shard_map/all_to_all | solution.py:206
  30.5 6.8 %layers.1 = (f32[128,128]{1,0:T(8,128)S(1)}, f32[128,128]{1,0:T(8,128)S(1)}, f32[128,128]{1,0:T(8,128)S(1)}, f32[128,128]{1,0:T(8,128)S(1)}, f32[128,128]{1,0:T(...) custom-call(f32[2048,128]{1,0:T(8,128)S(1)} %bitcast.12, ...), custom_call_target="tpu_custom_call" | custom-call | flops 5000000000 | bytes 10000000 | tf_op jit(solution)/shard_map/layers/pallas_call | solution.py:244
  37.3 5.1 %collective-permute-start = (f32[128,128]{1,0:T(8,128)S(1)}, f32[128,128]{1,0:T(8,128)S(1)}, u32[]{:S(2)}, u32[]{:S(2)}) collective-permute-start(f32[128,128]{1,0:T(8,128)S(1)} %get-tuple-element.26), channel_id=1, source_target_pairs={{0,16},{2,18},{4,20},{6,22},{8,24},{10,26},{12,28},{14,30},{16,0},... | collective-permute-start | bytes 196616 | tf_op jit(solution)/shard_map/ppermute | solution.py:240
  42.5 1.2 %collective-permute-start.2 = (f32[128,128]{1,0:T(8,128)S(1)}, f32[128,128]{1,0:T(8,128)S(1)}, u32[]{:S(2)}, u32[]{:S(2)}) collective-permute-start(f32[128,128]{1,0:T(8,128)S(1)} %get-tuple-element.28), channel_id=1, source_target_pairs={{0,8},{2,10},{4,12},{6,14},{8,0},{10,2},{12,4},{14,6},{16,24},{18,... | collective-permute-start | bytes 196616 | tf_op jit(solution)/shard_map/ppermute | solution.py:240
  43.6 0.4 collective-permute-start.3
  44.0 2.1 %collective-permute-start.4 = (f32[128,128]{1,0:T(8,128)S(1)}, f32[128,128]{1,0:T(8,128)S(1)}, u32[]{:S(2)}, u32[]{:S(2)}) collective-permute-start(f32[128,128]{1,0:T(8,128)S(1)} %get-tuple-element.30), channel_id=1, source_target_pairs={{0,20},{2,22},{4,16},{6,18},{8,28},{10,30},{12,24},{14,26},{16,4},... | collective-permute-start | bytes 196616 | tf_op jit(solution)/shard_map/ppermute | solution.py:240
  46.1 1.7 %collective-permute-done.rest_1_ = f32[128,128]{1,0:T(8,128)S(1)} collective-permute-done((f32[128,128]{1,0:T(8,128)S(1)}, f32[128,128]{1,0:T(8,128)S(1)}, u32[]{:S(2)}, u32[]{:S(2)}) %collective-permute-start) | collective-permute-done | bytes 65568 | tf_op jit(solution)/shard_map/ppermute | solution.py:240
  47.9 0.0 collective-permute-start.5
  47.9 0.9 %collective-permute-done.1.rest_2_ = f32[128,128]{1,0:T(8,128)S(1)} collective-permute-done((f32[128,128]{1,0:T(8,128)S(1)}, f32[128,128]{1,0:T(8,128)S(1)}, u32[]{:S(2)}, u32[]{:S(2)}) %collective-permute-start.1) | collective-permute-done | bytes 65568 | tf_op jit(solution)/shard_map/ppermute | solution.py:240
  48.8 1.1 %collective-permute-start.6 = (f32[128,128]{1,0:T(8,128)S(1)}, f32[128,128]{1,0:T(8,128)S(1)}, u32[]{:S(2)}, u32[]{:S(2)}) collective-permute-start(f32[128,128]{1,0:T(8,128)S(1)} %get-tuple-element.32), channel_id=1, source_target_pairs={{0,12},{2,14},{4,8},{6,10},{8,4},{10,6},{12,0},{14,2},{16,28},{18,... | collective-permute-start | bytes 196616 | tf_op jit(solution)/shard_map/ppermute | solution.py:240
  49.9 0.0 collective-permute-done.2.rest_3_
  49.9 1.5 %collective-permute-start.7 = (f32[128,128]{1,0:T(8,128)S(1)}, f32[128,128]{1,0:T(8,128)S(1)}, u32[]{:S(2)}, u32[]{:S(2)}) collective-permute-start(f32[128,128]{1,0:T(8,128)S(1)} %get-tuple-element.33), channel_id=1, source_target_pairs={{0,14},{2,12},{4,10},{6,8},{8,6},{10,4},{12,2},{14,0},{16,30},{18,... | collective-permute-start | bytes 196616 | tf_op jit(solution)/shard_map/ppermute | solution.py:240
  51.3 1.6 %collective-permute-start.8 = (f32[128,128]{1,0:T(8,128)S(1)}, f32[128,128]{1,0:T(8,128)S(1)}, u32[]{:S(2)}, u32[]{:S(2)}) collective-permute-start(f32[128,128]{1,0:T(8,128)S(1)} %get-tuple-element.34), channel_id=1, source_target_pairs={{0,24},{2,26},{4,28},{6,30},{8,16},{10,18},{12,20},{14,22},{16,8},... | collective-permute-start | bytes 196616 | tf_op jit(solution)/shard_map/ppermute | solution.py:240
  53.0 0.0 collective-permute-done.4.rest_5_
  53.0 2.0 %collective-permute-start.9 = (f32[128,128]{1,0:T(8,128)S(1)}, f32[128,128]{1,0:T(8,128)S(1)}, u32[]{:S(2)}, u32[]{:S(2)}) collective-permute-start(f32[128,128]{1,0:T(8,128)S(1)} %get-tuple-element.35), channel_id=1, source_target_pairs={{0,26},{2,24},{4,30},{6,28},{8,18},{10,16},{12,22},{14,20},{16,10}... | collective-permute-start | bytes 196616 | tf_op jit(solution)/shard_map/ppermute | solution.py:240
  55.0 0.2 collective-permute-done.5.rest_6_
  55.2 3.4 %collective-permute-start.10 = (f32[128,128]{1,0:T(8,128)S(1)}, f32[128,128]{1,0:T(8,128)S(1)}, u32[]{:S(2)}, u32[]{:S(2)}) collective-permute-start(f32[128,128]{1,0:T(8,128)S(1)} %get-tuple-element.36), channel_id=1, source_target_pairs={{0,28},{2,30},{4,24},{6,26},{8,20},{10,22},{12,16},{14,18},{16,12}... | collective-permute-start | bytes 196616 | tf_op jit(solution)/shard_map/ppermute | solution.py:240
  58.6 0.0 collective-permute-done.6.rest_7_
  58.6 1.7 %collective-permute-start.11 = (f32[128,128]{1,0:T(8,128)S(1)}, f32[128,128]{1,0:T(8,128)S(1)}, u32[]{:S(2)}, u32[]{:S(2)}) collective-permute-start(f32[128,128]{1,0:T(8,128)S(1)} %get-tuple-element.37), channel_id=1, source_target_pairs={{0,30},{2,28},{4,26},{6,24},{8,22},{10,20},{12,18},{14,16},{16,14}... | collective-permute-start | bytes 196616 | tf_op jit(solution)/shard_map/ppermute | solution.py:240
  60.3 0.6 collective-permute-start.12
  60.9 0.4 collective-permute-start.13
  61.4 1.1 %collective-permute-start.14 = (f32[128,128]{1,0:T(8,128)S(1)}, f32[128,128]{1,0:T(8,128)S(1)}, u32[]{:S(2)}, u32[]{:S(2)}) collective-permute-start(f32[128,128]{1,0:T(8,128)S(1)} %get-tuple-element.40), channel_id=1, source_target_pairs={{0,2},{2,0},{4,6},{6,4},{8,10},{10,8},{12,14},{14,12},{16,18},{18,... | collective-permute-start | bytes 196616 | tf_op jit(solution)/shard_map/ppermute | solution.py:240
  62.5 0.3 collective-permute-done.10.rest_11_
  62.8 2.9 %collective-permute-done.11.rest_12_ = f32[128,128]{1,0:T(8,128)S(1)} collective-permute-done((f32[128,128]{1,0:T(8,128)S(1)}, f32[128,128]{1,0:T(8,128)S(1)}, u32[]{:S(2)}, u32[]{:S(2)}) %collective-permute-start.11) | collective-permute-done | bytes 65568 | tf_op jit(solution)/shard_map/ppermute | solution.py:240
  65.7 0.9 %collective-permute-done.12.rest_13_ = f32[128,128]{1,0:T(8,128)S(1)} collective-permute-done((f32[128,128]{1,0:T(8,128)S(1)}, f32[128,128]{1,0:T(8,128)S(1)}, u32[]{:S(2)}, u32[]{:S(2)}) %collective-permute-start.12) | collective-permute-done | bytes 65568 | tf_op jit(solution)/shard_map/ppermute | solution.py:240
  66.6 0.1 collective-permute-done.13.rest_14_
  66.7 1.1 %place.1 = f32[2048,128]{1,0:T(8,128)} custom-call(f32[128,128]{1,0:T(8,128)S(1)} %get-tuple-element.25.rest_0_, f32[128,128]{1,0:T(8,128)S(1)} %collective-permute-done.rest_1_, f32[128,128]{1,0:T(8,128)S(1)} %collective-permute-done.1.rest_2_, f32[128,128]{1,0:T(8,128)S(1)} %collective-permute-done.2.rest_3_, ...), custom_call_target="tpu_custom_call" | custom-call | tf_op jit(solution)/shard_map/place/pallas_call | solution.py:260
  (14 shorter events, 0.0 us)
Async XLA Ops:
  0.0 7.5 %copy-start.3 = (s32[6,8]{1,0:T(8,128)S(1)}, s32[6,8]{1,0:T(8,128)}, u32[]{:S(2)}) copy-start(s32[6,8]{1,0:T(8,128)} %order_ref.1) | copy-start | bytes 580
  0.0 7.6 %copy-start.1 = (f32[6,128,128]{2,1,0:T(8,128)S(1)}, f32[6,128,128]{2,1,0:T(8,128)}, u32[]{:S(2)}) copy-start(f32[6,128,128]{2,1,0:T(8,128)} %im_ref.1) | copy-start | bytes 1179652
  0.0 7.6 %copy-start = (f32[6,128,128]{2,1,0:T(8,128)S(1)}, f32[6,128,128]{2,1,0:T(8,128)}, u32[]{:S(2)}) copy-start(f32[6,128,128]{2,1,0:T(8,128)} %re_ref.1) | copy-start | bytes 1179652
  0.0 30.5 %all-to-all-start = ((f32[16,128,128]{2,1,0:T(8,128)}), f32[16,128,128]{2,1,0:T(8,128)S(1)}, u32[]{:S(2)}, u32[]{:S(2)}) async-start(f32[16,128,128]{2,1,0:T(8,128)} %bitcast.14), calls=%async_computation | async-start | bytes 2097152 | tf_op jit(solution)/shard_map/all_to_all | solution.py:206
  7.6 1.2 %copy-start.2 = (s32[6,16,2]{1,2,0:T(2,128)S(1)}, s32[6,16,2]{1,2,0:T(2,128)}, u32[]{:S(2)}) copy-start(s32[6,16,2]{1,2,0:T(2,128)} %param.10) | copy-start | bytes 2308
  7.6 1.2 %copy-start.4 = (f32[6,16]{1,0:T(8,128)S(1)}, f32[6,16]{1,0:T(8,128)}, u32[]{:S(2)}) copy-start(f32[6,16]{1,0:T(8,128)} %angle_ref.1) | copy-start | bytes 1156
  37.3 10.5 %collective-permute-start = (f32[128,128]{1,0:T(8,128)S(1)}, f32[128,128]{1,0:T(8,128)S(1)}, u32[]{:S(2)}, u32[]{:S(2)}) collective-permute-start(f32[128,128]{1,0:T(8,128)S(1)} %get-tuple-element.26), channel_id=1, source_target_pairs={{0,16},{2,18},{4,20},{6,22},{8,24},{10,26},{12,28},{14,30},{16,0},... | collective-permute-start | bytes 196616 | tf_op jit(solution)/shard_map/ppermute | solution.py:240
  42.5 6.3 %collective-permute-start.1 = (f32[128,128]{1,0:T(8,128)S(1)}, f32[128,128]{1,0:T(8,128)S(1)}, u32[]{:S(2)}, u32[]{:S(2)}) collective-permute-start(f32[128,128]{1,0:T(8,128)S(1)} %get-tuple-element.27), channel_id=1, source_target_pairs={{0,18},{2,16},{4,22},{6,20},{8,26},{10,24},{12,30},{14,28},{16,2},... | collective-permute-start | bytes 196616 | tf_op jit(solution)/shard_map/ppermute | solution.py:240
  42.5 7.4 %collective-permute-start.2 = (f32[128,128]{1,0:T(8,128)S(1)}, f32[128,128]{1,0:T(8,128)S(1)}, u32[]{:S(2)}, u32[]{:S(2)}) collective-permute-start(f32[128,128]{1,0:T(8,128)S(1)} %get-tuple-element.28), channel_id=1, source_target_pairs={{0,8},{2,10},{4,12},{6,14},{8,0},{10,2},{12,4},{14,6},{16,24},{18,... | collective-permute-start | bytes 196616 | tf_op jit(solution)/shard_map/ppermute | solution.py:240
  43.6 7.7 %collective-permute-start.3 = (f32[128,128]{1,0:T(8,128)S(1)}, f32[128,128]{1,0:T(8,128)S(1)}, u32[]{:S(2)}, u32[]{:S(2)}) collective-permute-start(f32[128,128]{1,0:T(8,128)S(1)} %get-tuple-element.29), channel_id=1, source_target_pairs={{0,10},{2,8},{4,14},{6,12},{8,2},{10,0},{12,6},{14,4},{16,26},{18,... | collective-permute-start | bytes 196616 | tf_op jit(solution)/shard_map/ppermute | solution.py:240
  44.0 8.9 %collective-permute-start.4 = (f32[128,128]{1,0:T(8,128)S(1)}, f32[128,128]{1,0:T(8,128)S(1)}, u32[]{:S(2)}, u32[]{:S(2)}) collective-permute-start(f32[128,128]{1,0:T(8,128)S(1)} %get-tuple-element.30), channel_id=1, source_target_pairs={{0,20},{2,22},{4,16},{6,18},{8,28},{10,30},{12,24},{14,26},{16,4},... | collective-permute-start | bytes 196616 | tf_op jit(solution)/shard_map/ppermute | solution.py:240
  47.9 7.3 %collective-permute-start.5 = (f32[128,128]{1,0:T(8,128)S(1)}, f32[128,128]{1,0:T(8,128)S(1)}, u32[]{:S(2)}, u32[]{:S(2)}) collective-permute-start(f32[128,128]{1,0:T(8,128)S(1)} %get-tuple-element.31), channel_id=1, source_target_pairs={{0,22},{2,20},{4,18},{6,16},{8,30},{10,28},{12,26},{14,24},{16,6},... | collective-permute-start | bytes 196616 | tf_op jit(solution)/shard_map/ppermute | solution.py:240
  48.8 9.8 %collective-permute-start.6 = (f32[128,128]{1,0:T(8,128)S(1)}, f32[128,128]{1,0:T(8,128)S(1)}, u32[]{:S(2)}, u32[]{:S(2)}) collective-permute-start(f32[128,128]{1,0:T(8,128)S(1)} %get-tuple-element.32), channel_id=1, source_target_pairs={{0,12},{2,14},{4,8},{6,10},{8,4},{10,6},{12,0},{14,2},{16,28},{18,... | collective-permute-start | bytes 196616 | tf_op jit(solution)/shard_map/ppermute | solution.py:240
  49.9 10.4 %collective-permute-start.7 = (f32[128,128]{1,0:T(8,128)S(1)}, f32[128,128]{1,0:T(8,128)S(1)}, u32[]{:S(2)}, u32[]{:S(2)}) collective-permute-start(f32[128,128]{1,0:T(8,128)S(1)} %get-tuple-element.33), channel_id=1, source_target_pairs={{0,14},{2,12},{4,10},{6,8},{8,6},{10,4},{12,2},{14,0},{16,30},{18,... | collective-permute-start | bytes 196616 | tf_op jit(solution)/shard_map/ppermute | solution.py:240
  51.3 9.6 %collective-permute-start.8 = (f32[128,128]{1,0:T(8,128)S(1)}, f32[128,128]{1,0:T(8,128)S(1)}, u32[]{:S(2)}, u32[]{:S(2)}) collective-permute-start(f32[128,128]{1,0:T(8,128)S(1)} %get-tuple-element.34), channel_id=1, source_target_pairs={{0,24},{2,26},{4,28},{6,30},{8,16},{10,18},{12,20},{14,22},{16,8},... | collective-permute-start | bytes 196616 | tf_op jit(solution)/shard_map/ppermute | solution.py:240
  53.0 8.4 %collective-permute-start.9 = (f32[128,128]{1,0:T(8,128)S(1)}, f32[128,128]{1,0:T(8,128)S(1)}, u32[]{:S(2)}, u32[]{:S(2)}) collective-permute-start(f32[128,128]{1,0:T(8,128)S(1)} %get-tuple-element.35), channel_id=1, source_target_pairs={{0,26},{2,24},{4,30},{6,28},{8,18},{10,16},{12,22},{14,20},{16,10}... | collective-permute-start | bytes 196616 | tf_op jit(solution)/shard_map/ppermute | solution.py:240
  55.2 7.6 %collective-permute-start.10 = (f32[128,128]{1,0:T(8,128)S(1)}, f32[128,128]{1,0:T(8,128)S(1)}, u32[]{:S(2)}, u32[]{:S(2)}) collective-permute-start(f32[128,128]{1,0:T(8,128)S(1)} %get-tuple-element.36), channel_id=1, source_target_pairs={{0,28},{2,30},{4,24},{6,26},{8,20},{10,22},{12,16},{14,18},{16,12}... | collective-permute-start | bytes 196616 | tf_op jit(solution)/shard_map/ppermute | solution.py:240
  58.6 7.1 %collective-permute-start.11 = (f32[128,128]{1,0:T(8,128)S(1)}, f32[128,128]{1,0:T(8,128)S(1)}, u32[]{:S(2)}, u32[]{:S(2)}) collective-permute-start(f32[128,128]{1,0:T(8,128)S(1)} %get-tuple-element.37), channel_id=1, source_target_pairs={{0,30},{2,28},{4,26},{6,24},{8,22},{10,20},{12,18},{14,16},{16,14}... | collective-permute-start | bytes 196616 | tf_op jit(solution)/shard_map/ppermute | solution.py:240
  60.3 6.3 %collective-permute-start.12 = (f32[128,128]{1,0:T(8,128)S(1)}, f32[128,128]{1,0:T(8,128)S(1)}, u32[]{:S(2)}, u32[]{:S(2)}) collective-permute-start(f32[128,128]{1,0:T(8,128)S(1)} %get-tuple-element.38), channel_id=1, source_target_pairs={{0,4},{2,6},{4,0},{6,2},{8,12},{10,14},{12,8},{14,10},{16,20},{18,... | collective-permute-start | bytes 196616 | tf_op jit(solution)/shard_map/ppermute | solution.py:240
  60.9 5.8 %collective-permute-start.13 = (f32[128,128]{1,0:T(8,128)S(1)}, f32[128,128]{1,0:T(8,128)S(1)}, u32[]{:S(2)}, u32[]{:S(2)}) collective-permute-start(f32[128,128]{1,0:T(8,128)S(1)} %get-tuple-element.39), channel_id=1, source_target_pairs={{0,6},{2,4},{4,2},{6,0},{8,14},{10,12},{12,10},{14,8},{16,22},{18,... | collective-permute-start | bytes 196616 | tf_op jit(solution)/shard_map/ppermute | solution.py:240
  61.4 5.4 %collective-permute-start.14 = (f32[128,128]{1,0:T(8,128)S(1)}, f32[128,128]{1,0:T(8,128)S(1)}, u32[]{:S(2)}, u32[]{:S(2)}) collective-permute-start(f32[128,128]{1,0:T(8,128)S(1)} %get-tuple-element.40), channel_id=1, source_target_pairs={{0,2},{2,0},{4,6},{6,4},{8,10},{10,8},{12,14},{14,12},{16,18},{18,... | collective-permute-start | bytes 196616 | tf_op jit(solution)/shard_map/ppermute | solution.py:240

commit v22 on v21

--- a/solution.py
+++ b/solution.py
@@ -111,9 +111,6 @@
     joined = PACKED // rows_at_once
     tile = min(TILE, count // 2)
 
-    for part in range(2):
-        for lanes in range(2):
-            state[0, part, :, lanes * LANES : (lanes + 1) * LANES] = x[pl.ds(2 * lanes + part, count, stride=4), :]
     lane = lax.broadcasted_iota(jnp.int32, (rows_at_once, LANES), 1)
     taken = [(lane & (span << i)) != 0 for i in range(half.bit_length() - 1)]
 
@@ -142,7 +139,12 @@
 
     def load(layer, lanes, top, offset):
         slot = layer % 2
-        pieces = turned(slot, layer, [(top * half + m) * spect for m in range(half)], offset, lanes)
+        firsts = [(top * half + m) * spect for m in range(half)]
+        if layer:
+            pieces = turned(slot, layer, firsts, offset, lanes)
+        else:
+            starts = [4 * (first + offset) + 2 * lanes for first in firsts]
+            pieces = [[x[pl.ds(start + part, rows_at_once, stride=4), :] for part in range(2)] for start in starts]
         reals, imags = (exchange_modes([piece[part] for piece in pieces], span, taken) for part in range(2))
         for g in range(0, half, joined):
             at = (lanes * half + g) * spect + offset

time: 68.1 us -> 68 us (level)
  no operation moved by 1% of the time
where the time goes in v22:
time: 68 us; the launch traced here: 67.8 us
  starting transfers between devices  29.8 us (44%)
  waiting for transfers between devices  27.3 us (40%)
  Pallas kernels  10.5 us (15%)
    ppermute x15, starting transfers between devices, swap(): lax.ppermute(block, 'wide', [(i, i ^ k) for i in range(wide)])  22.3 us
    all_to_all x1, waiting for transfers between devices, local(): lax.all_to_all(rows, 'wide', split_axis=0, concat_axis=0, tiled=True)  20.2 us
    all_to_all x1, starting transfers between devices, local(): lax.all_to_all(rows, 'wide', split_axis=0, concat_axis=0, tiled=True)  7.53 us
    ppermute x15, waiting for transfers between devices, swap(): lax.ppermute(block, 'wide', [(i, i ^ k) for i in range(wide)])  7.12 us
    pallas_call x1, Pallas kernels, local(): pl.pallas_call(partial(layers_kernel, wide, spect), in_specs=[in_vmem] *...  6.8 us
    pallas_call x1, Pallas kernels, local(): pl.pallas_call(partial(phases_kernel, spect, narrow), in_specs=[in_smem,...  1.47 us
  transfers between devices with their start and end apart: 16, of which 8 were waited for; matrix products, arithmetic and copies ran while one was open for 0% of the time, Pallas kernels for 4%

profile of v22, /device:TPU:0, one launch (start us, length us, event | category | flops | bytes accessed | tf_op | source)
XLA Modules:
  0.0 67.8 jit_solution(10194115514974503264)
XLA Ops:
  0.0 7.5 %all-to-all-start = ((f32[16,128,128]{2,1,0:T(8,128)}), f32[16,128,128]{2,1,0:T(8,128)S(1)}, u32[]{:S(2)}, u32[]{:S(2)}) async-start(f32[16,128,128]{2,1,0:T(8,128)} %bitcast.14), calls=%async_computation | async-start | bytes 2097152 | tf_op jit(solution)/shard_map/all_to_all | solution.py:208
  7.6 0.0 copy-start.2
  7.6 0.0 copy-start.4
  7.6 1.2 %gates.1 = (bf16[6,2,256,256]{3,2,1,0:T(8,128)(2,1)S(1)}, s32[6,8,128]{2,1,0:T(8,128)S(1)}) custom-call(f32[6,128,128]{2,1,0:T(8,128)S(1)} %copy-done, f32[6,128,128]{2,1,0:T(8,128)S(1)} %copy-done.1, s32[6,8]{1,0:T(8,128)S(1)} %copy-done.3), custom_call_target="tpu_custom_call" | custom-call | flops 1000000000 | bytes 4000000 | tf_op jit(solution)/shard_map/gates/pallas_call | solution.py:218
  8.8 1.5 %phases.1.turn = f32[7,2,16,256]{3,2,1,0:T(8,128)S(1)} custom-call(s32[6,2,16]{2,1,0:T(2,128)S(1)} %bitcast.13, f32[6,16]{1,0:T(8,128)S(1)} %copy-done.4, s32[6,8,128]{2,1,0:T(8,128)S(1)} %get-tuple-element.24.half_ref.half_bit), custom_call_target="tpu_custom_call" | custom-call | flops 100000000 | bytes 1000000 | tf_op jit(solution)/shard_map/phases/pallas_call | solution.py:230
  10.3 20.2 %all-to-all-done = f32[16,128,128]{2,1,0:T(8,128)S(1)} async-done(((f32[16,128,128]{2,1,0:T(8,128)}), f32[16,128,128]{2,1,0:T(8,128)S(1)}, u32[]{:S(2)}, u32[]{:S(2)}) %all-to-all-start) | async-done | bytes 1048608 | tf_op jit(solution)/shard_map/all_to_all | solution.py:208
  30.5 6.8 %layers.1 = (f32[128,128]{1,0:T(8,128)S(1)}, f32[128,128]{1,0:T(8,128)S(1)}, f32[128,128]{1,0:T(8,128)S(1)}, f32[128,128]{1,0:T(8,128)S(1)}, f32[128,128]{1,0:T(...) custom-call(f32[2048,128]{1,0:T(8,128)S(1)} %bitcast.12, ...), custom_call_target="tpu_custom_call" | custom-call | flops 5000000000 | bytes 10000000 | tf_op jit(solution)/shard_map/layers/pallas_call | solution.py:246
  37.3 5.1 %collective-permute-start = (f32[128,128]{1,0:T(8,128)S(1)}, f32[128,128]{1,0:T(8,128)S(1)}, u32[]{:S(2)}, u32[]{:S(2)}) collective-permute-start(f32[128,128]{1,0:T(8,128)S(1)} %get-tuple-element.26), channel_id=1, source_target_pairs={{0,16},{2,18},{4,20},{6,22},{8,24},{10,26},{12,28},{14,30},{16,0},... | collective-permute-start | bytes 196616 | tf_op jit(solution)/shard_map/ppermute | solution.py:242
  42.4 1.2 %collective-permute-start.2 = (f32[128,128]{1,0:T(8,128)S(1)}, f32[128,128]{1,0:T(8,128)S(1)}, u32[]{:S(2)}, u32[]{:S(2)}) collective-permute-start(f32[128,128]{1,0:T(8,128)S(1)} %get-tuple-element.28), channel_id=1, source_target_pairs={{0,8},{2,10},{4,12},{6,14},{8,0},{10,2},{12,4},{14,6},{16,24},{18,... | collective-permute-start | bytes 196616 | tf_op jit(solution)/shard_map/ppermute | solution.py:242
  43.6 0.4 collective-permute-start.3
  44.0 2.1 %collective-permute-start.4 = (f32[128,128]{1,0:T(8,128)S(1)}, f32[128,128]{1,0:T(8,128)S(1)}, u32[]{:S(2)}, u32[]{:S(2)}) collective-permute-start(f32[128,128]{1,0:T(8,128)S(1)} %get-tuple-element.30), channel_id=1, source_target_pairs={{0,20},{2,22},{4,16},{6,18},{8,28},{10,30},{12,24},{14,26},{16,4},... | collective-permute-start | bytes 196616 | tf_op jit(solution)/shard_map/ppermute | solution.py:242
  46.1 1.7 %collective-permute-done.rest_1_ = f32[128,128]{1,0:T(8,128)S(1)} collective-permute-done((f32[128,128]{1,0:T(8,128)S(1)}, f32[128,128]{1,0:T(8,128)S(1)}, u32[]{:S(2)}, u32[]{:S(2)}) %collective-permute-start) | collective-permute-done | bytes 65568 | tf_op jit(solution)/shard_map/ppermute | solution.py:242
  47.8 0.0 collective-permute-start.5
  47.8 0.9 %collective-permute-done.1.rest_2_ = f32[128,128]{1,0:T(8,128)S(1)} collective-permute-done((f32[128,128]{1,0:T(8,128)S(1)}, f32[128,128]{1,0:T(8,128)S(1)}, u32[]{:S(2)}, u32[]{:S(2)}) %collective-permute-start.1) | collective-permute-done | bytes 65568 | tf_op jit(solution)/shard_map/ppermute | solution.py:242
  48.7 1.1 %collective-permute-start.6 = (f32[128,128]{1,0:T(8,128)S(1)}, f32[128,128]{1,0:T(8,128)S(1)}, u32[]{:S(2)}, u32[]{:S(2)}) collective-permute-start(f32[128,128]{1,0:T(8,128)S(1)} %get-tuple-element.32), channel_id=1, source_target_pairs={{0,12},{2,14},{4,8},{6,10},{8,4},{10,6},{12,0},{14,2},{16,28},{18,... | collective-permute-start | bytes 196616 | tf_op jit(solution)/shard_map/ppermute | solution.py:242
  49.8 0.0 collective-permute-done.2.rest_3_
  49.8 1.5 %collective-permute-start.7 = (f32[128,128]{1,0:T(8,128)S(1)}, f32[128,128]{1,0:T(8,128)S(1)}, u32[]{:S(2)}, u32[]{:S(2)}) collective-permute-start(f32[128,128]{1,0:T(8,128)S(1)} %get-tuple-element.33), channel_id=1, source_target_pairs={{0,14},{2,12},{4,10},{6,8},{8,6},{10,4},{12,2},{14,0},{16,30},{18,... | collective-permute-start | bytes 196616 | tf_op jit(solution)/shard_map/ppermute | solution.py:242
  51.3 1.6 %collective-permute-start.8 = (f32[128,128]{1,0:T(8,128)S(1)}, f32[128,128]{1,0:T(8,128)S(1)}, u32[]{:S(2)}, u32[]{:S(2)}) collective-permute-start(f32[128,128]{1,0:T(8,128)S(1)} %get-tuple-element.34), channel_id=1, source_target_pairs={{0,24},{2,26},{4,28},{6,30},{8,16},{10,18},{12,20},{14,22},{16,8},... | collective-permute-start | bytes 196616 | tf_op jit(solution)/shard_map/ppermute | solution.py:242
  52.9 0.0 collective-permute-done.4.rest_5_
  52.9 2.0 %collective-permute-start.9 = (f32[128,128]{1,0:T(8,128)S(1)}, f32[128,128]{1,0:T(8,128)S(1)}, u32[]{:S(2)}, u32[]{:S(2)}) collective-permute-start(f32[128,128]{1,0:T(8,128)S(1)} %get-tuple-element.35), channel_id=1, source_target_pairs={{0,26},{2,24},{4,30},{6,28},{8,18},{10,16},{12,22},{14,20},{16,10}... | collective-permute-start | bytes 196616 | tf_op jit(solution)/shard_map/ppermute | solution.py:242
  54.9 0.2 collective-permute-done.5.rest_6_
  55.1 3.4 %collective-permute-start.10 = (f32[128,128]{1,0:T(8,128)S(1)}, f32[128,128]{1,0:T(8,128)S(1)}, u32[]{:S(2)}, u32[]{:S(2)}) collective-permute-start(f32[128,128]{1,0:T(8,128)S(1)} %get-tuple-element.36), channel_id=1, source_target_pairs={{0,28},{2,30},{4,24},{6,26},{8,20},{10,22},{12,16},{14,18},{16,12}... | collective-permute-start | bytes 196616 | tf_op jit(solution)/shard_map/ppermute | solution.py:242
  58.5 1.7 %collective-permute-start.11 = (f32[128,128]{1,0:T(8,128)S(1)}, f32[128,128]{1,0:T(8,128)S(1)}, u32[]{:S(2)}, u32[]{:S(2)}) collective-permute-start(f32[128,128]{1,0:T(8,128)S(1)} %get-tuple-element.37), channel_id=1, source_target_pairs={{0,30},{2,28},{4,26},{6,24},{8,22},{10,20},{12,18},{14,16},{16,14}... | collective-permute-start | bytes 196616 | tf_op jit(solution)/shard_map/ppermute | solution.py:242
  60.2 0.0 collective-permute-done.7.rest_8_
  60.2 0.6 collective-permute-start.12
  60.9 0.4 collective-permute-start.13
  61.3 1.1 %collective-permute-start.14 = (f32[128,128]{1,0:T(8,128)S(1)}, f32[128,128]{1,0:T(8,128)S(1)}, u32[]{:S(2)}, u32[]{:S(2)}) collective-permute-start(f32[128,128]{1,0:T(8,128)S(1)} %get-tuple-element.40), channel_id=1, source_target_pairs={{0,2},{2,0},{4,6},{6,4},{8,10},{10,8},{12,14},{14,12},{16,18},{18,... | collective-permute-start | bytes 196616 | tf_op jit(solution)/shard_map/ppermute | solution.py:242
  62.4 0.3 collective-permute-done.10.rest_11_
  62.7 3.0 %collective-permute-done.11.rest_12_ = f32[128,128]{1,0:T(8,128)S(1)} collective-permute-done((f32[128,128]{1,0:T(8,128)S(1)}, f32[128,128]{1,0:T(8,128)S(1)}, u32[]{:S(2)}, u32[]{:S(2)}) %collective-permute-start.11) | collective-permute-done | bytes 65568 | tf_op jit(solution)/shard_map/ppermute | solution.py:242
  65.7 0.9 %collective-permute-done.12.rest_13_ = f32[128,128]{1,0:T(8,128)S(1)} collective-permute-done((f32[128,128]{1,0:T(8,128)S(1)}, f32[128,128]{1,0:T(8,128)S(1)}, u32[]{:S(2)}, u32[]{:S(2)}) %collective-permute-start.12) | collective-permute-done | bytes 65568 | tf_op jit(solution)/shard_map/ppermute | solution.py:242
  66.6 0.1 collective-permute-done.13.rest_14_
  66.7 1.1 %place.1 = f32[2048,128]{1,0:T(8,128)} custom-call(f32[128,128]{1,0:T(8,128)S(1)} %get-tuple-element.25.rest_0_, f32[128,128]{1,0:T(8,128)S(1)} %collective-permute-done.rest_1_, f32[128,128]{1,0:T(8,128)S(1)} %collective-permute-done.1.rest_2_, f32[128,128]{1,0:T(8,128)S(1)} %collective-permute-done.2.rest_3_, ...), custom_call_target="tpu_custom_call" | custom-call | tf_op jit(solution)/shard_map/place/pallas_call | solution.py:262
  (14 shorter events, 0.0 us)
Async XLA Ops:
  0.0 7.5 %copy-start.3 = (s32[6,8]{1,0:T(8,128)S(1)}, s32[6,8]{1,0:T(8,128)}, u32[]{:S(2)}) copy-start(s32[6,8]{1,0:T(8,128)} %order_ref.1) | copy-start | bytes 580
  0.0 7.6 %copy-start.1 = (f32[6,128,128]{2,1,0:T(8,128)S(1)}, f32[6,128,128]{2,1,0:T(8,128)}, u32[]{:S(2)}) copy-start(f32[6,128,128]{2,1,0:T(8,128)} %im_ref.1) | copy-start | bytes 1179652
  0.0 7.6 %copy-start = (f32[6,128,128]{2,1,0:T(8,128)S(1)}, f32[6,128,128]{2,1,0:T(8,128)}, u32[]{:S(2)}) copy-start(f32[6,128,128]{2,1,0:T(8,128)} %re_ref.1) | copy-start | bytes 1179652
  0.0 30.5 %all-to-all-start = ((f32[16,128,128]{2,1,0:T(8,128)}), f32[16,128,128]{2,1,0:T(8,128)S(1)}, u32[]{:S(2)}, u32[]{:S(2)}) async-start(f32[16,128,128]{2,1,0:T(8,128)} %bitcast.14), calls=%async_computation | async-start | bytes 2097152 | tf_op jit(solution)/shard_map/all_to_all | solution.py:208
  7.6 1.2 %copy-start.2 = (s32[6,16,2]{1,2,0:T(2,128)S(1)}, s32[6,16,2]{1,2,0:T(2,128)}, u32[]{:S(2)}) copy-start(s32[6,16,2]{1,2,0:T(2,128)} %param.10) | copy-start | bytes 2308
  7.6 1.2 %copy-start.4 = (f32[6,16]{1,0:T(8,128)S(1)}, f32[6,16]{1,0:T(8,128)}, u32[]{:S(2)}) copy-start(f32[6,16]{1,0:T(8,128)} %angle_ref.1) | copy-start | bytes 1156
  37.3 10.5 %collective-permute-start = (f32[128,128]{1,0:T(8,128)S(1)}, f32[128,128]{1,0:T(8,128)S(1)}, u32[]{:S(2)}, u32[]{:S(2)}) collective-permute-start(f32[128,128]{1,0:T(8,128)S(1)} %get-tuple-element.26), channel_id=1, source_target_pairs={{0,16},{2,18},{4,20},{6,22},{8,24},{10,26},{12,28},{14,30},{16,0},... | collective-permute-start | bytes 196616 | tf_op jit(solution)/shard_map/ppermute | solution.py:242
  42.4 6.3 %collective-permute-start.1 = (f32[128,128]{1,0:T(8,128)S(1)}, f32[128,128]{1,0:T(8,128)S(1)}, u32[]{:S(2)}, u32[]{:S(2)}) collective-permute-start(f32[128,128]{1,0:T(8,128)S(1)} %get-tuple-element.27), channel_id=1, source_target_pairs={{0,18},{2,16},{4,22},{6,20},{8,26},{10,24},{12,30},{14,28},{16,2},... | collective-permute-start | bytes 196616 | tf_op jit(solution)/shard_map/ppermute | solution.py:242
  42.4 7.4 %collective-permute-start.2 = (f32[128,128]{1,0:T(8,128)S(1)}, f32[128,128]{1,0:T(8,128)S(1)}, u32[]{:S(2)}, u32[]{:S(2)}) collective-permute-start(f32[128,128]{1,0:T(8,128)S(1)} %get-tuple-element.28), channel_id=1, source_target_pairs={{0,8},{2,10},{4,12},{6,14},{8,0},{10,2},{12,4},{14,6},{16,24},{18,... | collective-permute-start | bytes 196616 | tf_op jit(solution)/shard_map/ppermute | solution.py:242
  43.6 7.7 %collective-permute-start.3 = (f32[128,128]{1,0:T(8,128)S(1)}, f32[128,128]{1,0:T(8,128)S(1)}, u32[]{:S(2)}, u32[]{:S(2)}) collective-permute-start(f32[128,128]{1,0:T(8,128)S(1)} %get-tuple-element.29), channel_id=1, source_target_pairs={{0,10},{2,8},{4,14},{6,12},{8,2},{10,0},{12,6},{14,4},{16,26},{18,... | collective-permute-start | bytes 196616 | tf_op jit(solution)/shard_map/ppermute | solution.py:242
  44.0 8.9 %collective-permute-start.4 = (f32[128,128]{1,0:T(8,128)S(1)}, f32[128,128]{1,0:T(8,128)S(1)}, u32[]{:S(2)}, u32[]{:S(2)}) collective-permute-start(f32[128,128]{1,0:T(8,128)S(1)} %get-tuple-element.30), channel_id=1, source_target_pairs={{0,20},{2,22},{4,16},{6,18},{8,28},{10,30},{12,24},{14,26},{16,4},... | collective-permute-start | bytes 196616 | tf_op jit(solution)/shard_map/ppermute | solution.py:242
  47.8 7.3 %collective-permute-start.5 = (f32[128,128]{1,0:T(8,128)S(1)}, f32[128,128]{1,0:T(8,128)S(1)}, u32[]{:S(2)}, u32[]{:S(2)}) collective-permute-start(f32[128,128]{1,0:T(8,128)S(1)} %get-tuple-element.31), channel_id=1, source_target_pairs={{0,22},{2,20},{4,18},{6,16},{8,30},{10,28},{12,26},{14,24},{16,6},... | collective-permute-start | bytes 196616 | tf_op jit(solution)/shard_map/ppermute | solution.py:242
  48.7 9.8 %collective-permute-start.6 = (f32[128,128]{1,0:T(8,128)S(1)}, f32[128,128]{1,0:T(8,128)S(1)}, u32[]{:S(2)}, u32[]{:S(2)}) collective-permute-start(f32[128,128]{1,0:T(8,128)S(1)} %get-tuple-element.32), channel_id=1, source_target_pairs={{0,12},{2,14},{4,8},{6,10},{8,4},{10,6},{12,0},{14,2},{16,28},{18,... | collective-permute-start | bytes 196616 | tf_op jit(solution)/shard_map/ppermute | solution.py:242
  49.8 10.4 %collective-permute-start.7 = (f32[128,128]{1,0:T(8,128)S(1)}, f32[128,128]{1,0:T(8,128)S(1)}, u32[]{:S(2)}, u32[]{:S(2)}) collective-permute-start(f32[128,128]{1,0:T(8,128)S(1)} %get-tuple-element.33), channel_id=1, source_target_pairs={{0,14},{2,12},{4,10},{6,8},{8,6},{10,4},{12,2},{14,0},{16,30},{18,... | collective-permute-start | bytes 196616 | tf_op jit(solution)/shard_map/ppermute | solution.py:242
  51.3 9.6 %collective-permute-start.8 = (f32[128,128]{1,0:T(8,128)S(1)}, f32[128,128]{1,0:T(8,128)S(1)}, u32[]{:S(2)}, u32[]{:S(2)}) collective-permute-start(f32[128,128]{1,0:T(8,128)S(1)} %get-tuple-element.34), channel_id=1, source_target_pairs={{0,24},{2,26},{4,28},{6,30},{8,16},{10,18},{12,20},{14,22},{16,8},... | collective-permute-start | bytes 196616 | tf_op jit(solution)/shard_map/ppermute | solution.py:242
  52.9 8.4 %collective-permute-start.9 = (f32[128,128]{1,0:T(8,128)S(1)}, f32[128,128]{1,0:T(8,128)S(1)}, u32[]{:S(2)}, u32[]{:S(2)}) collective-permute-start(f32[128,128]{1,0:T(8,128)S(1)} %get-tuple-element.35), channel_id=1, source_target_pairs={{0,26},{2,24},{4,30},{6,28},{8,18},{10,16},{12,22},{14,20},{16,10}... | collective-permute-start | bytes 196616 | tf_op jit(solution)/shard_map/ppermute | solution.py:242
  55.1 7.6 %collective-permute-start.10 = (f32[128,128]{1,0:T(8,128)S(1)}, f32[128,128]{1,0:T(8,128)S(1)}, u32[]{:S(2)}, u32[]{:S(2)}) collective-permute-start(f32[128,128]{1,0:T(8,128)S(1)} %get-tuple-element.36), channel_id=1, source_target_pairs={{0,28},{2,30},{4,24},{6,26},{8,20},{10,22},{12,16},{14,18},{16,12}... | collective-permute-start | bytes 196616 | tf_op jit(solution)/shard_map/ppermute | solution.py:242
  58.5 7.1 %collective-permute-start.11 = (f32[128,128]{1,0:T(8,128)S(1)}, f32[128,128]{1,0:T(8,128)S(1)}, u32[]{:S(2)}, u32[]{:S(2)}) collective-permute-start(f32[128,128]{1,0:T(8,128)S(1)} %get-tuple-element.37), channel_id=1, source_target_pairs={{0,30},{2,28},{4,26},{6,24},{8,22},{10,20},{12,18},{14,16},{16,14}... | collective-permute-start | bytes 196616 | tf_op jit(solution)/shard_map/ppermute | solution.py:242
  60.2 6.3 %collective-permute-start.12 = (f32[128,128]{1,0:T(8,128)S(1)}, f32[128,128]{1,0:T(8,128)S(1)}, u32[]{:S(2)}, u32[]{:S(2)}) collective-permute-start(f32[128,128]{1,0:T(8,128)S(1)} %get-tuple-element.38), channel_id=1, source_target_pairs={{0,4},{2,6},{4,0},{6,2},{8,12},{10,14},{12,8},{14,10},{16,20},{18,... | collective-permute-start | bytes 196616 | tf_op jit(solution)/shard_map/ppermute | solution.py:242
  60.9 5.8 %collective-permute-start.13 = (f32[128,128]{1,0:T(8,128)S(1)}, f32[128,128]{1,0:T(8,128)S(1)}, u32[]{:S(2)}, u32[]{:S(2)}) collective-permute-start(f32[128,128]{1,0:T(8,128)S(1)} %get-tuple-element.39), channel_id=1, source_target_pairs={{0,6},{2,4},{4,2},{6,0},{8,14},{10,12},{12,10},{14,8},{16,22},{18,... | collective-permute-start | bytes 196616 | tf_op jit(solution)/shard_map/ppermute | solution.py:242
  61.3 5.4 %collective-permute-start.14 = (f32[128,128]{1,0:T(8,128)S(1)}, f32[128,128]{1,0:T(8,128)S(1)}, u32[]{:S(2)}, u32[]{:S(2)}) collective-permute-start(f32[128,128]{1,0:T(8,128)S(1)} %get-tuple-element.40), channel_id=1, source_target_pairs={{0,2},{2,0},{4,6},{6,4},{8,10},{10,8},{12,14},{14,12},{16,18},{18,... | collective-permute-start | bytes 196616 | tf_op jit(solution)/shard_map/ppermute | solution.py:242
